TPU v7x, 32 devices: a whole 2x2x4 slice. The times are simulated.
32 devices in a mesh: theta: 16 (over z, x, core), gz: 2 (over y).
Axes of the slice: x: 2, y: 2, z: 4, core: 2. Of those that a mesh axis runs over, the one named last changes fastest.
Arguments:
- velocity: float32 [3, 256, 16, 512], P(None, 'theta', 'gz'), may hold values from -2 to 3.5
- radial_op: float32 [512, 544], replicated, may hold values from -0.25 to 0.25
- azimuth_stencil: float32 [21], replicated, may hold values from -1.25 to 1.25
- viscous_factor: float32 [1], replicated, may hold values from 1000000 to 10000000
Outputs:
- new_velocity: float32 [3, 256, 16, 512], P(None, 'theta', 'gz')
- nonlinear: float32 [3, 256, 16, 512], P(None, 'theta', 'gz')
All inputs are finite; a program needn't handle non-finite values.
Results may differ from a plain program's by a relative error of at most 0.000098.
Values sent between devices are 32-bit elements; how exact they have to be, the bound alone decides.
No kernel may reach another device: no remote copies, remote signals or barrier semaphores. Data moves between devices by JAX's collectives and lax.ppermute only.
A program may use at most 64 MiB of HBM per device.

v0:
```python
import jax
import jax.numpy as jnp
from jax import lax
from jax.sharding import PartitionSpec as P

AXIAL_WEIGHTS = (0.75, -0.15, 1.0 / 60.0)
STEP_WEIGHT = 0.2
MIRROR_SIGNS = (-1.0, -1.0, 1.0)


def partner_2(block, axis, bit):
    count = lax.axis_size(axis)
    route = []
    for low in range(count):
        high = low | 1 << bit
        if high != low and high < count:
            route += [(low, high), (high, low)]
    return lax.ppermute(block, axis, route)


def extended_2(shard, sides, width):
    for axis, dim in sides:
        peers, length = (lax.axis_size(axis), shard.shape[dim])
        up = [(i, (i + 1) % peers) for i in range(peers)]
        down = [(j, i) for i, j in up]
        last = lax.slice_in_dim(shard, length - width, length, axis=dim)
        initial = lax.slice_in_dim(shard, 0, width, axis=dim)
        before = lax.ppermute(last, axis, up)
        after = lax.ppermute(initial, axis, down)
        shard = jnp.concatenate([before, shard, after], axis=dim)
    return shard


def from_behind(shard, axis, by):
    peers = lax.axis_size(axis)
    return lax.ppermute(shard, axis, [(i, (i + by) % peers) for i in range(peers)])


def next_excess(excess):
    return 4.0 * excess * (1.0 - excess) / (1.0 + 4.0 * excess - 4.0 * excess * excess)


def reduce_step(center, lower_side, upper_side, excess):
    return (center - (excess - 0.5) * (lower_side + upper_side)) / (
        0.5 + 2.0 * excess - 2.0 * excess * excess
    )


def final_step(center, opposite, excess):
    return (center + (1.0 - 2.0 * excess) * opposite) / (4.0 * excess * (1.0 - excess))


def local(velocity, radial_op, azimuth_stencil, viscous_factor):
    cycle_size = lax.axis_size("theta")
    top_bit = cycle_size.bit_length() - 2
    points = velocity.shape[1]
    planes = velocity.shape[2]
    radial = velocity.shape[3]
    stencil_reach = (azimuth_stencil.shape[0] - 1) // 2
    tile_width = radial_op.shape[1] - radial
    highest = lax.Precision.HIGHEST
    radius = jnp.arange(radial).astype(jnp.float32) + 0.5
    inverse_r = 1.0 / radius
    sign_flip = jnp.array(MIRROR_SIGNS, jnp.float32).reshape(3, 1, 1, 1)
    partner = partner_2(velocity[:, :, :, :tile_width], "theta", top_bit)
    radial_grad = jnp.einsum("ctzj,ij->ctzi", velocity, radial_op[:, :radial], precision=highest)
    radial_grad = radial_grad + jnp.einsum(
        "ctzj,ij->ctzi", sign_flip * partner, radial_op[:, radial:], precision=highest
    )
    beside = extended_2(velocity, (("theta", 1),), stencil_reach)
    offset = (
        jnp.arange(points + 2 * stencil_reach, dtype=jnp.int32)[None, :]
        - jnp.arange(points, dtype=jnp.int32)[:, None]
    )
    selector = (
        offset[:, :, None] == jnp.arange(2 * stencil_reach + 1, dtype=jnp.int32)[None, None, :]
    ).astype(jnp.float32)
    band_matrix = jnp.einsum("pqk,k->pq", selector, azimuth_stencil, precision=highest)
    theta_grad = jnp.einsum("pq,cqzr->cpzr", band_matrix, beside, precision=highest)
    axial_ext = extended_2(velocity, (("gz", 2),), 3)
    axial_grad = jnp.zeros_like(velocity)
    for position, weight in enumerate(AXIAL_WEIGHTS):
        shift_by = position + 1
        upper_planes = axial_ext[:, :, 3 + shift_by : 3 + shift_by + planes]
        lower_planes = axial_ext[:, :, 3 - shift_by : 3 - shift_by + planes]
        axial_grad = axial_grad + weight * (upper_planes - lower_planes)
    radial_vel = velocity[0]
    azimuth_vel = velocity[1]
    axial_vel = velocity[2]
    convective = (
        radial_vel[None] * radial_grad
        + (azimuth_vel * inverse_r)[None] * theta_grad
        + axial_vel[None] * axial_grad
    )
    metric = jnp.stack(
        [
            -azimuth_vel * azimuth_vel * inverse_r,
            radial_vel * azimuth_vel * inverse_r,
            jnp.zeros_like(axial_vel),
        ]
    )
    nonlinear = convective + metric
    right_side = velocity - STEP_WEIGHT * nonlinear
    implicit_coef = viscous_factor[0] * inverse_r * inverse_r
    first_excess = 0.5 / (1.0 + 2.0 * implicit_coef)
    reduced = right_side * (2.0 * first_excess)
    excess = first_excess
    stride = 1
    while stride < points:
        extended = extended_2(reduced, (("theta", 1),), stride)
        reduced = reduce_step(reduced, extended[:, :points], extended[:, 2 * stride :], excess)
        excess = next_excess(excess)
        stride = stride * 2
    for bit_index in range(top_bit):
        hops = 1 << bit_index
        lower_side, upper_side = [
            from_behind(reduced, "theta", direction) for direction in (hops, cycle_size - hops)
        ]
        reduced = reduce_step(reduced, lower_side, upper_side, excess)
        excess = next_excess(excess)
    opposite = partner_2(reduced, "theta", top_bit)
    new_velocity = final_step(reduced, opposite, excess)
    return (new_velocity, nonlinear)


def solution(mesh):
    in_specs = (P(None, "theta", "gz", None), P(), P(), P())
    out_specs = (P(None, "theta", "gz", None), P(None, "theta", "gz", None))
    return jax.shard_map(local, mesh=mesh, in_specs=in_specs, out_specs=out_specs, check_vma=False)
```

profile of v0, /device:TPU:0, one launch (start us, length us, event | category | flops | bytes accessed | tf_op | source)
XLA Modules:
  0.0 190.8 jit_solution(11961293074028801656)
XLA Ops:
  2.5 5.0 %collective-permute-start.2 = (f32[3,10,8,512]{3,2,1,0:T(8,128)S(1)}, f32[3,10,8,512]{3,2,1,0:T(8,128)S(1)}, u32[]{:S(2)}, u32[]{:S(2)}) collective-permute-start(f32[3,10,8,512]{3,2,1,0:T(8,128)S(1)} %get-tuple-element.19), channel_id=1, source_target_pairs={{2,0},{4,2},{6,4},{8,6},{10,8},{12,10},{14,12},{16,14},{18,16},{20... | collective-permute-start | bytes 1474568 | tf_op jit(solution)/shard_map/ppermute | solution.py:29
  7.7 2.0 %collective-permute-start.3 = (f32[3,16,3,512]{3,2,1,0:T(4,128)S(1)}, f32[3,16,3,512]{3,2,1,0:T(4,128)S(1)}, u32[]{:S(2)}, u32[]{:S(2)}) collective-permute-start(f32[3,16,3,512]{3,2,1,0:T(4,128)S(1)} %get-tuple-element.20), channel_id=1, source_target_pairs={{1,0},{0,1},{3,2},{2,3},{5,4},{4,5},{7,6},{6,7},{9,8},{8,9},{11,10... | collective-permute-start | bytes 884744 | tf_op jit(solution)/shard_map/ppermute | solution.py:29
  14.7 5.1 %collective-permute-done.3 = f32[3,16,3,512]{3,2,1,0:T(4,128)S(1)} collective-permute-done((f32[3,16,3,512]{3,2,1,0:T(4,128)S(1)}, f32[3,16,3,512]{3,2,1,0:T(4,128)S(1)}, u32[]{:S(2)}, u32[]{:S(2)}) %collective-permute-start.3) | collective-permute-done | bytes 294944 | tf_op jit(solution)/shard_map/ppermute | solution.py:29
  20.5 1.9 fusion
  24.7 2.8 %subtract_multiply_fusion = (f32[3,16,8,512]{3,2,1,0:T(8,128)S(1)}, f32[3,16,8,512]{3,2,1,0:T(8,128)}) fusion(f32[3,16,8,512]{3,2,1,0:T(8,128)S(1)} %copy-done.1, f32[512]{0:T(512)S(1)} %broadcast_multiply_fusion, f32[3]{0:T(128)S(1)} %pad.18.clone, f32[1,16,8,512]{3,2,1,0:T(8,128)S(1)} %get-tuple-element.15, f32[1,16,8,512]{3,2,1,0:T(8,128)S(1)} %get-tuple-element.16, ...), kind=kOutput, calls=%fused_computation.59 | convolution fusion | flops 80031744 | bytes 8260608 | tf_op jit(solution)/shard_map/ctzj,ij->ctzi/dot_general | solution.py:67
  27.6 4.4 %collective-permute-start.6 = (f32[3,1,8,512]{3,2,1,0:T(8,128)S(1)}, f32[3,1,8,512]{3,2,1,0:T(8,128)S(1)}, u32[]{:S(2)}, u32[]{:S(2)}) collective-permute-start(f32[3,1,8,512]{3,2,1,0:T(8,128)S(1)} %get-tuple-element.12), channel_id=1, source_target_pairs={{2,0},{4,2},{6,4},{8,6},{10,8},{12,10},{14,12},{16,14},{18,16},{20... | collective-permute-start | bytes 147464 | tf_op jit(solution)/shard_map/ppermute | solution.py:29
  34.1 4.5 %collective-permute-start.8 = (f32[3,2,8,512]{3,2,1,0:T(8,128)S(1)}, f32[3,2,8,512]{3,2,1,0:T(8,128)S(1)}, u32[]{:S(2)}, u32[]{:S(2)}) collective-permute-start(f32[3,2,8,512]{3,2,1,0:T(8,128)S(1)} %get-tuple-element.10), channel_id=1, source_target_pairs={{2,0},{4,2},{6,4},{8,6},{10,8},{12,10},{14,12},{16,14},{18,16},{20... | collective-permute-start | bytes 294920 | tf_op jit(solution)/shard_map/ppermute | solution.py:29
  38.6 2.2 %collective-permute-done.7 = f32[3,2,8,512]{3,2,1,0:T(8,128)S(1)} collective-permute-done((f32[3,2,8,512]{3,2,1,0:T(8,128)S(1)}, f32[3,2,8,512]{3,2,1,0:T(8,128)S(1)}, u32[]{:S(2)}, u32[]{:S(2)}) %collective-permute-start.7) | collective-permute-done | bytes 98336 | tf_op jit(solution)/shard_map/ppermute | solution.py:28
  41.0 4.6 %collective-permute-start.10 = (f32[3,4,8,512]{3,2,1,0:T(8,128)S(1)}, f32[3,4,8,512]{3,2,1,0:T(8,128)S(1)}, u32[]{:S(2)}, u32[]{:S(2)}) collective-permute-start(f32[3,4,8,512]{3,2,1,0:T(8,128)S(1)} %get-tuple-element.8), channel_id=1, source_target_pairs={{2,0},{4,2},{6,4},{8,6},{10,8},{12,10},{14,12},{16,14},{18,16},{20... | collective-permute-start | bytes 589832 | tf_op jit(solution)/shard_map/ppermute | solution.py:29
  45.6 3.2 %collective-permute-done.10 = f32[3,4,8,512]{3,2,1,0:T(8,128)S(1)} collective-permute-done((f32[3,4,8,512]{3,2,1,0:T(8,128)S(1)}, f32[3,4,8,512]{3,2,1,0:T(8,128)S(1)}, u32[]{:S(2)}, u32[]{:S(2)}) %collective-permute-start.10) | collective-permute-done | bytes 196640 | tf_op jit(solution)/shard_map/ppermute | solution.py:29
  48.8 4.7 %collective-permute-done.9 = f32[3,4,8,512]{3,2,1,0:T(8,128)S(1)} collective-permute-done((f32[3,4,8,512]{3,2,1,0:T(8,128)S(1)}, f32[3,4,8,512]{3,2,1,0:T(8,128)S(1)}, u32[]{:S(2)}, u32[]{:S(2)}) %collective-permute-start.9) | collective-permute-done | bytes 196640 | tf_op jit(solution)/shard_map/ppermute | solution.py:28
  53.8 4.4 %collective-permute-start.12 = (f32[3,8,8,512]{3,2,1,0:T(8,128)S(1)}, f32[3,8,8,512]{3,2,1,0:T(8,128)S(1)}, u32[]{:S(2)}, u32[]{:S(2)}) collective-permute-start(f32[3,8,8,512]{3,2,1,0:T(8,128)S(1)} %get-tuple-element.6), channel_id=1, source_target_pairs={{2,0},{4,2},{6,4},{8,6},{10,8},{12,10},{14,12},{16,14},{18,16},{20... | collective-permute-start | bytes 1179656 | tf_op jit(solution)/shard_map/ppermute | solution.py:29
  58.2 5.4 %collective-permute-done.11 = f32[3,8,8,512]{3,2,1,0:T(8,128)S(1)} collective-permute-done((f32[3,8,8,512]{3,2,1,0:T(8,128)S(1)}, f32[3,8,8,512]{3,2,1,0:T(8,128)S(1)}, u32[]{:S(2)}, u32[]{:S(2)}) %collective-permute-start.11) | collective-permute-done | bytes 393248 | tf_op jit(solution)/shard_map/ppermute | solution.py:28
  63.9 4.6 %collective-permute-start.14 = (f32[3,16,8,512]{3,2,1,0:T(8,128)S(1)}, f32[3,16,8,512]{3,2,1,0:T(8,128)S(1)}, u32[]{:S(2)}, u32[]{:S(2)}) collective-permute-start(f32[3,16,8,512]{3,2,1,0:T(8,128)S(1)} %fusion.25), channel_id=1, source_target_pairs={{0,30},{2,0},{4,2},{6,4},{8,6},{10,8},{12,10},{14,12},{16,14},{18,... | collective-permute-start | bytes 2359304 | tf_op jit(solution)/shard_map/ppermute | solution.py:36
  68.6 9.7 %collective-permute-done.13 = f32[3,16,8,512]{3,2,1,0:T(8,128)S(1)} collective-permute-done((f32[3,16,8,512]{3,2,1,0:T(8,128)S(1)}, f32[3,16,8,512]{3,2,1,0:T(8,128)S(1)}, u32[]{:S(2)}, u32[]{:S(2)}) %collective-permute-start.13) | collective-permute-done | bytes 786464 | tf_op jit(solution)/shard_map/ppermute | solution.py:36
  78.5 2.1 %collective-permute-start.15 = (f32[3,16,8,512]{3,2,1,0:T(8,128)S(1)}, f32[3,16,8,512]{3,2,1,0:T(8,128)S(1)}, u32[]{:S(2)}, u32[]{:S(2)}) collective-permute-start(f32[3,16,8,512]{3,2,1,0:T(8,128)S(1)} %subtract_divide_fusion.2), channel_id=1, source_target_pairs={{0,4},{2,6},{4,8},{6,10},{8,12},{10,14},{12,16},{14,18},{16,20},{1... | collective-permute-start | bytes 2359304 | tf_op jit(solution)/shard_map/ppermute | solution.py:36
  80.7 5.3 %collective-permute-start.16 = (f32[3,16,8,512]{3,2,1,0:T(8,128)S(1)}, f32[3,16,8,512]{3,2,1,0:T(8,128)S(1)}, u32[]{:S(2)}, u32[]{:S(2)}) collective-permute-start(f32[3,16,8,512]{3,2,1,0:T(8,128)S(1)} %subtract_divide_fusion.2), channel_id=1, source_target_pairs={{0,28},{2,30},{4,0},{6,2},{8,4},{10,6},{12,8},{14,10},{16,12},{18,... | collective-permute-start | bytes 2359304 | tf_op jit(solution)/shard_map/ppermute | solution.py:36
  86.0 28.4 %collective-permute-done.15 = f32[3,16,8,512]{3,2,1,0:T(8,128)S(1)} collective-permute-done((f32[3,16,8,512]{3,2,1,0:T(8,128)S(1)}, f32[3,16,8,512]{3,2,1,0:T(8,128)S(1)}, u32[]{:S(2)}, u32[]{:S(2)}) %collective-permute-start.15) | collective-permute-done | bytes 786464 | tf_op jit(solution)/shard_map/ppermute | solution.py:36
  114.4 2.9 %collective-permute-done.16 = f32[3,16,8,512]{3,2,1,0:T(8,128)S(1)} collective-permute-done((f32[3,16,8,512]{3,2,1,0:T(8,128)S(1)}, f32[3,16,8,512]{3,2,1,0:T(8,128)S(1)}, u32[]{:S(2)}, u32[]{:S(2)}) %collective-permute-start.16) | collective-permute-done | bytes 786464 | tf_op jit(solution)/shard_map/ppermute | solution.py:36
  117.6 3.8 %collective-permute-start.18 = (f32[3,16,8,512]{3,2,1,0:T(8,128)S(1)}, f32[3,16,8,512]{3,2,1,0:T(8,128)S(1)}, u32[]{:S(2)}, u32[]{:S(2)}) collective-permute-start(f32[3,16,8,512]{3,2,1,0:T(8,128)S(1)} %subtract_divide_fusion.1), channel_id=1, source_target_pairs={{0,24},{2,26},{4,28},{6,30},{8,0},{10,2},{12,4},{14,6},{16,8},{18,... | collective-permute-start | bytes 2359304 | tf_op jit(solution)/shard_map/ppermute | solution.py:36
  121.5 18.4 %collective-permute-done.17 = f32[3,16,8,512]{3,2,1,0:T(8,128)S(1)} collective-permute-done((f32[3,16,8,512]{3,2,1,0:T(8,128)S(1)}, f32[3,16,8,512]{3,2,1,0:T(8,128)S(1)}, u32[]{:S(2)}, u32[]{:S(2)}) %collective-permute-start.17) | collective-permute-done | bytes 786464 | tf_op jit(solution)/shard_map/ppermute | solution.py:36
  139.9 13.6 %collective-permute-done.18 = f32[3,16,8,512]{3,2,1,0:T(8,128)S(1)} collective-permute-done((f32[3,16,8,512]{3,2,1,0:T(8,128)S(1)}, f32[3,16,8,512]{3,2,1,0:T(8,128)S(1)}, u32[]{:S(2)}, u32[]{:S(2)}) %collective-permute-start.18) | collective-permute-done | bytes 786464 | tf_op jit(solution)/shard_map/ppermute | solution.py:36
  153.8 2.4 %collective-permute-start.19 = (f32[3,16,8,512]{3,2,1,0:T(8,128)S(1)}, f32[3,16,8,512]{3,2,1,0:T(8,128)S(1)}, u32[]{:S(2)}, u32[]{:S(2)}) collective-permute-start(f32[3,16,8,512]{3,2,1,0:T(8,128)S(1)} %subtract_divide_fusion), channel_id=1, source_target_pairs={{0,16},{16,0},{2,18},{18,2},{4,20},{20,4},{6,22},{22,6},{8,24},{24... | collective-permute-start | bytes 2359304 | tf_op jit(solution)/shard_map/ppermute | solution.py:18
  156.3 33.4 %collective-permute-done.19 = f32[3,16,8,512]{3,2,1,0:T(8,128)S(1)} collective-permute-done((f32[3,16,8,512]{3,2,1,0:T(8,128)S(1)}, f32[3,16,8,512]{3,2,1,0:T(8,128)S(1)}, u32[]{:S(2)}, u32[]{:S(2)}) %collective-permute-start.19) | collective-permute-done | bytes 786464 | tf_op jit(solution)/shard_map/ppermute | solution.py:18
  (61 shorter events, 14.3 us)
Async XLA Ops:
  0.6 11.3 %copy-start = (f32[21]{0:T(128)S(1)}, f32[21]{0:T(128)}, u32[]{:S(2)}) copy-start(f32[21]{0:T(128)} %param.7) | copy-start | bytes 256
  0.6 6.9 %copy-start.1 = (f32[3,16,8,512]{3,2,1,0:T(8,128)S(1)}, f32[3,16,8,512]{3,2,1,0:T(8,128)}, u32[]{:S(2)}) copy-start(f32[3,16,8,512]{3,2,1,0:T(8,128)} %param.5) | copy-start | bytes 2359300
  2.0 17.9 %collective-permute-start.1 = (f32[3,10,8,512]{3,2,1,0:T(8,128)S(1)}, f32[3,10,8,512]{3,2,1,0:T(8,128)S(1)}, u32[]{:S(2)}, u32[]{:S(2)}) collective-permute-start(f32[3,10,8,512]{3,2,1,0:T(8,128)S(1)} %get-tuple-element.18), channel_id=1, source_target_pairs={{0,2},{2,4},{4,6},{6,8},{8,10},{10,12},{12,14},{14,16},{16,18},{18... | collective-permute-start | bytes 1474568 | tf_op jit(solution)/shard_map/ppermute | solution.py:28
  2.5 17.7 %collective-permute-start.2 = (f32[3,10,8,512]{3,2,1,0:T(8,128)S(1)}, f32[3,10,8,512]{3,2,1,0:T(8,128)S(1)}, u32[]{:S(2)}, u32[]{:S(2)}) collective-permute-start(f32[3,10,8,512]{3,2,1,0:T(8,128)S(1)} %get-tuple-element.19), channel_id=1, source_target_pairs={{2,0},{4,2},{6,4},{8,6},{10,8},{12,10},{14,12},{16,14},{18,16},{20... | collective-permute-start | bytes 1474568 | tf_op jit(solution)/shard_map/ppermute | solution.py:29
  7.7 12.1 %collective-permute-start.3 = (f32[3,16,3,512]{3,2,1,0:T(4,128)S(1)}, f32[3,16,3,512]{3,2,1,0:T(4,128)S(1)}, u32[]{:S(2)}, u32[]{:S(2)}) collective-permute-start(f32[3,16,3,512]{3,2,1,0:T(4,128)S(1)} %get-tuple-element.20), channel_id=1, source_target_pairs={{1,0},{0,1},{3,2},{2,3},{5,4},{4,5},{7,6},{6,7},{9,8},{8,9},{11,10... | collective-permute-start | bytes 884744 | tf_op jit(solution)/shard_map/ppermute | solution.py:29
  9.6 15.1 %collective-permute-start.4 = (f32[3,16,3,512]{3,2,1,0:T(4,128)S(1)}, f32[3,16,3,512]{3,2,1,0:T(4,128)S(1)}, u32[]{:S(2)}, u32[]{:S(2)}) collective-permute-start(f32[3,16,3,512]{3,2,1,0:T(4,128)S(1)} %get-tuple-element.21), channel_id=1, source_target_pairs={{0,1},{1,0},{2,3},{3,2},{4,5},{5,4},{6,7},{7,6},{8,9},{9,8},{10,11... | collective-permute-start | bytes 884744 | tf_op jit(solution)/shard_map/ppermute | solution.py:28
  9.8 14.2 %collective-permute-start = (f32[3,16,8,32]{3,2,1,0:T(8,128)S(1)}, f32[3,16,8,32]{3,2,1,0:T(8,128)S(1)}, u32[]{:S(2)}, u32[]{:S(2)}) collective-permute-start(f32[3,16,8,32]{3,2,1,0:T(8,128)S(1)} %slice.112), channel_id=1, source_target_pairs={{0,16},{16,0},{2,18},{18,2},{4,20},{20,4},{6,22},{22,6},{8,24},{24... | collective-permute-start | bytes 147464 | tf_op jit(solution)/shard_map/ppermute | solution.py:18
  11.8 1.4 copy-start.2
  20.5 4.2 %copy-start.3 = (f32[3]{0:T(128)S(1)}, f32[3]{0:T(128)}, u32[]{:S(2)}) copy-start(f32[3]{0:T(128)} %constant.28.clone) | copy-start | bytes 40
  27.6 6.3 %collective-permute-start.5 = (f32[3,1,8,512]{3,2,1,0:T(8,128)S(1)}, f32[3,1,8,512]{3,2,1,0:T(8,128)S(1)}, u32[]{:S(2)}, u32[]{:S(2)}) collective-permute-start(f32[3,1,8,512]{3,2,1,0:T(8,128)S(1)} %get-tuple-element.11), channel_id=1, source_target_pairs={{0,2},{2,4},{4,6},{6,8},{8,10},{10,12},{12,14},{14,16},{16,18},{18... | collective-permute-start | bytes 147464 | tf_op jit(solution)/shard_map/ppermute | solution.py:28
  27.6 6.2 %collective-permute-start.6 = (f32[3,1,8,512]{3,2,1,0:T(8,128)S(1)}, f32[3,1,8,512]{3,2,1,0:T(8,128)S(1)}, u32[]{:S(2)}, u32[]{:S(2)}) collective-permute-start(f32[3,1,8,512]{3,2,1,0:T(8,128)S(1)} %get-tuple-element.12), channel_id=1, source_target_pairs={{2,0},{4,2},{6,4},{8,6},{10,8},{12,10},{14,12},{16,14},{18,16},{20... | collective-permute-start | bytes 147464 | tf_op jit(solution)/shard_map/ppermute | solution.py:29
  34.0 6.8 %collective-permute-start.7 = (f32[3,2,8,512]{3,2,1,0:T(8,128)S(1)}, f32[3,2,8,512]{3,2,1,0:T(8,128)S(1)}, u32[]{:S(2)}, u32[]{:S(2)}) collective-permute-start(f32[3,2,8,512]{3,2,1,0:T(8,128)S(1)} %get-tuple-element.9), channel_id=1, source_target_pairs={{0,2},{2,4},{4,6},{6,8},{8,10},{10,12},{12,14},{14,16},{16,18},{18... | collective-permute-start | bytes 294920 | tf_op jit(solution)/shard_map/ppermute | solution.py:28
  34.1 6.8 %collective-permute-start.8 = (f32[3,2,8,512]{3,2,1,0:T(8,128)S(1)}, f32[3,2,8,512]{3,2,1,0:T(8,128)S(1)}, u32[]{:S(2)}, u32[]{:S(2)}) collective-permute-start(f32[3,2,8,512]{3,2,1,0:T(8,128)S(1)} %get-tuple-element.10), channel_id=1, source_target_pairs={{2,0},{4,2},{6,4},{8,6},{10,8},{12,10},{14,12},{16,14},{18,16},{20... | collective-permute-start | bytes 294920 | tf_op jit(solution)/shard_map/ppermute | solution.py:29
  41.0 7.7 %collective-permute-start.10 = (f32[3,4,8,512]{3,2,1,0:T(8,128)S(1)}, f32[3,4,8,512]{3,2,1,0:T(8,128)S(1)}, u32[]{:S(2)}, u32[]{:S(2)}) collective-permute-start(f32[3,4,8,512]{3,2,1,0:T(8,128)S(1)} %get-tuple-element.8), channel_id=1, source_target_pairs={{2,0},{4,2},{6,4},{8,6},{10,8},{12,10},{14,12},{16,14},{18,16},{20... | collective-permute-start | bytes 589832 | tf_op jit(solution)/shard_map/ppermute | solution.py:29
  45.6 7.9 %collective-permute-start.9 = (f32[3,4,8,512]{3,2,1,0:T(8,128)S(1)}, f32[3,4,8,512]{3,2,1,0:T(8,128)S(1)}, u32[]{:S(2)}, u32[]{:S(2)}) collective-permute-start(f32[3,4,8,512]{3,2,1,0:T(8,128)S(1)} %get-tuple-element.7), channel_id=1, source_target_pairs={{0,2},{2,4},{4,6},{6,8},{8,10},{10,12},{12,14},{14,16},{16,18},{18... | collective-permute-start | bytes 589832 | tf_op jit(solution)/shard_map/ppermute | solution.py:28
  53.7 10.0 %collective-permute-start.11 = (f32[3,8,8,512]{3,2,1,0:T(8,128)S(1)}, f32[3,8,8,512]{3,2,1,0:T(8,128)S(1)}, u32[]{:S(2)}, u32[]{:S(2)}) collective-permute-start(f32[3,8,8,512]{3,2,1,0:T(8,128)S(1)} %get-tuple-element.5), channel_id=1, source_target_pairs={{0,2},{2,4},{4,6},{6,8},{8,10},{10,12},{12,14},{14,16},{16,18},{18... | collective-permute-start | bytes 1179656 | tf_op jit(solution)/shard_map/ppermute | solution.py:28
  53.8 9.9 %collective-permute-start.12 = (f32[3,8,8,512]{3,2,1,0:T(8,128)S(1)}, f32[3,8,8,512]{3,2,1,0:T(8,128)S(1)}, u32[]{:S(2)}, u32[]{:S(2)}) collective-permute-start(f32[3,8,8,512]{3,2,1,0:T(8,128)S(1)} %get-tuple-element.6), channel_id=1, source_target_pairs={{2,0},{4,2},{6,4},{8,6},{10,8},{12,10},{14,12},{16,14},{18,16},{20... | collective-permute-start | bytes 1179656 | tf_op jit(solution)/shard_map/ppermute | solution.py:29
  63.9 14.4 %collective-permute-start.13 = (f32[3,16,8,512]{3,2,1,0:T(8,128)S(1)}, f32[3,16,8,512]{3,2,1,0:T(8,128)S(1)}, u32[]{:S(2)}, u32[]{:S(2)}) collective-permute-start(f32[3,16,8,512]{3,2,1,0:T(8,128)S(1)} %fusion.25), channel_id=1, source_target_pairs={{0,2},{2,4},{4,6},{6,8},{8,10},{10,12},{12,14},{14,16},{16,18},{18... | collective-permute-start | bytes 2359304 | tf_op jit(solution)/shard_map/ppermute | solution.py:36
  63.9 14.3 %collective-permute-start.14 = (f32[3,16,8,512]{3,2,1,0:T(8,128)S(1)}, f32[3,16,8,512]{3,2,1,0:T(8,128)S(1)}, u32[]{:S(2)}, u32[]{:S(2)}) collective-permute-start(f32[3,16,8,512]{3,2,1,0:T(8,128)S(1)} %fusion.25), channel_id=1, source_target_pairs={{0,30},{2,0},{4,2},{6,4},{8,6},{10,8},{12,10},{14,12},{16,14},{18,... | collective-permute-start | bytes 2359304 | tf_op jit(solution)/shard_map/ppermute | solution.py:36
  78.5 35.9 %collective-permute-start.15 = (f32[3,16,8,512]{3,2,1,0:T(8,128)S(1)}, f32[3,16,8,512]{3,2,1,0:T(8,128)S(1)}, u32[]{:S(2)}, u32[]{:S(2)}) collective-permute-start(f32[3,16,8,512]{3,2,1,0:T(8,128)S(1)} %subtract_divide_fusion.2), channel_id=1, source_target_pairs={{0,4},{2,6},{4,8},{6,10},{8,12},{10,14},{12,16},{14,18},{16,20},{1... | collective-permute-start | bytes 2359304 | tf_op jit(solution)/shard_map/ppermute | solution.py:36
  80.7 36.6 %collective-permute-start.16 = (f32[3,16,8,512]{3,2,1,0:T(8,128)S(1)}, f32[3,16,8,512]{3,2,1,0:T(8,128)S(1)}, u32[]{:S(2)}, u32[]{:S(2)}) collective-permute-start(f32[3,16,8,512]{3,2,1,0:T(8,128)S(1)} %subtract_divide_fusion.2), channel_id=1, source_target_pairs={{0,28},{2,30},{4,0},{6,2},{8,4},{10,6},{12,8},{14,10},{16,12},{18,... | collective-permute-start | bytes 2359304 | tf_op jit(solution)/shard_map/ppermute | solution.py:36
  117.6 22.3 %collective-permute-start.17 = (f32[3,16,8,512]{3,2,1,0:T(8,128)S(1)}, f32[3,16,8,512]{3,2,1,0:T(8,128)S(1)}, u32[]{:S(2)}, u32[]{:S(2)}) collective-permute-start(f32[3,16,8,512]{3,2,1,0:T(8,128)S(1)} %subtract_divide_fusion.1), channel_id=1, source_target_pairs={{0,8},{2,10},{4,12},{6,14},{8,16},{10,18},{12,20},{14,22},{16,24},... | collective-permute-start | bytes 2359304 | tf_op jit(solution)/shard_map/ppermute | solution.py:36
  117.6 35.9 %collective-permute-start.18 = (f32[3,16,8,512]{3,2,1,0:T(8,128)S(1)}, f32[3,16,8,512]{3,2,1,0:T(8,128)S(1)}, u32[]{:S(2)}, u32[]{:S(2)}) collective-permute-start(f32[3,16,8,512]{3,2,1,0:T(8,128)S(1)} %subtract_divide_fusion.1), channel_id=1, source_target_pairs={{0,24},{2,26},{4,28},{6,30},{8,0},{10,2},{12,4},{14,6},{16,8},{18,... | collective-permute-start | bytes 2359304 | tf_op jit(solution)/shard_map/ppermute | solution.py:36
  153.8 35.9 %collective-permute-start.19 = (f32[3,16,8,512]{3,2,1,0:T(8,128)S(1)}, f32[3,16,8,512]{3,2,1,0:T(8,128)S(1)}, u32[]{:S(2)}, u32[]{:S(2)}) collective-permute-start(f32[3,16,8,512]{3,2,1,0:T(8,128)S(1)} %subtract_divide_fusion), channel_id=1, source_target_pairs={{0,16},{16,0},{2,18},{18,2},{4,20},{20,4},{6,22},{22,6},{8,24},{24... | collective-permute-start | bytes 2359304 | tf_op jit(solution)/shard_map/ppermute | solution.py:18
where the time goes:
time: 191 us
  waiting for transfers between devices  131 us (69%)
  starting transfers between devices  45.3 us (24%)
  matrix products  6.86 us (4%)
  local copies, waits for them, and re-layouts  2.95 us (2%)
  other arithmetic  2.95 us (2%)
    ppermute x6, waiting for transfers between devices, from_behind(): lax.ppermute(shard, axis, [(i, (i + by) % peers) for i in range(peers)])  73 us
    ppermute x2, waiting for transfers between devices, partner_2(): return lax.ppermute(block, axis, route)  34.9 us
    ppermute x6, starting transfers between devices, extended_2(): after = lax.ppermute(initial, axis, down)  25 us
    ppermute x6, starting transfers between devices, from_behind(): lax.ppermute(shard, axis, [(i, (i + by) % peers) for i in range(peers)])  15.9 us
    ppermute x6, waiting for transfers between devices, extended_2(): before = lax.ppermute(last, axis, up)  14.9 us
    ppermute x6, waiting for transfers between devices, extended_2(): after = lax.ppermute(initial, axis, down)  8.27 us
  transfers between devices with their start and end apart: 20, of which 14 were waited for; matrix products, arithmetic and copies ran while one was open for 3% of the time, Pallas kernels for 0%

commit v1 on v0

v1 whole, which is shorter than its diff:
```python
import functools

import jax
import jax.numpy as jnp
from jax import lax
from jax.experimental import pallas as pl
from jax.experimental.pallas import tpu as pltpu
from jax.sharding import PartitionSpec as P

AXIAL_WEIGHTS = (0.75, -0.15, 1.0 / 60.0)
AXIAL_REACH = len(AXIAL_WEIGHTS)
STEP_WEIGHT = 0.2
MIRROR_SIGNS = (-1.0, -1.0, 1.0)
LANES = 128
UNROLL = 16

VMEM = pl.BlockSpec(memory_space=pltpu.VMEM)
SMEM = pl.BlockSpec(memory_space=pltpu.SMEM)


def params(block_bytes, blocks):
    return pltpu.CompilerParams(vmem_limit_bytes=(6 << 20) + blocks * block_bytes)


def each(count, body):
    if count <= UNROLL:
        for i in range(count):
            body(i)
    else:
        pl.loop(0, count)(body)


def swap(block, axis, bit):
    size = lax.axis_size(axis)
    return lax.ppermute(block, axis, [(i, i ^ bit) for i in range(size)])


def swap_across(block, axis):
    size = lax.axis_size(axis)
    route = []
    for odd in range(1, size, 2):
        route += [(odd, (odd + 1) % size), ((odd + 1) % size, odd)]
    return lax.ppermute(block, axis, route)


def split(x):
    high = x.astype(jnp.bfloat16)
    return high, (x - high.astype(jnp.float32)).astype(jnp.bfloat16)


def product(left, right):
    dot = functools.partial(jnp.dot, preferred_element_type=jnp.float32)
    return dot(left[0], right[0]) + (dot(left[0], right[1]) + dot(left[1], right[0]))


def pack_planes_kernel(v_ref, y_ref):
    carriers = y_ref.shape[1]
    riders = v_ref.shape[1] - carriers
    lo, hi = AXIAL_REACH, v_ref.shape[2] - AXIAL_REACH

    def carry(t):
        for c in range(3):
            y_ref[c, t] = v_ref[c, t]

    def ride(j):
        for c in range(3):
            t = carriers + j
            y_ref[c, 3 * j, lo:hi] = v_ref[c, t, 0:2]
            y_ref[c, 3 * j + 1, lo : lo + 1] = v_ref[c, t, 2:3]
            y_ref[c, 3 * j + 1, lo + 1 : hi] = v_ref[c, t, hi : hi + 1]
            y_ref[c, 3 * j + 2, lo:hi] = v_ref[c, t, hi + 1 :]

    each(carriers, carry)
    each(riders, ride)


def pack_planes(v):
    comps, points, planes, radial = v.shape
    return pl.pallas_call(
        pack_planes_kernel,
        name="pack_planes",
        out_shape=jax.ShapeDtypeStruct((comps, points - points // 4, planes, radial), v.dtype),
        in_specs=[VMEM],
        out_specs=VMEM,
        compiler_params=params(v.size * 4, 2),
    )(v)


def pack_sides_kernel(me_ref, v_ref, core_ref, chip_ref, mirror_ref):
    points = v_ref.shape[1]
    reach = core_ref.shape[1]
    even = me_ref[0] % 2 == 0
    to_core = jnp.where(even, points - reach, 0)
    to_chip = jnp.where(even, 0, points - reach)
    for c in range(3):
        for h in range(reach):
            core_ref[c, h] = v_ref[c, to_core + h]
            chip_ref[c, h] = v_ref[c, to_chip + h]
    tiles = mirror_ref.shape[1]
    width = LANES // (points // tiles)
    lane = lax.broadcasted_iota(jnp.int32, mirror_ref.shape[2:], 1)

    def put(p):
        for c in range(3):
            tile = v_ref[c, p, :, :LANES]
            for q in range(1, points // tiles):
                part = pltpu.roll(v_ref[c, q * tiles + p, :, :LANES], q * width, 1)
                tile = jnp.where(lane < q * width, tile, part)
            mirror_ref[c, p] = tile

    each(tiles, put)


def pack_sides(me, v, reach, width):
    comps, points, planes, radial = v.shape
    tiles = points // (LANES // width)
    side = jax.ShapeDtypeStruct((comps, reach, planes, radial), v.dtype)
    return pl.pallas_call(
        pack_sides_kernel,
        name="pack_sides",
        out_shape=(side, side, jax.ShapeDtypeStruct((comps, tiles, planes, LANES), v.dtype)),
        in_specs=[SMEM, VMEM],
        out_specs=(VMEM, VMEM, VMEM),
        compiler_params=params(v.size * 4, 3),
    )(me, v)


def inverse_radius(radial):
    return 1.0 / (lax.broadcasted_iota(jnp.int32, (1, radial), 1).astype(jnp.float32) + 0.5)


def axial_weights(planes, inside):
    row = lax.broadcasted_iota(jnp.int32, (planes, 1), 0)
    weights = []
    for m, w in enumerate(AXIAL_WEIGHTS, 1):
        for shift, own, sign in ((m, row < planes - m, 1.0), (planes - m, row >= m, -1.0)):
            keep = own if inside else jnp.logical_not(own)
            weights.append((shift, jnp.where(keep, sign * w, 0.0)))
    return weights


def axial_part(tile, weights):
    planes = tile.shape[0]
    total = None
    for shift, weight in weights:
        term = weight * pltpu.roll(tile, planes - shift, 0)
        total = term if total is None else total + term
    return total


def inner_kernel(stencil_ref, v_ref, op_ref, n_ref, grad_ref):
    comps, points, planes, radial = v_ref.shape
    reach = (stencil_ref.shape[0] - 1) // 2
    rows = points * planes
    right = split(op_ref[:radial])
    for c in range(comps):
        grad_ref[c * rows : (c + 1) * rows] = product(split(v_ref[c].reshape(rows, radial)), right)
    inv_r = inverse_radius(radial)
    weights = axial_weights(planes, True)

    def point(t, lows, highs):
        a, b, e = v_ref[0, t], v_ref[1, t], v_ref[2, t]
        b_inv = b * inv_r
        for c in range(comps):
            around = None
            for m in range(-lows, highs + 1):
                term = stencil_ref[m + reach] * v_ref[c, t + m]
                around = term if around is None else around + term
            start = c * rows + t * planes
            grad = grad_ref[pl.ds(pl.multiple_of(start, planes), planes)]
            n = a * grad + b_inv * around + e * axial_part(v_ref[c, t], weights)
            if c == 0:
                n = n - b_inv * b
            elif c == 1:
                n = n + a * b_inv
            n_ref[c, t] = n

    for t in range(reach):
        point(t, t, min(reach, points - 1 - t))
    each(points - 2 * reach, lambda i: point(i + reach, reach, reach)) if points >= 2 * reach else None
    for t in range(max(reach, points - reach), points):
        point(t, min(reach, t), points - 1 - t)


def inner_terms(stencil, v, op):
    return pl.pallas_call(
        inner_kernel,
        name="inner_terms",
        out_shape=jax.ShapeDtypeStruct(v.shape, v.dtype),
        in_specs=[SMEM, VMEM, VMEM],
        out_specs=VMEM,
        scratch_shapes=[pltpu.VMEM((v.size // v.shape[3], v.shape[3]), jnp.float32)],
        compiler_params=params(v.size * 4, 6),
        cost_estimate=pl.CostEstimate(flops=6 * v.size * v.shape[3], bytes_accessed=16 * v.size, transcendentals=0),
    )(stencil, v, op)


def sides_kernel(me_ref, stencil_ref, v_ref, op_ref, core_ref, chip_ref, mirror_ref, n_in_ref, n_ref, grad_ref):
    comps, points, planes, radial = v_ref.shape
    reach = core_ref.shape[1]
    tiles = mirror_ref.shape[1]
    count = points // tiles
    width = LANES // count
    rows = tiles * planes
    right = split(jnp.concatenate([op_ref[radial:]] * count, axis=0))
    lane = lax.broadcasted_iota(jnp.int32, (rows, LANES), 1)
    for c in range(comps):
        high, low = split(MIRROR_SIGNS[c] * mirror_ref[c].reshape(rows, LANES))
        zero = jnp.zeros_like(high)
        parts = [
            [jnp.where((lane >= q * width) & (lane < (q + 1) * width), x, zero) for q in range(count)]
            for x in (high, low)
        ]
        left = [jnp.concatenate(x, axis=0) for x in parts]
        grad_ref[c * points * planes : (c + 1) * points * planes] = product(left, right)
    inv_r = inverse_radius(radial)

    def finish(t, taps):
        a = v_ref[0, t]
        b_inv = v_ref[1, t] * inv_r
        for c in range(comps):
            start = (c * points + t) * planes
            n = n_in_ref[c, t] + a * grad_ref[pl.ds(pl.multiple_of(start, planes), planes)]
            around = None
            for ref, h, k in taps:
                term = stencil_ref[k] * ref[c, h]
                around = term if around is None else around + term
            if around is not None:
                n = n + b_inv * around
            n_ref[c, t] = n

    def all_points(before, after):
        def taps(t):
            found = [(before, h, h - t) for h in range(t, reach)]
            found += [(after, h, points + h - t + reach) for h in range(min(reach, reach - points + t + 1))]
            return found

        for t in range(reach):
            finish(t, taps(t))
        if points > 2 * reach:
            each(points - 2 * reach, lambda i: finish(i + reach, []))
        for t in range(max(reach, points - reach), points):
            finish(t, taps(t))

    even = me_ref[0] % 2 == 0
    pl.when(even)(lambda: all_points(chip_ref, core_ref))
    pl.when(jnp.logical_not(even))(lambda: all_points(core_ref, chip_ref))


def sides_terms(me, stencil, v, op, core, chip, mirror, n):
    return pl.pallas_call(
        sides_kernel,
        name="sides_terms",
        out_shape=jax.ShapeDtypeStruct(v.shape, v.dtype),
        in_specs=[SMEM, SMEM, VMEM, VMEM, VMEM, VMEM, VMEM, VMEM],
        out_specs=VMEM,
        scratch_shapes=[pltpu.VMEM((v.size // v.shape[3], v.shape[3]), jnp.float32)],
        input_output_aliases={7: 0},
        compiler_params=params(v.size * 4, 8),
        cost_estimate=pl.CostEstimate(flops=2 * v.size * LANES, bytes_accessed=16 * v.size, transcendentals=0),
    )(me, stencil, v, op, core, chip, mirror, n)


def planes_kernel(v_ref, y_ref, power_ref, n_in_ref, n_ref, ends_ref, tile_ref):
    comps, points, planes, radial = v_ref.shape
    carriers = y_ref.shape[1]
    lo, hi = AXIAL_REACH, planes - AXIAL_REACH
    weights = axial_weights(planes, False)
    decay = power_ref[1:2]
    ends_ref[...] = jnp.zeros_like(ends_ref)

    def finish(t, c, tile):
        n = n_in_ref[c, t] + v_ref[2, t] * axial_part(tile, weights)
        n_ref[c, t] = n
        right_side = v_ref[c, t] - STEP_WEIGHT * n
        ends_ref[0, c] = decay * ends_ref[0, c] + right_side
        ends_ref[1, c] = ends_ref[1, c] + power_ref[pl.ds(t, 1)] * right_side

    def carried(t):
        for c in range(comps):
            finish(t, c, y_ref[c, t])

    def ridden(j):
        for c in range(comps):
            tile_ref[c, 0:2] = y_ref[c, 3 * j, lo:hi]
            tile_ref[c, 2:3] = y_ref[c, 3 * j + 1, lo : lo + 1]
            tile_ref[c, lo:hi] = jnp.zeros_like(tile_ref[c, lo:hi])
            tile_ref[c, hi : hi + 1] = y_ref[c, 3 * j + 1, lo + 1 : hi]
            tile_ref[c, hi + 1 :] = y_ref[c, 3 * j + 2, lo:hi]
            finish(carriers + j, c, tile_ref[c])

    each(carriers, carried)
    each(points - carriers, ridden)


def planes_terms(v, y, power, n):
    comps, points, planes, radial = v.shape
    return pl.pallas_call(
        planes_kernel,
        name="planes_terms",
        out_shape=(
            jax.ShapeDtypeStruct(v.shape, v.dtype),
            jax.ShapeDtypeStruct((2, comps, planes, radial), v.dtype),
        ),
        in_specs=[VMEM] * 4,
        out_specs=(VMEM, VMEM),
        scratch_shapes=[pltpu.VMEM((comps, planes, radial), jnp.float32)],
        input_output_aliases={3: 0},
        compiler_params=params(v.size * 4, 6),
        cost_estimate=pl.CostEstimate(flops=20 * v.size, bytes_accessed=16 * v.size, transcendentals=0),
    )(v, y, power, n)


def powers(viscous_factor, points, sectors, radial):
    radius = jnp.arange(radial).astype(jnp.float32) + 0.5
    half = 0.5 * radius * lax.rsqrt(viscous_factor[0])
    root = jnp.sqrt(1.0 + half * half)
    loss = 2.0 * half * (root - half)
    rows = [jnp.ones_like(loss)]
    for _ in range(points):
        rows.append(rows[-1] * (1.0 - loss))
    total, have = loss, 1
    left, result = points * sectors, None
    while left:
        if left & 1:
            result = total if result is None else result + total - result * total
        total = total * (2.0 - total)
        left >>= 1
    return jnp.stack(rows + [half / root, 1.0 / result])


def sweep_kernel(v_ref, n_ref, power_ref, s_ref):
    comps, points, planes, radial = v_ref.shape
    decay = power_ref[1:2]
    height = power_ref[points + 1 : points + 2]
    for c in range(comps):
        s_ref[c, 0] = height * (v_ref[c, 0] - STEP_WEIGHT * n_ref[c, 0])

        def forward(i):
            t = i + 1
            s_ref[c, t] = decay * s_ref[c, t - 1] + height * (v_ref[c, t] - STEP_WEIGHT * n_ref[c, t])

        each(points - 1, forward)

    def backward(i, carry):
        t = points - 1 - i
        after = []
        for c in range(comps):
            s_ref[c, t] = s_ref[c, t] + carry[c]
            after.append(decay * (carry[c] + height * (v_ref[c, t] - STEP_WEIGHT * n_ref[c, t])))
        return tuple(after)

    start = (jnp.zeros((planes, radial), jnp.float32),) * comps
    lax.fori_loop(0, points, backward, start, unroll=points <= UNROLL)


def sweep(v, n, power):
    return pl.pallas_call(
        sweep_kernel,
        name="sweep",
        out_shape=jax.ShapeDtypeStruct(v.shape, v.dtype),
        in_specs=[VMEM] * 3,
        out_specs=VMEM,
        compiler_params=params(v.size * 4, 4),
        cost_estimate=pl.CostEstimate(flops=10 * v.size, bytes_accessed=12 * v.size, transcendentals=0),
    )(v, n, power)


def close_kernel(me_ref, s_ref, power_ref, ends_ref, x_ref):
    comps, points, planes, radial = s_ref.shape
    sectors = ends_ref.shape[0]
    me = me_ref[0]
    hop = power_ref[points : points + 1]
    scale = power_ref[points + 1 : points + 2] * power_ref[points + 2 : points + 3]
    for c in range(comps):
        before = jnp.zeros((planes, radial), jnp.float32)
        after = before
        for j in range(sectors, 0, -1):
            before = hop * before + ends_ref[lax.rem(me + sectors - j, sectors), 0, c]
            after = hop * after + ends_ref[lax.rem(me + j, sectors), 1, c]
        before = scale * before
        after = scale * after

        def point(t):
            x_ref[c, t] = s_ref[c, t] + power_ref[pl.ds(t + 1, 1)] * before + power_ref[pl.ds(points - t, 1)] * after

        each(points, point)


def close(me, s, power, ends):
    return pl.pallas_call(
        close_kernel,
        name="close",
        out_shape=jax.ShapeDtypeStruct(s.shape, s.dtype),
        in_specs=[SMEM, VMEM, VMEM, VMEM],
        out_specs=VMEM,
        compiler_params=params(s.size * 4, 5),
    )(me, s, power, ends)


def local(velocity, radial_op, azimuth_stencil, viscous_factor):
    sectors = lax.axis_size("theta")
    comps, points, planes, radial = velocity.shape
    reach = (azimuth_stencil.shape[0] - 1) // 2
    width = radial_op.shape[1] - radial
    me = lax.axis_index("theta").astype(jnp.int32).reshape(1)
    op = radial_op.T

    planes_out = pack_planes(velocity)
    planes_in = swap(planes_out, "gz", 1)
    core_out, chip_out, mirror_out = pack_sides(me, velocity, reach, width)
    chip_in = swap_across(chip_out, "theta")
    core_in = swap(core_out, "theta", 1)
    mirror_in = swap(mirror_out, "theta", sectors // 2)
    power = powers(viscous_factor, points, sectors, radial)
    n = inner_terms(azimuth_stencil, velocity, op)
    n = sides_terms(me, azimuth_stencil, velocity, op, core_in, chip_in, mirror_in, n)
    nonlinear, ends = planes_terms(velocity, planes_in, power, n)
    everyone = lax.all_gather(ends, "theta")
    s = sweep(velocity, nonlinear, power)
    new_velocity = close(me, s, power, everyone)
    return (new_velocity, nonlinear)


def solution(mesh):
    in_specs = (P(None, "theta", "gz", None), P(), P(), P())
    out_specs = (P(None, "theta", "gz", None), P(None, "theta", "gz", None))
    return jax.shard_map(local, mesh=mesh, in_specs=in_specs, out_specs=out_specs, check_vma=False)
```

time: 191 us -> 83.1 us (0.44)
  waiting for transfers between devices: 131 us -> 44.2 us
  starting transfers between devices: 45.3 us -> 8.05 us
  between operations: 1.59 us -> 14.8 us
  Pallas kernels: 0 us -> 11.6 us
  matrix products: 6.86 us -> 0 us
  other arithmetic: 2.95 us -> 0.27 us
    ppermute x20 -> x4, waiting for transfers between devices: 131 us -> 4.66 us  [the longest x1 4.65 us: swap_across(): return lax.ppermute(block, axis, route)]
    all_gather x0 -> x1, waiting for transfers between devices: none -> 39.5 us  [local(): everyone = lax.all_gather(ends, 'theta')]
    ppermute x20 -> x4, starting transfers between devices: 45.3 us -> 8.01 us  [the longest x3 5.62 us: swap(): return lax.ppermute(block, axis, [(i, i ^ bit) for i in range(size)])]
    pallas_call x0 -> x7, Pallas kernels: none -> 11.6 us  [the longest x1 3.24 us: sides_terms(): pl.pallas_call(sides_kernel, name='sides_terms', out_shape=jax.ShapeDtype...]
    dot_general x4 -> x0, matrix products: 6.86 us -> none  [the longest x1 2.82 us: local(): jnp.einsum('ctzj,ij->ctzi', sign_flip * partner, radial_op[:, radial:], p...]
    unnamed x10 -> x12, local copies, waits for them, and re-layouts: 0.56 us -> 3.67 us
    div x9 -> x1, other arithmetic: 2.49 us -> 0.04 us  [powers(): return jnp.stack(rows + [half / root, 1.0 / result])]
  transfers between devices with their start and end apart: 20 -> 5, of which waited for: 14 -> 2; matrix products, arithmetic and copies ran while one was open for 3% -> 0% of each run, Pallas kernels for 0% -> 9%
where the time goes in v1:
time: 83.1 us; the launch traced here: 82.8 us
  waiting for transfers between devices  44.2 us (53%)
  between operations  14.8 us (18%)
  Pallas kernels  11.6 us (14%)
  starting transfers between devices  8.05 us (10%)
  local copies, waits for them, and re-layouts  3.78 us (5%)
    all_gather x1, waiting for transfers between devices, local(): everyone = lax.all_gather(ends, 'theta')  39.5 us
    ppermute x3, starting transfers between devices, swap(): return lax.ppermute(block, axis, [(i, i ^ bit) for i in range(size)])  5.62 us
    ppermute x1, waiting for transfers between devices, swap_across(): return lax.ppermute(block, axis, route)  4.65 us
    unnamed x12, local copies, waits for them, and re-layouts  3.67 us
    pallas_call x1, Pallas kernels, sides_terms(): pl.pallas_call(sides_kernel, name='sides_terms', out_shape=jax.ShapeDtype...  3.24 us
    pallas_call x1, Pallas kernels, inner_terms(): pl.pallas_call(inner_kernel, name='inner_terms', out_shape=jax.ShapeDtype...  3.17 us
    pallas_call x1, Pallas kernels, planes_terms(): pl.pallas_call(planes_kernel, name='planes_terms', out_shape=(jax.ShapeDt...  2.72 us
    ppermute x1, starting transfers between devices, swap_across(): return lax.ppermute(block, axis, route)  2.39 us
  transfers between devices with their start and end apart: 5, of which 2 were waited for; matrix products, arithmetic and copies ran while one was open for 0% of the time, Pallas kernels for 9%

profile of v1, /device:TPU:0, one launch (start us, length us, event | category | flops | bytes accessed | tf_op | source)
XLA Modules:
  0.0 82.8 jit_solution(4899953206075585957)
XLA Ops:
  7.2 0.0 all-gather.3.cloned.1.call-start
  7.2 0.0 copy-start
  7.2 1.1 %copy-done = f32[3,16,8,512]{3,2,1,0:T(8,128)S(1)} copy-done((f32[3,16,8,512]{3,2,1,0:T(8,128)S(1)}, f32[3,16,8,512]{3,2,1,0:T(8,128)}, u32[]{:S(2)}) %copy-start) | copy-done | bytes 786456
  8.4 0.1 pack_planes.1
  8.5 3.0 %collective-permute-start = (f32[3,12,8,512]{3,2,1,0:T(8,128)S(1)}, f32[3,12,8,512]{3,2,1,0:T(8,128)S(1)}, u32[]{:S(2)}, u32[]{:S(2)}) collective-permute-start(f32[3,12,8,512]{3,2,1,0:T(8,128)S(1)} %pack_planes.1), channel_id=1, source_target_pairs={{0,1},{1,0},{2,3},{3,2},{4,5},{5,4},{6,7},{7,6},{8,9},{9,8},{10,11... | collective-permute-start | bytes 1769480 | tf_op jit(solution)/shard_map/ppermute | solution.py:35
  11.5 1.0 %pack_sides.1 = (f32[3,10,8,512]{3,2,1,0:T(8,128)}, f32[3,10,8,512]{3,2,1,0:T(8,128)}, f32[3,4,8,128]{3,2,1,0:T(8,128)S(1)}) custom-call(s32[1]{0:T(128)} %bitcast.me_ref, f32[3,16,8,512]{3,2,1,0:T(8,128)S(1)} %copy-done.1), custom_call_target="tpu_custom_call" | custom-call | tf_op jit(solution)/shard_map/pack_sides/pallas_call | solution.py:118
  12.5 2.6 %collective-permute-start.3 = (f32[3,4,8,128]{3,2,1,0:T(8,128)S(1)}, f32[3,4,8,128]{3,2,1,0:T(8,128)S(1)}, u32[]{:S(2)}, u32[]{:S(2)}) collective-permute-start(f32[3,4,8,128]{3,2,1,0:T(8,128)S(1)} %get-tuple-element.9), channel_id=1, source_target_pairs={{0,16},{2,18},{4,20},{6,22},{8,24},{10,26},{12,28},{14,30},{16,0},... | collective-permute-start | bytes 147464 | tf_op jit(solution)/shard_map/ppermute | solution.py:35
  15.1 0.0 collective-permute-start.1
  15.1 2.4 %collective-permute-start.2 = (f32[3,10,8,512]{3,2,1,0:T(8,128)}, f32[3,10,8,512]{3,2,1,0:T(8,128)}, u32[]{:S(2)}, u32[]{:S(2)}) collective-permute-start(f32[3,10,8,512]{3,2,1,0:T(8,128)} %get-tuple-element.8), channel_id=1, source_target_pairs={{2,4},{4,2},{6,8},{8,6},{10,12},{12,10},{14,16},{16,14},{18,20},{2... | collective-permute-start | bytes 1474568 | tf_op jit(solution)/shard_map/ppermute | solution.py:43
  18.5 0.1 stack.2.power_ref
  18.6 3.2 %inner_terms.1.n_in_ref = f32[3,16,8,512]{3,2,1,0:T(8,128)} custom-call(f32[21]{0:T(128)S(1)} %copy-done.5, f32[3,16,8,512]{3,2,1,0:T(8,128)S(1)} %copy-done.1, f32[544,512]{1,0:T(8,128)S(1)} %bitcast.4), custom_call_target="tpu_custom_call" | custom-call | flops 603979776 | bytes 3145728 | tf_op jit(solution)/shard_map/inner_terms/pallas_call | solution.py:186
  21.8 0.0 collective-permute-done.3.mirror_ref
  21.8 0.0 collective-permute-done.1.core_ref
  21.8 4.7 %collective-permute-done.2.chip_ref = f32[3,10,8,512]{3,2,1,0:T(8,128)} collective-permute-done((f32[3,10,8,512]{3,2,1,0:T(8,128)}, f32[3,10,8,512]{3,2,1,0:T(8,128)}, u32[]{:S(2)}, u32[]{:S(2)}) %collective-permute-start.2) | collective-permute-done | bytes 491552 | tf_op jit(solution)/shard_map/ppermute | solution.py:43
  26.5 3.2 %sides_terms.1.n_in_ref = f32[3,16,8,512]{3,2,1,0:T(8,128)} custom-call(s32[1]{0:T(128)} %bitcast.me_ref, f32[21]{0:T(128)S(1)} %copy-done.5, f32[3,16,8,512]{3,2,1,0:T(8,128)S(1)} %copy-done.1, f32[544,512]{1,0:T(8,128)S(1)} %bitcast.5, f32[3,10,8,512]{3,2,1,0:T(8,128)} %collective-permute-done.1.core_ref, ...), custom_call_target="tpu_custom_call", output_to_operand_aliasing={{}: (7, {})} | custom-call | flops 50331648 | bytes 3145728 | tf_op jit(solution)/shard_map/sides_terms/pallas_call | solution.py:251
  29.7 0.0 collective-permute-done.y_ref
  29.7 2.7 %planes_terms.1 = (f32[3,16,8,512]{3,2,1,0:T(8,128)}, f32[2,3,8,512]{3,2,1,0:T(8,128)}) custom-call(f32[3,16,8,512]{3,2,1,0:T(8,128)S(1)} %copy-done.1, f32[3,12,8,512]{3,2,1,0:T(8,128)S(1)} %collective-permute-done.y_ref, f32[19,512]{1,0:T(8,128)S(1)} %stack.2.power_ref, f32[3,16,8,512]{3,2,1,0:T(8,128)} %sides_terms.1.n_in_ref), custom_call_target="tpu_custom_call", output_to_operand_aliasing={{0}: (3, {})} | custom-call | flops 3932160 | bytes 3145728 | tf_op jit(solution)/shard_map/planes_terms/pallas_call | solution.py:298
  32.4 0.0 all-gather.3.cloned.1.call-update
  32.4 0.0 copy-start.2
  32.5 1.1 %copy-done.2 = f32[3,16,8,512]{3,2,1,0:T(8,128)S(1)} copy-done((f32[3,16,8,512]{3,2,1,0:T(8,128)S(1)}, f32[3,16,8,512]{3,2,1,0:T(8,128)}, u32[]{:S(2)}) %copy-start.2) | copy-done | bytes 786456
  33.6 0.3 sweep.1.s_ref
  33.9 39.5 %all-gather.3.cloned.1.call-done = f32[32,3,8,512]{3,2,1,0:T(8,128)} async-done(((f32[2,3,8,512]{3,2,1,0:T(8,128)}), f32[32,3,8,512]{3,2,1,0:T(8,128)}) %all-gather.3.cloned.1.call-update) | async-done | bytes 1572880 | tf_op jit(solution)/shard_map/all_gather | solution.py:419
  73.4 1.4 %copy-done.4 = f32[32,3,8,512]{3,2,1,0:T(8,128)S(1)} copy-done((f32[32,3,8,512]{3,2,1,0:T(8,128)S(1)}, f32[32,3,8,512]{3,2,1,0:T(8,128)}, u32[]{:S(2)}) %copy-start.4) | copy-done | bytes 1572888
  74.8 1.1 %close.1 = f32[3,16,8,512]{3,2,1,0:T(8,128)} custom-call(s32[1]{0:T(128)} %bitcast.me_ref, f32[3,16,8,512]{3,2,1,0:T(8,128)S(1)} %sweep.1.s_ref, f32[19,512]{1,0:T(8,128)S(1)} %stack.2.power_ref, f32[16,2,3,8,512]{4,3,2,1,0:T(8,128)S(1)} %bitcast.6), custom_call_target="tpu_custom_call" | custom-call | tf_op jit(solution)/shard_map/close/pallas_call | solution.py:391
  (17 shorter events, 0.3 us)
Async XLA Ops:
  7.2 66.2 %all-gather.3.cloned.1.call-start = ((), (), s32[]{:S(2)}) async-start(), calls=%async_computation | async-start | bytes 1671168 | tf_op jit(solution)/shard_map/all_gather | solution.py:419
  7.2 1.1 %copy-start = (f32[3,16,8,512]{3,2,1,0:T(8,128)S(1)}, f32[3,16,8,512]{3,2,1,0:T(8,128)}, u32[]{:S(2)}) copy-start(f32[3,16,8,512]{3,2,1,0:T(8,128)} %v_ref.11) | copy-start | bytes 2359300
  8.3 3.1 %copy-start.1 = (f32[3,16,8,512]{3,2,1,0:T(8,128)S(1)}, f32[3,16,8,512]{3,2,1,0:T(8,128)}, u32[]{:S(2)}) copy-start(f32[3,16,8,512]{3,2,1,0:T(8,128)} %v_ref.11) | copy-start | bytes 2359300
  8.3 10.3 %copy-start.3 = (f32[512,544]{0,1:T(8,128)S(1)}, f32[512,544]{0,1:T(8,128)}, u32[]{:S(2)}) copy-start(f32[512,544]{0,1:T(8,128)} %param.5) | copy-start | bytes 3342340
  8.3 10.3 %copy-start.5 = (f32[21]{0:T(128)S(1)}, f32[21]{0:T(128)}, u32[]{:S(2)}) copy-start(f32[21]{0:T(128)} %stencil_ref.3) | copy-start | bytes 256
  8.5 21.2 %collective-permute-start = (f32[3,12,8,512]{3,2,1,0:T(8,128)S(1)}, f32[3,12,8,512]{3,2,1,0:T(8,128)S(1)}, u32[]{:S(2)}, u32[]{:S(2)}) collective-permute-start(f32[3,12,8,512]{3,2,1,0:T(8,128)S(1)} %pack_planes.1), channel_id=1, source_target_pairs={{0,1},{1,0},{2,3},{3,2},{4,5},{5,4},{6,7},{7,6},{8,9},{9,8},{10,11... | collective-permute-start | bytes 1769480 | tf_op jit(solution)/shard_map/ppermute | solution.py:35
  12.5 9.3 %collective-permute-start.3 = (f32[3,4,8,128]{3,2,1,0:T(8,128)S(1)}, f32[3,4,8,128]{3,2,1,0:T(8,128)S(1)}, u32[]{:S(2)}, u32[]{:S(2)}) collective-permute-start(f32[3,4,8,128]{3,2,1,0:T(8,128)S(1)} %get-tuple-element.9), channel_id=1, source_target_pairs={{0,16},{2,18},{4,20},{6,22},{8,24},{10,26},{12,28},{14,30},{16,0},... | collective-permute-start | bytes 147464 | tf_op jit(solution)/shard_map/ppermute | solution.py:35
  15.1 6.7 %collective-permute-start.1 = (f32[3,10,8,512]{3,2,1,0:T(8,128)}, f32[3,10,8,512]{3,2,1,0:T(8,128)}, u32[]{:S(2)}, u32[]{:S(2)}) collective-permute-start(f32[3,10,8,512]{3,2,1,0:T(8,128)} %get-tuple-element.7), channel_id=1, source_target_pairs={{0,2},{2,0},{4,6},{6,4},{8,10},{10,8},{12,14},{14,12},{16,18},{18,... | collective-permute-start | bytes 1474568 | tf_op jit(solution)/shard_map/ppermute | solution.py:35
  15.1 11.4 %collective-permute-start.2 = (f32[3,10,8,512]{3,2,1,0:T(8,128)}, f32[3,10,8,512]{3,2,1,0:T(8,128)}, u32[]{:S(2)}, u32[]{:S(2)}) collective-permute-start(f32[3,10,8,512]{3,2,1,0:T(8,128)} %get-tuple-element.8), channel_id=1, source_target_pairs={{2,4},{4,2},{6,8},{8,6},{10,12},{12,10},{14,16},{16,14},{18,20},{2... | collective-permute-start | bytes 1474568 | tf_op jit(solution)/shard_map/ppermute | solution.py:43
  32.4 1.1 %copy-start.2 = (f32[3,16,8,512]{3,2,1,0:T(8,128)S(1)}, f32[3,16,8,512]{3,2,1,0:T(8,128)}, u32[]{:S(2)}) copy-start(f32[3,16,8,512]{3,2,1,0:T(8,128)} %get-tuple-element.6.n_ref) | copy-start | bytes 2359300
  73.4 1.4 %copy-start.4 = (f32[32,3,8,512]{3,2,1,0:T(8,128)S(1)}, f32[32,3,8,512]{3,2,1,0:T(8,128)}, u32[]{:S(2)}) copy-start(f32[32,3,8,512]{3,2,1,0:T(8,128)} %all-gather.3.cloned.1.call-done) | copy-start | bytes 4718596
Sparse Core Ops, SparseCore 0:
  32.6 40.7 all-gather.2

commit v2 on v1

--- a/solution.py
+++ b/solution.py
@@ -261,7 +261,21 @@
     )(me, stencil, v, op, core, chip, mirror, n)
 
 
-def planes_kernel(v_ref, y_ref, power_ref, n_in_ref, n_ref, ends_ref, tile_ref):
+def share(sectors, shape):
+    comps, _, planes, radial = shape
+    return -(-comps * planes * (radial // LANES) // sectors)
+
+
+def dealt(sectors, shape):
+    comps, _, planes, radial = shape
+    per = share(sectors, shape)
+    for q in range(comps * planes * (radial // LANES)):
+        tile, c = divmod(q, comps)
+        z, k = divmod(tile, radial // LANES)
+        yield q // per, q % per, (c, slice(z, z + 1), slice(k * LANES, (k + 1) * LANES))
+
+
+def planes_kernel(v_ref, y_ref, power_ref, n_in_ref, n_ref, out_ref, tile_ref, ends_ref):
     comps, points, planes, radial = v_ref.shape
     carriers = y_ref.shape[1]
     lo, hi = AXIAL_REACH, planes - AXIAL_REACH
@@ -291,20 +305,26 @@
 
     each(carriers, carried)
     each(points - carriers, ridden)
-
-
-def planes_terms(v, y, power, n):
+    for j, row, index in dealt(out_ref.shape[0], v_ref.shape):
+        for side in range(2):
+            out_ref[j, side, row : row + 1] = ends_ref[(side,) + index]
+
+
+def planes_terms(v, y, power, n, sectors):
     comps, points, planes, radial = v.shape
     return pl.pallas_call(
         planes_kernel,
         name="planes_terms",
         out_shape=(
             jax.ShapeDtypeStruct(v.shape, v.dtype),
-            jax.ShapeDtypeStruct((2, comps, planes, radial), v.dtype),
+            jax.ShapeDtypeStruct((sectors, 2, share(sectors, v.shape), LANES), v.dtype),
         ),
         in_specs=[VMEM] * 4,
         out_specs=(VMEM, VMEM),
-        scratch_shapes=[pltpu.VMEM((comps, planes, radial), jnp.float32)],
+        scratch_shapes=[
+            pltpu.VMEM((comps, planes, radial), jnp.float32),
+            pltpu.VMEM((2, comps, planes, radial), jnp.float32),
+        ],
         input_output_aliases={3: 0},
         compiler_params=params(v.size * 4, 6),
         cost_estimate=pl.CostEstimate(flops=20 * v.size, bytes_accessed=16 * v.size, transcendentals=0),
@@ -366,20 +386,50 @@
     )(v, n, power)
 
 
-def close_kernel(me_ref, s_ref, power_ref, ends_ref, x_ref):
+def link_kernel(me_ref, power_ref, ends_ref, out_ref, hop_ref, height_ref, wrap_ref, *, points, comps):
+    sectors, _, per, _ = ends_ref.shape
+    tiles = power_ref.shape[1] // LANES
+    for row in range(per):
+        tile = lax.rem(lax.div(me_ref[0] * per + row, comps), tiles)
+        lanes = pl.ds(pl.multiple_of(tile * LANES, LANES), LANES)
+        for k, ref in enumerate((hop_ref, height_ref, wrap_ref)):
+            ref[row : row + 1] = power_ref[points + k : points + k + 1, lanes]
+    hop, height = hop_ref[...], height_ref[...]
+    scale = height * wrap_ref[...]
+    before = jnp.zeros((per, LANES), jnp.float32)
+    after = before
+    for j in range(sectors):
+        before = hop * before + ends_ref[j, 0]
+        after = hop * after + ends_ref[sectors - 1 - j, 1]
+    before = scale * before
+    after = scale * after
+    for j in range(sectors):
+        out_ref[j, 0] = before
+        out_ref[sectors - 1 - j, 1] = after
+        before = hop * before + height * ends_ref[j, 0]
+        after = hop * after + height * ends_ref[sectors - 1 - j, 1]
+
+
+def link(me, power, ends, points, comps):
+    row = pltpu.VMEM(ends.shape[2:], jnp.float32)
+    return pl.pallas_call(
+        functools.partial(link_kernel, points=points, comps=comps),
+        name="link",
+        out_shape=jax.ShapeDtypeStruct(ends.shape, ends.dtype),
+        in_specs=[SMEM, VMEM, VMEM],
+        out_specs=VMEM,
+        scratch_shapes=[row, row, row],
+        compiler_params=params(ends.size * 4, 8),
+    )(me, power, ends)
+
+
+def close_kernel(s_ref, power_ref, entries_ref, x_ref, both_ref):
     comps, points, planes, radial = s_ref.shape
-    sectors = ends_ref.shape[0]
-    me = me_ref[0]
-    hop = power_ref[points : points + 1]
-    scale = power_ref[points + 1 : points + 2] * power_ref[points + 2 : points + 3]
+    for j, row, index in dealt(entries_ref.shape[0], s_ref.shape):
+        for side in range(2):
+            both_ref[(side,) + index] = entries_ref[j, side, row : row + 1]
     for c in range(comps):
-        before = jnp.zeros((planes, radial), jnp.float32)
-        after = before
-        for j in range(sectors, 0, -1):
-            before = hop * before + ends_ref[lax.rem(me + sectors - j, sectors), 0, c]
-            after = hop * after + ends_ref[lax.rem(me + j, sectors), 1, c]
-        before = scale * before
-        after = scale * after
+        before, after = both_ref[0, c], both_ref[1, c]
 
         def point(t):
             x_ref[c, t] = s_ref[c, t] + power_ref[pl.ds(t + 1, 1)] * before + power_ref[pl.ds(points - t, 1)] * after
@@ -387,15 +437,16 @@
         each(points, point)
 
 
-def close(me, s, power, ends):
+def close(s, power, entries):
     return pl.pallas_call(
         close_kernel,
         name="close",
         out_shape=jax.ShapeDtypeStruct(s.shape, s.dtype),
-        in_specs=[SMEM, VMEM, VMEM, VMEM],
-        out_specs=VMEM,
+        in_specs=[VMEM, VMEM, VMEM],
+        out_specs=VMEM,
+        scratch_shapes=[pltpu.VMEM((2,) + s.shape[:1] + s.shape[2:], jnp.float32)],
         compiler_params=params(s.size * 4, 5),
-    )(me, s, power, ends)
+    )(s, power, entries)
 
 
 def local(velocity, radial_op, azimuth_stencil, viscous_factor):
@@ -415,10 +466,11 @@
     power = powers(viscous_factor, points, sectors, radial)
     n = inner_terms(azimuth_stencil, velocity, op)
     n = sides_terms(me, azimuth_stencil, velocity, op, core_in, chip_in, mirror_in, n)
-    nonlinear, ends = planes_terms(velocity, planes_in, power, n)
-    everyone = lax.all_gather(ends, "theta")
+    nonlinear, ends = planes_terms(velocity, planes_in, power, n, sectors)
+    lines = lax.all_to_all(ends, "theta", 0, 0)
     s = sweep(velocity, nonlinear, power)
-    new_velocity = close(me, s, power, everyone)
+    entries = lax.all_to_all(link(me, power, lines, points, comps), "theta", 0, 0)
+    new_velocity = close(s, power, entries)
     return (new_velocity, nonlinear)
 
 

time: 83.1 us -> 51.5 us (0.62)
  waiting for transfers between devices: 44.2 us -> 12.9 us
  between operations: 14.8 us -> 1.46 us
  blocking collectives: 0 us -> 11.1 us
  starting transfers between devices: 8.05 us -> 11.1 us
  local copies, waits for them, and re-layouts: 3.78 us -> 2.03 us
    all_gather x1 -> x0, waiting for transfers between devices: 39.5 us -> none  [local(): everyone = lax.all_gather(ends, 'theta')]
    all_to_all x0 -> x1, blocking collectives: none -> 11.1 us  [local(): lines = lax.all_to_all(ends, 'theta', 0, 0)]
    all_to_all x0 -> x1, waiting for transfers between devices: none -> 7.09 us  [local(): lax.all_to_all(link(me, power, lines, points, comps), 'theta', 0, 0)]
    ppermute x3, waiting for transfers between devices: 0.01 us -> 5.77 us  [swap(): return lax.ppermute(block, axis, [(i, i ^ bit) for i in range(size)])]
    ppermute x1, waiting for transfers between devices: 4.65 us -> 0.01 us  [swap_across(): return lax.ppermute(block, axis, route)]
    ppermute x3, starting transfers between devices: 5.62 us -> 1.97 us  [swap(): return lax.ppermute(block, axis, [(i, i ^ bit) for i in range(size)])]
    all_to_all x0 -> x1, starting transfers between devices: none -> 3.51 us  [local(): lax.all_to_all(link(me, power, lines, points, comps), 'theta', 0, 0)]
    ppermute x1, starting transfers between devices: 2.39 us -> 5.64 us  [swap_across(): return lax.ppermute(block, axis, route)]
  transfers between devices with their start and end apart: 5 -> 5, of which waited for: 2 -> 3; matrix products, arithmetic and copies ran while one was open for 0% -> 1% of each run, Pallas kernels for 9% -> 15%
where the time goes in v2:
time: 51.5 us; the launch traced here: 51.2 us
  waiting for transfers between devices  12.9 us (25%)
  Pallas kernels  12.4 us (24%)
  starting transfers between devices  11.1 us (22%)
  blocking collectives  11.1 us (22%)
  local copies, waits for them, and re-layouts  2.03 us (4%)
  between operations  1.46 us (3%)
    all_to_all x1, blocking collectives, local(): lines = lax.all_to_all(ends, 'theta', 0, 0)  11.1 us
    all_to_all x1, waiting for transfers between devices, local(): lax.all_to_all(link(me, power, lines, points, comps), 'theta', 0, 0)  7.09 us
    ppermute x3, waiting for transfers between devices, swap(): return lax.ppermute(block, axis, [(i, i ^ bit) for i in range(size)])  5.77 us
    ppermute x1, starting transfers between devices, swap_across(): return lax.ppermute(block, axis, route)  5.64 us
    all_to_all x1, starting transfers between devices, local(): lax.all_to_all(link(me, power, lines, points, comps), 'theta', 0, 0)  3.51 us
    pallas_call x1, Pallas kernels, inner_terms(): pl.pallas_call(inner_kernel, name='inner_terms', out_shape=jax.ShapeDtype...  3.17 us
    pallas_call x1, Pallas kernels, sides_terms(): pl.pallas_call(sides_kernel, name='sides_terms', out_shape=jax.ShapeDtype...  3.1 us
    pallas_call x1, Pallas kernels, planes_terms(): pl.pallas_call(planes_kernel, name='planes_terms', out_shape=(jax.ShapeDt...  2.73 us
  transfers between devices with their start and end apart: 5, of which 3 were waited for; matrix products, arithmetic and copies ran while one was open for 1% of the time, Pallas kernels for 15%

profile of v2, /device:TPU:0, one launch (start us, length us, event | category | flops | bytes accessed | tf_op | source)
XLA Modules:
  0.0 51.2 jit_solution(12323511040772262049)
XLA Ops:
  0.6 1.1 %copy-done = f32[3,16,8,512]{3,2,1,0:T(8,128)S(1)} copy-done((f32[3,16,8,512]{3,2,1,0:T(8,128)S(1)}, f32[3,16,8,512]{3,2,1,0:T(8,128)}, u32[]{:S(2)}) %copy-start) | copy-done | bytes 786456
  1.8 1.0 %pack_sides.1 = (f32[3,10,8,512]{3,2,1,0:T(8,128)}, f32[3,10,8,512]{3,2,1,0:T(8,128)}, f32[3,4,8,128]{3,2,1,0:T(8,128)S(1)}) custom-call(s32[1]{0:T(128)} %bitcast.1.me_ref, f32[3,16,8,512]{3,2,1,0:T(8,128)S(1)} %copy-done), custom_call_target="tpu_custom_call" | custom-call | tf_op jit(solution)/shard_map/pack_sides/pallas_call | solution.py:118
  2.8 0.5 collective-permute-start.1
  3.2 5.6 %collective-permute-start.2 = (f32[3,10,8,512]{3,2,1,0:T(8,128)}, f32[3,10,8,512]{3,2,1,0:T(8,128)}, u32[]{:S(2)}, u32[]{:S(2)}) collective-permute-start(f32[3,10,8,512]{3,2,1,0:T(8,128)} %get-tuple-element.8), channel_id=1, source_target_pairs={{2,4},{4,2},{6,8},{8,6},{10,12},{12,10},{14,16},{16,14},{18,20},{2... | collective-permute-start | bytes 1474568 | tf_op jit(solution)/shard_map/ppermute | solution.py:43
  8.9 0.0 collective-permute-start.3
  8.9 0.0 copy-done.1
  8.9 0.9 %pack_planes.1 = f32[3,12,8,512]{3,2,1,0:T(8,128)} custom-call(f32[3,16,8,512]{3,2,1,0:T(8,128)S(1)} %copy-done.1), custom_call_target="tpu_custom_call" | custom-call | tf_op jit(solution)/shard_map/pack_planes/pallas_call | solution.py:79
  9.8 1.5 %collective-permute-start = (f32[3,12,8,512]{3,2,1,0:T(8,128)}, f32[3,12,8,512]{3,2,1,0:T(8,128)S(1)}, u32[]{:S(2)}, u32[]{:S(2)}) collective-permute-start(f32[3,12,8,512]{3,2,1,0:T(8,128)} %pack_planes.1), channel_id=1, source_target_pairs={{0,1},{1,0},{2,3},{3,2},{4,5},{5,4},{6,7},{7,6},{8,9},{9,8},{10,11... | collective-permute-start | bytes 1769480 | tf_op jit(solution)/shard_map/ppermute | solution.py:35
  12.4 0.1 stack.2.power_ref
  12.5 3.2 %inner_terms.1.n_in_ref = f32[3,16,8,512]{3,2,1,0:T(8,128)} custom-call(f32[21]{0:T(128)S(1)} %copy-done.4, f32[3,16,8,512]{3,2,1,0:T(8,128)S(1)} %copy-done.1, f32[544,512]{1,0:T(8,128)S(1)} %bitcast.3), custom_call_target="tpu_custom_call" | custom-call | flops 603979776 | bytes 3145728 | tf_op jit(solution)/shard_map/inner_terms/pallas_call | solution.py:186
  15.7 0.7 %collective-permute-done.3.mirror_ref = f32[3,4,8,128]{3,2,1,0:T(8,128)S(1)} collective-permute-done((f32[3,4,8,128]{3,2,1,0:T(8,128)S(1)}, f32[3,4,8,128]{3,2,1,0:T(8,128)S(1)}, u32[]{:S(2)}, u32[]{:S(2)}) %collective-permute-start.3) | collective-permute-done | bytes 49184 | tf_op jit(solution)/shard_map/ppermute | solution.py:35
  16.4 0.0 collective-permute-done.1.core_ref
  16.4 0.0 collective-permute-done.2.chip_ref
  16.4 3.1 %sides_terms.1.n_in_ref = f32[3,16,8,512]{3,2,1,0:T(8,128)} custom-call(s32[1]{0:T(128)} %bitcast.1.me_ref, f32[21]{0:T(128)S(1)} %copy-done.4, f32[3,16,8,512]{3,2,1,0:T(8,128)S(1)} %copy-done.1, f32[544,512]{1,0:T(8,128)S(1)} %bitcast.4, f32[3,10,8,512]{3,2,1,0:T(8,128)S(1)} %collective-permute-done.1.core_ref, ...), custom_call_target="tpu_custom_call", output_to_operand_aliasing={{}: (7, {})} | custom-call | flops 50331648 | bytes 3145728 | tf_op jit(solution)/shard_map/sides_terms/pallas_call | solution.py:251
  19.5 5.0 %collective-permute-done.y_ref = f32[3,12,8,512]{3,2,1,0:T(8,128)S(1)} collective-permute-done((f32[3,12,8,512]{3,2,1,0:T(8,128)}, f32[3,12,8,512]{3,2,1,0:T(8,128)S(1)}, u32[]{:S(2)}, u32[]{:S(2)}) %collective-permute-start) | collective-permute-done | bytes 589856 | tf_op jit(solution)/shard_map/ppermute | solution.py:35
  24.5 2.7 %planes_terms.1 = (f32[3,16,8,512]{3,2,1,0:T(8,128)}, f32[16,2,6,128]{3,2,1,0:T(8,128)S(1)}) custom-call(f32[3,16,8,512]{3,2,1,0:T(8,128)S(1)} %copy-done.1, f32[3,12,8,512]{3,2,1,0:T(8,128)S(1)} %collective-permute-done.y_ref, f32[19,512]{1,0:T(8,128)S(1)} %stack.2.power_ref, f32[3,16,8,512]{3,2,1,0:T(8,128)} %sides_terms.1.n_in_ref), custom_call_target="tpu_custom_call", output_to_operand_aliasing={{0}: (3, {})} | custom-call | flops 3932160 | bytes 3145728 | tf_op jit(solution)/shard_map/planes_terms/pallas_call | solution.py:315
  27.3 0.1 copy.8
  27.3 11.1 %all_to_all.10 = f32[16,2,6,128]{3,1,2,0:T(2,128)S(1)} all-to-all(f32[16,2,6,128]{3,1,2,0:T(2,128)S(1)} %copy.8), channel_id=1, replica_groups=mesh['theta'=16,'gz'=2] {'theta'}, dimensions={0} | all-to-all | bytes 196608 | tf_op jit(solution)/shard_map/all_to_all | solution.py:470
  38.4 0.1 link.1
  38.5 0.7 %copy.10 = f32[16,2,6,128]{3,1,2,0:T(2,128)} copy(f32[16,2,6,128]{3,2,1,0:T(8,128)S(1)} %link.1) | data formatting | bytes 196608 | tf_op jit(solution)/shard_map/link/pallas_call | solution.py:415
  39.2 3.5 %all-to-all-start.1 = ((f32[16,2,6,128]{3,1,2,0:T(2,128)}), f32[16,2,6,128]{3,1,2,0:T(2,128)S(1)}, u32[]{:S(2)}, u32[]{:S(2)}) async-start(f32[16,2,6,128]{3,1,2,0:T(2,128)} %copy.10), calls=%async_computation.1 | async-start | bytes 196608 | tf_op jit(solution)/shard_map/all_to_all | solution.py:472
  42.7 0.3 sweep.1.s_ref
  43.0 7.1 %all-to-all-done.1 = f32[16,2,6,128]{3,1,2,0:T(2,128)S(1)} async-done(((f32[16,2,6,128]{3,1,2,0:T(2,128)}), f32[16,2,6,128]{3,1,2,0:T(2,128)S(1)}, u32[]{:S(2)}, u32[]{:S(2)}) %all-to-all-start.1) | async-done | bytes 98336 | tf_op jit(solution)/shard_map/all_to_all | solution.py:472
  50.1 1.1 %close.1 = f32[3,16,8,512]{3,2,1,0:T(8,128)} custom-call(f32[3,16,8,512]{3,2,1,0:T(8,128)S(1)} %sweep.1.s_ref, f32[19,512]{1,0:T(8,128)S(1)} %stack.2.power_ref, f32[16,2,6,128]{3,2,1,0:T(8,128)S(1)} %copy.11.entries_ref), custom_call_target="tpu_custom_call" | custom-call | tf_op jit(solution)/shard_map/close/pallas_call | solution.py:441
  (20 shorter events, 0.3 us)
Async XLA Ops:
  0.6 1.1 %copy-start = (f32[3,16,8,512]{3,2,1,0:T(8,128)S(1)}, f32[3,16,8,512]{3,2,1,0:T(8,128)}, u32[]{:S(2)}) copy-start(f32[3,16,8,512]{3,2,1,0:T(8,128)} %v_ref.11) | copy-start | bytes 2359300
  1.8 7.1 %copy-start.1 = (f32[3,16,8,512]{3,2,1,0:T(8,128)S(1)}, f32[3,16,8,512]{3,2,1,0:T(8,128)}, u32[]{:S(2)}) copy-start(f32[3,16,8,512]{3,2,1,0:T(8,128)} %v_ref.11) | copy-start | bytes 2359300
  1.8 10.7 %copy-start.3 = (f32[512,544]{0,1:T(8,128)S(1)}, f32[512,544]{0,1:T(8,128)}, u32[]{:S(2)}) copy-start(f32[512,544]{0,1:T(8,128)} %param.5) | copy-start | bytes 3342340
  1.8 10.7 %copy-start.4 = (f32[21]{0:T(128)S(1)}, f32[21]{0:T(128)}, u32[]{:S(2)}) copy-start(f32[21]{0:T(128)} %stencil_ref.3) | copy-start | bytes 256
  2.8 13.6 %collective-permute-start.1 = (f32[3,10,8,512]{3,2,1,0:T(8,128)}, f32[3,10,8,512]{3,2,1,0:T(8,128)S(1)}, u32[]{:S(2)}, u32[]{:S(2)}) collective-permute-start(f32[3,10,8,512]{3,2,1,0:T(8,128)} %get-tuple-element.7), channel_id=1, source_target_pairs={{0,2},{2,0},{4,6},{6,4},{8,10},{10,8},{12,14},{14,12},{16,18},{18,... | collective-permute-start | bytes 1474568 | tf_op jit(solution)/shard_map/ppermute | solution.py:35
  3.2 13.1 %collective-permute-start.2 = (f32[3,10,8,512]{3,2,1,0:T(8,128)}, f32[3,10,8,512]{3,2,1,0:T(8,128)}, u32[]{:S(2)}, u32[]{:S(2)}) collective-permute-start(f32[3,10,8,512]{3,2,1,0:T(8,128)} %get-tuple-element.8), channel_id=1, source_target_pairs={{2,4},{4,2},{6,8},{8,6},{10,12},{12,10},{14,16},{16,14},{18,20},{2... | collective-permute-start | bytes 1474568 | tf_op jit(solution)/shard_map/ppermute | solution.py:43
  8.9 7.5 %collective-permute-start.3 = (f32[3,4,8,128]{3,2,1,0:T(8,128)S(1)}, f32[3,4,8,128]{3,2,1,0:T(8,128)S(1)}, u32[]{:S(2)}, u32[]{:S(2)}) collective-permute-start(f32[3,4,8,128]{3,2,1,0:T(8,128)S(1)} %get-tuple-element.9), channel_id=1, source_target_pairs={{0,16},{2,18},{4,20},{6,22},{8,24},{10,26},{12,28},{14,30},{16,0},... | collective-permute-start | bytes 147464 | tf_op jit(solution)/shard_map/ppermute | solution.py:35
  9.8 14.7 %collective-permute-start = (f32[3,12,8,512]{3,2,1,0:T(8,128)}, f32[3,12,8,512]{3,2,1,0:T(8,128)S(1)}, u32[]{:S(2)}, u32[]{:S(2)}) collective-permute-start(f32[3,12,8,512]{3,2,1,0:T(8,128)} %pack_planes.1), channel_id=1, source_target_pairs={{0,1},{1,0},{2,3},{3,2},{4,5},{5,4},{6,7},{7,6},{8,9},{9,8},{10,11... | collective-permute-start | bytes 1769480 | tf_op jit(solution)/shard_map/ppermute | solution.py:35
  27.2 15.5 %copy-start.2 = (f32[3,16,8,512]{3,2,1,0:T(8,128)S(1)}, f32[3,16,8,512]{3,2,1,0:T(8,128)}, u32[]{:S(2)}) copy-start(f32[3,16,8,512]{3,2,1,0:T(8,128)} %get-tuple-element.6.n_ref) | copy-start | bytes 2359300
  39.2 10.9 %all-to-all-start.1 = ((f32[16,2,6,128]{3,1,2,0:T(2,128)}), f32[16,2,6,128]{3,1,2,0:T(2,128)S(1)}, u32[]{:S(2)}, u32[]{:S(2)}) async-start(f32[16,2,6,128]{3,1,2,0:T(2,128)} %copy.10), calls=%async_computation.1 | async-start | bytes 196608 | tf_op jit(solution)/shard_map/all_to_all | solution.py:472

commit v3 on v1

--- a/solution.py
+++ b/solution.py
@@ -16,10 +16,15 @@
 
 VMEM = pl.BlockSpec(memory_space=pltpu.VMEM)
 SMEM = pl.BlockSpec(memory_space=pltpu.SMEM)
+ANY = pl.BlockSpec(memory_space=pl.ANY)
 
 
 def params(block_bytes, blocks):
     return pltpu.CompilerParams(vmem_limit_bytes=(6 << 20) + blocks * block_bytes)
+
+
+def held(*shape):
+    return pltpu.VMEM(shape, jnp.float32)
 
 
 def each(count, body):
@@ -79,14 +84,14 @@
     return pl.pallas_call(
         pack_planes_kernel,
         name="pack_planes",
-        out_shape=jax.ShapeDtypeStruct((comps, points - points // 4, planes, radial), v.dtype),
+        out_shape=held(comps, points - points // 4, planes, radial),
         in_specs=[VMEM],
         out_specs=VMEM,
         compiler_params=params(v.size * 4, 2),
     )(v)
 
 
-def pack_sides_kernel(me_ref, v_ref, core_ref, chip_ref, mirror_ref):
+def pack_sides_kernel(me_ref, v_ref, first_ref, core_ref, chip_ref, mirror_ref):
     points = v_ref.shape[1]
     reach = core_ref.shape[1]
     even = me_ref[0] % 2 == 0
@@ -111,18 +116,18 @@
     each(tiles, put)
 
 
-def pack_sides(me, v, reach, width):
+def pack_sides(me, v, first, reach, width):
     comps, points, planes, radial = v.shape
     tiles = points // (LANES // width)
-    side = jax.ShapeDtypeStruct((comps, reach, planes, radial), v.dtype)
+    side = held(comps, reach, planes, radial)
     return pl.pallas_call(
         pack_sides_kernel,
         name="pack_sides",
-        out_shape=(side, side, jax.ShapeDtypeStruct((comps, tiles, planes, LANES), v.dtype)),
-        in_specs=[SMEM, VMEM],
+        out_shape=(side, side, held(comps, tiles, planes, LANES)),
+        in_specs=[SMEM, VMEM, ANY],
         out_specs=(VMEM, VMEM, VMEM),
         compiler_params=params(v.size * 4, 3),
-    )(me, v)
+    )(me, v, first)
 
 
 def inverse_radius(radial):
@@ -186,7 +191,7 @@
     return pl.pallas_call(
         inner_kernel,
         name="inner_terms",
-        out_shape=jax.ShapeDtypeStruct(v.shape, v.dtype),
+        out_shape=held(*v.shape),
         in_specs=[SMEM, VMEM, VMEM],
         out_specs=VMEM,
         scratch_shapes=[pltpu.VMEM((v.size // v.shape[3], v.shape[3]), jnp.float32)],
@@ -195,9 +200,23 @@
     )(stencil, v, op)
 
 
-def sides_kernel(me_ref, stencil_ref, v_ref, op_ref, core_ref, chip_ref, mirror_ref, n_in_ref, n_ref, grad_ref):
+def add_side(stencil_ref, v_ref, side_ref, n_in_ref, n_ref, inv_r, before):
+    comps, points, _, _ = v_ref.shape
+    reach = side_ref.shape[1]
+    for u in range(reach):
+        t = u if before else points - reach + u
+        taps = [(h, h - u) for h in range(u, reach)] if before else [(h, 2 * reach + h - u) for h in range(u + 1)]
+        b_inv = v_ref[1, t] * inv_r
+        for c in range(comps):
+            around = None
+            for h, k in taps:
+                term = stencil_ref[k] * side_ref[c, h]
+                around = term if around is None else around + term
+            n_ref[c, t] = n_in_ref[c, t] + b_inv * around
+
+
+def early_kernel(me_ref, stencil_ref, v_ref, op_ref, core_ref, mirror_ref, n_in_ref, n_ref, grad_ref):
     comps, points, planes, radial = v_ref.shape
-    reach = core_ref.shape[1]
     tiles = mirror_ref.shape[1]
     count = points // tiles
     width = LANES // count
@@ -213,55 +232,56 @@
         ]
         left = [jnp.concatenate(x, axis=0) for x in parts]
         grad_ref[c * points * planes : (c + 1) * points * planes] = product(left, right)
-    inv_r = inverse_radius(radial)
-
-    def finish(t, taps):
-        a = v_ref[0, t]
-        b_inv = v_ref[1, t] * inv_r
+
+    def finish(t):
         for c in range(comps):
-            start = (c * points + t) * planes
-            n = n_in_ref[c, t] + a * grad_ref[pl.ds(pl.multiple_of(start, planes), planes)]
-            around = None
-            for ref, h, k in taps:
-                term = stencil_ref[k] * ref[c, h]
-                around = term if around is None else around + term
-            if around is not None:
-                n = n + b_inv * around
-            n_ref[c, t] = n
-
-    def all_points(before, after):
-        def taps(t):
-            found = [(before, h, h - t) for h in range(t, reach)]
-            found += [(after, h, points + h - t + reach) for h in range(min(reach, reach - points + t + 1))]
-            return found
-
-        for t in range(reach):
-            finish(t, taps(t))
-        if points > 2 * reach:
-            each(points - 2 * reach, lambda i: finish(i + reach, []))
-        for t in range(max(reach, points - reach), points):
-            finish(t, taps(t))
-
+            start = pl.multiple_of((c * points + t) * planes, planes)
+            n_ref[c, t] = n_in_ref[c, t] + v_ref[0, t] * grad_ref[pl.ds(start, planes)]
+
+    each(points, finish)
     even = me_ref[0] % 2 == 0
-    pl.when(even)(lambda: all_points(chip_ref, core_ref))
-    pl.when(jnp.logical_not(even))(lambda: all_points(core_ref, chip_ref))
-
-
-def sides_terms(me, stencil, v, op, core, chip, mirror, n):
-    return pl.pallas_call(
-        sides_kernel,
-        name="sides_terms",
-        out_shape=jax.ShapeDtypeStruct(v.shape, v.dtype),
-        in_specs=[SMEM, SMEM, VMEM, VMEM, VMEM, VMEM, VMEM, VMEM],
+    add = functools.partial(add_side, stencil_ref, v_ref, core_ref, n_ref, n_ref, inverse_radius(radial))
+    pl.when(even)(lambda: add(False))
+    pl.when(jnp.logical_not(even))(lambda: add(True))
+
+
+def early_terms(me, stencil, v, op, core, mirror, n):
+    return pl.pallas_call(
+        early_kernel,
+        name="early_terms",
+        out_shape=held(*v.shape),
+        in_specs=[SMEM, SMEM, VMEM, VMEM, VMEM, VMEM, VMEM],
         out_specs=VMEM,
         scratch_shapes=[pltpu.VMEM((v.size // v.shape[3], v.shape[3]), jnp.float32)],
-        input_output_aliases={7: 0},
+        input_output_aliases={6: 0},
         compiler_params=params(v.size * 4, 8),
         cost_estimate=pl.CostEstimate(flops=2 * v.size * LANES, bytes_accessed=16 * v.size, transcendentals=0),
-    )(me, stencil, v, op, core, chip, mirror, n)
-
-
-def planes_kernel(v_ref, y_ref, power_ref, n_in_ref, n_ref, ends_ref, tile_ref):
+    )(me, stencil, v, op, core, mirror, n)
+
+
+def late_kernel(me_ref, stencil_ref, v_ref, chip_ref, n_in_ref, n_ref):
+    even = me_ref[0] % 2 == 0
+    add = functools.partial(
+        add_side, stencil_ref, v_ref, chip_ref, n_in_ref, n_ref, inverse_radius(v_ref.shape[3])
+    )
+    pl.when(even)(lambda: add(True))
+    pl.when(jnp.logical_not(even))(lambda: add(False))
+
+
+def late_terms(me, stencil, v, chip, n):
+    return pl.pallas_call(
+        late_kernel,
+        name="late_terms",
+        out_shape=held(*v.shape),
+        in_specs=[SMEM, SMEM, VMEM, VMEM, VMEM],
+        out_specs=VMEM,
+        input_output_aliases={4: 0},
+        compiler_params=params(v.size * 4, 5),
+        cost_estimate=pl.CostEstimate(flops=20 * v.size, bytes_accessed=12 * v.size, transcendentals=0),
+    )(me, stencil, v, chip, n)
+
+
+def planes_kernel(me_ref, v_ref, y_ref, power_ref, n_in_ref, n_ref, keep_ref, send_ref, tile_ref, ends_ref):
     comps, points, planes, radial = v_ref.shape
     carriers = y_ref.shape[1]
     lo, hi = AXIAL_REACH, planes - AXIAL_REACH
@@ -291,27 +311,32 @@
 
     each(carriers, carried)
     each(points - carriers, ridden)
-
-
-def planes_terms(v, y, power, n):
+    half = radial // 2
+    core = me_ref[0] % 2
+    keep_ref[...] = ends_ref[:, :, :, pl.ds(pl.multiple_of(core * half, half), half)]
+    send_ref[...] = ends_ref[:, :, :, pl.ds(pl.multiple_of((1 - core) * half, half), half)]
+
+
+def planes_terms(me, v, y, power, n):
     comps, points, planes, radial = v.shape
+    part = held(2, comps, planes, radial // 2)
     return pl.pallas_call(
         planes_kernel,
         name="planes_terms",
-        out_shape=(
-            jax.ShapeDtypeStruct(v.shape, v.dtype),
-            jax.ShapeDtypeStruct((2, comps, planes, radial), v.dtype),
-        ),
-        in_specs=[VMEM] * 4,
-        out_specs=(VMEM, VMEM),
-        scratch_shapes=[pltpu.VMEM((comps, planes, radial), jnp.float32)],
-        input_output_aliases={3: 0},
+        out_shape=(held(*v.shape), part, part),
+        in_specs=[SMEM] + [VMEM] * 4,
+        out_specs=(VMEM, VMEM, VMEM),
+        scratch_shapes=[
+            pltpu.VMEM((comps, planes, radial), jnp.float32),
+            pltpu.VMEM((2, comps, planes, radial), jnp.float32),
+        ],
+        input_output_aliases={4: 0},
         compiler_params=params(v.size * 4, 6),
         cost_estimate=pl.CostEstimate(flops=20 * v.size, bytes_accessed=16 * v.size, transcendentals=0),
-    )(v, y, power, n)
-
-
-def powers(viscous_factor, points, sectors, radial):
+    )(me, v, y, power, n)
+
+
+def powers(me, viscous_factor, points, sectors, radial):
     radius = jnp.arange(radial).astype(jnp.float32) + 0.5
     half = 0.5 * radius * lax.rsqrt(viscous_factor[0])
     root = jnp.sqrt(1.0 + half * half)
@@ -319,17 +344,27 @@
     rows = [jnp.ones_like(loss)]
     for _ in range(points):
         rows.append(rows[-1] * (1.0 - loss))
-    total, have = loss, 1
+    total = loss
     left, result = points * sectors, None
     while left:
         if left & 1:
             result = total if result is None else result + total - result * total
         total = total * (2.0 - total)
         left >>= 1
-    return jnp.stack(rows + [half / root, 1.0 / result])
-
-
-def sweep_kernel(v_ref, n_ref, power_ref, s_ref):
+    across = rows[points] * rows[points]
+    rows += [half / root, 1.0 / result]
+    before = after = rows[0]
+    for bit in range(1, sectors.bit_length() - 1):
+        upper = (me >> bit) % 2 == 1
+        rows += [across, before, after]
+        before, after = jnp.where(upper, before * across, before), jnp.where(upper, after, after * across)
+        across = across * across
+    return jnp.stack(rows + [before, after])
+
+
+def sweep_kernel(v_ref, n_ref, power_ref, s_ref, nonlinear_ref, sem):
+    leave = pltpu.make_async_copy(n_ref, nonlinear_ref, sem)
+    leave.start()
     comps, points, planes, radial = v_ref.shape
     decay = power_ref[1:2]
     height = power_ref[points + 1 : points + 2]
@@ -352,50 +387,142 @@
 
     start = (jnp.zeros((planes, radial), jnp.float32),) * comps
     lax.fori_loop(0, points, backward, start, unroll=points <= UNROLL)
+    leave.wait()
 
 
 def sweep(v, n, power):
     return pl.pallas_call(
         sweep_kernel,
         name="sweep",
-        out_shape=jax.ShapeDtypeStruct(v.shape, v.dtype),
+        out_shape=(held(*v.shape), jax.ShapeDtypeStruct(v.shape, v.dtype)),
         in_specs=[VMEM] * 3,
-        out_specs=VMEM,
+        out_specs=(VMEM, ANY),
+        scratch_shapes=[pltpu.SemaphoreType.DMA],
         compiler_params=params(v.size * 4, 4),
         cost_estimate=pl.CostEstimate(flops=10 * v.size, bytes_accessed=12 * v.size, transcendentals=0),
     )(v, n, power)
 
 
-def close_kernel(me_ref, s_ref, power_ref, ends_ref, x_ref):
+def my_lanes(me_ref, radial, half):
+    core = me_ref[0] % 2
+    return pl.ds(pl.multiple_of(core * half, half), half)
+
+
+def pair_kernel(me_ref, power_ref, own_ref, other_ref, block_ref, *, points):
+    half = own_ref.shape[3]
+    hop = power_ref[points : points + 1, my_lanes(me_ref, power_ref.shape[1], half)]
+    odd = me_ref[0] % 2 == 1
+    for c in range(own_ref.shape[1]):
+        for side in range(2):
+            own, other = own_ref[side, c], other_ref[side, c]
+            far, near = (own, other) if side == 0 else (other, own)
+            block_ref[side, c] = jnp.where(odd, hop * near + far, hop * far + near)
+
+
+def pair(me, power, own, other, points):
+    return pl.pallas_call(
+        functools.partial(pair_kernel, points=points),
+        name="pair",
+        out_shape=held(*own.shape),
+        in_specs=[SMEM, VMEM, VMEM, VMEM],
+        out_specs=VMEM,
+        compiler_params=params(own.size * 4, 8),
+    )(me, power, own, other)
+
+
+def merge_kernel(me_ref, power_ref, block_ref, entry_ref, other_ref, block_out_ref, entry_out_ref, *, points, bit):
+    comps, half = block_ref.shape[1], block_ref.shape[3]
+    lanes = my_lanes(me_ref, power_ref.shape[1], half)
+    first = points + 3 * bit
+    across, before, after = [power_ref[first + k : first + k + 1, lanes] for k in range(3)]
+    upper = (me_ref[0] >> bit) % 2 == 1
+    before = jnp.where(upper, before, 0.0)
+    after = jnp.where(upper, 0.0, after)
+    for c in range(comps):
+        low, high = block_ref[0, c], block_ref[1, c]
+        other_low, other_high = other_ref[0, c], other_ref[1, c]
+        block_out_ref[0, c] = jnp.where(upper, across * other_low + low, across * low + other_low)
+        block_out_ref[1, c] = jnp.where(upper, other_high + across * high, high + across * other_high)
+        entry_out_ref[0, c] = entry_ref[0, c] + before * other_low
+        entry_out_ref[1, c] = entry_ref[1, c] + after * other_high
+
+
+def merge(me, power, block, entry, other, points, bit):
+    return pl.pallas_call(
+        functools.partial(merge_kernel, points=points, bit=bit),
+        name="merge",
+        out_shape=(held(*block.shape), held(*block.shape)),
+        in_specs=[SMEM, VMEM, VMEM, VMEM, VMEM],
+        out_specs=(VMEM, VMEM),
+        compiler_params=params(block.size * 4, 8),
+    )(me, power, block, entry, other)
+
+
+def enter_kernel(me_ref, power_ref, block_ref, entry_ref, own_ref, other_ref, mine_ref, send_ref, *, points):
+    comps, half = block_ref.shape[1], block_ref.shape[3]
+    lanes = my_lanes(me_ref, power_ref.shape[1], half)
+    row = lambda k: power_ref[k : k + 1, lanes]
+    hop, height, wrap = row(points), row(points + 1), row(points + 2)
+    last = power_ref.shape[0]
+    before, after = row(last - 2) * wrap, row(last - 1) * wrap
+    odd = me_ref[0] % 2 == 1
+    for c in range(comps):
+        low = height * (entry_ref[0, c] + before * block_ref[0, c])
+        high = height * (entry_ref[1, c] + after * block_ref[1, c])
+        even_low = height * jnp.where(odd, other_ref[0, c], own_ref[0, c])
+        odd_high = height * jnp.where(odd, own_ref[1, c], other_ref[1, c])
+        even_in = (low, odd_high + hop * high)
+        odd_in = (even_low + hop * low, high)
+        for side in range(2):
+            mine_ref[side, c] = jnp.where(odd, odd_in[side], even_in[side])
+            send_ref[side, c] = jnp.where(odd, even_in[side], odd_in[side])
+
+
+def enter(me, power, block, entry, own, other, points):
+    return pl.pallas_call(
+        functools.partial(enter_kernel, points=points),
+        name="enter",
+        out_shape=(held(*block.shape), held(*block.shape)),
+        in_specs=[SMEM] + [VMEM] * 5,
+        out_specs=(VMEM, VMEM),
+        compiler_params=params(block.size * 4, 12),
+    )(me, power, block, entry, own, other)
+
+
+def close_kernel(me_ref, s_ref, power_ref, mine_ref, got_ref, out_ref, x_ref, both_ref, sems):
     comps, points, planes, radial = s_ref.shape
-    sectors = ends_ref.shape[0]
-    me = me_ref[0]
-    hop = power_ref[points : points + 1]
-    scale = power_ref[points + 1 : points + 2] * power_ref[points + 2 : points + 3]
+    half = mine_ref.shape[3]
+    core = me_ref[0] % 2
+    both_ref[:, :, :, pl.ds(pl.multiple_of(core * half, half), half)] = mine_ref[...]
+    both_ref[:, :, :, pl.ds(pl.multiple_of((1 - core) * half, half), half)] = got_ref[...]
+    leaves = []
     for c in range(comps):
-        before = jnp.zeros((planes, radial), jnp.float32)
-        after = before
-        for j in range(sectors, 0, -1):
-            before = hop * before + ends_ref[lax.rem(me + sectors - j, sectors), 0, c]
-            after = hop * after + ends_ref[lax.rem(me + j, sectors), 1, c]
-        before = scale * before
-        after = scale * after
+        before, after = both_ref[0, c], both_ref[1, c]
 
         def point(t):
             x_ref[c, t] = s_ref[c, t] + power_ref[pl.ds(t + 1, 1)] * before + power_ref[pl.ds(points - t, 1)] * after
 
         each(points, point)
-
-
-def close(me, s, power, ends):
+        leaves.append(pltpu.make_async_copy(x_ref.at[c], out_ref.at[c], sems.at[c]))
+        leaves[c].start()
+    for leave in leaves:
+        leave.wait()
+
+
+def close(me, s, power, mine, got):
     return pl.pallas_call(
         close_kernel,
         name="close",
         out_shape=jax.ShapeDtypeStruct(s.shape, s.dtype),
-        in_specs=[SMEM, VMEM, VMEM, VMEM],
-        out_specs=VMEM,
+        in_specs=[SMEM] + [VMEM] * 4,
+        out_specs=ANY,
+        scratch_shapes=[
+            pltpu.VMEM(s.shape, jnp.float32),
+            pltpu.VMEM((2,) + s.shape[:1] + s.shape[2:], jnp.float32),
+            pltpu.SemaphoreType.DMA((s.shape[0],)),
+        ],
         compiler_params=params(s.size * 4, 5),
-    )(me, s, power, ends)
+    )(me, s, power, mine, got)
 
 
 def local(velocity, radial_op, azimuth_stencil, viscous_factor):
@@ -408,17 +535,23 @@
 
     planes_out = pack_planes(velocity)
     planes_in = swap(planes_out, "gz", 1)
-    core_out, chip_out, mirror_out = pack_sides(me, velocity, reach, width)
+    core_out, chip_out, mirror_out = pack_sides(me, velocity, planes_out, reach, width)
     chip_in = swap_across(chip_out, "theta")
     core_in = swap(core_out, "theta", 1)
     mirror_in = swap(mirror_out, "theta", sectors // 2)
-    power = powers(viscous_factor, points, sectors, radial)
+    power = powers(me, viscous_factor, points, sectors, radial)
     n = inner_terms(azimuth_stencil, velocity, op)
-    n = sides_terms(me, azimuth_stencil, velocity, op, core_in, chip_in, mirror_in, n)
-    nonlinear, ends = planes_terms(velocity, planes_in, power, n)
-    everyone = lax.all_gather(ends, "theta")
-    s = sweep(velocity, nonlinear, power)
-    new_velocity = close(me, s, power, everyone)
+    n = early_terms(me, azimuth_stencil, velocity, op, core_in, mirror_in, n)
+    n = late_terms(me, azimuth_stencil, velocity, chip_in, n)
+    n, own, send = planes_terms(me, velocity, planes_in, power, n)
+    other = swap(send, "theta", 1)
+    s, nonlinear = sweep(velocity, n, power)
+    block = pair(me, power, own, other, points)
+    entry = jnp.zeros_like(block)
+    for bit in range(1, sectors.bit_length() - 1):
+        block, entry = merge(me, power, block, entry, swap(block, "theta", 1 << bit), points, bit)
+    mine, send = enter(me, power, block, entry, own, other, points)
+    new_velocity = close(me, s, power, mine, swap(send, "theta", 1))
     return (new_velocity, nonlinear)
 
 

time: 83.1 us -> 39 us (0.47)
  waiting for transfers between devices: 44.2 us -> 12.1 us
  between operations: 14.8 us -> 1.59 us
  starting transfers between devices: 8.05 us -> 14 us
  local copies, waits for them, and re-layouts: 3.78 us -> 1.3 us
  Pallas kernels: 11.6 us -> 9.27 us
    all_gather x1 -> x0, waiting for transfers between devices: 39.5 us -> none  [local(): everyone = lax.all_gather(ends, 'theta')]
    ppermute x3 -> x8, waiting for transfers between devices: 0.01 us -> 12.1 us  [swap(): return lax.ppermute(block, axis, [(i, i ^ bit) for i in range(size)])]
    ppermute x3 -> x8, starting transfers between devices: 5.62 us -> 10.3 us  [swap(): return lax.ppermute(block, axis, [(i, i ^ bit) for i in range(size)])]
    ppermute x1, waiting for transfers between devices: 4.65 us -> 0.01 us  [swap_across(): return lax.ppermute(block, axis, route)]
    unnamed x12 -> x8, local copies, waits for them, and re-layouts: 3.67 us -> 1.14 us
    pallas_call x5 -> x11, Pallas kernels: 9.49 us -> 7.31 us  [the longest x1 2.3 us: inner_terms(): pl.pallas_call(inner_kernel, name='inner_terms', out_shape=held(*v.shape)...]
    ppermute x1, starting transfers between devices: 2.39 us -> 3.69 us  [swap_across(): return lax.ppermute(block, axis, route)]
  transfers between devices with their start and end apart: 5 -> 9, of which waited for: 2 -> 6; matrix products, arithmetic and copies ran while one was open for 0% -> 2% of each run, Pallas kernels for 9% -> 19%
where the time goes in v3:
time: 39 us; the launch traced here: 38.8 us
  starting transfers between devices  14 us (36%)
  waiting for transfers between devices  12.1 us (31%)
  Pallas kernels  9.27 us (24%)
  between operations  1.59 us (4%)
  local copies, waits for them, and re-layouts  1.3 us (3%)
  other arithmetic  0.48 us (1%)
    ppermute x8, waiting for transfers between devices, swap(): return lax.ppermute(block, axis, [(i, i ^ bit) for i in range(size)])  12.1 us
    ppermute x8, starting transfers between devices, swap(): return lax.ppermute(block, axis, [(i, i ^ bit) for i in range(size)])  10.3 us
    ppermute x1, starting transfers between devices, swap_across(): return lax.ppermute(block, axis, route)  3.69 us
    pallas_call x1, Pallas kernels, inner_terms(): pl.pallas_call(inner_kernel, name='inner_terms', out_shape=held(*v.shape)...  2.3 us
    pallas_call x1, Pallas kernels, early_terms(): pl.pallas_call(early_kernel, name='early_terms', out_shape=held(*v.shape)...  1.79 us
    pallas_call x1, Pallas kernels, late_terms(): pl.pallas_call(late_kernel, name='late_terms', out_shape=held(*v.shape),...  1.42 us
    unnamed x8, local copies, waits for them, and re-layouts  1.14 us
    pallas_call x1, Pallas kernels, pack_sides(): pl.pallas_call(pack_sides_kernel, name='pack_sides', out_shape=(side, sid...  0.99 us
  transfers between devices with their start and end apart: 9, of which 6 were waited for; matrix products, arithmetic and copies ran while one was open for 2% of the time, Pallas kernels for 19%

profile of v3, /device:TPU:0, one launch (start us, length us, event | category | flops | bytes accessed | tf_op | source)
XLA Modules:
  0.0 38.8 jit_solution(3355032644457074877)
XLA Ops:
  0.6 1.1 %copy-done = f32[3,16,8,512]{3,2,1,0:T(8,128)S(1)} copy-done((f32[3,16,8,512]{3,2,1,0:T(8,128)S(1)}, f32[3,16,8,512]{3,2,1,0:T(8,128)}, u32[]{:S(2)}) %copy-start) | copy-done | bytes 786456
  1.8 0.1 pack_planes.1.first_ref
  1.9 3.0 %collective-permute-start = (f32[3,12,8,512]{3,2,1,0:T(8,128)S(1)}, f32[3,12,8,512]{3,2,1,0:T(8,128)S(1)}, u32[]{:S(2)}, u32[]{:S(2)}) collective-permute-start(f32[3,12,8,512]{3,2,1,0:T(8,128)S(1)} %pack_planes.1.first_ref), channel_id=1, source_target_pairs={{0,1},{1,0},{2,3},{3,2},{4,5},{5,4},{6,7},{7,6},{8,9},{9,8},{10,11... | collective-permute-start | bytes 1769480 | tf_op jit(solution)/shard_map/ppermute | solution.py:40
  4.9 1.0 %pack_sides.1 = (f32[3,10,8,512]{3,2,1,0:T(8,128)}, f32[3,10,8,512]{3,2,1,0:T(8,128)}, f32[3,4,8,128]{3,2,1,0:T(8,128)S(1)}) custom-call(s32[1]{0:T(128)} %bitcast.me_ref, f32[3,16,8,512]{3,2,1,0:T(8,128)S(1)} %copy-done.1, f32[3,12,8,512]{3,2,1,0:T(8,128)S(1)} %pack_planes.1.first_ref), custom_call_target="tpu_custom_call" | custom-call | tf_op jit(solution)/shard_map/pack_sides/pallas_call | solution.py:123
  5.9 3.7 %collective-permute-start.1 = (f32[3,10,8,512]{3,2,1,0:T(8,128)}, f32[3,10,8,512]{3,2,1,0:T(8,128)}, u32[]{:S(2)}, u32[]{:S(2)}) collective-permute-start(f32[3,10,8,512]{3,2,1,0:T(8,128)} %get-tuple-element.18), channel_id=1, source_target_pairs={{2,4},{4,2},{6,8},{8,6},{10,12},{12,10},{14,16},{16,14},{18,20},{2... | collective-permute-start | bytes 1474568 | tf_op jit(solution)/shard_map/ppermute | solution.py:48
  9.6 0.5 %collective-permute-start.3 = (f32[3,4,8,128]{3,2,1,0:T(8,128)S(1)}, f32[3,4,8,128]{3,2,1,0:T(8,128)S(1)}, u32[]{:S(2)}, u32[]{:S(2)}) collective-permute-start(f32[3,4,8,128]{3,2,1,0:T(8,128)S(1)} %get-tuple-element.20), channel_id=1, source_target_pairs={{0,16},{2,18},{4,20},{6,22},{8,24},{10,26},{12,28},{14,30},{16,0},... | collective-permute-start | bytes 147464 | tf_op jit(solution)/shard_map/ppermute | solution.py:40
  11.4 0.1 stack.5.power_ref
  11.6 2.3 %inner_terms.1.n_in_ref = f32[3,16,8,512]{3,2,1,0:T(8,128)S(1)} custom-call(f32[21]{0:T(128)S(1)} %copy-done.3, f32[3,16,8,512]{3,2,1,0:T(8,128)S(1)} %copy-done.1, f32[544,512]{1,0:T(8,128)S(1)} %bitcast.6), custom_call_target="tpu_custom_call" | custom-call | flops 603979776 | bytes 3145728 | tf_op jit(solution)/shard_map/inner_terms/pallas_call | solution.py:191
  13.9 3.8 %collective-permute-done.3.mirror_ref = f32[3,4,8,128]{3,2,1,0:T(8,128)S(1)} collective-permute-done((f32[3,4,8,128]{3,2,1,0:T(8,128)S(1)}, f32[3,4,8,128]{3,2,1,0:T(8,128)S(1)}, u32[]{:S(2)}, u32[]{:S(2)}) %collective-permute-start.3) | collective-permute-done | bytes 49184 | tf_op jit(solution)/shard_map/ppermute | solution.py:40
  17.7 1.8 %early_terms.1.n_in_ref = f32[3,16,8,512]{3,2,1,0:T(8,128)S(1)} custom-call(s32[1]{0:T(128)} %bitcast.me_ref, f32[21]{0:T(128)S(1)} %copy-done.3, f32[3,16,8,512]{3,2,1,0:T(8,128)S(1)} %copy-done.1, f32[544,512]{1,0:T(8,128)S(1)} %bitcast.7, f32[3,10,8,512]{3,2,1,0:T(8,128)} %collective-permute-done.2.core_ref, ...), custom_call_target="tpu_custom_call", output_to_operand_aliasing={{}: (6, {})} | custom-call | flops 50331648 | bytes 3145728 | tf_op jit(solution)/shard_map/early_terms/pallas_call | solution.py:249
  19.5 1.4 %late_terms.1.n_in_ref = f32[3,16,8,512]{3,2,1,0:T(8,128)S(1)} custom-call(s32[1]{0:T(128)} %bitcast.me_ref, f32[21]{0:T(128)S(1)} %copy-done.3, f32[3,16,8,512]{3,2,1,0:T(8,128)S(1)} %copy-done.1, f32[3,10,8,512]{3,2,1,0:T(8,128)} %collective-permute-done.1.chip_ref, f32[3,16,8,512]{3,2,1,0:T(8,128)S(1)} %early_terms.1.n_in_ref), custom_call_target="tpu_custom_call", output_to_operand_aliasing={{}: (4, {})} | custom-call | flops 3932160 | bytes 2359296 | tf_op jit(solution)/shard_map/late_terms/pallas_call | solution.py:272
  20.9 0.7 %planes_terms.1 = (f32[3,16,8,512]{3,2,1,0:T(8,128)S(1)}, f32[2,3,8,256]{3,2,1,0:T(8,128)S(1)}, f32[2,3,8,256]{3,2,1,0:T(8,128)S(1)}) custom-call(s32[1]{0:T(128)} %bitcast.me_ref, f32[3,16,8,512]{3,2,1,0:T(8,128)S(1)} %copy-done.1, f32[3,12,8,512]{3,2,1,0:T(8,128)S(1)} %collective-permute-done.y_ref, ...), custom_call_target="tpu_custom_call", output_to_operand_aliasing={{0}: (4, {})} | custom-call | flops 3932160 | bytes 3145728 | tf_op jit(solution)/shard_map/planes_terms/pallas_call | solution.py:323
  21.7 0.2 collective-permute-start.4
  21.8 1.1 %collective-permute-done.4.other_ref = f32[2,3,8,256]{3,2,1,0:T(8,128)S(1)} collective-permute-done((f32[2,3,8,256]{3,2,1,0:T(8,128)S(1)}, f32[2,3,8,256]{3,2,1,0:T(8,128)S(1)}, u32[]{:S(2)}, u32[]{:S(2)}) %collective-permute-start.4) | collective-permute-done | bytes 49184 | tf_op jit(solution)/shard_map/ppermute | solution.py:40
  23.0 2.1 %collective-permute-start.5 = (f32[2,3,8,256]{3,2,1,0:T(8,128)S(1)}, f32[2,3,8,256]{3,2,1,0:T(8,128)S(1)}, u32[]{:S(2)}, u32[]{:S(2)}) collective-permute-start(f32[2,3,8,256]{3,2,1,0:T(8,128)S(1)} %pair.1.block_ref), channel_id=1, source_target_pairs={{0,4},{2,6},{4,0},{6,2},{8,12},{10,14},{12,8},{14,10},{16,20},{18,... | collective-permute-start | bytes 147464 | tf_op jit(solution)/shard_map/ppermute | solution.py:40
  25.1 2.1 %collective-permute-done.5.other_ref = f32[2,3,8,256]{3,2,1,0:T(8,128)S(1)} collective-permute-done((f32[2,3,8,256]{3,2,1,0:T(8,128)S(1)}, f32[2,3,8,256]{3,2,1,0:T(8,128)S(1)}, u32[]{:S(2)}, u32[]{:S(2)}) %collective-permute-start.5) | collective-permute-done | bytes 49184 | tf_op jit(solution)/shard_map/ppermute | solution.py:40
  27.2 1.5 %collective-permute-start.6 = (f32[2,3,8,256]{3,2,1,0:T(8,128)S(1)}, f32[2,3,8,256]{3,2,1,0:T(8,128)S(1)}, u32[]{:S(2)}, u32[]{:S(2)}) collective-permute-start(f32[2,3,8,256]{3,2,1,0:T(8,128)S(1)} %get-tuple-element.25.block_ref), channel_id=1, source_target_pairs={{0,8},{2,10},{4,12},{6,14},{8,0},{10,2},{12,4},{14,6},{16,24},{18,... | collective-permute-start | bytes 147464 | tf_op jit(solution)/shard_map/ppermute | solution.py:40
  28.7 2.6 %collective-permute-done.6.other_ref = f32[2,3,8,256]{3,2,1,0:T(8,128)S(1)} collective-permute-done((f32[2,3,8,256]{3,2,1,0:T(8,128)S(1)}, f32[2,3,8,256]{3,2,1,0:T(8,128)S(1)}, u32[]{:S(2)}, u32[]{:S(2)}) %collective-permute-start.6) | collective-permute-done | bytes 49184 | tf_op jit(solution)/shard_map/ppermute | solution.py:40
  31.4 2.9 %collective-permute-start.7 = (f32[2,3,8,256]{3,2,1,0:T(8,128)S(1)}, f32[2,3,8,256]{3,2,1,0:T(8,128)S(1)}, u32[]{:S(2)}, u32[]{:S(2)}) collective-permute-start(f32[2,3,8,256]{3,2,1,0:T(8,128)S(1)} %get-tuple-element.27.block_ref), channel_id=1, source_target_pairs={{0,16},{2,18},{4,20},{6,22},{8,24},{10,26},{12,28},{14,30},{16,0},... | collective-permute-start | bytes 147464 | tf_op jit(solution)/shard_map/ppermute | solution.py:40
  34.2 2.2 %collective-permute-done.7.other_ref = f32[2,3,8,256]{3,2,1,0:T(8,128)S(1)} collective-permute-done((f32[2,3,8,256]{3,2,1,0:T(8,128)S(1)}, f32[2,3,8,256]{3,2,1,0:T(8,128)S(1)}, u32[]{:S(2)}, u32[]{:S(2)}) %collective-permute-start.7) | collective-permute-done | bytes 49184 | tf_op jit(solution)/shard_map/ppermute | solution.py:40
  36.5 0.1 collective-permute-start.8
  36.6 0.9 %sweep.1 = (f32[3,16,8,512]{3,2,1,0:T(8,128)S(1)}, f32[3,16,8,512]{3,2,1,0:T(8,128)}) custom-call(f32[3,16,8,512]{3,2,1,0:T(8,128)S(1)} %copy-done.1, f32[3,16,8,512]{3,2,1,0:T(8,128)S(1)} %get-tuple-element.21.n_ref, f32[30,512]{1,0:T(8,128)S(1)} %stack.5.power_ref), custom_call_target="tpu_custom_call" | custom-call | flops 1966080 | bytes 2359296 | tf_op jit(solution)/shard_map/sweep/pallas_call | solution.py:394
  37.5 0.3 collective-permute-done.8.got_ref
  37.8 1.0 %close.1 = f32[3,16,8,512]{3,2,1,0:T(8,128)} custom-call(s32[1]{0:T(128)} %bitcast.me_ref, f32[3,16,8,512]{3,2,1,0:T(8,128)S(1)} %get-tuple-element.22.s_ref, f32[30,512]{1,0:T(8,128)S(1)} %stack.5.power_ref, f32[2,3,8,256]{3,2,1,0:T(8,128)S(1)} %get-tuple-element.31.mine_ref, f32[2,3,8,256]{3,2,1,0:T(8,128)S(1)} %collective-permute-done.8.got_ref), custom_call_target="tpu_custom_call" | custom-call | tf_op jit(solution)/shard_map/close/pallas_call | solution.py:513
  (33 shorter events, 0.6 us)
Async XLA Ops:
  0.6 1.1 %copy-start = (f32[3,16,8,512]{3,2,1,0:T(8,128)S(1)}, f32[3,16,8,512]{3,2,1,0:T(8,128)}, u32[]{:S(2)}) copy-start(f32[3,16,8,512]{3,2,1,0:T(8,128)} %v_ref.13) | copy-start | bytes 2359300
  1.8 3.2 %copy-start.1 = (f32[3,16,8,512]{3,2,1,0:T(8,128)S(1)}, f32[3,16,8,512]{3,2,1,0:T(8,128)}, u32[]{:S(2)}) copy-start(f32[3,16,8,512]{3,2,1,0:T(8,128)} %v_ref.13) | copy-start | bytes 2359300
  1.9 9.7 %copy-start.2 = (f32[512,544]{0,1:T(8,128)S(1)}, f32[512,544]{0,1:T(8,128)}, u32[]{:S(2)}) copy-start(f32[512,544]{0,1:T(8,128)} %param.5) | copy-start | bytes 3342340
  1.9 9.7 %copy-start.3 = (f32[21]{0:T(128)S(1)}, f32[21]{0:T(128)}, u32[]{:S(2)}) copy-start(f32[21]{0:T(128)} %stencil_ref.5) | copy-start | bytes 256
  1.9 19.0 %collective-permute-start = (f32[3,12,8,512]{3,2,1,0:T(8,128)S(1)}, f32[3,12,8,512]{3,2,1,0:T(8,128)S(1)}, u32[]{:S(2)}, u32[]{:S(2)}) collective-permute-start(f32[3,12,8,512]{3,2,1,0:T(8,128)S(1)} %pack_planes.1.first_ref), channel_id=1, source_target_pairs={{0,1},{1,0},{2,3},{3,2},{4,5},{5,4},{6,7},{7,6},{8,9},{9,8},{10,11... | collective-permute-start | bytes 1769480 | tf_op jit(solution)/shard_map/ppermute | solution.py:40
  5.9 13.6 %collective-permute-start.1 = (f32[3,10,8,512]{3,2,1,0:T(8,128)}, f32[3,10,8,512]{3,2,1,0:T(8,128)}, u32[]{:S(2)}, u32[]{:S(2)}) collective-permute-start(f32[3,10,8,512]{3,2,1,0:T(8,128)} %get-tuple-element.18), channel_id=1, source_target_pairs={{2,4},{4,2},{6,8},{8,6},{10,12},{12,10},{14,16},{16,14},{18,20},{2... | collective-permute-start | bytes 1474568 | tf_op jit(solution)/shard_map/ppermute | solution.py:48
  9.6 8.1 %collective-permute-start.2 = (f32[3,10,8,512]{3,2,1,0:T(8,128)}, f32[3,10,8,512]{3,2,1,0:T(8,128)}, u32[]{:S(2)}, u32[]{:S(2)}) collective-permute-start(f32[3,10,8,512]{3,2,1,0:T(8,128)} %get-tuple-element.19), channel_id=1, source_target_pairs={{0,2},{2,0},{4,6},{6,4},{8,10},{10,8},{12,14},{14,12},{16,18},{18,... | collective-permute-start | bytes 1474568 | tf_op jit(solution)/shard_map/ppermute | solution.py:40
  9.6 8.1 %collective-permute-start.3 = (f32[3,4,8,128]{3,2,1,0:T(8,128)S(1)}, f32[3,4,8,128]{3,2,1,0:T(8,128)S(1)}, u32[]{:S(2)}, u32[]{:S(2)}) collective-permute-start(f32[3,4,8,128]{3,2,1,0:T(8,128)S(1)} %get-tuple-element.20), channel_id=1, source_target_pairs={{0,16},{2,18},{4,20},{6,22},{8,24},{10,26},{12,28},{14,30},{16,0},... | collective-permute-start | bytes 147464 | tf_op jit(solution)/shard_map/ppermute | solution.py:40
  21.7 1.3 %collective-permute-start.4 = (f32[2,3,8,256]{3,2,1,0:T(8,128)S(1)}, f32[2,3,8,256]{3,2,1,0:T(8,128)S(1)}, u32[]{:S(2)}, u32[]{:S(2)}) collective-permute-start(f32[2,3,8,256]{3,2,1,0:T(8,128)S(1)} %get-tuple-element.24), channel_id=1, source_target_pairs={{0,2},{2,0},{4,6},{6,4},{8,10},{10,8},{12,14},{14,12},{16,18},{18,... | collective-permute-start | bytes 147464 | tf_op jit(solution)/shard_map/ppermute | solution.py:40
  23.0 4.2 %collective-permute-start.5 = (f32[2,3,8,256]{3,2,1,0:T(8,128)S(1)}, f32[2,3,8,256]{3,2,1,0:T(8,128)S(1)}, u32[]{:S(2)}, u32[]{:S(2)}) collective-permute-start(f32[2,3,8,256]{3,2,1,0:T(8,128)S(1)} %pair.1.block_ref), channel_id=1, source_target_pairs={{0,4},{2,6},{4,0},{6,2},{8,12},{10,14},{12,8},{14,10},{16,20},{18,... | collective-permute-start | bytes 147464 | tf_op jit(solution)/shard_map/ppermute | solution.py:40
  27.2 4.2 %collective-permute-start.6 = (f32[2,3,8,256]{3,2,1,0:T(8,128)S(1)}, f32[2,3,8,256]{3,2,1,0:T(8,128)S(1)}, u32[]{:S(2)}, u32[]{:S(2)}) collective-permute-start(f32[2,3,8,256]{3,2,1,0:T(8,128)S(1)} %get-tuple-element.25.block_ref), channel_id=1, source_target_pairs={{0,8},{2,10},{4,12},{6,14},{8,0},{10,2},{12,4},{14,6},{16,24},{18,... | collective-permute-start | bytes 147464 | tf_op jit(solution)/shard_map/ppermute | solution.py:40
  31.4 5.1 %collective-permute-start.7 = (f32[2,3,8,256]{3,2,1,0:T(8,128)S(1)}, f32[2,3,8,256]{3,2,1,0:T(8,128)S(1)}, u32[]{:S(2)}, u32[]{:S(2)}) collective-permute-start(f32[2,3,8,256]{3,2,1,0:T(8,128)S(1)} %get-tuple-element.27.block_ref), channel_id=1, source_target_pairs={{0,16},{2,18},{4,20},{6,22},{8,24},{10,26},{12,28},{14,30},{16,0},... | collective-permute-start | bytes 147464 | tf_op jit(solution)/shard_map/ppermute | solution.py:40
  36.5 1.3 %collective-permute-start.8 = (f32[2,3,8,256]{3,2,1,0:T(8,128)S(1)}, f32[2,3,8,256]{3,2,1,0:T(8,128)S(1)}, u32[]{:S(2)}, u32[]{:S(2)}) collective-permute-start(f32[2,3,8,256]{3,2,1,0:T(8,128)S(1)} %get-tuple-element.32), channel_id=1, source_target_pairs={{0,2},{2,0},{4,6},{6,4},{8,10},{10,8},{12,14},{14,12},{16,18},{18,... | collective-permute-start | bytes 147464 | tf_op jit(solution)/shard_map/ppermute | solution.py:40

commit v4 on v3

--- a/solution.py
+++ b/solution.py
@@ -17,6 +17,7 @@
 VMEM = pl.BlockSpec(memory_space=pltpu.VMEM)
 SMEM = pl.BlockSpec(memory_space=pltpu.SMEM)
 ANY = pl.BlockSpec(memory_space=pl.ANY)
+HBM = pl.BlockSpec(memory_space=pltpu.HBM)
 
 
 def params(block_bytes, blocks):
@@ -58,55 +59,76 @@
     return dot(left[0], right[0]) + (dot(left[0], right[1]) + dot(left[1], right[0]))
 
 
-def pack_planes_kernel(v_ref, y_ref):
+def load_kernel(hbm_ref, v_ref, y_ref, sems):
+    comps, points, planes, _ = v_ref.shape
     carriers = y_ref.shape[1]
-    riders = v_ref.shape[1] - carriers
-    lo, hi = AXIAL_REACH, v_ref.shape[2] - AXIAL_REACH
-
-    def carry(t):
-        for c in range(3):
+    lo, hi = AXIAL_REACH, planes - AXIAL_REACH
+    loads = [pltpu.make_async_copy(hbm_ref.at[c], v_ref.at[c], sems.at[c]) for c in range(comps)]
+    for load in loads:
+        load.start()
+    for c in range(comps):
+        loads[c].wait()
+
+        def carry(t):
             y_ref[c, t] = v_ref[c, t]
 
-    def ride(j):
-        for c in range(3):
+        def ride(j):
             t = carriers + j
             y_ref[c, 3 * j, lo:hi] = v_ref[c, t, 0:2]
             y_ref[c, 3 * j + 1, lo : lo + 1] = v_ref[c, t, 2:3]
             y_ref[c, 3 * j + 1, lo + 1 : hi] = v_ref[c, t, hi : hi + 1]
             y_ref[c, 3 * j + 2, lo:hi] = v_ref[c, t, hi + 1 :]
 
-    each(carriers, carry)
-    each(riders, ride)
-
-
-def pack_planes(v):
+        each(carriers, carry)
+        each(points - carriers, ride)
+
+
+def load(v):
     comps, points, planes, radial = v.shape
     return pl.pallas_call(
-        pack_planes_kernel,
-        name="pack_planes",
-        out_shape=held(comps, points - points // 4, planes, radial),
-        in_specs=[VMEM],
-        out_specs=VMEM,
+        load_kernel,
+        name="load",
+        out_shape=(held(*v.shape), held(comps, points - points // 4, planes, radial)),
+        in_specs=[HBM],
+        out_specs=(VMEM, VMEM),
+        scratch_shapes=[pltpu.SemaphoreType.DMA((comps,))],
         compiler_params=params(v.size * 4, 2),
     )(v)
 
 
-def pack_sides_kernel(me_ref, v_ref, first_ref, core_ref, chip_ref, mirror_ref):
-    points = v_ref.shape[1]
-    reach = core_ref.shape[1]
+def pack_side_kernel(me_ref, v_ref, first_ref, side_ref, *, after):
+    points, reach = v_ref.shape[1], side_ref.shape[1]
+
+    def put(start):
+        for c in range(v_ref.shape[0]):
+            for h in range(reach):
+                side_ref[c, h] = v_ref[c, start + h]
+
     even = me_ref[0] % 2 == 0
-    to_core = jnp.where(even, points - reach, 0)
-    to_chip = jnp.where(even, 0, points - reach)
-    for c in range(3):
-        for h in range(reach):
-            core_ref[c, h] = v_ref[c, to_core + h]
-            chip_ref[c, h] = v_ref[c, to_chip + h]
-    tiles = mirror_ref.shape[1]
+    last = even if after else jnp.logical_not(even)
+    pl.when(last)(lambda: put(points - reach))
+    pl.when(jnp.logical_not(last))(lambda: put(0))
+
+
+def pack_side(me, v, first, reach, after):
+    comps, _, planes, radial = v.shape
+    return pl.pallas_call(
+        functools.partial(pack_side_kernel, after=after),
+        name="pack_core" if after else "pack_chip",
+        out_shape=held(comps, reach, planes, radial),
+        in_specs=[SMEM, VMEM, ANY],
+        out_specs=VMEM,
+        compiler_params=params(v.size * 4, 3),
+    )(me, v, first)
+
+
+def pack_mirror_kernel(v_ref, first_ref, mirror_ref):
+    points, tiles = v_ref.shape[1], mirror_ref.shape[1]
     width = LANES // (points // tiles)
     lane = lax.broadcasted_iota(jnp.int32, mirror_ref.shape[2:], 1)
 
     def put(p):
-        for c in range(3):
+        for c in range(v_ref.shape[0]):
             tile = v_ref[c, p, :, :LANES]
             for q in range(1, points // tiles):
                 part = pltpu.roll(v_ref[c, q * tiles + p, :, :LANES], q * width, 1)
@@ -116,22 +138,20 @@
     each(tiles, put)
 
 
-def pack_sides(me, v, first, reach, width):
-    comps, points, planes, radial = v.shape
-    tiles = points // (LANES // width)
-    side = held(comps, reach, planes, radial)
-    return pl.pallas_call(
-        pack_sides_kernel,
-        name="pack_sides",
-        out_shape=(side, side, held(comps, tiles, planes, LANES)),
-        in_specs=[SMEM, VMEM, ANY],
-        out_specs=(VMEM, VMEM, VMEM),
-        compiler_params=params(v.size * 4, 3),
-    )(me, v, first)
-
-
-def inverse_radius(radial):
-    return 1.0 / (lax.broadcasted_iota(jnp.int32, (1, radial), 1).astype(jnp.float32) + 0.5)
+def pack_mirror(v, first, width):
+    comps, points, planes, _ = v.shape
+    return pl.pallas_call(
+        pack_mirror_kernel,
+        name="pack_mirror",
+        out_shape=held(comps, points // (LANES // width), planes, LANES),
+        in_specs=[VMEM, ANY],
+        out_specs=VMEM,
+        compiler_params=params(v.size * 4, 2),
+    )(v, first)
+
+
+def inverse_radius(radial, start=0):
+    return 1.0 / ((lax.broadcasted_iota(jnp.int32, (1, radial), 1) + start).astype(jnp.float32) + 0.5)
 
 
 def axial_weights(planes, inside):
@@ -200,19 +220,26 @@
     )(stencil, v, op)
 
 
-def add_side(stencil_ref, v_ref, side_ref, n_in_ref, n_ref, inv_r, before):
-    comps, points, _, _ = v_ref.shape
+def add_side(stencil_ref, v_ref, side_ref, n_in_ref, n_ref, before):
+    comps, points, _, radial = v_ref.shape
     reach = side_ref.shape[1]
-    for u in range(reach):
-        t = u if before else points - reach + u
-        taps = [(h, h - u) for h in range(u, reach)] if before else [(h, 2 * reach + h - u) for h in range(u + 1)]
-        b_inv = v_ref[1, t] * inv_r
+    first = 0 if before else reach + 1
+    weights = [stencil_ref[first + k] for k in range(reach)]
+
+    @pl.loop(0, radial // LANES)
+    def column(k):
+        lanes = pl.ds(pl.multiple_of(k * LANES, LANES), LANES)
+        inv_r = inverse_radius(LANES, k * LANES)
         for c in range(comps):
-            around = None
-            for h, k in taps:
-                term = stencil_ref[k] * side_ref[c, h]
-                around = term if around is None else around + term
-            n_ref[c, t] = n_in_ref[c, t] + b_inv * around
+            side = [side_ref[c, h, :, lanes] for h in range(reach)]
+            for u in range(reach):
+                t = u if before else points - reach + u
+                taps = [(h, h - u) for h in range(u, reach)] if before else [(h, reach - 1 + h - u) for h in range(u + 1)]
+                around = None
+                for h, w in taps:
+                    term = weights[w] * side[h]
+                    around = term if around is None else around + term
+                n_ref[c, t, :, lanes] = n_in_ref[c, t, :, lanes] + v_ref[1, t, :, lanes] * inv_r * around
 
 
 def early_kernel(me_ref, stencil_ref, v_ref, op_ref, core_ref, mirror_ref, n_in_ref, n_ref, grad_ref):
@@ -240,7 +267,7 @@
 
     each(points, finish)
     even = me_ref[0] % 2 == 0
-    add = functools.partial(add_side, stencil_ref, v_ref, core_ref, n_ref, n_ref, inverse_radius(radial))
+    add = functools.partial(add_side, stencil_ref, v_ref, core_ref, n_ref, n_ref)
     pl.when(even)(lambda: add(False))
     pl.when(jnp.logical_not(even))(lambda: add(True))
 
@@ -261,9 +288,7 @@
 
 def late_kernel(me_ref, stencil_ref, v_ref, chip_ref, n_in_ref, n_ref):
     even = me_ref[0] % 2 == 0
-    add = functools.partial(
-        add_side, stencil_ref, v_ref, chip_ref, n_in_ref, n_ref, inverse_radius(v_ref.shape[3])
-    )
+    add = functools.partial(add_side, stencil_ref, v_ref, chip_ref, n_in_ref, n_ref)
     pl.when(even)(lambda: add(True))
     pl.when(jnp.logical_not(even))(lambda: add(False))
 
@@ -286,31 +311,30 @@
     carriers = y_ref.shape[1]
     lo, hi = AXIAL_REACH, planes - AXIAL_REACH
     weights = axial_weights(planes, False)
-    decay = power_ref[1:2]
-    ends_ref[...] = jnp.zeros_like(ends_ref)
-
-    def finish(t, c, tile):
-        n = n_in_ref[c, t] + v_ref[2, t] * axial_part(tile, weights)
-        n_ref[c, t] = n
-        right_side = v_ref[c, t] - STEP_WEIGHT * n
-        ends_ref[0, c] = decay * ends_ref[0, c] + right_side
-        ends_ref[1, c] = ends_ref[1, c] + power_ref[pl.ds(t, 1)] * right_side
-
-    def carried(t):
+    for c in range(comps):
+        for j in range(points - carriers):
+            tile_ref[c, j, 0:2] = y_ref[c, 3 * j, lo:hi]
+            tile_ref[c, j, 2:3] = y_ref[c, 3 * j + 1, lo : lo + 1]
+            tile_ref[c, j, lo:hi] = jnp.zeros((hi - lo, radial), jnp.float32)
+            tile_ref[c, j, hi : hi + 1] = y_ref[c, 3 * j + 1, lo + 1 : hi]
+            tile_ref[c, j, hi + 1 :] = y_ref[c, 3 * j + 2, lo:hi]
+
+    @pl.loop(0, radial // LANES)
+    def column(k):
+        lanes = pl.ds(pl.multiple_of(k * LANES, LANES), LANES)
+        decay = power_ref[1:2, lanes]
         for c in range(comps):
-            finish(t, c, y_ref[c, t])
-
-    def ridden(j):
-        for c in range(comps):
-            tile_ref[c, 0:2] = y_ref[c, 3 * j, lo:hi]
-            tile_ref[c, 2:3] = y_ref[c, 3 * j + 1, lo : lo + 1]
-            tile_ref[c, lo:hi] = jnp.zeros_like(tile_ref[c, lo:hi])
-            tile_ref[c, hi : hi + 1] = y_ref[c, 3 * j + 1, lo + 1 : hi]
-            tile_ref[c, hi + 1 :] = y_ref[c, 3 * j + 2, lo:hi]
-            finish(carriers + j, c, tile_ref[c])
-
-    each(carriers, carried)
-    each(points - carriers, ridden)
+            low = high = None
+            for t in range(points):
+                tile = y_ref[c, t, :, lanes] if t < carriers else tile_ref[c, t - carriers, :, lanes]
+                n = n_in_ref[c, t, :, lanes] + v_ref[2, t, :, lanes] * axial_part(tile, weights)
+                n_ref[c, t, :, lanes] = n
+                right_side = v_ref[c, t, :, lanes] - STEP_WEIGHT * n
+                low = right_side if t == 0 else decay * low + right_side
+                high = right_side if t == 0 else high + power_ref[t : t + 1, lanes] * right_side
+            ends_ref[0, c, :, lanes] = low
+            ends_ref[1, c, :, lanes] = high
+
     half = radial // 2
     core = me_ref[0] % 2
     keep_ref[...] = ends_ref[:, :, :, pl.ds(pl.multiple_of(core * half, half), half)]
@@ -327,7 +351,7 @@
         in_specs=[SMEM] + [VMEM] * 4,
         out_specs=(VMEM, VMEM, VMEM),
         scratch_shapes=[
-            pltpu.VMEM((comps, planes, radial), jnp.float32),
+            pltpu.VMEM((comps, points - y.shape[1], planes, radial), jnp.float32),
             pltpu.VMEM((2, comps, planes, radial), jnp.float32),
         ],
         input_output_aliases={4: 0},
@@ -458,7 +482,7 @@
     )(me, power, block, entry, other)
 
 
-def enter_kernel(me_ref, power_ref, block_ref, entry_ref, own_ref, other_ref, mine_ref, send_ref, *, points):
+def enter_kernel(me_ref, power_ref, block_ref, entry_ref, own_ref, other_ref, ready_ref, mine_ref, send_ref, *, points):
     comps, half = block_ref.shape[1], block_ref.shape[3]
     lanes = my_lanes(me_ref, power_ref.shape[1], half)
     row = lambda k: power_ref[k : k + 1, lanes]
@@ -478,15 +502,15 @@
             send_ref[side, c] = jnp.where(odd, even_in[side], odd_in[side])
 
 
-def enter(me, power, block, entry, own, other, points):
+def enter(me, power, block, entry, own, other, ready, points):
     return pl.pallas_call(
         functools.partial(enter_kernel, points=points),
         name="enter",
         out_shape=(held(*block.shape), held(*block.shape)),
-        in_specs=[SMEM] + [VMEM] * 5,
+        in_specs=[SMEM] + [VMEM] * 5 + [ANY],
         out_specs=(VMEM, VMEM),
         compiler_params=params(block.size * 4, 12),
-    )(me, power, block, entry, own, other)
+    )(me, power, block, entry, own, other, ready)
 
 
 def close_kernel(me_ref, s_ref, power_ref, mine_ref, got_ref, out_ref, x_ref, both_ref, sems):
@@ -533,12 +557,14 @@
     me = lax.axis_index("theta").astype(jnp.int32).reshape(1)
     op = radial_op.T
 
-    planes_out = pack_planes(velocity)
+    velocity, planes_out = load(velocity)
     planes_in = swap(planes_out, "gz", 1)
-    core_out, chip_out, mirror_out = pack_sides(me, velocity, planes_out, reach, width)
+    chip_out = pack_side(me, velocity, planes_out, reach, False)
     chip_in = swap_across(chip_out, "theta")
+    mirror_out = pack_mirror(velocity, chip_out, width)
+    mirror_in = swap(mirror_out, "theta", sectors // 2)
+    core_out = pack_side(me, velocity, mirror_out, reach, True)
     core_in = swap(core_out, "theta", 1)
-    mirror_in = swap(mirror_out, "theta", sectors // 2)
     power = powers(me, viscous_factor, points, sectors, radial)
     n = inner_terms(azimuth_stencil, velocity, op)
     n = early_terms(me, azimuth_stencil, velocity, op, core_in, mirror_in, n)
@@ -550,7 +576,7 @@
     entry = jnp.zeros_like(block)
     for bit in range(1, sectors.bit_length() - 1):
         block, entry = merge(me, power, block, entry, swap(block, "theta", 1 << bit), points, bit)
-    mine, send = enter(me, power, block, entry, own, other, points)
+    mine, send = enter(me, power, block, entry, own, other, s, points)
     new_velocity = close(me, s, power, mine, swap(send, "theta", 1))
     return (new_velocity, nonlinear)
 

time: 39 us -> 47.4 us (1.22)
  other arithmetic: 0.48 us -> 8.1 us
  waiting for transfers between devices: 12.1 us -> 8.42 us
  local copies, waits for them, and re-layouts: 1.3 us -> 4.62 us
  Pallas kernels: 9.27 us -> 10.8 us
    mul x8, other arithmetic: 0.26 us -> 4.96 us  [powers(): rows.append(rows[-1] * (1.0 - loss))]
    ppermute x8, waiting for transfers between devices: 12.1 us -> 8.42 us  [swap(): return lax.ppermute(block, axis, [(i, i ^ bit) for i in range(size)])]
    another operation x3, local copies, waits for them, and re-layouts: 0.15 us -> 3.48 us  [powers(): return jnp.stack(rows + [before, after])]
    pallas_call x2 -> x4, Pallas kernels: 1.09 us -> 2.56 us  [the longest x1 1 us: load(): pl.pallas_call(load_kernel, name='load', out_shape=(held(*v.shape), held(...]
    select_n x3, other arithmetic: 0.12 us -> 1.29 us  [powers(): jnp.where(upper, after, after * across)]
    sub x1, other arithmetic: 0.02 us -> 0.62 us  [powers(): rows.append(rows[-1] * (1.0 - loss))]
    div x1, other arithmetic: 0.04 us -> 0.62 us  [powers(): rows += [half / root, 1.0 / result]]
    mul x1, other arithmetic: 0.04 us -> 0.62 us  [powers(): across = across * across]
  transfers between devices with their start and end apart: 9 -> 9, of which waited for: 6 -> 5; matrix products, arithmetic and copies ran while one was open for 2% -> 25% of each run, Pallas kernels for 19% -> 16%
where the time goes in v4:
time: 47.4 us; the launch traced here: 47.1 us
  starting transfers between devices  13.6 us (29%)
  Pallas kernels  10.8 us (23%)
  waiting for transfers between devices  8.42 us (18%)
  other arithmetic  8.1 us (17%)
  local copies, waits for them, and re-layouts  4.62 us (10%)
  between operations  1.48 us (3%)
    ppermute x8, starting transfers between devices, swap(): return lax.ppermute(block, axis, [(i, i ^ bit) for i in range(size)])  9.89 us
    ppermute x8, waiting for transfers between devices, swap(): return lax.ppermute(block, axis, [(i, i ^ bit) for i in range(size)])  8.42 us
    mul x8, other arithmetic, powers(): rows.append(rows[-1] * (1.0 - loss))  4.96 us
    ppermute x1, starting transfers between devices, swap_across(): return lax.ppermute(block, axis, route)  3.76 us
    another operation x3, local copies, waits for them, and re-layouts, powers(): return jnp.stack(rows + [before, after])  3.48 us
    pallas_call x1, Pallas kernels, inner_terms(): pl.pallas_call(inner_kernel, name='inner_terms', out_shape=held(*v.shape)...  2.3 us
    pallas_call x1, Pallas kernels, early_terms(): pl.pallas_call(early_kernel, name='early_terms', out_shape=held(*v.shape)...  1.81 us
    select_n x3, other arithmetic, powers(): jnp.where(upper, after, after * across)  1.29 us
  transfers between devices with their start and end apart: 9, of which 5 were waited for; matrix products, arithmetic and copies ran while one was open for 25% of the time, Pallas kernels for 16%

profile of v4, /device:TPU:0, one launch (start us, length us, event | category | flops | bytes accessed | tf_op | source)
XLA Modules:
  0.0 47.1 jit_solution(18094993042174661948)
XLA Ops:
  0.6 1.1 %copy-done.1 = f32[3,16,8,512]{3,2,1,0:T(8,128)S(1)} copy-done((f32[3,16,8,512]{3,2,1,0:T(8,128)S(1)}, f32[3,16,8,512]{3,2,1,0:T(8,128)}, u32[]{:S(2)}) %copy-start.1) | copy-done | bytes 786456
  1.8 1.0 %load.1 = (f32[3,16,8,512]{3,2,1,0:T(8,128)S(1)}, f32[3,12,8,512]{3,2,1,0:T(8,128)}) custom-call(f32[3,16,8,512]{3,2,1,0:T(8,128)S(1)} %copy-done.1), custom_call_target="tpu_custom_call" | custom-call | tf_op jit(solution)/shard_map/load/pallas_call | solution.py:88
  2.8 3.0 %collective-permute-start = (f32[3,12,8,512]{3,2,1,0:T(8,128)}, f32[3,12,8,512]{3,2,1,0:T(8,128)S(1)}, u32[]{:S(2)}, u32[]{:S(2)}) collective-permute-start(f32[3,12,8,512]{3,2,1,0:T(8,128)} %get-tuple-element.18.first_ref), channel_id=1, source_target_pairs={{0,1},{1,0},{2,3},{3,2},{4,5},{5,4},{6,7},{7,6},{8,9},{9,8},{10,11... | collective-permute-start | bytes 1769480 | tf_op jit(solution)/shard_map/ppermute | solution.py:41
  5.8 3.8 %collective-permute-start.1 = (f32[3,10,8,512]{3,2,1,0:T(8,128)S(1)}, f32[3,10,8,512]{3,2,1,0:T(8,128)S(1)}, u32[]{:S(2)}, u32[]{:S(2)}) collective-permute-start(f32[3,10,8,512]{3,2,1,0:T(8,128)S(1)} %pack_chip.1.first_ref), channel_id=1, source_target_pairs={{2,4},{4,2},{6,8},{8,6},{10,12},{12,10},{14,16},{16,14},{18,20},{2... | collective-permute-start | bytes 1474568 | tf_op jit(solution)/shard_map/ppermute | solution.py:49
  9.6 0.7 %pack_mirror.1.first_ref = f32[3,4,8,128]{3,2,1,0:T(8,128)} custom-call(f32[3,16,8,512]{3,2,1,0:T(8,128)S(1)} %get-tuple-element.17.v_ref, f32[3,10,8,512]{3,2,1,0:T(8,128)S(1)} %pack_chip.1.first_ref), custom_call_target="tpu_custom_call" | custom-call | tf_op jit(solution)/shard_map/pack_mirror/pallas_call | solution.py:143
  10.3 0.8 %pack_core.1 = f32[3,10,8,512]{3,2,1,0:T(8,128)} custom-call(s32[1]{0:T(128)} %bitcast.me_ref, f32[3,16,8,512]{3,2,1,0:T(8,128)S(1)} %get-tuple-element.17.v_ref, f32[3,4,8,128]{3,2,1,0:T(8,128)} %pack_mirror.1.first_ref), custom_call_target="tpu_custom_call" | custom-call | tf_op jit(solution)/shard_map/pack_core/pallas_call | solution.py:115
  14.5 0.6 %fusion.4 = (f32[1,512]{1,0:T(1,128)}, f32[1,512]{1,0:T(1,128)}) fusion(f32[]{:T(128)} %bitcast.1), kind=kLoop, calls=%fused_computation.25 | loop fusion | flops 12288 | bytes 4100 | tf_op jit(solution)/shard_map/mul | solution.py:370
  16.4 0.6 %fusion.10 = (f32[1,512]{1,0:T(1,128)}, f32[1,512]{1,0:T(1,128)}) fusion(f32[]{:T(128)} %bitcast.1), kind=kLoop, calls=%fused_computation.31 | loop fusion | flops 9216 | bytes 4100 | tf_op jit(solution)/shard_map/mul | solution.py:370
  17.6 0.6 %fusion.14 = (f32[1,512]{1,0:T(1,128)}, f32[1,512]{1,0:T(1,128)}) fusion(f32[]{:T(128)} %bitcast.1), kind=kLoop, calls=%fused_computation.35 | loop fusion | flops 12800 | bytes 4100 | tf_op jit(solution)/shard_map/mul | solution.py:370
  20.7 2.9 %stack.5.power_ref = f32[30,512]{1,0:T(8,128)S(1)} concatenate(f32[1,512]{1,0:T(1,128)} %stack_broadcast_in_dim.3, f32[1,512]{1,0:T(1,128)} %get-tuple-element.40, f32[1,512]{1,0:T(1,128)} %get-tuple-element.56, f32[1,512]{1,0:T(1,128)} %get-tuple-element.41, f32[1,512]{1,0:T(1,128)} %get-tuple-element.42, f32[1,512]{1,0:T(1,128)} %get-tuple-element.43, ...), dimensions={0} | concatenate | bytes 122880 | tf_op jit(solution)/shard_map/stack | solution.py:386
  23.7 2.3 %inner_terms.1.n_in_ref = f32[3,16,8,512]{3,2,1,0:T(8,128)S(1)} custom-call(f32[21]{0:T(128)S(1)} %copy-done.2, f32[3,16,8,512]{3,2,1,0:T(8,128)S(1)} %get-tuple-element.17.v_ref, f32[544,512]{1,0:T(8,128)S(1)} %bitcast.6), custom_call_target="tpu_custom_call" | custom-call | flops 603979776 | bytes 3145728 | tf_op jit(solution)/shard_map/inner_terms/pallas_call | solution.py:211
  26.0 1.8 %early_terms.1.n_in_ref = f32[3,16,8,512]{3,2,1,0:T(8,128)S(1)} custom-call(s32[1]{0:T(128)} %bitcast.me_ref, f32[21]{0:T(128)S(1)} %copy-done.2, f32[3,16,8,512]{3,2,1,0:T(8,128)S(1)} %get-tuple-element.17.v_ref, f32[544,512]{1,0:T(8,128)S(1)} %bitcast.7, f32[3,10,8,512]{3,2,1,0:T(8,128)} %collective-permute-done.2.core_ref, ...), custom_call_target="tpu_custom_call", output_to_operand_aliasing={{}: (6, {})} | custom-call | flops 50331648 | bytes 3145728 | tf_op jit(solution)/shard_map/early_terms/pallas_call | solution.py:276
  27.8 1.0 %late_terms.1.n_in_ref = f32[3,16,8,512]{3,2,1,0:T(8,128)S(1)} custom-call(s32[1]{0:T(128)} %bitcast.me_ref, f32[21]{0:T(128)S(1)} %copy-done.2, f32[3,16,8,512]{3,2,1,0:T(8,128)S(1)} %get-tuple-element.17.v_ref, f32[3,10,8,512]{3,2,1,0:T(8,128)S(1)} %collective-permute-done.1.chip_ref, ...), custom_call_target="tpu_custom_call", output_to_operand_aliasing={{}: (4, {})} | custom-call | flops 3932160 | bytes 2359296 | tf_op jit(solution)/shard_map/late_terms/pallas_call | solution.py:297
  28.9 1.1 %planes_terms.1 = (f32[3,16,8,512]{3,2,1,0:T(8,128)S(1)}, f32[2,3,8,256]{3,2,1,0:T(8,128)S(1)}, f32[2,3,8,256]{3,2,1,0:T(8,128)S(1)}) custom-call(s32[1]{0:T(128)} %bitcast.me_ref, f32[3,16,8,512]{3,2,1,0:T(8,128)S(1)} %get-tuple-element.17.v_ref, f32[3,12,8,512]{3,2,1,0:T(8,128)S(1)} %collective-permute-done.y_ref, ...), custom_call_target="tpu_custom_call", output_to_operand_aliasing={{0}: (4, {})} | custom-call | flops 3932160 | bytes 3145728 | tf_op jit(solution)/shard_map/planes_terms/pallas_call | solution.py:347
  30.4 0.9 %collective-permute-done.4.other_ref = f32[2,3,8,256]{3,2,1,0:T(8,128)S(1)} collective-permute-done((f32[2,3,8,256]{3,2,1,0:T(8,128)S(1)}, f32[2,3,8,256]{3,2,1,0:T(8,128)S(1)}, u32[]{:S(2)}, u32[]{:S(2)}) %collective-permute-start.4) | collective-permute-done | bytes 49184 | tf_op jit(solution)/shard_map/ppermute | solution.py:41
  31.3 1.6 %collective-permute-start.5 = (f32[2,3,8,256]{3,2,1,0:T(8,128)S(1)}, f32[2,3,8,256]{3,2,1,0:T(8,128)S(1)}, u32[]{:S(2)}, u32[]{:S(2)}) collective-permute-start(f32[2,3,8,256]{3,2,1,0:T(8,128)S(1)} %pair.1.block_ref), channel_id=1, source_target_pairs={{0,4},{2,6},{4,0},{6,2},{8,12},{10,14},{12,8},{14,10},{16,20},{18,... | collective-permute-start | bytes 147464 | tf_op jit(solution)/shard_map/ppermute | solution.py:41
  32.9 2.5 %collective-permute-done.5.other_ref = f32[2,3,8,256]{3,2,1,0:T(8,128)S(1)} collective-permute-done((f32[2,3,8,256]{3,2,1,0:T(8,128)S(1)}, f32[2,3,8,256]{3,2,1,0:T(8,128)S(1)}, u32[]{:S(2)}, u32[]{:S(2)}) %collective-permute-start.5) | collective-permute-done | bytes 49184 | tf_op jit(solution)/shard_map/ppermute | solution.py:41
  35.5 1.6 %collective-permute-start.6 = (f32[2,3,8,256]{3,2,1,0:T(8,128)S(1)}, f32[2,3,8,256]{3,2,1,0:T(8,128)S(1)}, u32[]{:S(2)}, u32[]{:S(2)}) collective-permute-start(f32[2,3,8,256]{3,2,1,0:T(8,128)S(1)} %get-tuple-element.23.block_ref), channel_id=1, source_target_pairs={{0,8},{2,10},{4,12},{6,14},{8,0},{10,2},{12,4},{14,6},{16,24},{18,... | collective-permute-start | bytes 147464 | tf_op jit(solution)/shard_map/ppermute | solution.py:41
  37.2 2.5 %collective-permute-done.6.other_ref = f32[2,3,8,256]{3,2,1,0:T(8,128)S(1)} collective-permute-done((f32[2,3,8,256]{3,2,1,0:T(8,128)S(1)}, f32[2,3,8,256]{3,2,1,0:T(8,128)S(1)}, u32[]{:S(2)}, u32[]{:S(2)}) %collective-permute-start.6) | collective-permute-done | bytes 49184 | tf_op jit(solution)/shard_map/ppermute | solution.py:41
  39.7 2.9 %collective-permute-start.7 = (f32[2,3,8,256]{3,2,1,0:T(8,128)S(1)}, f32[2,3,8,256]{3,2,1,0:T(8,128)S(1)}, u32[]{:S(2)}, u32[]{:S(2)}) collective-permute-start(f32[2,3,8,256]{3,2,1,0:T(8,128)S(1)} %get-tuple-element.25.block_ref), channel_id=1, source_target_pairs={{0,16},{2,18},{4,20},{6,22},{8,24},{10,26},{12,28},{14,30},{16,0},... | collective-permute-start | bytes 147464 | tf_op jit(solution)/shard_map/ppermute | solution.py:41
  42.6 0.9 %sweep.1 = (f32[3,16,8,512]{3,2,1,0:T(8,128)S(1)}, f32[3,16,8,512]{3,2,1,0:T(8,128)}) custom-call(f32[3,16,8,512]{3,2,1,0:T(8,128)S(1)} %get-tuple-element.17.v_ref, f32[3,16,8,512]{3,2,1,0:T(8,128)S(1)} %get-tuple-element.19.n_ref, f32[30,512]{1,0:T(8,128)S(1)} %stack.5.power_ref), custom_call_target="tpu_custom_call" | custom-call | flops 1966080 | bytes 2359296 | tf_op jit(solution)/shard_map/sweep/pallas_call | solution.py:418
  43.5 1.2 %collective-permute-done.7.other_ref = f32[2,3,8,256]{3,2,1,0:T(8,128)S(1)} collective-permute-done((f32[2,3,8,256]{3,2,1,0:T(8,128)S(1)}, f32[2,3,8,256]{3,2,1,0:T(8,128)S(1)}, u32[]{:S(2)}, u32[]{:S(2)}) %collective-permute-start.7) | collective-permute-done | bytes 49184 | tf_op jit(solution)/shard_map/ppermute | solution.py:41
  44.9 1.2 %collective-permute-done.8.got_ref = f32[2,3,8,256]{3,2,1,0:T(8,128)S(1)} collective-permute-done((f32[2,3,8,256]{3,2,1,0:T(8,128)S(1)}, f32[2,3,8,256]{3,2,1,0:T(8,128)S(1)}, u32[]{:S(2)}, u32[]{:S(2)}) %collective-permute-start.8) | collective-permute-done | bytes 49184 | tf_op jit(solution)/shard_map/ppermute | solution.py:41
  46.1 1.0 %close.1 = f32[3,16,8,512]{3,2,1,0:T(8,128)} custom-call(s32[1]{0:T(128)} %bitcast.me_ref, f32[3,16,8,512]{3,2,1,0:T(8,128)S(1)} %get-tuple-element.20.ready_ref.s_ref, f32[30,512]{1,0:T(8,128)S(1)} %stack.5.power_ref, f32[2,3,8,256]{3,2,1,0:T(8,128)S(1)} %get-tuple-element.29.mine_ref, f32[2,3,8,256]{3,2,1,0:T(8,128)S(1)} %collective-permute-done.8.got_ref), custom_call_target="tpu_custom_call" | custom-call | tf_op jit(solution)/shard_map/close/pallas_call | solution.py:537
  (33 shorter events, 7.6 us)
Async XLA Ops:
  0.6 1.1 %copy-start.1 = (f32[3,16,8,512]{3,2,1,0:T(8,128)S(1)}, f32[3,16,8,512]{3,2,1,0:T(8,128)}, u32[]{:S(2)}) copy-start(f32[3,16,8,512]{3,2,1,0:T(8,128)} %hbm_ref.1) | copy-start | bytes 2359300
  2.8 26.1 %collective-permute-start = (f32[3,12,8,512]{3,2,1,0:T(8,128)}, f32[3,12,8,512]{3,2,1,0:T(8,128)S(1)}, u32[]{:S(2)}, u32[]{:S(2)}) collective-permute-start(f32[3,12,8,512]{3,2,1,0:T(8,128)} %get-tuple-element.18.first_ref), channel_id=1, source_target_pairs={{0,1},{1,0},{2,3},{3,2},{4,5},{5,4},{6,7},{7,6},{8,9},{9,8},{10,11... | collective-permute-start | bytes 1769480 | tf_op jit(solution)/shard_map/ppermute | solution.py:41
  5.8 22.0 %collective-permute-start.1 = (f32[3,10,8,512]{3,2,1,0:T(8,128)S(1)}, f32[3,10,8,512]{3,2,1,0:T(8,128)S(1)}, u32[]{:S(2)}, u32[]{:S(2)}) collective-permute-start(f32[3,10,8,512]{3,2,1,0:T(8,128)S(1)} %pack_chip.1.first_ref), channel_id=1, source_target_pairs={{2,4},{4,2},{6,8},{8,6},{10,12},{12,10},{14,16},{16,14},{18,20},{2... | collective-permute-start | bytes 1474568 | tf_op jit(solution)/shard_map/ppermute | solution.py:49
  10.3 13.3 %copy-start = (f32[512,544]{0,1:T(8,128)S(1)}, f32[512,544]{0,1:T(8,128)}, u32[]{:S(2)}) copy-start(f32[512,544]{0,1:T(8,128)} %param.5) | copy-start | bytes 3342340
  10.3 13.3 %copy-start.2 = (f32[21]{0:T(128)S(1)}, f32[21]{0:T(128)}, u32[]{:S(2)}) copy-start(f32[21]{0:T(128)} %stencil_ref.5) | copy-start | bytes 256
  10.3 15.7 %collective-permute-start.3 = (f32[3,4,8,128]{3,2,1,0:T(8,128)}, f32[3,4,8,128]{3,2,1,0:T(8,128)}, u32[]{:S(2)}, u32[]{:S(2)}) collective-permute-start(f32[3,4,8,128]{3,2,1,0:T(8,128)} %pack_mirror.1.first_ref), channel_id=1, source_target_pairs={{0,16},{2,18},{4,20},{6,22},{8,24},{10,26},{12,28},{14,30},{16,0},... | collective-permute-start | bytes 147464 | tf_op jit(solution)/shard_map/ppermute | solution.py:41
  11.1 14.8 %collective-permute-start.2 = (f32[3,10,8,512]{3,2,1,0:T(8,128)}, f32[3,10,8,512]{3,2,1,0:T(8,128)}, u32[]{:S(2)}, u32[]{:S(2)}) collective-permute-start(f32[3,10,8,512]{3,2,1,0:T(8,128)} %pack_core.1), channel_id=1, source_target_pairs={{0,2},{2,0},{4,6},{6,4},{8,10},{10,8},{12,14},{14,12},{16,18},{18,... | collective-permute-start | bytes 1474568 | tf_op jit(solution)/shard_map/ppermute | solution.py:41
  30.0 1.3 %collective-permute-start.4 = (f32[2,3,8,256]{3,2,1,0:T(8,128)S(1)}, f32[2,3,8,256]{3,2,1,0:T(8,128)S(1)}, u32[]{:S(2)}, u32[]{:S(2)}) collective-permute-start(f32[2,3,8,256]{3,2,1,0:T(8,128)S(1)} %get-tuple-element.22), channel_id=1, source_target_pairs={{0,2},{2,0},{4,6},{6,4},{8,10},{10,8},{12,14},{14,12},{16,18},{18,... | collective-permute-start | bytes 147464 | tf_op jit(solution)/shard_map/ppermute | solution.py:41
  31.3 4.2 %collective-permute-start.5 = (f32[2,3,8,256]{3,2,1,0:T(8,128)S(1)}, f32[2,3,8,256]{3,2,1,0:T(8,128)S(1)}, u32[]{:S(2)}, u32[]{:S(2)}) collective-permute-start(f32[2,3,8,256]{3,2,1,0:T(8,128)S(1)} %pair.1.block_ref), channel_id=1, source_target_pairs={{0,4},{2,6},{4,0},{6,2},{8,12},{10,14},{12,8},{14,10},{16,20},{18,... | collective-permute-start | bytes 147464 | tf_op jit(solution)/shard_map/ppermute | solution.py:41
  35.5 4.2 %collective-permute-start.6 = (f32[2,3,8,256]{3,2,1,0:T(8,128)S(1)}, f32[2,3,8,256]{3,2,1,0:T(8,128)S(1)}, u32[]{:S(2)}, u32[]{:S(2)}) collective-permute-start(f32[2,3,8,256]{3,2,1,0:T(8,128)S(1)} %get-tuple-element.23.block_ref), channel_id=1, source_target_pairs={{0,8},{2,10},{4,12},{6,14},{8,0},{10,2},{12,4},{14,6},{16,24},{18,... | collective-permute-start | bytes 147464 | tf_op jit(solution)/shard_map/ppermute | solution.py:41
  39.7 5.1 %collective-permute-start.7 = (f32[2,3,8,256]{3,2,1,0:T(8,128)S(1)}, f32[2,3,8,256]{3,2,1,0:T(8,128)S(1)}, u32[]{:S(2)}, u32[]{:S(2)}) collective-permute-start(f32[2,3,8,256]{3,2,1,0:T(8,128)S(1)} %get-tuple-element.25.block_ref), channel_id=1, source_target_pairs={{0,16},{2,18},{4,20},{6,22},{8,24},{10,26},{12,28},{14,30},{16,0},... | collective-permute-start | bytes 147464 | tf_op jit(solution)/shard_map/ppermute | solution.py:41
  44.8 1.3 %collective-permute-start.8 = (f32[2,3,8,256]{3,2,1,0:T(8,128)S(1)}, f32[2,3,8,256]{3,2,1,0:T(8,128)S(1)}, u32[]{:S(2)}, u32[]{:S(2)}) collective-permute-start(f32[2,3,8,256]{3,2,1,0:T(8,128)S(1)} %get-tuple-element.30), channel_id=1, source_target_pairs={{0,2},{2,0},{4,6},{6,4},{8,10},{10,8},{12,14},{14,12},{16,18},{18,... | collective-permute-start | bytes 147464 | tf_op jit(solution)/shard_map/ppermute | solution.py:41

commit v5 on v4

--- a/solution.py
+++ b/solution.py
@@ -21,7 +21,7 @@
 
 
 def params(block_bytes, blocks):
-    return pltpu.CompilerParams(vmem_limit_bytes=(6 << 20) + blocks * block_bytes)
+    return pltpu.CompilerParams(vmem_limit_bytes=(2 << 20) + blocks * block_bytes)
 
 
 def held(*shape):
@@ -155,7 +155,7 @@
 
 
 def axial_weights(planes, inside):
-    row = lax.broadcasted_iota(jnp.int32, (planes, 1), 0)
+    row = lax.broadcasted_iota(jnp.int32, (planes, LANES), 0)
     weights = []
     for m, w in enumerate(AXIAL_WEIGHTS, 1):
         for shift, own, sign in ((m, row < planes - m, 1.0), (planes - m, row >= m, -1.0)):
@@ -173,63 +173,60 @@
     return total
 
 
-def inner_kernel(stencil_ref, v_ref, op_ref, n_ref, grad_ref):
+def inner_kernel(tap_ref, v_ref, op_ref, n_ref, grad_ref):
     comps, points, planes, radial = v_ref.shape
-    reach = (stencil_ref.shape[0] - 1) // 2
+    reach = (tap_ref.shape[0] - 1) // 2
     rows = points * planes
     right = split(op_ref[:radial])
     for c in range(comps):
         grad_ref[c * rows : (c + 1) * rows] = product(split(v_ref[c].reshape(rows, radial)), right)
-    inv_r = inverse_radius(radial)
     weights = axial_weights(planes, True)
 
-    def point(t, lows, highs):
-        a, b, e = v_ref[0, t], v_ref[1, t], v_ref[2, t]
-        b_inv = b * inv_r
+    @pl.loop(0, radial // LANES)
+    def column(k):
+        lanes = pl.ds(pl.multiple_of(k * LANES, LANES), LANES)
+        inv_r = inverse_radius(LANES, k * LANES)
         for c in range(comps):
-            around = None
-            for m in range(-lows, highs + 1):
-                term = stencil_ref[m + reach] * v_ref[c, t + m]
-                around = term if around is None else around + term
-            start = c * rows + t * planes
-            grad = grad_ref[pl.ds(pl.multiple_of(start, planes), planes)]
-            n = a * grad + b_inv * around + e * axial_part(v_ref[c, t], weights)
-            if c == 0:
-                n = n - b_inv * b
-            elif c == 1:
-                n = n + a * b_inv
-            n_ref[c, t] = n
-
-    for t in range(reach):
-        point(t, t, min(reach, points - 1 - t))
-    each(points - 2 * reach, lambda i: point(i + reach, reach, reach)) if points >= 2 * reach else None
-    for t in range(max(reach, points - reach), points):
-        point(t, min(reach, t), points - 1 - t)
-
-
-def inner_terms(stencil, v, op):
+            for t in range(points):
+                a, b, e = [v_ref[i, t, :, lanes] for i in range(3)]
+                b_inv = b * inv_r
+                around = None
+                for m in range(max(-reach, -t), min(reach, points - 1 - t) + 1):
+                    term = tap_ref[m + reach] * v_ref[c, t + m, :, lanes]
+                    around = term if around is None else around + term
+                start = c * rows + t * planes
+                n = a * grad_ref[start : start + planes, lanes] + b_inv * around
+                n = n + e * axial_part(v_ref[c, t, :, lanes], weights)
+                if c == 0:
+                    n = n - b_inv * b
+                elif c == 1:
+                    n = n + a * b_inv
+                n_ref[c, t, :, lanes] = n
+
+
+def inner_terms(taps, v, op):
     return pl.pallas_call(
         inner_kernel,
         name="inner_terms",
         out_shape=held(*v.shape),
-        in_specs=[SMEM, VMEM, VMEM],
+        in_specs=[VMEM, VMEM, VMEM],
         out_specs=VMEM,
         scratch_shapes=[pltpu.VMEM((v.size // v.shape[3], v.shape[3]), jnp.float32)],
         compiler_params=params(v.size * 4, 6),
         cost_estimate=pl.CostEstimate(flops=6 * v.size * v.shape[3], bytes_accessed=16 * v.size, transcendentals=0),
-    )(stencil, v, op)
-
-
-def add_side(stencil_ref, v_ref, side_ref, n_in_ref, n_ref, before):
+    )(taps, v, op)
+
+
+def add_side(tap_ref, v_ref, side_ref, n_in_ref, n_ref, before):
     comps, points, _, radial = v_ref.shape
     reach = side_ref.shape[1]
     first = 0 if before else reach + 1
-    weights = [stencil_ref[first + k] for k in range(reach)]
 
     @pl.loop(0, radial // LANES)
     def column(k):
         lanes = pl.ds(pl.multiple_of(k * LANES, LANES), LANES)
         inv_r = inverse_radius(LANES, k * LANES)
+        weights = [tap_ref[first + i] for i in range(reach)]
         for c in range(comps):
             side = [side_ref[c, h, :, lanes] for h in range(reach)]
             for u in range(reach):
@@ -242,7 +239,7 @@
                 n_ref[c, t, :, lanes] = n_in_ref[c, t, :, lanes] + v_ref[1, t, :, lanes] * inv_r * around
 
 
-def early_kernel(me_ref, stencil_ref, v_ref, op_ref, core_ref, mirror_ref, n_in_ref, n_ref, grad_ref):
+def early_kernel(me_ref, tap_ref, v_ref, op_ref, core_ref, mirror_ref, n_in_ref, n_ref, grad_ref):
     comps, points, planes, radial = v_ref.shape
     tiles = mirror_ref.shape[1]
     count = points // tiles
@@ -267,43 +264,43 @@
 
     each(points, finish)
     even = me_ref[0] % 2 == 0
-    add = functools.partial(add_side, stencil_ref, v_ref, core_ref, n_ref, n_ref)
+    add = functools.partial(add_side, tap_ref, v_ref, core_ref, n_ref, n_ref)
     pl.when(even)(lambda: add(False))
     pl.when(jnp.logical_not(even))(lambda: add(True))
 
 
-def early_terms(me, stencil, v, op, core, mirror, n):
+def early_terms(me, taps, v, op, core, mirror, n):
     return pl.pallas_call(
         early_kernel,
         name="early_terms",
         out_shape=held(*v.shape),
-        in_specs=[SMEM, SMEM, VMEM, VMEM, VMEM, VMEM, VMEM],
+        in_specs=[SMEM, VMEM, VMEM, VMEM, VMEM, VMEM, VMEM],
         out_specs=VMEM,
         scratch_shapes=[pltpu.VMEM((v.size // v.shape[3], v.shape[3]), jnp.float32)],
         input_output_aliases={6: 0},
         compiler_params=params(v.size * 4, 8),
         cost_estimate=pl.CostEstimate(flops=2 * v.size * LANES, bytes_accessed=16 * v.size, transcendentals=0),
-    )(me, stencil, v, op, core, mirror, n)
-
-
-def late_kernel(me_ref, stencil_ref, v_ref, chip_ref, n_in_ref, n_ref):
+    )(me, taps, v, op, core, mirror, n)
+
+
+def late_kernel(me_ref, tap_ref, v_ref, chip_ref, n_in_ref, n_ref):
     even = me_ref[0] % 2 == 0
-    add = functools.partial(add_side, stencil_ref, v_ref, chip_ref, n_in_ref, n_ref)
+    add = functools.partial(add_side, tap_ref, v_ref, chip_ref, n_in_ref, n_ref)
     pl.when(even)(lambda: add(True))
     pl.when(jnp.logical_not(even))(lambda: add(False))
 
 
-def late_terms(me, stencil, v, chip, n):
+def late_terms(me, taps, v, chip, n):
     return pl.pallas_call(
         late_kernel,
         name="late_terms",
         out_shape=held(*v.shape),
-        in_specs=[SMEM, SMEM, VMEM, VMEM, VMEM],
+        in_specs=[SMEM, VMEM, VMEM, VMEM, VMEM],
         out_specs=VMEM,
         input_output_aliases={4: 0},
         compiler_params=params(v.size * 4, 5),
         cost_estimate=pl.CostEstimate(flops=20 * v.size, bytes_accessed=12 * v.size, transcendentals=0),
-    )(me, stencil, v, chip, n)
+    )(me, taps, v, chip, n)
 
 
 def planes_kernel(me_ref, v_ref, y_ref, power_ref, n_in_ref, n_ref, keep_ref, send_ref, tile_ref, ends_ref):
@@ -360,12 +357,13 @@
     )(me, v, y, power, n)
 
 
-def powers(me, viscous_factor, points, sectors, radial):
-    radius = jnp.arange(radial).astype(jnp.float32) + 0.5
-    half = 0.5 * radius * lax.rsqrt(viscous_factor[0])
+def table_kernel(me_ref, factor_ref, stencil_ref, row_ref, tap_ref, *, points, sectors):
+    radial = row_ref.shape[1]
+    one = jnp.ones((1, radial), jnp.float32)
+    half = (0.5 * lax.rsqrt(factor_ref[0] * one)) / inverse_radius(radial)
     root = jnp.sqrt(1.0 + half * half)
     loss = 2.0 * half * (root - half)
-    rows = [jnp.ones_like(loss)]
+    rows = [one]
     for _ in range(points):
         rows.append(rows[-1] * (1.0 - loss))
     total = loss
@@ -377,13 +375,29 @@
         left >>= 1
     across = rows[points] * rows[points]
     rows += [half / root, 1.0 / result]
-    before = after = rows[0]
+    before = after = one
     for bit in range(1, sectors.bit_length() - 1):
-        upper = (me >> bit) % 2 == 1
+        upper = (me_ref[0] >> bit) % 2 == 1
         rows += [across, before, after]
         before, after = jnp.where(upper, before * across, before), jnp.where(upper, after, after * across)
         across = across * across
-    return jnp.stack(rows + [before, after])
+    for k, row in enumerate(rows + [before, after]):
+        row_ref[k : k + 1] = row
+    for k in range(tap_ref.shape[0]):
+        tap_ref[k] = jnp.full(tap_ref.shape[1:], stencil_ref[k], jnp.float32)
+
+
+def table(me, viscous_factor, stencil, points, sectors, planes, radial):
+    count = points + 5 + 3 * (sectors.bit_length() - 2)
+    return pl.pallas_call(
+        functools.partial(table_kernel, points=points, sectors=sectors),
+        name="table",
+        out_shape=(held(count, radial), held(stencil.shape[0], planes, LANES)),
+        in_specs=[SMEM, SMEM, SMEM],
+        out_specs=(VMEM, VMEM),
+        compiler_params=params(1 << 20, 1),
+        cost_estimate=pl.CostEstimate(flops=1000 * radial, bytes_accessed=400 * radial, transcendentals=0),
+    )(me, viscous_factor, stencil)
 
 
 def sweep_kernel(v_ref, n_ref, power_ref, s_ref, nonlinear_ref, sem):
@@ -454,7 +468,8 @@
     )(me, power, own, other)
 
 
-def merge_kernel(me_ref, power_ref, block_ref, entry_ref, other_ref, block_out_ref, entry_out_ref, *, points, bit):
+def merge_kernel(me_ref, power_ref, block_ref, other_ref, *refs, points, bit):
+    *entry_refs, block_out_ref, entry_out_ref = refs
     comps, half = block_ref.shape[1], block_ref.shape[3]
     lanes = my_lanes(me_ref, power_ref.shape[1], half)
     first = points + 3 * bit
@@ -467,19 +482,19 @@
         other_low, other_high = other_ref[0, c], other_ref[1, c]
         block_out_ref[0, c] = jnp.where(upper, across * other_low + low, across * low + other_low)
         block_out_ref[1, c] = jnp.where(upper, other_high + across * high, high + across * other_high)
-        entry_out_ref[0, c] = entry_ref[0, c] + before * other_low
-        entry_out_ref[1, c] = entry_ref[1, c] + after * other_high
-
-
-def merge(me, power, block, entry, other, points, bit):
+        for side, enters in enumerate((before * other_low, after * other_high)):
+            entry_out_ref[side, c] = entry_refs[0][side, c] + enters if entry_refs else enters
+
+
+def merge(me, power, block, other, entries, points, bit):
     return pl.pallas_call(
         functools.partial(merge_kernel, points=points, bit=bit),
         name="merge",
         out_shape=(held(*block.shape), held(*block.shape)),
-        in_specs=[SMEM, VMEM, VMEM, VMEM, VMEM],
+        in_specs=[SMEM] + [VMEM] * (3 + len(entries)),
         out_specs=(VMEM, VMEM),
         compiler_params=params(block.size * 4, 8),
-    )(me, power, block, entry, other)
+    )(me, power, block, other, *entries)
 
 
 def enter_kernel(me_ref, power_ref, block_ref, entry_ref, own_ref, other_ref, ready_ref, mine_ref, send_ref, *, points):
@@ -557,7 +572,7 @@
     me = lax.axis_index("theta").astype(jnp.int32).reshape(1)
     op = radial_op.T
 
-    velocity, planes_out = load(velocity)
+    velocity, planes_out = load(pltpu.with_memory_space_constraint(velocity, pltpu.HBM))
     planes_in = swap(planes_out, "gz", 1)
     chip_out = pack_side(me, velocity, planes_out, reach, False)
     chip_in = swap_across(chip_out, "theta")
@@ -565,17 +580,18 @@
     mirror_in = swap(mirror_out, "theta", sectors // 2)
     core_out = pack_side(me, velocity, mirror_out, reach, True)
     core_in = swap(core_out, "theta", 1)
-    power = powers(me, viscous_factor, points, sectors, radial)
-    n = inner_terms(azimuth_stencil, velocity, op)
-    n = early_terms(me, azimuth_stencil, velocity, op, core_in, mirror_in, n)
-    n = late_terms(me, azimuth_stencil, velocity, chip_in, n)
+    power, taps = table(me, viscous_factor, azimuth_stencil, points, sectors, planes, radial)
+    n = inner_terms(taps, velocity, op)
+    n = early_terms(me, taps, velocity, op, core_in, mirror_in, n)
+    n = late_terms(me, taps, velocity, chip_in, n)
     n, own, send = planes_terms(me, velocity, planes_in, power, n)
     other = swap(send, "theta", 1)
     s, nonlinear = sweep(velocity, n, power)
     block = pair(me, power, own, other, points)
-    entry = jnp.zeros_like(block)
+    entries = ()
     for bit in range(1, sectors.bit_length() - 1):
-        block, entry = merge(me, power, block, entry, swap(block, "theta", 1 << bit), points, bit)
+        block, entry = merge(me, power, block, swap(block, "theta", 1 << bit), entries, points, bit)
+        entries = (entry,)
     mine, send = enter(me, power, block, entry, own, other, s, points)
     new_velocity = close(me, s, power, mine, swap(send, "theta", 1))
     return (new_velocity, nonlinear)

time: 47.4 us -> 37.7 us (0.80)
  other arithmetic: 8.1 us -> 0 us
  local copies, waits for them, and re-layouts: 4.62 us -> 0.01 us
  waiting for transfers between devices: 8.42 us -> 12.7 us
  Pallas kernels: 10.8 us -> 8.57 us
  starting transfers between devices: 13.6 us -> 14.8 us
    mul x9 -> x0, other arithmetic: 5.57 us -> none  [the longest x8 4.96 us: powers(): rows.append(rows[-1] * (1.0 - loss))]
    ppermute x8, waiting for transfers between devices: 8.42 us -> 12.7 us  [swap(): return lax.ppermute(block, axis, [(i, i ^ bit) for i in range(size)])]
    another operation x3 -> x0, local copies, waits for them, and re-layouts: 3.48 us -> none  [powers(): return jnp.stack(rows + [before, after])]
    select_n x3 -> x0, other arithmetic: 1.29 us -> none  [powers(): jnp.where(upper, after, after * across)]
    unnamed x6 -> x4, local copies, waits for them, and re-layouts: 1.13 us -> 0.01 us
    pallas_call x1, Pallas kernels: 1.81 us -> 0.78 us  [early_terms(): pl.pallas_call(early_kernel, name='early_terms', out_shape=held(*v.shape)...]
    ppermute x1, starting transfers between devices: 3.76 us -> 4.63 us  [swap_across(): return lax.ppermute(block, axis, route)]
    pallas_call x2, Pallas kernels: 0.85 us -> 0.08 us  [pack_side(): pl.pallas_call(functools.partial(pack_side_kernel, after=after), name='pa...]
  transfers between devices with their start and end apart: 9 -> 9, of which waited for: 5 -> 6; matrix products, arithmetic and copies ran while one was open for 25% -> 0% of each run, Pallas kernels for 16% -> 14%
where the time goes in v5:
time: 37.7 us; the launch traced here: 37.5 us
  starting transfers between devices  14.8 us (39%)
  waiting for transfers between devices  12.7 us (34%)
  Pallas kernels  8.57 us (23%)
  between operations  1.44 us (4%)
    ppermute x8, waiting for transfers between devices, swap(): return lax.ppermute(block, axis, [(i, i ^ bit) for i in range(size)])  12.7 us
    ppermute x8, starting transfers between devices, swap(): return lax.ppermute(block, axis, [(i, i ^ bit) for i in range(size)])  10.2 us
    ppermute x1, starting transfers between devices, swap_across(): return lax.ppermute(block, axis, route)  4.63 us
    pallas_call x1, Pallas kernels, inner_terms(): pl.pallas_call(inner_kernel, name='inner_terms', out_shape=held(*v.shape)...  2.23 us
    pallas_call x1, Pallas kernels, load(): pl.pallas_call(load_kernel, name='load', out_shape=(held(*v.shape), held(...  1.17 us
    pallas_call x1, Pallas kernels, planes_terms(): pl.pallas_call(planes_kernel, name='planes_terms', out_shape=(held(*v.sha...  1.13 us
    pallas_call x1, Pallas kernels, close(): pl.pallas_call(close_kernel, name='close', out_shape=jax.ShapeDtypeStruct...  0.97 us
    pallas_call x1, Pallas kernels, sweep(): pl.pallas_call(sweep_kernel, name='sweep', out_shape=(held(*v.shape), jax...  0.89 us
  transfers between devices with their start and end apart: 9, of which 6 were waited for; matrix products, arithmetic and copies ran while one was open for 0% of the time, Pallas kernels for 14%

profile of v5, /device:TPU:0, one launch (start us, length us, event | category | flops | bytes accessed | tf_op | source)
XLA Modules:
  0.0 37.5 jit_solution(17577718822948209680)
XLA Ops:
  0.6 1.2 %load.1 = (f32[3,16,8,512]{3,2,1,0:T(8,128)S(1)}, f32[3,12,8,512]{3,2,1,0:T(8,128)S(1)}) custom-call(f32[3,16,8,512]{3,2,1,0:T(8,128)} %hbm_ref.1), custom_call_target="tpu_custom_call" | custom-call | tf_op jit(solution)/shard_map/load/pallas_call | solution.py:88
  1.8 3.0 %collective-permute-start = (f32[3,12,8,512]{3,2,1,0:T(8,128)S(1)}, f32[3,12,8,512]{3,2,1,0:T(8,128)S(1)}, u32[]{:S(2)}, u32[]{:S(2)}) collective-permute-start(f32[3,12,8,512]{3,2,1,0:T(8,128)S(1)} %get-tuple-element.20.first_ref), channel_id=1, source_target_pairs={{0,1},{1,0},{2,3},{3,2},{4,5},{5,4},{6,7},{7,6},{8,9},{9,8},{10,11... | collective-permute-start | bytes 1769480 | tf_op jit(solution)/shard_map/ppermute | solution.py:41
  4.9 0.0 copy-start.1
  4.9 0.1 pack_mirror.1.first_ref
  5.1 0.1 collective-permute-start.2
  5.1 4.6 %collective-permute-start.1 = (f32[3,10,8,512]{3,2,1,0:T(8,128)S(1)}, f32[3,10,8,512]{3,2,1,0:T(8,128)S(1)}, u32[]{:S(2)}, u32[]{:S(2)}) collective-permute-start(f32[3,10,8,512]{3,2,1,0:T(8,128)S(1)} %pack_chip.1.first_ref), channel_id=1, source_target_pairs={{2,4},{4,2},{6,8},{8,6},{10,12},{12,10},{14,16},{16,14},{18,20},{2... | collective-permute-start | bytes 1474568 | tf_op jit(solution)/shard_map/ppermute | solution.py:49
  10.4 0.6 %table.1 = (f32[30,512]{1,0:T(8,128)S(1)}, f32[21,8,128]{2,1,0:T(8,128)S(1)}) custom-call(s32[1]{0:T(128)} %bitcast.me_ref, f32[1]{0:T(128)S(6)} %copy.12.factor_ref, f32[21]{0:T(128)S(1)} %copy-done.1), custom_call_target="tpu_custom_call" | custom-call | flops 512000 | bytes 204800 | tf_op jit(solution)/shard_map/table/pallas_call | solution.py:392
  11.1 2.2 %inner_terms.1.n_in_ref = f32[3,16,8,512]{3,2,1,0:T(8,128)S(1)} custom-call(f32[21,8,128]{2,1,0:T(8,128)S(1)} %get-tuple-element.22.tap_ref, f32[3,16,8,512]{3,2,1,0:T(8,128)S(1)} %get-tuple-element.19.v_ref, f32[544,512]{1,0:T(8,128)S(1)} %bitcast.2), custom_call_target="tpu_custom_call" | custom-call | flops 603979776 | bytes 3145728 | tf_op jit(solution)/shard_map/inner_terms/pallas_call | solution.py:208
  13.3 3.9 %collective-permute-done.3.mirror_ref = f32[3,4,8,128]{3,2,1,0:T(8,128)S(1)} collective-permute-done((f32[3,4,8,128]{3,2,1,0:T(8,128)S(1)}, f32[3,4,8,128]{3,2,1,0:T(8,128)S(1)}, u32[]{:S(2)}, u32[]{:S(2)}) %collective-permute-start.3) | collective-permute-done | bytes 49184 | tf_op jit(solution)/shard_map/ppermute | solution.py:41
  17.2 0.8 %early_terms.1.n_in_ref = f32[3,16,8,512]{3,2,1,0:T(8,128)S(1)} custom-call(s32[1]{0:T(128)} %bitcast.me_ref, f32[21,8,128]{2,1,0:T(8,128)S(1)} %get-tuple-element.22.tap_ref, f32[3,16,8,512]{3,2,1,0:T(8,128)S(1)} %get-tuple-element.19.v_ref, f32[544,512]{1,0:T(8,128)S(1)} %bitcast.3, ...), custom_call_target="tpu_custom_call", output_to_operand_aliasing={{}: (6, {})} | custom-call | flops 50331648 | bytes 3145728 | tf_op jit(solution)/shard_map/early_terms/pallas_call | solution.py:273
  18.0 0.5 %late_terms.1.n_in_ref = f32[3,16,8,512]{3,2,1,0:T(8,128)S(1)} custom-call(s32[1]{0:T(128)} %bitcast.me_ref, f32[21,8,128]{2,1,0:T(8,128)S(1)} %get-tuple-element.22.tap_ref, f32[3,16,8,512]{3,2,1,0:T(8,128)S(1)} %get-tuple-element.19.v_ref, f32[3,10,8,512]{3,2,1,0:T(8,128)S(1)} %collective-permute-done.1.chip_ref, ...), custom_call_target="tpu_custom_call", output_to_operand_aliasing={{}: (4, {})} | custom-call | flops 3932160 | bytes 2359296 | tf_op jit(solution)/shard_map/late_terms/pallas_call | solution.py:294
  18.5 1.1 %planes_terms.1 = (f32[3,16,8,512]{3,2,1,0:T(8,128)S(1)}, f32[2,3,8,256]{3,2,1,0:T(8,128)S(1)}, f32[2,3,8,256]{3,2,1,0:T(8,128)S(1)}) custom-call(s32[1]{0:T(128)} %bitcast.me_ref, f32[3,16,8,512]{3,2,1,0:T(8,128)S(1)} %get-tuple-element.19.v_ref, f32[3,12,8,512]{3,2,1,0:T(8,128)S(1)} %collective-permute-done.y_ref, ...), custom_call_target="tpu_custom_call", output_to_operand_aliasing={{0}: (4, {})} | custom-call | flops 3932160 | bytes 3145728 | tf_op jit(solution)/shard_map/planes_terms/pallas_call | solution.py:344
  19.6 1.3 %collective-permute-start.4 = (f32[2,3,8,256]{3,2,1,0:T(8,128)S(1)}, f32[2,3,8,256]{3,2,1,0:T(8,128)S(1)}, u32[]{:S(2)}, u32[]{:S(2)}) collective-permute-start(f32[2,3,8,256]{3,2,1,0:T(8,128)S(1)} %get-tuple-element.26), channel_id=1, source_target_pairs={{0,2},{2,0},{4,6},{6,4},{8,10},{10,8},{12,14},{14,12},{16,18},{18,... | collective-permute-start | bytes 147464 | tf_op jit(solution)/shard_map/ppermute | solution.py:41
  20.9 0.9 %collective-permute-done.4.other_ref = f32[2,3,8,256]{3,2,1,0:T(8,128)S(1)} collective-permute-done((f32[2,3,8,256]{3,2,1,0:T(8,128)S(1)}, f32[2,3,8,256]{3,2,1,0:T(8,128)S(1)}, u32[]{:S(2)}, u32[]{:S(2)}) %collective-permute-start.4) | collective-permute-done | bytes 49184 | tf_op jit(solution)/shard_map/ppermute | solution.py:41
  21.8 1.5 %collective-permute-start.5 = (f32[2,3,8,256]{3,2,1,0:T(8,128)S(1)}, f32[2,3,8,256]{3,2,1,0:T(8,128)S(1)}, u32[]{:S(2)}, u32[]{:S(2)}) collective-permute-start(f32[2,3,8,256]{3,2,1,0:T(8,128)S(1)} %pair.1.block_ref), channel_id=1, source_target_pairs={{0,4},{2,6},{4,0},{6,2},{8,12},{10,14},{12,8},{14,10},{16,20},{18,... | collective-permute-start | bytes 147464 | tf_op jit(solution)/shard_map/ppermute | solution.py:41
  23.2 2.7 %collective-permute-done.5.other_ref = f32[2,3,8,256]{3,2,1,0:T(8,128)S(1)} collective-permute-done((f32[2,3,8,256]{3,2,1,0:T(8,128)S(1)}, f32[2,3,8,256]{3,2,1,0:T(8,128)S(1)}, u32[]{:S(2)}, u32[]{:S(2)}) %collective-permute-start.5) | collective-permute-done | bytes 49184 | tf_op jit(solution)/shard_map/ppermute | solution.py:41
  26.0 1.6 %collective-permute-start.6 = (f32[2,3,8,256]{3,2,1,0:T(8,128)S(1)}, f32[2,3,8,256]{3,2,1,0:T(8,128)S(1)}, u32[]{:S(2)}, u32[]{:S(2)}) collective-permute-start(f32[2,3,8,256]{3,2,1,0:T(8,128)S(1)} %get-tuple-element.27.block_ref), channel_id=1, source_target_pairs={{0,8},{2,10},{4,12},{6,14},{8,0},{10,2},{12,4},{14,6},{16,24},{18,... | collective-permute-start | bytes 147464 | tf_op jit(solution)/shard_map/ppermute | solution.py:41
  27.6 2.5 %collective-permute-done.6.other_ref = f32[2,3,8,256]{3,2,1,0:T(8,128)S(1)} collective-permute-done((f32[2,3,8,256]{3,2,1,0:T(8,128)S(1)}, f32[2,3,8,256]{3,2,1,0:T(8,128)S(1)}, u32[]{:S(2)}, u32[]{:S(2)}) %collective-permute-start.6) | collective-permute-done | bytes 49184 | tf_op jit(solution)/shard_map/ppermute | solution.py:41
  30.1 2.7 %collective-permute-start.7 = (f32[2,3,8,256]{3,2,1,0:T(8,128)S(1)}, f32[2,3,8,256]{3,2,1,0:T(8,128)S(1)}, u32[]{:S(2)}, u32[]{:S(2)}) collective-permute-start(f32[2,3,8,256]{3,2,1,0:T(8,128)S(1)} %get-tuple-element.29.block_ref), channel_id=1, source_target_pairs={{0,16},{2,18},{4,20},{6,22},{8,24},{10,26},{12,28},{14,30},{16,0},... | collective-permute-start | bytes 147464 | tf_op jit(solution)/shard_map/ppermute | solution.py:41
  32.8 0.9 %sweep.1 = (f32[3,16,8,512]{3,2,1,0:T(8,128)S(1)}, f32[3,16,8,512]{3,2,1,0:T(8,128)}) custom-call(f32[3,16,8,512]{3,2,1,0:T(8,128)S(1)} %get-tuple-element.19.v_ref, f32[3,16,8,512]{3,2,1,0:T(8,128)S(1)} %get-tuple-element.23.n_ref, f32[30,512]{1,0:T(8,128)S(1)} %get-tuple-element.21.power_ref), custom_call_target="tpu_custom_call" | custom-call | flops 1966080 | bytes 2359296 | tf_op jit(solution)/shard_map/sweep/pallas_call | solution.py:432
  33.7 1.5 %collective-permute-done.7.other_ref = f32[2,3,8,256]{3,2,1,0:T(8,128)S(1)} collective-permute-done((f32[2,3,8,256]{3,2,1,0:T(8,128)S(1)}, f32[2,3,8,256]{3,2,1,0:T(8,128)S(1)}, u32[]{:S(2)}, u32[]{:S(2)}) %collective-permute-start.7) | collective-permute-done | bytes 49184 | tf_op jit(solution)/shard_map/ppermute | solution.py:41
  35.3 0.1 collective-permute-start.8
  35.3 1.2 %collective-permute-done.8.got_ref = f32[2,3,8,256]{3,2,1,0:T(8,128)S(1)} collective-permute-done((f32[2,3,8,256]{3,2,1,0:T(8,128)S(1)}, f32[2,3,8,256]{3,2,1,0:T(8,128)S(1)}, u32[]{:S(2)}, u32[]{:S(2)}) %collective-permute-start.8) | collective-permute-done | bytes 49184 | tf_op jit(solution)/shard_map/ppermute | solution.py:41
  36.6 1.0 %close.1 = f32[3,16,8,512]{3,2,1,0:T(8,128)} custom-call(s32[1]{0:T(128)} %bitcast.me_ref, f32[3,16,8,512]{3,2,1,0:T(8,128)S(1)} %get-tuple-element.24.ready_ref.s_ref, f32[30,512]{1,0:T(8,128)S(1)} %get-tuple-element.21.power_ref, f32[2,3,8,256]{3,2,1,0:T(8,128)S(1)} %get-tuple-element.33.mine_ref, f32[2,3,8,256]{3,2,1,0:T(8,128)S(1)} %collective-permute-done.8.got_ref), custom_call_target="tpu_custom_call" | custom-call | tf_op jit(solution)/shard_map/close/pallas_call | solution.py:552
  (14 shorter events, 0.2 us)
Async XLA Ops:
  1.8 16.7 %collective-permute-start = (f32[3,12,8,512]{3,2,1,0:T(8,128)S(1)}, f32[3,12,8,512]{3,2,1,0:T(8,128)S(1)}, u32[]{:S(2)}, u32[]{:S(2)}) collective-permute-start(f32[3,12,8,512]{3,2,1,0:T(8,128)S(1)} %get-tuple-element.20.first_ref), channel_id=1, source_target_pairs={{0,1},{1,0},{2,3},{3,2},{4,5},{5,4},{6,7},{7,6},{8,9},{9,8},{10,11... | collective-permute-start | bytes 1769480 | tf_op jit(solution)/shard_map/ppermute | solution.py:41
  4.9 5.6 %copy-start.1 = (f32[21]{0:T(128)S(1)}, f32[21]{0:T(128)}, u32[]{:S(2)}) copy-start(f32[21]{0:T(128)} %stencil_ref.1) | copy-start | bytes 256
  4.9 6.2 %copy-start = (f32[512,544]{0,1:T(8,128)S(1)}, f32[512,544]{0,1:T(8,128)}, u32[]{:S(2)}) copy-start(f32[512,544]{0,1:T(8,128)} %param.5) | copy-start | bytes 3342340
  5.1 12.1 %collective-permute-start.2 = (f32[3,10,8,512]{3,2,1,0:T(8,128)S(1)}, f32[3,10,8,512]{3,2,1,0:T(8,128)S(1)}, u32[]{:S(2)}, u32[]{:S(2)}) collective-permute-start(f32[3,10,8,512]{3,2,1,0:T(8,128)S(1)} %pack_core.1), channel_id=1, source_target_pairs={{0,2},{2,0},{4,6},{6,4},{8,10},{10,8},{12,14},{14,12},{16,18},{18,... | collective-permute-start | bytes 1474568 | tf_op jit(solution)/shard_map/ppermute | solution.py:41
  5.1 12.8 %collective-permute-start.1 = (f32[3,10,8,512]{3,2,1,0:T(8,128)S(1)}, f32[3,10,8,512]{3,2,1,0:T(8,128)S(1)}, u32[]{:S(2)}, u32[]{:S(2)}) collective-permute-start(f32[3,10,8,512]{3,2,1,0:T(8,128)S(1)} %pack_chip.1.first_ref), channel_id=1, source_target_pairs={{2,4},{4,2},{6,8},{8,6},{10,12},{12,10},{14,16},{16,14},{18,20},{2... | collective-permute-start | bytes 1474568 | tf_op jit(solution)/shard_map/ppermute | solution.py:49
  9.8 7.4 %collective-permute-start.3 = (f32[3,4,8,128]{3,2,1,0:T(8,128)S(1)}, f32[3,4,8,128]{3,2,1,0:T(8,128)S(1)}, u32[]{:S(2)}, u32[]{:S(2)}) collective-permute-start(f32[3,4,8,128]{3,2,1,0:T(8,128)S(1)} %pack_mirror.1.first_ref), channel_id=1, source_target_pairs={{0,16},{2,18},{4,20},{6,22},{8,24},{10,26},{12,28},{14,30},{16,0},... | collective-permute-start | bytes 147464 | tf_op jit(solution)/shard_map/ppermute | solution.py:41
  19.6 2.2 %collective-permute-start.4 = (f32[2,3,8,256]{3,2,1,0:T(8,128)S(1)}, f32[2,3,8,256]{3,2,1,0:T(8,128)S(1)}, u32[]{:S(2)}, u32[]{:S(2)}) collective-permute-start(f32[2,3,8,256]{3,2,1,0:T(8,128)S(1)} %get-tuple-element.26), channel_id=1, source_target_pairs={{0,2},{2,0},{4,6},{6,4},{8,10},{10,8},{12,14},{14,12},{16,18},{18,... | collective-permute-start | bytes 147464 | tf_op jit(solution)/shard_map/ppermute | solution.py:41
  21.8 4.2 %collective-permute-start.5 = (f32[2,3,8,256]{3,2,1,0:T(8,128)S(1)}, f32[2,3,8,256]{3,2,1,0:T(8,128)S(1)}, u32[]{:S(2)}, u32[]{:S(2)}) collective-permute-start(f32[2,3,8,256]{3,2,1,0:T(8,128)S(1)} %pair.1.block_ref), channel_id=1, source_target_pairs={{0,4},{2,6},{4,0},{6,2},{8,12},{10,14},{12,8},{14,10},{16,20},{18,... | collective-permute-start | bytes 147464 | tf_op jit(solution)/shard_map/ppermute | solution.py:41
  26.0 4.2 %collective-permute-start.6 = (f32[2,3,8,256]{3,2,1,0:T(8,128)S(1)}, f32[2,3,8,256]{3,2,1,0:T(8,128)S(1)}, u32[]{:S(2)}, u32[]{:S(2)}) collective-permute-start(f32[2,3,8,256]{3,2,1,0:T(8,128)S(1)} %get-tuple-element.27.block_ref), channel_id=1, source_target_pairs={{0,8},{2,10},{4,12},{6,14},{8,0},{10,2},{12,4},{14,6},{16,24},{18,... | collective-permute-start | bytes 147464 | tf_op jit(solution)/shard_map/ppermute | solution.py:41
  30.1 5.1 %collective-permute-start.7 = (f32[2,3,8,256]{3,2,1,0:T(8,128)S(1)}, f32[2,3,8,256]{3,2,1,0:T(8,128)S(1)}, u32[]{:S(2)}, u32[]{:S(2)}) collective-permute-start(f32[2,3,8,256]{3,2,1,0:T(8,128)S(1)} %get-tuple-element.29.block_ref), channel_id=1, source_target_pairs={{0,16},{2,18},{4,20},{6,22},{8,24},{10,26},{12,28},{14,30},{16,0},... | collective-permute-start | bytes 147464 | tf_op jit(solution)/shard_map/ppermute | solution.py:41
  35.3 1.3 %collective-permute-start.8 = (f32[2,3,8,256]{3,2,1,0:T(8,128)S(1)}, f32[2,3,8,256]{3,2,1,0:T(8,128)S(1)}, u32[]{:S(2)}, u32[]{:S(2)}) collective-permute-start(f32[2,3,8,256]{3,2,1,0:T(8,128)S(1)} %get-tuple-element.34), channel_id=1, source_target_pairs={{0,2},{2,0},{4,6},{6,4},{8,10},{10,8},{12,14},{14,12},{16,18},{18,... | collective-permute-start | bytes 147464 | tf_op jit(solution)/shard_map/ppermute | solution.py:41

commit v6 on v5

v6 whole, which is shorter than its diff:
```python
import functools

import jax
import jax.numpy as jnp
from jax import lax
from jax.experimental import pallas as pl
from jax.experimental.pallas import tpu as pltpu
from jax.sharding import PartitionSpec as P

AXIAL_WEIGHTS = (0.75, -0.15, 1.0 / 60.0)
AXIAL_REACH = len(AXIAL_WEIGHTS)
STEP_WEIGHT = 0.2
MIRROR_SIGNS = (-1.0, -1.0, 1.0)
PIECES = ((0, 1), (2,))
LANES = 128
UNROLL = 16

VMEM = pl.BlockSpec(memory_space=pltpu.VMEM)
SMEM = pl.BlockSpec(memory_space=pltpu.SMEM)
ANY = pl.BlockSpec(memory_space=pl.ANY)
HBM = pl.BlockSpec(memory_space=pltpu.HBM)


def params(block_bytes, blocks):
    return pltpu.CompilerParams(vmem_limit_bytes=(2 << 20) + blocks * block_bytes)


def held(*shape):
    return pltpu.VMEM(shape, jnp.float32)


def each(count, body):
    if count <= UNROLL:
        for i in range(count):
            body(i)
    else:
        pl.loop(0, count)(body)


def swap(block, axis, bit):
    size = lax.axis_size(axis)
    return lax.ppermute(block, axis, [(i, i ^ bit) for i in range(size)])


def swap_across(block, axis):
    size = lax.axis_size(axis)
    route = []
    for odd in range(1, size, 2):
        route += [(odd, (odd + 1) % size), ((odd + 1) % size, odd)]
    return lax.ppermute(block, axis, route)


def split(x):
    high = x.astype(jnp.bfloat16)
    return high, (x - high.astype(jnp.float32)).astype(jnp.bfloat16)


def product(left, right):
    dot = functools.partial(jnp.dot, preferred_element_type=jnp.float32)
    return dot(left[0], right[0]) + (dot(left[0], right[1]) + dot(left[1], right[0]))


def load_kernel(hbm_ref, v_ref, *refs):
    *y_refs, sems = refs
    comps, points, planes, _ = v_ref.shape
    carriers = y_refs[0].shape[1]
    lo, hi = AXIAL_REACH, planes - AXIAL_REACH
    loads = [pltpu.make_async_copy(hbm_ref.at[c], v_ref.at[c], sems.at[c]) for c in range(comps)]
    for load in loads:
        load.start()
    for y_ref, piece in zip(y_refs, PIECES):
        for i, c in enumerate(piece):
            loads[c].wait()

            def carry(t):
                y_ref[i, t] = v_ref[c, t]

            def ride(j):
                t = carriers + j
                y_ref[i, 3 * j, lo:hi] = v_ref[c, t, 0:2]
                y_ref[i, 3 * j + 1, lo : lo + 1] = v_ref[c, t, 2:3]
                y_ref[i, 3 * j + 1, lo + 1 : hi] = v_ref[c, t, hi : hi + 1]
                y_ref[i, 3 * j + 2, lo:hi] = v_ref[c, t, hi + 1 :]

            each(carriers, carry)
            each(points - carriers, ride)


def load(v):
    comps, points, planes, radial = v.shape
    sent = [held(len(piece), points - points // 4, planes, radial) for piece in PIECES]
    return pl.pallas_call(
        load_kernel,
        name="load",
        out_shape=(held(*v.shape), *sent),
        in_specs=[HBM],
        out_specs=(VMEM,) * (1 + len(sent)),
        scratch_shapes=[pltpu.SemaphoreType.DMA((comps,))],
        compiler_params=params(v.size * 4, 2),
    )(v)


def pack_side_kernel(me_ref, v_ref, first_ref, *side_refs, after, pieces):
    points, reach = v_ref.shape[1], side_refs[0].shape[1]

    def put(start):
        for side_ref, piece in zip(side_refs, pieces):
            for i, c in enumerate(piece):
                for h in range(reach):
                    side_ref[i, h] = v_ref[c, start + h]

    even = me_ref[0] % 2 == 0
    last = even if after else jnp.logical_not(even)
    pl.when(last)(lambda: put(points - reach))
    pl.when(jnp.logical_not(last))(lambda: put(0))


def pack_side(me, v, first, reach, after, pieces):
    comps, _, planes, radial = v.shape
    return pl.pallas_call(
        functools.partial(pack_side_kernel, after=after, pieces=pieces),
        name="pack_core" if after else "pack_chip",
        out_shape=tuple(held(len(piece), reach, planes, radial) for piece in pieces),
        in_specs=[SMEM, VMEM, ANY],
        out_specs=(VMEM,) * len(pieces),
        compiler_params=params(v.size * 4, 3),
    )(me, v, first)


def pack_mirror_kernel(v_ref, first_ref, mirror_ref):
    points, tiles = v_ref.shape[1], mirror_ref.shape[1]
    width = LANES // (points // tiles)
    lane = lax.broadcasted_iota(jnp.int32, mirror_ref.shape[2:], 1)

    def put(p):
        for c in range(v_ref.shape[0]):
            tile = v_ref[c, p, :, :LANES]
            for q in range(1, points // tiles):
                part = pltpu.roll(v_ref[c, q * tiles + p, :, :LANES], q * width, 1)
                tile = jnp.where(lane < q * width, tile, part)
            mirror_ref[c, p] = tile

    each(tiles, put)


def pack_mirror(v, first, width):
    comps, points, planes, _ = v.shape
    return pl.pallas_call(
        pack_mirror_kernel,
        name="pack_mirror",
        out_shape=held(comps, points // (LANES // width), planes, LANES),
        in_specs=[VMEM, ANY],
        out_specs=VMEM,
        compiler_params=params(v.size * 4, 2),
    )(v, first)


def inverse_radius(radial, start=0):
    return 1.0 / ((lax.broadcasted_iota(jnp.int32, (1, radial), 1) + start).astype(jnp.float32) + 0.5)


def axial_weights(planes, inside):
    row = lax.broadcasted_iota(jnp.int32, (planes, LANES), 0)
    weights = []
    for m, w in enumerate(AXIAL_WEIGHTS, 1):
        for shift, own, sign in ((m, row < planes - m, 1.0), (planes - m, row >= m, -1.0)):
            keep = own if inside else jnp.logical_not(own)
            weights.append((shift, jnp.where(keep, sign * w, 0.0)))
    return weights


def axial_part(tile, weights):
    planes, width = tile.shape
    weights = [(shift, jnp.concatenate([weight] * (width // LANES), axis=1)) for shift, weight in weights]
    total = None
    for shift, weight in weights:
        term = weight * pltpu.roll(tile, planes - shift, 0)
        total = term if total is None else total + term
    return total


def inner_kernel(tap_ref, v_ref, op_ref, n_ref, grad_ref):
    comps, points, planes, radial = v_ref.shape
    reach = (tap_ref.shape[0] - 1) // 2
    rows = points * planes
    right = split(op_ref[:radial])
    for c in range(comps):
        grad_ref[c * rows : (c + 1) * rows] = product(split(v_ref[c].reshape(rows, radial)), right)
    weights = axial_weights(planes, True)

    @pl.loop(0, radial // LANES)
    def column(k):
        lanes = pl.ds(pl.multiple_of(k * LANES, LANES), LANES)
        inv_r = inverse_radius(LANES, k * LANES)
        for c in range(comps):
            for t in range(points):
                a, b, e = [v_ref[i, t, :, lanes] for i in range(3)]
                b_inv = b * inv_r
                around = None
                for m in range(max(-reach, -t), min(reach, points - 1 - t) + 1):
                    term = tap_ref[m + reach] * v_ref[c, t + m, :, lanes]
                    around = term if around is None else around + term
                start = c * rows + t * planes
                n = a * grad_ref[start : start + planes, lanes] + b_inv * around
                n = n + e * axial_part(v_ref[c, t, :, lanes], weights)
                if c == 0:
                    n = n - b_inv * b
                elif c == 1:
                    n = n + a * b_inv
                n_ref[c, t, :, lanes] = n


def inner_terms(taps, v, op):
    return pl.pallas_call(
        inner_kernel,
        name="inner_terms",
        out_shape=held(*v.shape),
        in_specs=[VMEM, VMEM, VMEM],
        out_specs=VMEM,
        scratch_shapes=[pltpu.VMEM((v.size // v.shape[3], v.shape[3]), jnp.float32)],
        compiler_params=params(v.size * 4, 6),
        cost_estimate=pl.CostEstimate(flops=6 * v.size * v.shape[3], bytes_accessed=16 * v.size, transcendentals=0),
    )(taps, v, op)


def add_side(tap_ref, v_ref, side_ref, n_in_ref, n_ref, before, piece):
    comps, points, _, radial = v_ref.shape
    reach = side_ref.shape[1]
    first = 0 if before else reach + 1

    @pl.loop(0, radial // LANES)
    def column(k):
        lanes = pl.ds(pl.multiple_of(k * LANES, LANES), LANES)
        inv_r = inverse_radius(LANES, k * LANES)
        weights = [tap_ref[first + i] for i in range(reach)]
        for i, c in enumerate(piece):
            side = [side_ref[i, h, :, lanes] for h in range(reach)]
            for u in range(reach):
                t = u if before else points - reach + u
                taps = [(h, h - u) for h in range(u, reach)] if before else [(h, reach - 1 + h - u) for h in range(u + 1)]
                around = None
                for h, w in taps:
                    term = weights[w] * side[h]
                    around = term if around is None else around + term
                n_ref[i, t, :, lanes] = n_in_ref[c, t, :, lanes] + v_ref[1, t, :, lanes] * inv_r * around


def early_kernel(me_ref, tap_ref, v_ref, op_ref, core_ref, mirror_ref, n_in_ref, n_ref, grad_ref):
    comps, points, planes, radial = v_ref.shape
    tiles = mirror_ref.shape[1]
    count = points // tiles
    width = LANES // count
    rows = tiles * planes
    right = split(jnp.concatenate([op_ref[radial:]] * count, axis=0))
    lane = lax.broadcasted_iota(jnp.int32, (rows, LANES), 1)
    for c in range(comps):
        high, low = split(MIRROR_SIGNS[c] * mirror_ref[c].reshape(rows, LANES))
        zero = jnp.zeros_like(high)
        parts = [
            [jnp.where((lane >= q * width) & (lane < (q + 1) * width), x, zero) for q in range(count)]
            for x in (high, low)
        ]
        left = [jnp.concatenate(x, axis=0) for x in parts]
        grad_ref[c * points * planes : (c + 1) * points * planes] = product(left, right)

    def finish(t):
        for c in range(comps):
            start = pl.multiple_of((c * points + t) * planes, planes)
            n_ref[c, t] = n_in_ref[c, t] + v_ref[0, t] * grad_ref[pl.ds(start, planes)]

    each(points, finish)
    even = me_ref[0] % 2 == 0
    add = functools.partial(add_side, tap_ref, v_ref, core_ref, n_ref, n_ref, piece=range(comps))
    pl.when(even)(lambda: add(before=False))
    pl.when(jnp.logical_not(even))(lambda: add(before=True))


def early_terms(me, taps, v, op, core, mirror, n):
    return pl.pallas_call(
        early_kernel,
        name="early_terms",
        out_shape=held(*v.shape),
        in_specs=[SMEM, VMEM, VMEM, VMEM, VMEM, VMEM, VMEM],
        out_specs=VMEM,
        scratch_shapes=[pltpu.VMEM((v.size // v.shape[3], v.shape[3]), jnp.float32)],
        input_output_aliases={6: 0},
        compiler_params=params(v.size * 4, 8),
        cost_estimate=pl.CostEstimate(flops=2 * v.size * LANES, bytes_accessed=16 * v.size, transcendentals=0),
    )(me, taps, v, op, core, mirror, n)


def late_kernel(me_ref, tap_ref, v_ref, chip_ref, n_in_ref, n_ref, *, piece):
    points, reach = v_ref.shape[1], chip_ref.shape[1]

    def add(before):
        add_side(tap_ref, v_ref, chip_ref, n_in_ref, n_ref, before, piece)
        for i, c in enumerate(piece):
            for t in range(reach, points) if before else range(points - reach):
                n_ref[i, t] = n_in_ref[c, t]

    even = me_ref[0] % 2 == 0
    pl.when(even)(lambda: add(True))
    pl.when(jnp.logical_not(even))(lambda: add(False))


def late_terms(me, taps, v, chip, n, piece):
    return pl.pallas_call(
        functools.partial(late_kernel, piece=piece),
        name="late_terms",
        out_shape=held(len(piece), *v.shape[1:]),
        in_specs=[SMEM, VMEM, VMEM, VMEM, VMEM],
        out_specs=VMEM,
        compiler_params=params(v.size * 4, 5),
        cost_estimate=pl.CostEstimate(flops=20 * v.size, bytes_accessed=12 * v.size, transcendentals=0),
    )(me, taps, v, chip, n)


def planes_kernel(v_ref, y_ref, row_ref, n_in_ref, n_ref, ends_ref, tile_ref, *, piece):
    comps, points, planes, radial = v_ref.shape
    carriers = y_ref.shape[1]
    lo, hi = AXIAL_REACH, planes - AXIAL_REACH
    weights = axial_weights(planes, False)
    decay = row_ref[1:2]
    for i in range(len(piece)):
        for j in range(points - carriers):
            tile_ref[i, j, 0:2] = y_ref[i, 3 * j, lo:hi]
            tile_ref[i, j, 2:3] = y_ref[i, 3 * j + 1, lo : lo + 1]
            tile_ref[i, j, lo:hi] = jnp.zeros((hi - lo, radial), jnp.float32)
            tile_ref[i, j, hi : hi + 1] = y_ref[i, 3 * j + 1, lo + 1 : hi]
            tile_ref[i, j, hi + 1 :] = y_ref[i, 3 * j + 2, lo:hi]
        ends_ref[0, i] = jnp.zeros((planes, radial), jnp.float32)
        ends_ref[1, i] = jnp.zeros((planes, radial), jnp.float32)

    def finish(t):
        for i, c in enumerate(piece):
            tile = y_ref[i, t] if t < carriers else tile_ref[i, t - carriers]
            n = n_in_ref[i, t] + v_ref[2, t] * axial_part(tile, weights)
            n_ref[i, t] = n
            right_side = v_ref[c, t] - STEP_WEIGHT * n
            ends_ref[0, i] = decay * ends_ref[0, i] + right_side
            ends_ref[1, i] = ends_ref[1, i] + row_ref[t : t + 1] * right_side

    for t in range(points):
        finish(t)


def planes_terms(v, y, rows, n, piece):
    comps, points, planes, radial = v.shape
    return pl.pallas_call(
        functools.partial(planes_kernel, piece=piece),
        name="planes_terms",
        out_shape=(held(*n.shape), held(2, len(piece), planes, radial)),
        in_specs=[VMEM] * 4,
        out_specs=(VMEM, VMEM),
        scratch_shapes=[pltpu.VMEM((len(piece), points - y.shape[1], planes, radial), jnp.float32)],
        input_output_aliases={3: 0},
        compiler_params=params(v.size * 4, 6),
        cost_estimate=pl.CostEstimate(flops=20 * v.size, bytes_accessed=16 * v.size, transcendentals=0),
    )(v, y, rows, n)


def stages(sectors):
    bits = sectors.bit_length() - 1
    return [(bit, 1 << min(2, bits - bit)) for bit in range(0, bits, 2)]


def stage_rows(points, sectors):
    first, found = points + 2, []
    for _, group in stages(sectors):
        found.append(first)
        first += 4 * group
    return found, first


def table_kernel(me_ref, factor_ref, stencil_ref, row_ref, tap_ref, *, points, sectors):
    radial = row_ref.shape[1]
    one = jnp.ones((1, radial), jnp.float32)
    half = (0.5 * lax.rsqrt(factor_ref[0] * one)) / inverse_radius(radial)
    root = jnp.sqrt(1.0 + half * half)
    loss = 2.0 * half * (root - half)
    rows = [one]
    for _ in range(points):
        rows.append(rows[-1] * (1.0 - loss))
    total = loss
    left, result = points * sectors, None
    while left:
        if left & 1:
            result = total if result is None else result + total - result * total
        total = total * (2.0 - total)
        left >>= 1
    height, wrap = half / root, 1.0 / result
    across = rows[points]
    rows.append(height)
    before = after = one

    def pick(index, choices):
        found = choices[-1]
        for k in range(len(choices) - 2, -1, -1):
            found = jnp.where(index == k, choices[k], found)
        return found

    for bit, group in stages(sectors):
        place = lax.rem(lax.div(me_ref[0], 1 << bit), group)
        powers = [one]
        for _ in range(group):
            powers.append(powers[-1] * across)
        kinds = [[], [], [], []]
        for x in range(group):
            other = place ^ x
            kinds[0].append(pick(group - 1 - other, powers[:group]))
            kinds[1].append(pick(other, powers[:group]))
            kinds[2].append(before * jnp.where(other < place, pick(place - 1 - other, powers[:group]), 0.0))
            kinds[3].append(after * jnp.where(other > place, pick(other - place - 1, powers[:group]), 0.0))
        before = before * pick(place, powers[:group])
        after = after * pick(group - 1 - place, powers[:group])
        across = powers[group]
        if 1 << bit == sectors // group:
            for x in range(group):
                kinds[2][x] = height * (kinds[2][x] + before * wrap * kinds[0][x])
                kinds[3][x] = height * (kinds[3][x] + after * wrap * kinds[1][x])
        for kind in kinds:
            rows += kind
    for k, row in enumerate(rows):
        row_ref[k : k + 1] = row
    for k in range(tap_ref.shape[0]):
        tap_ref[k] = jnp.full(tap_ref.shape[1:], stencil_ref[k], jnp.float32)


def table(me, viscous_factor, stencil, points, sectors, planes, radial):
    return pl.pallas_call(
        functools.partial(table_kernel, points=points, sectors=sectors),
        name="table",
        out_shape=(held(stage_rows(points, sectors)[1], radial), held(stencil.shape[0], planes, LANES)),
        in_specs=[SMEM, SMEM, SMEM],
        out_specs=(VMEM, VMEM),
        compiler_params=params(1 << 20, 1),
        cost_estimate=pl.CostEstimate(flops=1000 * radial, bytes_accessed=400 * radial, transcendentals=0),
    )(me, viscous_factor, stencil)


def sweep_kernel(v_ref, n_ref, row_ref, *refs, piece):
    s_ref, out_ref, sem = refs[-3:]
    leave = pltpu.make_async_copy(n_ref, out_ref.at[pl.ds(piece[0], len(piece))], sem)
    leave.start()
    _, points, planes, radial = v_ref.shape
    decay = row_ref[1:2]
    height = row_ref[points + 1 : points + 2]
    for i, c in enumerate(piece):
        s_ref[i, 0] = height * (v_ref[c, 0] - STEP_WEIGHT * n_ref[i, 0])

        def forward(k):
            t = k + 1
            s_ref[i, t] = decay * s_ref[i, t - 1] + height * (v_ref[c, t] - STEP_WEIGHT * n_ref[i, t])

        each(points - 1, forward)

    def backward(k, carry):
        t = points - 1 - k
        after = []
        for i, c in enumerate(piece):
            s_ref[i, t] = s_ref[i, t] + carry[i]
            after.append(decay * (carry[i] + height * (v_ref[c, t] - STEP_WEIGHT * n_ref[i, t])))
        return tuple(after)

    start = (jnp.zeros((planes, radial), jnp.float32),) * len(piece)
    lax.fori_loop(0, points, backward, start, unroll=points <= UNROLL)
    leave.wait()


def sweep(v, n, rows, out, piece):
    return pl.pallas_call(
        functools.partial(sweep_kernel, piece=piece),
        name="sweep",
        out_shape=(held(*n.shape), jax.ShapeDtypeStruct(v.shape, v.dtype)),
        in_specs=[VMEM] * 3 + [ANY] * len(out),
        out_specs=(VMEM, ANY),
        scratch_shapes=[pltpu.SemaphoreType.DMA],
        input_output_aliases={3: 1} if out else {},
        compiler_params=params(v.size * 4, 4),
        cost_estimate=pl.CostEstimate(flops=10 * v.size, bytes_accessed=12 * v.size, transcendentals=0),
    )(v, n, rows, *out)


def weighted(row_ref, first, refs, side, c):
    total = None
    for x, ref in enumerate(refs):
        term = row_ref[first + x : first + x + 1] * ref[side, c]
        total = term if total is None else total + term
    return total


def merge_kernel(row_ref, *refs, first, group):
    blocks, entries, (block_ref, entry_ref) = refs[:group], refs[group:-2], refs[-2:]
    for side in range(2):
        for c in range(block_ref.shape[1]):
            block_ref[side, c] = weighted(row_ref, first + side * group, blocks, side, c)
            enters = weighted(row_ref, first + (2 + side) * group, blocks, side, c)
            entry_ref[side, c] = entries[0][side, c] + enters if entries else enters


def merge(rows, blocks, entries, first):
    return pl.pallas_call(
        functools.partial(merge_kernel, first=first, group=len(blocks)),
        name="merge",
        out_shape=(held(*blocks[0].shape),) * 2,
        in_specs=[VMEM] * (1 + len(blocks) + len(entries)),
        out_specs=(VMEM, VMEM),
        compiler_params=params(blocks[0].size * 4, 8),
    )(rows, *blocks, *entries)


def close_kernel(s_ref, row_ref, *refs, first, group, piece, chained):
    blocks, entries = refs[:group], refs[group : -4 - chained]
    out_ref, x_ref, both_ref, sems = refs[-4:]
    count, points, _, _ = s_ref.shape
    height = row_ref[points + 1 : points + 2]
    leaves = []
    for i in range(count):
        for side in range(2):
            enters = weighted(row_ref, first + (2 + side) * group, blocks, side, i)
            both_ref[side, i] = enters + height * entries[0][side, i] if entries else enters
        before, after = both_ref[0, i], both_ref[1, i]

        def point(t):
            x_ref[i, t] = s_ref[i, t] + row_ref[pl.ds(t + 1, 1)] * before + row_ref[pl.ds(points - t, 1)] * after

        each(points, point)
        leaves.append(pltpu.make_async_copy(x_ref.at[i], out_ref.at[piece[i]], sems.at[i]))
        leaves[i].start()
    for leave in leaves:
        leave.wait()


def close(s, rows, blocks, entries, out, shape, first, piece):
    return pl.pallas_call(
        functools.partial(close_kernel, first=first, group=len(blocks), piece=piece, chained=len(out)),
        name="close",
        out_shape=jax.ShapeDtypeStruct(shape, s.dtype),
        in_specs=[VMEM] * (2 + len(blocks) + len(entries)) + [ANY] * len(out),
        out_specs=ANY,
        scratch_shapes=[
            pltpu.VMEM(s.shape, jnp.float32),
            pltpu.VMEM(blocks[0].shape, jnp.float32),
            pltpu.SemaphoreType.DMA((len(piece),)),
        ],
        input_output_aliases={2 + len(blocks) + len(entries): 0} if out else {},
        compiler_params=params(s.size * 4, 5),
    )(s, rows, *blocks, *entries, *out)


def local(velocity, radial_op, azimuth_stencil, viscous_factor):
    sectors = lax.axis_size("theta")
    comps, points, planes, radial = velocity.shape
    shape = velocity.shape
    reach = (azimuth_stencil.shape[0] - 1) // 2
    width = radial_op.shape[1] - radial
    me = lax.axis_index("theta").astype(jnp.int32).reshape(1)
    op = radial_op.T

    velocity, *planes_out = load(pltpu.with_memory_space_constraint(velocity, pltpu.HBM))
    chip_out = pack_side(me, velocity, planes_out[0], reach, False, PIECES)
    mirror_out = pack_mirror(velocity, chip_out[0], width)
    (core_out,) = pack_side(me, velocity, mirror_out, reach, True, (tuple(range(comps)),))
    planes_in, chip_in = [], []
    for k in range(len(PIECES)):
        planes_in.append(swap(planes_out[k], "gz", 1))
        chip_in.append(swap_across(chip_out[k], "theta"))
    mirror_in = swap(mirror_out, "theta", sectors // 2)
    core_in = swap(core_out, "theta", 1)
    rows, taps = table(me, viscous_factor, azimuth_stencil, points, sectors, planes, radial)
    firsts, _ = stage_rows(points, sectors)
    n = inner_terms(taps, velocity, op)
    n = early_terms(me, taps, velocity, op, core_in, mirror_in, n)
    nonlinear, solved, parts = (), (), []
    for k, piece in enumerate(PIECES):
        part = late_terms(me, taps, velocity, chip_in[k], n, piece)
        part, block = planes_terms(velocity, planes_in[k], rows, part, piece)
        entries = ()
        for (bit, group), first in zip(stages(sectors), firsts):
            blocks = [block] + [swap(block, "theta", x << bit) for x in range(1, group)]
            if first != firsts[-1]:
                block, entry = merge(rows, blocks, entries, first)
                entries = (entry,)
        s, out = sweep(velocity, part, rows, nonlinear, piece)
        nonlinear = (out,)
        parts.append((s, blocks, entries))
    for (s, blocks, entries), piece in zip(parts, PIECES):
        solved = (close(s, rows, blocks, entries, solved, shape, firsts[-1], piece),)
    return (solved[0], nonlinear[0])


def solution(mesh):
    in_specs = (P(None, "theta", "gz", None), P(), P(), P())
    out_specs = (P(None, "theta", "gz", None), P(None, "theta", "gz", None))
    return jax.shard_map(local, mesh=mesh, in_specs=in_specs, out_specs=out_specs, check_vma=False)
```

time: 37.7 us -> 42.4 us (1.12)
  starting transfers between devices: 14.8 us -> 22.4 us
  waiting for transfers between devices: 12.7 us -> 8.99 us
  Pallas kernels: 8.57 us -> 9.34 us
    ppermute x8 -> x16, starting transfers between devices: 10.2 us -> 15.9 us  [swap(): return lax.ppermute(block, axis, [(i, i ^ bit) for i in range(size)])]
    ppermute x8 -> x16, waiting for transfers between devices: 12.7 us -> 8.99 us  [swap(): return lax.ppermute(block, axis, [(i, i ^ bit) for i in range(size)])]
    ppermute x1 -> x2, starting transfers between devices: 4.63 us -> 6.58 us  [swap_across(): return lax.ppermute(block, axis, route)]
    pallas_call x12 -> x13, Pallas kernels: 4.85 us -> 5.5 us  [the longest x2 1.65 us: close(): pl.pallas_call(functools.partial(close_kernel, first=first, group=len(blo...]
  transfers between devices with their start and end apart: 9 -> 18, of which waited for: 6 -> 4; matrix products, arithmetic and copies ran while one was open for 0% -> 0% of each run, Pallas kernels for 14% -> 17%
where the time goes in v6:
time: 42.4 us; the launch traced here: 42.3 us
  starting transfers between devices  22.4 us (53%)
  Pallas kernels  9.34 us (22%)
  waiting for transfers between devices  8.99 us (21%)
  between operations  1.52 us (4%)
    ppermute x16, starting transfers between devices, swap(): return lax.ppermute(block, axis, [(i, i ^ bit) for i in range(size)])  15.9 us
    ppermute x16, waiting for transfers between devices, swap(): return lax.ppermute(block, axis, [(i, i ^ bit) for i in range(size)])  8.99 us
    ppermute x2, starting transfers between devices, swap_across(): return lax.ppermute(block, axis, route)  6.58 us
    pallas_call x1, Pallas kernels, inner_terms(): pl.pallas_call(inner_kernel, name='inner_terms', out_shape=held(*v.shape)...  2.23 us
    pallas_call x2, Pallas kernels, close(): pl.pallas_call(functools.partial(close_kernel, first=first, group=len(blo...  1.65 us
    pallas_call x2, Pallas kernels, sweep(): pl.pallas_call(functools.partial(sweep_kernel, piece=piece), name='sweep'...  1.52 us
    pallas_call x1, Pallas kernels, load(): pl.pallas_call(load_kernel, name='load', out_shape=(held(*v.shape), *sent...  1.17 us
  transfers between devices with their start and end apart: 18, of which 4 were waited for; matrix products, arithmetic and copies ran while one was open for 0% of the time, Pallas kernels for 17%

profile of v6, /device:TPU:0, one launch (start us, length us, event | category | flops | bytes accessed | tf_op | source)
XLA Modules:
  0.0 42.3 jit_solution(5946766633474456780)
XLA Ops:
  0.6 1.2 %load.1 = (f32[3,16,8,512]{3,2,1,0:T(8,128)S(1)}, f32[2,12,8,512]{3,2,1,0:T(8,128)S(1)}, f32[1,12,8,512]{3,2,1,0:T(8,128)S(1)}) custom-call(f32[3,16,8,512]{3,2,1,0:T(8,128)} %hbm_ref.1), custom_call_target="tpu_custom_call" | custom-call | tf_op jit(solution)/shard_map/load/pallas_call | solution.py:92
  2.1 0.5 %collective-permute-start.2 = (f32[3,10,8,512]{3,2,1,0:T(8,128)S(1)}, f32[3,10,8,512]{3,2,1,0:T(8,128)S(1)}, u32[]{:S(2)}, u32[]{:S(2)}) collective-permute-start(f32[3,10,8,512]{3,2,1,0:T(8,128)S(1)} %pack_core.1), channel_id=1, source_target_pairs={{0,2},{2,0},{4,6},{6,4},{8,10},{10,8},{12,14},{14,12},{16,18},{18,... | collective-permute-start | bytes 1474568 | tf_op jit(solution)/shard_map/ppermute | solution.py:42
  2.6 2.6 %collective-permute-start.4 = (f32[2,12,8,512]{3,2,1,0:T(8,128)S(1)}, f32[2,12,8,512]{3,2,1,0:T(8,128)S(1)}, u32[]{:S(2)}, u32[]{:S(2)}) collective-permute-start(f32[2,12,8,512]{3,2,1,0:T(8,128)S(1)} %get-tuple-element.25.first_ref), channel_id=1, source_target_pairs={{0,1},{1,0},{2,3},{3,2},{4,5},{5,4},{6,7},{7,6},{8,9},{9,8},{10,11... | collective-permute-start | bytes 1179656 | tf_op jit(solution)/shard_map/ppermute | solution.py:42
  5.2 4.3 %collective-permute-start.5 = (f32[2,10,8,512]{3,2,1,0:T(8,128)S(1)}, f32[2,10,8,512]{3,2,1,0:T(8,128)S(1)}, u32[]{:S(2)}, u32[]{:S(2)}) collective-permute-start(f32[2,10,8,512]{3,2,1,0:T(8,128)S(1)} %get-tuple-element.27.first_ref), channel_id=1, source_target_pairs={{2,4},{4,2},{6,8},{8,6},{10,12},{12,10},{14,16},{16,14},{18,20},{2... | collective-permute-start | bytes 983048 | tf_op jit(solution)/shard_map/ppermute | solution.py:50
  10.0 5.4 %collective-permute-done.3.mirror_ref = f32[3,4,8,128]{3,2,1,0:T(8,128)S(1)} collective-permute-done((f32[3,4,8,128]{3,2,1,0:T(8,128)S(1)}, f32[3,4,8,128]{3,2,1,0:T(8,128)S(1)}, u32[]{:S(2)}, u32[]{:S(2)}) %collective-permute-start.3) | collective-permute-done | bytes 49184 | tf_op jit(solution)/shard_map/ppermute | solution.py:42
  15.4 2.3 %collective-permute-start.1 = (f32[1,10,8,512]{3,2,1,0:T(8,128)S(1)}, f32[1,10,8,512]{3,2,1,0:T(8,128)S(1)}, u32[]{:S(2)}, u32[]{:S(2)}) collective-permute-start(f32[1,10,8,512]{3,2,1,0:T(8,128)S(1)} %get-tuple-element.26), channel_id=1, source_target_pairs={{2,4},{4,2},{6,8},{8,6},{10,12},{12,10},{14,16},{16,14},{18,20},{2... | collective-permute-start | bytes 491528 | tf_op jit(solution)/shard_map/ppermute | solution.py:50
  18.3 0.7 %table.1 = (f32[50,512]{1,0:T(8,128)S(1)}, f32[21,8,128]{2,1,0:T(8,128)S(1)}) custom-call(s32[1]{0:T(128)} %bitcast.me_ref, f32[1]{0:T(128)S(6)} %copy.16.factor_ref, f32[21]{0:T(128)S(1)} %copy-done.1), custom_call_target="tpu_custom_call" | custom-call | flops 512000 | bytes 204800 | tf_op jit(solution)/shard_map/table/pallas_call | solution.py:430
  19.0 2.2 %inner_terms.1.n_in_ref = f32[3,16,8,512]{3,2,1,0:T(8,128)S(1)} custom-call(f32[21,8,128]{2,1,0:T(8,128)S(1)} %get-tuple-element.24.tap_ref, f32[3,16,8,512]{3,2,1,0:T(8,128)S(1)} %get-tuple-element.21.v_ref, f32[544,512]{1,0:T(8,128)S(1)} %bitcast.2), custom_call_target="tpu_custom_call" | custom-call | flops 603979776 | bytes 3145728 | tf_op jit(solution)/shard_map/inner_terms/pallas_call | solution.py:214
  21.3 0.8 %early_terms.1.n_in_ref = f32[3,16,8,512]{3,2,1,0:T(8,128)S(1)} custom-call(s32[1]{0:T(128)} %bitcast.me_ref, f32[21,8,128]{2,1,0:T(8,128)S(1)} %get-tuple-element.24.tap_ref, f32[3,16,8,512]{3,2,1,0:T(8,128)S(1)} %get-tuple-element.21.v_ref, f32[544,512]{1,0:T(8,128)S(1)} %bitcast.3, ...), custom_call_target="tpu_custom_call", output_to_operand_aliasing={{}: (6, {})} | custom-call | flops 50331648 | bytes 3145728 | tf_op jit(solution)/shard_map/early_terms/pallas_call | solution.py:279
  23.0 1.0 %collective-permute-start.13 = (f32[2,2,8,512]{3,2,1,0:T(8,128)S(1)}, f32[2,2,8,512]{3,2,1,0:T(8,128)S(1)}, u32[]{:S(2)}, u32[]{:S(2)}) collective-permute-start(f32[2,2,8,512]{3,2,1,0:T(8,128)S(1)} %get-tuple-element.36.refs_0_), channel_id=1, source_target_pairs={{0,4},{2,6},{4,0},{6,2},{8,12},{10,14},{12,8},{14,10},{16,20},{18,... | collective-permute-start | bytes 196616 | tf_op jit(solution)/shard_map/ppermute | solution.py:42
  24.0 0.8 %collective-permute-start.12 = (f32[2,2,8,512]{3,2,1,0:T(8,128)S(1)}, f32[2,2,8,512]{3,2,1,0:T(8,128)S(1)}, u32[]{:S(2)}, u32[]{:S(2)}) collective-permute-start(f32[2,2,8,512]{3,2,1,0:T(8,128)S(1)} %get-tuple-element.36.refs_0_), channel_id=1, source_target_pairs={{0,2},{2,0},{4,6},{6,4},{8,10},{10,8},{12,14},{14,12},{16,18},{18,... | collective-permute-start | bytes 196616 | tf_op jit(solution)/shard_map/ppermute | solution.py:42
  25.6 1.7 %collective-permute-done.14.refs_3_ = f32[2,2,8,512]{3,2,1,0:T(8,128)S(1)} collective-permute-done((f32[2,2,8,512]{3,2,1,0:T(8,128)S(1)}, f32[2,2,8,512]{3,2,1,0:T(8,128)S(1)}, u32[]{:S(2)}, u32[]{:S(2)}) %collective-permute-start.14) | collective-permute-done | bytes 65568 | tf_op jit(solution)/shard_map/ppermute | solution.py:42
  27.2 0.7 %collective-permute-done.13.refs_2_ = f32[2,2,8,512]{3,2,1,0:T(8,128)S(1)} collective-permute-done((f32[2,2,8,512]{3,2,1,0:T(8,128)S(1)}, f32[2,2,8,512]{3,2,1,0:T(8,128)S(1)}, u32[]{:S(2)}, u32[]{:S(2)}) %collective-permute-start.13) | collective-permute-done | bytes 65568 | tf_op jit(solution)/shard_map/ppermute | solution.py:42
  28.0 2.6 %collective-permute-start.17 = (f32[2,2,8,512]{3,2,1,0:T(8,128)S(1)}, f32[2,2,8,512]{3,2,1,0:T(8,128)S(1)}, u32[]{:S(2)}, u32[]{:S(2)}) collective-permute-start(f32[2,2,8,512]{3,2,1,0:T(8,128)S(1)} %get-tuple-element.37.refs_0_), channel_id=1, source_target_pairs={{0,24},{2,26},{4,28},{6,30},{8,16},{10,18},{12,20},{14,22},{16,8},... | collective-permute-start | bytes 196616 | tf_op jit(solution)/shard_map/ppermute | solution.py:42
  30.6 1.3 %collective-permute-start.7 = (f32[2,1,8,512]{3,2,1,0:T(8,128)S(1)}, f32[2,1,8,512]{3,2,1,0:T(8,128)S(1)}, u32[]{:S(2)}, u32[]{:S(2)}) collective-permute-start(f32[2,1,8,512]{3,2,1,0:T(8,128)S(1)} %get-tuple-element.32.refs_0_), channel_id=1, source_target_pairs={{0,4},{2,6},{4,0},{6,2},{8,12},{10,14},{12,8},{14,10},{16,20},{18,... | collective-permute-start | bytes 98312 | tf_op jit(solution)/shard_map/ppermute | solution.py:42
  32.0 1.4 %collective-permute-start.15 = (f32[2,2,8,512]{3,2,1,0:T(8,128)S(1)}, f32[2,2,8,512]{3,2,1,0:T(8,128)S(1)}, u32[]{:S(2)}, u32[]{:S(2)}) collective-permute-start(f32[2,2,8,512]{3,2,1,0:T(8,128)S(1)} %get-tuple-element.37.refs_0_), channel_id=1, source_target_pairs={{0,8},{2,10},{4,12},{6,14},{8,0},{10,2},{12,4},{14,6},{16,24},{18,... | collective-permute-start | bytes 196616 | tf_op jit(solution)/shard_map/ppermute | solution.py:42
  33.4 1.2 %collective-permute-done.7.refs_2_ = f32[2,1,8,512]{3,2,1,0:T(8,128)S(1)} collective-permute-done((f32[2,1,8,512]{3,2,1,0:T(8,128)S(1)}, f32[2,1,8,512]{3,2,1,0:T(8,128)S(1)}, u32[]{:S(2)}, u32[]{:S(2)}) %collective-permute-start.7) | collective-permute-done | bytes 32800 | tf_op jit(solution)/shard_map/ppermute | solution.py:42
  34.6 1.9 %collective-permute-start.11 = (f32[2,1,8,512]{3,2,1,0:T(8,128)S(1)}, f32[2,1,8,512]{3,2,1,0:T(8,128)S(1)}, u32[]{:S(2)}, u32[]{:S(2)}) collective-permute-start(f32[2,1,8,512]{3,2,1,0:T(8,128)S(1)} %get-tuple-element.33.refs_0_), channel_id=1, source_target_pairs={{0,24},{2,26},{4,28},{6,30},{8,16},{10,18},{12,20},{14,22},{16,8},... | collective-permute-start | bytes 98312 | tf_op jit(solution)/shard_map/ppermute | solution.py:42
  36.5 0.6 %collective-permute-start.10 = (f32[2,1,8,512]{3,2,1,0:T(8,128)S(1)}, f32[2,1,8,512]{3,2,1,0:T(8,128)S(1)}, u32[]{:S(2)}, u32[]{:S(2)}) collective-permute-start(f32[2,1,8,512]{3,2,1,0:T(8,128)S(1)} %get-tuple-element.33.refs_0_), channel_id=1, source_target_pairs={{0,16},{2,18},{4,20},{6,22},{8,24},{10,26},{12,28},{14,30},{16,0},... | collective-permute-start | bytes 98312 | tf_op jit(solution)/shard_map/ppermute | solution.py:42
  37.1 2.0 %collective-permute-start.9 = (f32[2,1,8,512]{3,2,1,0:T(8,128)S(1)}, f32[2,1,8,512]{3,2,1,0:T(8,128)S(1)}, u32[]{:S(2)}, u32[]{:S(2)}) collective-permute-start(f32[2,1,8,512]{3,2,1,0:T(8,128)S(1)} %get-tuple-element.33.refs_0_), channel_id=1, source_target_pairs={{0,8},{2,10},{4,12},{6,14},{8,0},{10,2},{12,4},{14,6},{16,24},{18,... | collective-permute-start | bytes 98312 | tf_op jit(solution)/shard_map/ppermute | solution.py:42
  39.0 0.8 %sweep.2 = (f32[2,16,8,512]{3,2,1,0:T(8,128)S(1)}, f32[3,16,8,512]{3,2,1,0:T(8,128)}) custom-call(f32[3,16,8,512]{3,2,1,0:T(8,128)S(1)} %get-tuple-element.21.v_ref, f32[2,16,8,512]{3,2,1,0:T(8,128)S(1)} %get-tuple-element.29.n_ref, f32[50,512]{1,0:T(8,128)S(1)} %get-tuple-element.23.row_ref), custom_call_target="tpu_custom_call" | custom-call | flops 1966080 | bytes 2359296 | tf_op jit(solution)/shard_map/sweep/pallas_call | solution.py:471
  39.9 0.7 %sweep.3 = (f32[1,16,8,512]{3,2,1,0:T(8,128)S(1)}, f32[3,16,8,512]{3,2,1,0:T(8,128)}) custom-call(f32[3,16,8,512]{3,2,1,0:T(8,128)S(1)} %get-tuple-element.21.v_ref, f32[1,16,8,512]{3,2,1,0:T(8,128)S(1)} %get-tuple-element.28.n_ref, f32[50,512]{1,0:T(8,128)S(1)} %get-tuple-element.23.row_ref, ...), custom_call_target="tpu_custom_call", output_to_operand_aliasing={{1}: (3, {})} | custom-call | flops 1966080 | bytes 2359296 | tf_op jit(solution)/shard_map/sweep/pallas_call | solution.py:471
  40.6 0.9 %close.2.refs_5_ = f32[3,16,8,512]{3,2,1,0:T(8,128)} custom-call(f32[2,16,8,512]{3,2,1,0:T(8,128)S(1)} %get-tuple-element.35.s_ref, f32[50,512]{1,0:T(8,128)S(1)} %get-tuple-element.23.row_ref, f32[2,2,8,512]{3,2,1,0:T(8,128)S(1)} %get-tuple-element.37.refs_0_, f32[2,2,8,512]{3,2,1,0:T(8,128)S(1)} %collective-permute-done.15.refs_1_, ...), custom_call_target="tpu_custom_call" | custom-call | tf_op jit(solution)/shard_map/close/pallas_call | solution.py:535
  41.5 0.8 %close.3 = f32[3,16,8,512]{3,2,1,0:T(8,128)} custom-call(f32[1,16,8,512]{3,2,1,0:T(8,128)S(1)} %get-tuple-element.31.s_ref, f32[50,512]{1,0:T(8,128)S(1)} %get-tuple-element.23.row_ref, f32[2,1,8,512]{3,2,1,0:T(8,128)S(1)} %get-tuple-element.33.refs_0_, f32[2,1,8,512]{3,2,1,0:T(8,128)S(1)} %collective-permute-done.9.refs_1_, ...), custom_call_target="tpu_custom_call", output_to_operand_aliasing={{}: (7, {})} | custom-call | tf_op jit(solution)/shard_map/close/pallas_call | solution.py:535
  (33 shorter events, 2.5 us)
Async XLA Ops:
  1.9 16.4 %copy-start.1 = (f32[21]{0:T(128)S(1)}, f32[21]{0:T(128)}, u32[]{:S(2)}) copy-start(f32[21]{0:T(128)} %stencil_ref.1) | copy-start | bytes 256
  1.9 17.2 %copy-start = (f32[512,544]{0,1:T(8,128)S(1)}, f32[512,544]{0,1:T(8,128)}, u32[]{:S(2)}) copy-start(f32[512,544]{0,1:T(8,128)} %param.5) | copy-start | bytes 3342340
  2.1 19.2 %collective-permute-start.2 = (f32[3,10,8,512]{3,2,1,0:T(8,128)S(1)}, f32[3,10,8,512]{3,2,1,0:T(8,128)S(1)}, u32[]{:S(2)}, u32[]{:S(2)}) collective-permute-start(f32[3,10,8,512]{3,2,1,0:T(8,128)S(1)} %pack_core.1), channel_id=1, source_target_pairs={{0,2},{2,0},{4,6},{6,4},{8,10},{10,8},{12,14},{14,12},{16,18},{18,... | collective-permute-start | bytes 1474568 | tf_op jit(solution)/shard_map/ppermute | solution.py:42
  2.6 19.7 %collective-permute-start.4 = (f32[2,12,8,512]{3,2,1,0:T(8,128)S(1)}, f32[2,12,8,512]{3,2,1,0:T(8,128)S(1)}, u32[]{:S(2)}, u32[]{:S(2)}) collective-permute-start(f32[2,12,8,512]{3,2,1,0:T(8,128)S(1)} %get-tuple-element.25.first_ref), channel_id=1, source_target_pairs={{0,1},{1,0},{2,3},{3,2},{4,5},{5,4},{6,7},{7,6},{8,9},{9,8},{10,11... | collective-permute-start | bytes 1179656 | tf_op jit(solution)/shard_map/ppermute | solution.py:42
  5.2 16.9 %collective-permute-start.5 = (f32[2,10,8,512]{3,2,1,0:T(8,128)S(1)}, f32[2,10,8,512]{3,2,1,0:T(8,128)S(1)}, u32[]{:S(2)}, u32[]{:S(2)}) collective-permute-start(f32[2,10,8,512]{3,2,1,0:T(8,128)S(1)} %get-tuple-element.27.first_ref), channel_id=1, source_target_pairs={{2,4},{4,2},{6,8},{8,6},{10,12},{12,10},{14,16},{16,14},{18,20},{2... | collective-permute-start | bytes 983048 | tf_op jit(solution)/shard_map/ppermute | solution.py:50
  9.5 5.9 %collective-permute-start.3 = (f32[3,4,8,128]{3,2,1,0:T(8,128)S(1)}, f32[3,4,8,128]{3,2,1,0:T(8,128)S(1)}, u32[]{:S(2)}, u32[]{:S(2)}) collective-permute-start(f32[3,4,8,128]{3,2,1,0:T(8,128)S(1)} %pack_mirror.1.first_ref), channel_id=1, source_target_pairs={{0,16},{2,18},{4,20},{6,22},{8,24},{10,26},{12,28},{14,30},{16,0},... | collective-permute-start | bytes 147464 | tf_op jit(solution)/shard_map/ppermute | solution.py:42
  9.5 15.4 %collective-permute-start = (f32[1,12,8,512]{3,2,1,0:T(8,128)S(1)}, f32[1,12,8,512]{3,2,1,0:T(8,128)S(1)}, u32[]{:S(2)}, u32[]{:S(2)}) collective-permute-start(f32[1,12,8,512]{3,2,1,0:T(8,128)S(1)} %get-tuple-element.22), channel_id=1, source_target_pairs={{0,1},{1,0},{2,3},{3,2},{4,5},{5,4},{6,7},{7,6},{8,9},{9,8},{10,11... | collective-permute-start | bytes 589832 | tf_op jit(solution)/shard_map/ppermute | solution.py:42
  15.4 9.4 %collective-permute-start.1 = (f32[1,10,8,512]{3,2,1,0:T(8,128)S(1)}, f32[1,10,8,512]{3,2,1,0:T(8,128)S(1)}, u32[]{:S(2)}, u32[]{:S(2)}) collective-permute-start(f32[1,10,8,512]{3,2,1,0:T(8,128)S(1)} %get-tuple-element.26), channel_id=1, source_target_pairs={{2,4},{4,2},{6,8},{8,6},{10,12},{12,10},{14,16},{16,14},{18,20},{2... | collective-permute-start | bytes 491528 | tf_op jit(solution)/shard_map/ppermute | solution.py:50
  22.8 4.5 %collective-permute-start.14 = (f32[2,2,8,512]{3,2,1,0:T(8,128)S(1)}, f32[2,2,8,512]{3,2,1,0:T(8,128)S(1)}, u32[]{:S(2)}, u32[]{:S(2)}) collective-permute-start(f32[2,2,8,512]{3,2,1,0:T(8,128)S(1)} %get-tuple-element.36.refs_0_), channel_id=1, source_target_pairs={{0,6},{2,4},{4,2},{6,0},{8,14},{10,12},{12,10},{14,8},{16,22},{18,... | collective-permute-start | bytes 196616 | tf_op jit(solution)/shard_map/ppermute | solution.py:42
  23.0 5.0 %collective-permute-start.13 = (f32[2,2,8,512]{3,2,1,0:T(8,128)S(1)}, f32[2,2,8,512]{3,2,1,0:T(8,128)S(1)}, u32[]{:S(2)}, u32[]{:S(2)}) collective-permute-start(f32[2,2,8,512]{3,2,1,0:T(8,128)S(1)} %get-tuple-element.36.refs_0_), channel_id=1, source_target_pairs={{0,4},{2,6},{4,0},{6,2},{8,12},{10,14},{12,8},{14,10},{16,20},{18,... | collective-permute-start | bytes 196616 | tf_op jit(solution)/shard_map/ppermute | solution.py:42
  24.0 4.0 %collective-permute-start.12 = (f32[2,2,8,512]{3,2,1,0:T(8,128)S(1)}, f32[2,2,8,512]{3,2,1,0:T(8,128)S(1)}, u32[]{:S(2)}, u32[]{:S(2)}) collective-permute-start(f32[2,2,8,512]{3,2,1,0:T(8,128)S(1)} %get-tuple-element.36.refs_0_), channel_id=1, source_target_pairs={{0,2},{2,0},{4,6},{6,4},{8,10},{10,8},{12,14},{14,12},{16,18},{18,... | collective-permute-start | bytes 196616 | tf_op jit(solution)/shard_map/ppermute | solution.py:42
  25.1 6.9 %collective-permute-start.8 = (f32[2,1,8,512]{3,2,1,0:T(8,128)S(1)}, f32[2,1,8,512]{3,2,1,0:T(8,128)S(1)}, u32[]{:S(2)}, u32[]{:S(2)}) collective-permute-start(f32[2,1,8,512]{3,2,1,0:T(8,128)S(1)} %get-tuple-element.32.refs_0_), channel_id=1, source_target_pairs={{0,6},{2,4},{4,2},{6,0},{8,14},{10,12},{12,10},{14,8},{16,22},{18,... | collective-permute-start | bytes 98312 | tf_op jit(solution)/shard_map/ppermute | solution.py:42
  28.0 9.1 %collective-permute-start.17 = (f32[2,2,8,512]{3,2,1,0:T(8,128)S(1)}, f32[2,2,8,512]{3,2,1,0:T(8,128)S(1)}, u32[]{:S(2)}, u32[]{:S(2)}) collective-permute-start(f32[2,2,8,512]{3,2,1,0:T(8,128)S(1)} %get-tuple-element.37.refs_0_), channel_id=1, source_target_pairs={{0,24},{2,26},{4,28},{6,30},{8,16},{10,18},{12,20},{14,22},{16,8},... | collective-permute-start | bytes 196616 | tf_op jit(solution)/shard_map/ppermute | solution.py:42
  30.6 3.9 %collective-permute-start.7 = (f32[2,1,8,512]{3,2,1,0:T(8,128)S(1)}, f32[2,1,8,512]{3,2,1,0:T(8,128)S(1)}, u32[]{:S(2)}, u32[]{:S(2)}) collective-permute-start(f32[2,1,8,512]{3,2,1,0:T(8,128)S(1)} %get-tuple-element.32.refs_0_), channel_id=1, source_target_pairs={{0,4},{2,6},{4,0},{6,2},{8,12},{10,14},{12,8},{14,10},{16,20},{18,... | collective-permute-start | bytes 98312 | tf_op jit(solution)/shard_map/ppermute | solution.py:42
  32.0 2.6 %collective-permute-start.6 = (f32[2,1,8,512]{3,2,1,0:T(8,128)S(1)}, f32[2,1,8,512]{3,2,1,0:T(8,128)S(1)}, u32[]{:S(2)}, u32[]{:S(2)}) collective-permute-start(f32[2,1,8,512]{3,2,1,0:T(8,128)S(1)} %get-tuple-element.32.refs_0_), channel_id=1, source_target_pairs={{0,2},{2,0},{4,6},{6,4},{8,10},{10,8},{12,14},{14,12},{16,18},{18,... | collective-permute-start | bytes 98312 | tf_op jit(solution)/shard_map/ppermute | solution.py:42
  32.0 8.6 %collective-permute-start.16 = (f32[2,2,8,512]{3,2,1,0:T(8,128)S(1)}, f32[2,2,8,512]{3,2,1,0:T(8,128)S(1)}, u32[]{:S(2)}, u32[]{:S(2)}) collective-permute-start(f32[2,2,8,512]{3,2,1,0:T(8,128)S(1)} %get-tuple-element.37.refs_0_), channel_id=1, source_target_pairs={{0,16},{2,18},{4,20},{6,22},{8,24},{10,26},{12,28},{14,30},{16,0},... | collective-permute-start | bytes 196616 | tf_op jit(solution)/shard_map/ppermute | solution.py:42
  32.0 8.6 %collective-permute-start.15 = (f32[2,2,8,512]{3,2,1,0:T(8,128)S(1)}, f32[2,2,8,512]{3,2,1,0:T(8,128)S(1)}, u32[]{:S(2)}, u32[]{:S(2)}) collective-permute-start(f32[2,2,8,512]{3,2,1,0:T(8,128)S(1)} %get-tuple-element.37.refs_0_), channel_id=1, source_target_pairs={{0,8},{2,10},{4,12},{6,14},{8,0},{10,2},{12,4},{14,6},{16,24},{18,... | collective-permute-start | bytes 196616 | tf_op jit(solution)/shard_map/ppermute | solution.py:42
  34.6 6.9 %collective-permute-start.11 = (f32[2,1,8,512]{3,2,1,0:T(8,128)S(1)}, f32[2,1,8,512]{3,2,1,0:T(8,128)S(1)}, u32[]{:S(2)}, u32[]{:S(2)}) collective-permute-start(f32[2,1,8,512]{3,2,1,0:T(8,128)S(1)} %get-tuple-element.33.refs_0_), channel_id=1, source_target_pairs={{0,24},{2,26},{4,28},{6,30},{8,16},{10,18},{12,20},{14,22},{16,8},... | collective-permute-start | bytes 98312 | tf_op jit(solution)/shard_map/ppermute | solution.py:42
  36.5 5.0 %collective-permute-start.10 = (f32[2,1,8,512]{3,2,1,0:T(8,128)S(1)}, f32[2,1,8,512]{3,2,1,0:T(8,128)S(1)}, u32[]{:S(2)}, u32[]{:S(2)}) collective-permute-start(f32[2,1,8,512]{3,2,1,0:T(8,128)S(1)} %get-tuple-element.33.refs_0_), channel_id=1, source_target_pairs={{0,16},{2,18},{4,20},{6,22},{8,24},{10,26},{12,28},{14,30},{16,0},... | collective-permute-start | bytes 98312 | tf_op jit(solution)/shard_map/ppermute | solution.py:42
  37.1 4.4 %collective-permute-start.9 = (f32[2,1,8,512]{3,2,1,0:T(8,128)S(1)}, f32[2,1,8,512]{3,2,1,0:T(8,128)S(1)}, u32[]{:S(2)}, u32[]{:S(2)}) collective-permute-start(f32[2,1,8,512]{3,2,1,0:T(8,128)S(1)} %get-tuple-element.33.refs_0_), channel_id=1, source_target_pairs={{0,8},{2,10},{4,12},{6,14},{8,0},{10,2},{12,4},{14,6},{16,24},{18,... | collective-permute-start | bytes 98312 | tf_op jit(solution)/shard_map/ppermute | solution.py:42

commit v7 on v6

--- a/solution.py
+++ b/solution.py
@@ -179,7 +179,7 @@
     return total
 
 
-def inner_kernel(tap_ref, v_ref, op_ref, n_ref, grad_ref):
+def inner_kernel(me_ref, tap_ref, v_ref, op_ref, core_ref, n_ref, grad_ref):
     comps, points, planes, radial = v_ref.shape
     reach = (tap_ref.shape[0] - 1) // 2
     rows = points * planes
@@ -209,18 +209,23 @@
                     n = n + a * b_inv
                 n_ref[c, t, :, lanes] = n
 
-
-def inner_terms(taps, v, op):
+    even = me_ref[0] % 2 == 0
+    add = functools.partial(add_side, tap_ref, v_ref, core_ref, n_ref, n_ref, piece=range(comps))
+    pl.when(even)(lambda: add(before=False))
+    pl.when(jnp.logical_not(even))(lambda: add(before=True))
+
+
+def inner_terms(me, taps, v, op, core):
     return pl.pallas_call(
         inner_kernel,
         name="inner_terms",
         out_shape=held(*v.shape),
-        in_specs=[VMEM, VMEM, VMEM],
+        in_specs=[SMEM] + [VMEM] * 4,
         out_specs=VMEM,
         scratch_shapes=[pltpu.VMEM((v.size // v.shape[3], v.shape[3]), jnp.float32)],
         compiler_params=params(v.size * 4, 6),
         cost_estimate=pl.CostEstimate(flops=6 * v.size * v.shape[3], bytes_accessed=16 * v.size, transcendentals=0),
-    )(taps, v, op)
+    )(me, taps, v, op, core)
 
 
 def add_side(tap_ref, v_ref, side_ref, n_in_ref, n_ref, before, piece):
@@ -245,7 +250,7 @@
                 n_ref[i, t, :, lanes] = n_in_ref[c, t, :, lanes] + v_ref[1, t, :, lanes] * inv_r * around
 
 
-def early_kernel(me_ref, tap_ref, v_ref, op_ref, core_ref, mirror_ref, n_in_ref, n_ref, grad_ref):
+def mirror_kernel(v_ref, op_ref, mirror_ref, n_in_ref, n_ref, grad_ref):
     comps, points, planes, radial = v_ref.shape
     tiles = mirror_ref.shape[1]
     count = points // tiles
@@ -269,24 +274,20 @@
             n_ref[c, t] = n_in_ref[c, t] + v_ref[0, t] * grad_ref[pl.ds(start, planes)]
 
     each(points, finish)
-    even = me_ref[0] % 2 == 0
-    add = functools.partial(add_side, tap_ref, v_ref, core_ref, n_ref, n_ref, piece=range(comps))
-    pl.when(even)(lambda: add(before=False))
-    pl.when(jnp.logical_not(even))(lambda: add(before=True))
-
-
-def early_terms(me, taps, v, op, core, mirror, n):
-    return pl.pallas_call(
-        early_kernel,
-        name="early_terms",
+
+
+def mirror_terms(v, op, mirror, n):
+    return pl.pallas_call(
+        mirror_kernel,
+        name="mirror_terms",
         out_shape=held(*v.shape),
-        in_specs=[SMEM, VMEM, VMEM, VMEM, VMEM, VMEM, VMEM],
+        in_specs=[VMEM] * 4,
         out_specs=VMEM,
         scratch_shapes=[pltpu.VMEM((v.size // v.shape[3], v.shape[3]), jnp.float32)],
-        input_output_aliases={6: 0},
+        input_output_aliases={3: 0},
         compiler_params=params(v.size * 4, 8),
         cost_estimate=pl.CostEstimate(flops=2 * v.size * LANES, bytes_accessed=16 * v.size, transcendentals=0),
-    )(me, taps, v, op, core, mirror, n)
+    )(v, op, mirror, n)
 
 
 def late_kernel(me_ref, tap_ref, v_ref, chip_ref, n_in_ref, n_ref, *, piece):
@@ -360,8 +361,7 @@
 
 
 def stages(sectors):
-    bits = sectors.bit_length() - 1
-    return [(bit, 1 << min(2, bits - bit)) for bit in range(0, bits, 2)]
+    return [(bit, 2) for bit in range(sectors.bit_length() - 1)]
 
 
 def stage_rows(points, sectors):
@@ -558,9 +558,9 @@
     op = radial_op.T
 
     velocity, *planes_out = load(pltpu.with_memory_space_constraint(velocity, pltpu.HBM))
-    chip_out = pack_side(me, velocity, planes_out[0], reach, False, PIECES)
+    (core_out,) = pack_side(me, velocity, planes_out[0], reach, True, (tuple(range(comps)),))
+    chip_out = pack_side(me, velocity, core_out, reach, False, PIECES)
     mirror_out = pack_mirror(velocity, chip_out[0], width)
-    (core_out,) = pack_side(me, velocity, mirror_out, reach, True, (tuple(range(comps)),))
     planes_in, chip_in = [], []
     for k in range(len(PIECES)):
         planes_in.append(swap(planes_out[k], "gz", 1))
@@ -569,8 +569,8 @@
     core_in = swap(core_out, "theta", 1)
     rows, taps = table(me, viscous_factor, azimuth_stencil, points, sectors, planes, radial)
     firsts, _ = stage_rows(points, sectors)
-    n = inner_terms(taps, velocity, op)
-    n = early_terms(me, taps, velocity, op, core_in, mirror_in, n)
+    n = inner_terms(me, taps, velocity, op, core_in)
+    n = mirror_terms(velocity, op, mirror_in, n)
     nonlinear, solved, parts = (), (), []
     for k, piece in enumerate(PIECES):
         part = late_terms(me, taps, velocity, chip_in[k], n, piece)

time: 42.4 us -> 41.1 us (0.969)
  starting transfers between devices: 22.4 us -> 19.6 us
  waiting for transfers between devices: 8.99 us -> 10.6 us
    ppermute x2, starting transfers between devices: 6.58 us -> 4.37 us  [swap_across(): return lax.ppermute(block, axis, route)]
    ppermute x16 -> x12, waiting for transfers between devices: 8.99 us -> 10.6 us  [swap(): return lax.ppermute(block, axis, [(i, i ^ bit) for i in range(size)])]
    ppermute x16 -> x12, starting transfers between devices: 15.9 us -> 15.2 us  [swap(): return lax.ppermute(block, axis, [(i, i ^ bit) for i in range(size)])]
  transfers between devices with their start and end apart: 18 -> 14, of which waited for: 4 -> 5; matrix products, arithmetic and copies ran while one was open for 0% -> 0% of each run, Pallas kernels for 17% -> 18%
where the time goes in v7:
time: 41.1 us; the launch traced here: 41 us
  starting transfers between devices  19.6 us (48%)
  waiting for transfers between devices  10.6 us (26%)
  Pallas kernels  9.23 us (22%)
  between operations  1.52 us (4%)
    ppermute x12, starting transfers between devices, swap(): return lax.ppermute(block, axis, [(i, i ^ bit) for i in range(size)])  15.2 us
    ppermute x12, waiting for transfers between devices, swap(): return lax.ppermute(block, axis, [(i, i ^ bit) for i in range(size)])  10.6 us
    ppermute x2, starting transfers between devices, swap_across(): return lax.ppermute(block, axis, route)  4.37 us
    pallas_call x1, Pallas kernels, inner_terms(): pl.pallas_call(inner_kernel, name='inner_terms', out_shape=held(*v.shape)...  2.46 us
    pallas_call x2, Pallas kernels, close(): pl.pallas_call(functools.partial(close_kernel, first=first, group=len(blo...  1.62 us
    pallas_call x2, Pallas kernels, sweep(): pl.pallas_call(functools.partial(sweep_kernel, piece=piece), name='sweep'...  1.52 us
    pallas_call x1, Pallas kernels, load(): pl.pallas_call(load_kernel, name='load', out_shape=(held(*v.shape), *sent...  1.17 us
  transfers between devices with their start and end apart: 14, of which 5 were waited for; matrix products, arithmetic and copies ran while one was open for 0% of the time, Pallas kernels for 18%

profile of v7, /device:TPU:0, one launch (start us, length us, event | category | flops | bytes accessed | tf_op | source)
XLA Modules:
  0.0 41.0 jit_solution(12190225600224178705)
XLA Ops:
  0.6 1.2 %load.1 = (f32[3,16,8,512]{3,2,1,0:T(8,128)S(1)}, f32[2,12,8,512]{3,2,1,0:T(8,128)S(1)}, f32[1,12,8,512]{3,2,1,0:T(8,128)S(1)}) custom-call(f32[3,16,8,512]{3,2,1,0:T(8,128)} %hbm_ref.1), custom_call_target="tpu_custom_call" | custom-call | tf_op jit(solution)/shard_map/load/pallas_call | solution.py:92
  1.9 0.5 %collective-permute-start.3 = (f32[3,10,8,512]{3,2,1,0:T(8,128)S(1)}, f32[3,10,8,512]{3,2,1,0:T(8,128)S(1)}, u32[]{:S(2)}, u32[]{:S(2)}) collective-permute-start(f32[3,10,8,512]{3,2,1,0:T(8,128)S(1)} %pack_core.1.first_ref), channel_id=1, source_target_pairs={{0,2},{2,0},{4,6},{6,4},{8,10},{10,8},{12,14},{14,12},{16,18},{18,... | collective-permute-start | bytes 1474568 | tf_op jit(solution)/shard_map/ppermute | solution.py:42
  2.4 2.6 %collective-permute-start.4 = (f32[2,12,8,512]{3,2,1,0:T(8,128)S(1)}, f32[2,12,8,512]{3,2,1,0:T(8,128)S(1)}, u32[]{:S(2)}, u32[]{:S(2)}) collective-permute-start(f32[2,12,8,512]{3,2,1,0:T(8,128)S(1)} %get-tuple-element.33.first_ref), channel_id=1, source_target_pairs={{0,1},{1,0},{2,3},{3,2},{4,5},{5,4},{6,7},{7,6},{8,9},{9,8},{10,11... | collective-permute-start | bytes 1179656 | tf_op jit(solution)/shard_map/ppermute | solution.py:42
  5.0 4.4 %collective-permute-start.5 = (f32[2,10,8,512]{3,2,1,0:T(8,128)S(1)}, f32[2,10,8,512]{3,2,1,0:T(8,128)S(1)}, u32[]{:S(2)}, u32[]{:S(2)}) collective-permute-start(f32[2,10,8,512]{3,2,1,0:T(8,128)S(1)} %get-tuple-element.35.first_ref), channel_id=1, source_target_pairs={{2,4},{4,2},{6,8},{8,6},{10,12},{12,10},{14,16},{16,14},{18,20},{2... | collective-permute-start | bytes 983048 | tf_op jit(solution)/shard_map/ppermute | solution.py:50
  9.4 0.5 %collective-permute-start = (f32[1,12,8,512]{3,2,1,0:T(8,128)S(1)}, f32[1,12,8,512]{3,2,1,0:T(8,128)S(1)}, u32[]{:S(2)}, u32[]{:S(2)}) collective-permute-start(f32[1,12,8,512]{3,2,1,0:T(8,128)S(1)} %get-tuple-element.30), channel_id=1, source_target_pairs={{0,1},{1,0},{2,3},{3,2},{4,5},{5,4},{6,7},{7,6},{8,9},{9,8},{10,11... | collective-permute-start | bytes 589832 | tf_op jit(solution)/shard_map/ppermute | solution.py:42
  10.6 0.7 %table.1 = (f32[50,512]{1,0:T(8,128)S(1)}, f32[21,8,128]{2,1,0:T(8,128)S(1)}) custom-call(s32[1]{0:T(128)} %bitcast.me_ref, f32[1]{0:T(128)S(6)} %copy.16.factor_ref, f32[21]{0:T(128)S(1)} %copy-done.1), custom_call_target="tpu_custom_call" | custom-call | flops 512000 | bytes 204800 | tf_op jit(solution)/shard_map/table/pallas_call | solution.py:430
  11.4 0.7 %collective-permute-start.2 = (f32[3,4,8,128]{3,2,1,0:T(8,128)S(1)}, f32[3,4,8,128]{3,2,1,0:T(8,128)S(1)}, u32[]{:S(2)}, u32[]{:S(2)}) collective-permute-start(f32[3,4,8,128]{3,2,1,0:T(8,128)S(1)} %pack_mirror.1), channel_id=1, source_target_pairs={{0,16},{2,18},{4,20},{6,22},{8,24},{10,26},{12,28},{14,30},{16,0},... | collective-permute-start | bytes 147464 | tf_op jit(solution)/shard_map/ppermute | solution.py:42
  12.1 2.5 %inner_terms.1.n_in_ref = f32[3,16,8,512]{3,2,1,0:T(8,128)S(1)} custom-call(s32[1]{0:T(128)} %bitcast.me_ref, f32[21,8,128]{2,1,0:T(8,128)S(1)} %get-tuple-element.32.tap_ref, f32[3,16,8,512]{3,2,1,0:T(8,128)S(1)} %get-tuple-element.29.v_ref, f32[544,512]{1,0:T(8,128)S(1)} %bitcast.2, f32[3,10,8,512]{3,2,1,0:T(8,128)S(1)} %collective-permute-done.3.core_ref), custom_call_target="tpu_custom_call" | custom-call | flops 603979776 | bytes 3145728 | tf_op jit(solution)/shard_map/inner_terms/pallas_call | solution.py:219
  14.6 2.7 %collective-permute-done.2.mirror_ref = f32[3,4,8,128]{3,2,1,0:T(8,128)S(1)} collective-permute-done((f32[3,4,8,128]{3,2,1,0:T(8,128)S(1)}, f32[3,4,8,128]{3,2,1,0:T(8,128)S(1)}, u32[]{:S(2)}, u32[]{:S(2)}) %collective-permute-start.2) | collective-permute-done | bytes 49184 | tf_op jit(solution)/shard_map/ppermute | solution.py:42
  17.3 0.5 %mirror_terms.1.n_in_ref = f32[3,16,8,512]{3,2,1,0:T(8,128)S(1)} custom-call(f32[3,16,8,512]{3,2,1,0:T(8,128)S(1)} %get-tuple-element.29.v_ref, f32[544,512]{1,0:T(8,128)S(1)} %bitcast.3, f32[3,4,8,128]{3,2,1,0:T(8,128)S(1)} %collective-permute-done.2.mirror_ref, f32[3,16,8,512]{3,2,1,0:T(8,128)S(1)} %inner_terms.1.n_in_ref), custom_call_target="tpu_custom_call", output_to_operand_aliasing={{}: (3, {})} | custom-call | flops 50331648 | bytes 3145728 | tf_op jit(solution)/shard_map/mirror_terms/pallas_call | solution.py:280
  18.0 0.5 %planes_terms.3 = (f32[2,16,8,512]{3,2,1,0:T(8,128)S(1)}, f32[2,2,8,512]{3,2,1,0:T(8,128)S(1)}) custom-call(f32[3,16,8,512]{3,2,1,0:T(8,128)S(1)} %get-tuple-element.29.v_ref, f32[2,12,8,512]{3,2,1,0:T(8,128)S(1)} %collective-permute-done.4.y_ref, f32[50,512]{1,0:T(8,128)S(1)} %get-tuple-element.31.row_ref, ...), custom_call_target="tpu_custom_call", output_to_operand_aliasing={{0}: (3, {})} | custom-call | flops 3932160 | bytes 3145728 | tf_op jit(solution)/shard_map/planes_terms/pallas_call | solution.py:350
  18.6 1.2 %collective-permute-done.10.refs_1_ = f32[2,2,8,512]{3,2,1,0:T(8,128)S(1)} collective-permute-done((f32[2,2,8,512]{3,2,1,0:T(8,128)S(1)}, f32[2,2,8,512]{3,2,1,0:T(8,128)S(1)}, u32[]{:S(2)}, u32[]{:S(2)}) %collective-permute-start.10) | collective-permute-done | bytes 65568 | tf_op jit(solution)/shard_map/ppermute | solution.py:42
  19.8 1.4 %collective-permute-start.11 = (f32[2,2,8,512]{3,2,1,0:T(8,128)S(1)}, f32[2,2,8,512]{3,2,1,0:T(8,128)S(1)}, u32[]{:S(2)}, u32[]{:S(2)}) collective-permute-start(f32[2,2,8,512]{3,2,1,0:T(8,128)S(1)} %get-tuple-element.49.refs_0_), channel_id=1, source_target_pairs={{0,4},{2,6},{4,0},{6,2},{8,12},{10,14},{12,8},{14,10},{16,20},{18,... | collective-permute-start | bytes 196616 | tf_op jit(solution)/shard_map/ppermute | solution.py:42
  21.7 2.5 %collective-permute-done.11.refs_1_ = f32[2,2,8,512]{3,2,1,0:T(8,128)S(1)} collective-permute-done((f32[2,2,8,512]{3,2,1,0:T(8,128)S(1)}, f32[2,2,8,512]{3,2,1,0:T(8,128)S(1)}, u32[]{:S(2)}, u32[]{:S(2)}) %collective-permute-start.11) | collective-permute-done | bytes 65568 | tf_op jit(solution)/shard_map/ppermute | solution.py:42
  24.2 2.1 %collective-permute-start.12 = (f32[2,2,8,512]{3,2,1,0:T(8,128)S(1)}, f32[2,2,8,512]{3,2,1,0:T(8,128)S(1)}, u32[]{:S(2)}, u32[]{:S(2)}) collective-permute-start(f32[2,2,8,512]{3,2,1,0:T(8,128)S(1)} %get-tuple-element.51.refs_0_), channel_id=1, source_target_pairs={{0,8},{2,10},{4,12},{6,14},{8,0},{10,2},{12,4},{14,6},{16,24},{18,... | collective-permute-start | bytes 196616 | tf_op jit(solution)/shard_map/ppermute | solution.py:42
  26.3 0.2 collective-permute-start.7
  26.6 3.7 %collective-permute-done.7.refs_1_ = f32[2,1,8,512]{3,2,1,0:T(8,128)S(1)} collective-permute-done((f32[2,1,8,512]{3,2,1,0:T(8,128)S(1)}, f32[2,1,8,512]{3,2,1,0:T(8,128)S(1)}, u32[]{:S(2)}, u32[]{:S(2)}) %collective-permute-start.7) | collective-permute-done | bytes 32800 | tf_op jit(solution)/shard_map/ppermute | solution.py:42
  30.4 3.4 %collective-permute-start.13 = (f32[2,2,8,512]{3,2,1,0:T(8,128)S(1)}, f32[2,2,8,512]{3,2,1,0:T(8,128)S(1)}, u32[]{:S(2)}, u32[]{:S(2)}) collective-permute-start(f32[2,2,8,512]{3,2,1,0:T(8,128)S(1)} %get-tuple-element.53.refs_0_), channel_id=1, source_target_pairs={{0,16},{2,18},{4,20},{6,22},{8,24},{10,26},{12,28},{14,30},{16,0},... | collective-permute-start | bytes 196616 | tf_op jit(solution)/shard_map/ppermute | solution.py:42
  33.9 0.4 %collective-permute-done.8.refs_1_ = f32[2,1,8,512]{3,2,1,0:T(8,128)S(1)} collective-permute-done((f32[2,1,8,512]{3,2,1,0:T(8,128)S(1)}, f32[2,1,8,512]{3,2,1,0:T(8,128)S(1)}, u32[]{:S(2)}, u32[]{:S(2)}) %collective-permute-start.8) | collective-permute-done | bytes 32800 | tf_op jit(solution)/shard_map/ppermute | solution.py:42
  34.3 3.4 %collective-permute-start.9 = (f32[2,1,8,512]{3,2,1,0:T(8,128)S(1)}, f32[2,1,8,512]{3,2,1,0:T(8,128)S(1)}, u32[]{:S(2)}, u32[]{:S(2)}) collective-permute-start(f32[2,1,8,512]{3,2,1,0:T(8,128)S(1)} %get-tuple-element.45.refs_0_), channel_id=1, source_target_pairs={{0,16},{2,18},{4,20},{6,22},{8,24},{10,26},{12,28},{14,30},{16,0},... | collective-permute-start | bytes 98312 | tf_op jit(solution)/shard_map/ppermute | solution.py:42
  37.8 0.8 %sweep.2 = (f32[2,16,8,512]{3,2,1,0:T(8,128)S(1)}, f32[3,16,8,512]{3,2,1,0:T(8,128)}) custom-call(f32[3,16,8,512]{3,2,1,0:T(8,128)S(1)} %get-tuple-element.29.v_ref, f32[2,16,8,512]{3,2,1,0:T(8,128)S(1)} %get-tuple-element.37.n_ref, f32[50,512]{1,0:T(8,128)S(1)} %get-tuple-element.31.row_ref), custom_call_target="tpu_custom_call" | custom-call | flops 1966080 | bytes 2359296 | tf_op jit(solution)/shard_map/sweep/pallas_call | solution.py:471
  38.6 0.7 %sweep.3 = (f32[1,16,8,512]{3,2,1,0:T(8,128)S(1)}, f32[3,16,8,512]{3,2,1,0:T(8,128)}) custom-call(f32[3,16,8,512]{3,2,1,0:T(8,128)S(1)} %get-tuple-element.29.v_ref, f32[1,16,8,512]{3,2,1,0:T(8,128)S(1)} %get-tuple-element.36.n_ref, f32[50,512]{1,0:T(8,128)S(1)} %get-tuple-element.31.row_ref, ...), custom_call_target="tpu_custom_call", output_to_operand_aliasing={{1}: (3, {})} | custom-call | flops 1966080 | bytes 2359296 | tf_op jit(solution)/shard_map/sweep/pallas_call | solution.py:471
  39.3 0.9 %close.2.refs_3_ = f32[3,16,8,512]{3,2,1,0:T(8,128)} custom-call(f32[2,16,8,512]{3,2,1,0:T(8,128)S(1)} %get-tuple-element.47.s_ref, f32[50,512]{1,0:T(8,128)S(1)} %get-tuple-element.31.row_ref, f32[2,2,8,512]{3,2,1,0:T(8,128)S(1)} %get-tuple-element.53.refs_0_, f32[2,2,8,512]{3,2,1,0:T(8,128)S(1)} %collective-permute-done.13.refs_1_, ...), custom_call_target="tpu_custom_call" | custom-call | tf_op jit(solution)/shard_map/close/pallas_call | solution.py:535
  40.2 0.8 %close.3 = f32[3,16,8,512]{3,2,1,0:T(8,128)} custom-call(f32[1,16,8,512]{3,2,1,0:T(8,128)S(1)} %get-tuple-element.39.s_ref, f32[50,512]{1,0:T(8,128)S(1)} %get-tuple-element.31.row_ref, f32[2,1,8,512]{3,2,1,0:T(8,128)S(1)} %get-tuple-element.45.refs_0_, f32[2,1,8,512]{3,2,1,0:T(8,128)S(1)} %collective-permute-done.9.refs_1_, ...), custom_call_target="tpu_custom_call", output_to_operand_aliasing={{}: (5, {})} | custom-call | tf_op jit(solution)/shard_map/close/pallas_call | solution.py:535
  (29 shorter events, 1.1 us)
Async XLA Ops:
  1.8 8.8 %copy-start.1 = (f32[21]{0:T(128)S(1)}, f32[21]{0:T(128)}, u32[]{:S(2)}) copy-start(f32[21]{0:T(128)} %stencil_ref.1) | copy-start | bytes 256
  1.9 10.2 %copy-start = (f32[512,544]{0,1:T(8,128)S(1)}, f32[512,544]{0,1:T(8,128)}, u32[]{:S(2)}) copy-start(f32[512,544]{0,1:T(8,128)} %param.5) | copy-start | bytes 3342340
  1.9 9.5 %collective-permute-start.3 = (f32[3,10,8,512]{3,2,1,0:T(8,128)S(1)}, f32[3,10,8,512]{3,2,1,0:T(8,128)S(1)}, u32[]{:S(2)}, u32[]{:S(2)}) collective-permute-start(f32[3,10,8,512]{3,2,1,0:T(8,128)S(1)} %pack_core.1.first_ref), channel_id=1, source_target_pairs={{0,2},{2,0},{4,6},{6,4},{8,10},{10,8},{12,14},{14,12},{16,18},{18,... | collective-permute-start | bytes 1474568 | tf_op jit(solution)/shard_map/ppermute | solution.py:42
  2.4 15.6 %collective-permute-start.4 = (f32[2,12,8,512]{3,2,1,0:T(8,128)S(1)}, f32[2,12,8,512]{3,2,1,0:T(8,128)S(1)}, u32[]{:S(2)}, u32[]{:S(2)}) collective-permute-start(f32[2,12,8,512]{3,2,1,0:T(8,128)S(1)} %get-tuple-element.33.first_ref), channel_id=1, source_target_pairs={{0,1},{1,0},{2,3},{3,2},{4,5},{5,4},{6,7},{7,6},{8,9},{9,8},{10,11... | collective-permute-start | bytes 1179656 | tf_op jit(solution)/shard_map/ppermute | solution.py:42
  5.0 12.8 %collective-permute-start.5 = (f32[2,10,8,512]{3,2,1,0:T(8,128)S(1)}, f32[2,10,8,512]{3,2,1,0:T(8,128)S(1)}, u32[]{:S(2)}, u32[]{:S(2)}) collective-permute-start(f32[2,10,8,512]{3,2,1,0:T(8,128)S(1)} %get-tuple-element.35.first_ref), channel_id=1, source_target_pairs={{2,4},{4,2},{6,8},{8,6},{10,12},{12,10},{14,16},{16,14},{18,20},{2... | collective-permute-start | bytes 983048 | tf_op jit(solution)/shard_map/ppermute | solution.py:50
  9.4 12.0 %collective-permute-start = (f32[1,12,8,512]{3,2,1,0:T(8,128)S(1)}, f32[1,12,8,512]{3,2,1,0:T(8,128)S(1)}, u32[]{:S(2)}, u32[]{:S(2)}) collective-permute-start(f32[1,12,8,512]{3,2,1,0:T(8,128)S(1)} %get-tuple-element.30), channel_id=1, source_target_pairs={{0,1},{1,0},{2,3},{3,2},{4,5},{5,4},{6,7},{7,6},{8,9},{9,8},{10,11... | collective-permute-start | bytes 589832 | tf_op jit(solution)/shard_map/ppermute | solution.py:42
  9.9 11.4 %collective-permute-start.1 = (f32[1,10,8,512]{3,2,1,0:T(8,128)S(1)}, f32[1,10,8,512]{3,2,1,0:T(8,128)S(1)}, u32[]{:S(2)}, u32[]{:S(2)}) collective-permute-start(f32[1,10,8,512]{3,2,1,0:T(8,128)S(1)} %get-tuple-element.34), channel_id=1, source_target_pairs={{2,4},{4,2},{6,8},{8,6},{10,12},{12,10},{14,16},{16,14},{18,20},{2... | collective-permute-start | bytes 491528 | tf_op jit(solution)/shard_map/ppermute | solution.py:50
  11.4 5.9 %collective-permute-start.2 = (f32[3,4,8,128]{3,2,1,0:T(8,128)S(1)}, f32[3,4,8,128]{3,2,1,0:T(8,128)S(1)}, u32[]{:S(2)}, u32[]{:S(2)}) collective-permute-start(f32[3,4,8,128]{3,2,1,0:T(8,128)S(1)} %pack_mirror.1), channel_id=1, source_target_pairs={{0,16},{2,18},{4,20},{6,22},{8,24},{10,26},{12,28},{14,30},{16,0},... | collective-permute-start | bytes 147464 | tf_op jit(solution)/shard_map/ppermute | solution.py:42
  18.5 1.3 %collective-permute-start.10 = (f32[2,2,8,512]{3,2,1,0:T(8,128)S(1)}, f32[2,2,8,512]{3,2,1,0:T(8,128)S(1)}, u32[]{:S(2)}, u32[]{:S(2)}) collective-permute-start(f32[2,2,8,512]{3,2,1,0:T(8,128)S(1)} %get-tuple-element.48.refs_0_), channel_id=1, source_target_pairs={{0,2},{2,0},{4,6},{6,4},{8,10},{10,8},{12,14},{14,12},{16,18},{18,... | collective-permute-start | bytes 196616 | tf_op jit(solution)/shard_map/ppermute | solution.py:42
  19.8 4.3 %collective-permute-start.11 = (f32[2,2,8,512]{3,2,1,0:T(8,128)S(1)}, f32[2,2,8,512]{3,2,1,0:T(8,128)S(1)}, u32[]{:S(2)}, u32[]{:S(2)}) collective-permute-start(f32[2,2,8,512]{3,2,1,0:T(8,128)S(1)} %get-tuple-element.49.refs_0_), channel_id=1, source_target_pairs={{0,4},{2,6},{4,0},{6,2},{8,12},{10,14},{12,8},{14,10},{16,20},{18,... | collective-permute-start | bytes 196616 | tf_op jit(solution)/shard_map/ppermute | solution.py:42
  21.6 4.7 %collective-permute-start.6 = (f32[2,1,8,512]{3,2,1,0:T(8,128)S(1)}, f32[2,1,8,512]{3,2,1,0:T(8,128)S(1)}, u32[]{:S(2)}, u32[]{:S(2)}) collective-permute-start(f32[2,1,8,512]{3,2,1,0:T(8,128)S(1)} %get-tuple-element.40.refs_0_), channel_id=1, source_target_pairs={{0,2},{2,0},{4,6},{6,4},{8,10},{10,8},{12,14},{14,12},{16,18},{18,... | collective-permute-start | bytes 98312 | tf_op jit(solution)/shard_map/ppermute | solution.py:42
  24.2 6.2 %collective-permute-start.12 = (f32[2,2,8,512]{3,2,1,0:T(8,128)S(1)}, f32[2,2,8,512]{3,2,1,0:T(8,128)S(1)}, u32[]{:S(2)}, u32[]{:S(2)}) collective-permute-start(f32[2,2,8,512]{3,2,1,0:T(8,128)S(1)} %get-tuple-element.51.refs_0_), channel_id=1, source_target_pairs={{0,8},{2,10},{4,12},{6,14},{8,0},{10,2},{12,4},{14,6},{16,24},{18,... | collective-permute-start | bytes 196616 | tf_op jit(solution)/shard_map/ppermute | solution.py:42
  26.3 4.0 %collective-permute-start.7 = (f32[2,1,8,512]{3,2,1,0:T(8,128)S(1)}, f32[2,1,8,512]{3,2,1,0:T(8,128)S(1)}, u32[]{:S(2)}, u32[]{:S(2)}) collective-permute-start(f32[2,1,8,512]{3,2,1,0:T(8,128)S(1)} %get-tuple-element.41.refs_0_), channel_id=1, source_target_pairs={{0,4},{2,6},{4,0},{6,2},{8,12},{10,14},{12,8},{14,10},{16,20},{18,... | collective-permute-start | bytes 98312 | tf_op jit(solution)/shard_map/ppermute | solution.py:42
  30.3 4.0 %collective-permute-start.8 = (f32[2,1,8,512]{3,2,1,0:T(8,128)S(1)}, f32[2,1,8,512]{3,2,1,0:T(8,128)S(1)}, u32[]{:S(2)}, u32[]{:S(2)}) collective-permute-start(f32[2,1,8,512]{3,2,1,0:T(8,128)S(1)} %get-tuple-element.43.refs_0_), channel_id=1, source_target_pairs={{0,8},{2,10},{4,12},{6,14},{8,0},{10,2},{12,4},{14,6},{16,24},{18,... | collective-permute-start | bytes 98312 | tf_op jit(solution)/shard_map/ppermute | solution.py:42
  30.4 8.9 %collective-permute-start.13 = (f32[2,2,8,512]{3,2,1,0:T(8,128)S(1)}, f32[2,2,8,512]{3,2,1,0:T(8,128)S(1)}, u32[]{:S(2)}, u32[]{:S(2)}) collective-permute-start(f32[2,2,8,512]{3,2,1,0:T(8,128)S(1)} %get-tuple-element.53.refs_0_), channel_id=1, source_target_pairs={{0,16},{2,18},{4,20},{6,22},{8,24},{10,26},{12,28},{14,30},{16,0},... | collective-permute-start | bytes 196616 | tf_op jit(solution)/shard_map/ppermute | solution.py:42
  34.3 5.9 %collective-permute-start.9 = (f32[2,1,8,512]{3,2,1,0:T(8,128)S(1)}, f32[2,1,8,512]{3,2,1,0:T(8,128)S(1)}, u32[]{:S(2)}, u32[]{:S(2)}) collective-permute-start(f32[2,1,8,512]{3,2,1,0:T(8,128)S(1)} %get-tuple-element.45.refs_0_), channel_id=1, source_target_pairs={{0,16},{2,18},{4,20},{6,22},{8,24},{10,26},{12,28},{14,30},{16,0},... | collective-permute-start | bytes 98312 | tf_op jit(solution)/shard_map/ppermute | solution.py:42

commit v8 on v5

--- a/solution.py
+++ b/solution.py
@@ -13,6 +13,7 @@
 MIRROR_SIGNS = (-1.0, -1.0, 1.0)
 LANES = 128
 UNROLL = 16
+INNER = 10 << 29
 
 VMEM = pl.BlockSpec(memory_space=pltpu.VMEM)
 SMEM = pl.BlockSpec(memory_space=pltpu.SMEM)
@@ -165,7 +166,8 @@
 
 
 def axial_part(tile, weights):
-    planes = tile.shape[0]
+    planes, width = tile.shape
+    weights = [(shift, jnp.concatenate([weight] * (width // LANES), axis=1)) for shift, weight in weights]
     total = None
     for shift, weight in weights:
         term = weight * pltpu.roll(tile, planes - shift, 0)
@@ -173,7 +175,46 @@
     return total
 
 
-def inner_kernel(tap_ref, v_ref, op_ref, n_ref, grad_ref):
+def mirror_kernel(v_ref, op_ref, mirror_ref, n_ref, grad_ref):
+    comps, points, planes, radial = v_ref.shape
+    tiles = mirror_ref.shape[1]
+    count = points // tiles
+    width = LANES // count
+    rows = tiles * planes
+    right = split(jnp.concatenate([op_ref[radial:]] * count, axis=0))
+    lane = lax.broadcasted_iota(jnp.int32, (rows, LANES), 1)
+    for c in range(comps):
+        high, low = split(MIRROR_SIGNS[c] * mirror_ref[c].reshape(rows, LANES))
+        zero = jnp.zeros_like(high)
+        parts = [
+            [jnp.where((lane >= q * width) & (lane < (q + 1) * width), x, zero) for q in range(count)]
+            for x in (high, low)
+        ]
+        left = [jnp.concatenate(x, axis=0) for x in parts]
+        grad_ref[c * points * planes : (c + 1) * points * planes] = product(left, right)
+
+    def finish(t):
+        for c in range(comps):
+            start = pl.multiple_of((c * points + t) * planes, planes)
+            n_ref[c, t] = v_ref[0, t] * grad_ref[pl.ds(start, planes)]
+
+    each(points, finish)
+
+
+def mirror_terms(v, op, mirror):
+    return pl.pallas_call(
+        mirror_kernel,
+        name="mirror_terms",
+        out_shape=held(*v.shape),
+        in_specs=[VMEM, VMEM, VMEM],
+        out_specs=VMEM,
+        scratch_shapes=[pltpu.VMEM((v.size // v.shape[3], v.shape[3]), jnp.float32)],
+        compiler_params=params(v.size * 4, 8),
+        cost_estimate=pl.CostEstimate(flops=2 * v.size * LANES, bytes_accessed=16 * v.size, transcendentals=0),
+    )(v, op, mirror)
+
+
+def inner_kernel(tap_ref, v_ref, op_ref, n_in_ref, n_ref, grad_ref):
     comps, points, planes, radial = v_ref.shape
     reach = (tap_ref.shape[0] - 1) // 2
     rows = points * planes
@@ -196,7 +237,7 @@
                     around = term if around is None else around + term
                 start = c * rows + t * planes
                 n = a * grad_ref[start : start + planes, lanes] + b_inv * around
-                n = n + e * axial_part(v_ref[c, t, :, lanes], weights)
+                n = n + e * axial_part(v_ref[c, t, :, lanes], weights) + n_in_ref[c, t, :, lanes]
                 if c == 0:
                     n = n - b_inv * b
                 elif c == 1:
@@ -204,17 +245,18 @@
                 n_ref[c, t, :, lanes] = n
 
 
-def inner_terms(taps, v, op):
+def inner_terms(taps, v, op, n):
     return pl.pallas_call(
         inner_kernel,
         name="inner_terms",
         out_shape=held(*v.shape),
-        in_specs=[VMEM, VMEM, VMEM],
+        in_specs=[VMEM] * 4,
         out_specs=VMEM,
         scratch_shapes=[pltpu.VMEM((v.size // v.shape[3], v.shape[3]), jnp.float32)],
-        compiler_params=params(v.size * 4, 6),
-        cost_estimate=pl.CostEstimate(flops=6 * v.size * v.shape[3], bytes_accessed=16 * v.size, transcendentals=0),
-    )(taps, v, op)
+        input_output_aliases={3: 0},
+        compiler_params=params(v.size * 4, 7),
+        cost_estimate=pl.CostEstimate(flops=INNER, bytes_accessed=16 * v.size, transcendentals=0),
+    )(taps, v, op, n)
 
 
 def add_side(tap_ref, v_ref, side_ref, n_in_ref, n_ref, before):
@@ -239,48 +281,11 @@
                 n_ref[c, t, :, lanes] = n_in_ref[c, t, :, lanes] + v_ref[1, t, :, lanes] * inv_r * around
 
 
-def early_kernel(me_ref, tap_ref, v_ref, op_ref, core_ref, mirror_ref, n_in_ref, n_ref, grad_ref):
-    comps, points, planes, radial = v_ref.shape
-    tiles = mirror_ref.shape[1]
-    count = points // tiles
-    width = LANES // count
-    rows = tiles * planes
-    right = split(jnp.concatenate([op_ref[radial:]] * count, axis=0))
-    lane = lax.broadcasted_iota(jnp.int32, (rows, LANES), 1)
-    for c in range(comps):
-        high, low = split(MIRROR_SIGNS[c] * mirror_ref[c].reshape(rows, LANES))
-        zero = jnp.zeros_like(high)
-        parts = [
-            [jnp.where((lane >= q * width) & (lane < (q + 1) * width), x, zero) for q in range(count)]
-            for x in (high, low)
-        ]
-        left = [jnp.concatenate(x, axis=0) for x in parts]
-        grad_ref[c * points * planes : (c + 1) * points * planes] = product(left, right)
-
-    def finish(t):
-        for c in range(comps):
-            start = pl.multiple_of((c * points + t) * planes, planes)
-            n_ref[c, t] = n_in_ref[c, t] + v_ref[0, t] * grad_ref[pl.ds(start, planes)]
-
-    each(points, finish)
+def core_kernel(me_ref, tap_ref, v_ref, core_ref, n_in_ref, n_ref):
     even = me_ref[0] % 2 == 0
-    add = functools.partial(add_side, tap_ref, v_ref, core_ref, n_ref, n_ref)
+    add = functools.partial(add_side, tap_ref, v_ref, core_ref, n_in_ref, n_ref)
     pl.when(even)(lambda: add(False))
     pl.when(jnp.logical_not(even))(lambda: add(True))
-
-
-def early_terms(me, taps, v, op, core, mirror, n):
-    return pl.pallas_call(
-        early_kernel,
-        name="early_terms",
-        out_shape=held(*v.shape),
-        in_specs=[SMEM, VMEM, VMEM, VMEM, VMEM, VMEM, VMEM],
-        out_specs=VMEM,
-        scratch_shapes=[pltpu.VMEM((v.size // v.shape[3], v.shape[3]), jnp.float32)],
-        input_output_aliases={6: 0},
-        compiler_params=params(v.size * 4, 8),
-        cost_estimate=pl.CostEstimate(flops=2 * v.size * LANES, bytes_accessed=16 * v.size, transcendentals=0),
-    )(me, taps, v, op, core, mirror, n)
 
 
 def late_kernel(me_ref, tap_ref, v_ref, chip_ref, n_in_ref, n_ref):
@@ -290,17 +295,17 @@
     pl.when(jnp.logical_not(even))(lambda: add(False))
 
 
-def late_terms(me, taps, v, chip, n):
-    return pl.pallas_call(
-        late_kernel,
-        name="late_terms",
+def side_terms(kernel, name, me, taps, v, side, n):
+    return pl.pallas_call(
+        kernel,
+        name=name,
         out_shape=held(*v.shape),
         in_specs=[SMEM, VMEM, VMEM, VMEM, VMEM],
         out_specs=VMEM,
         input_output_aliases={4: 0},
         compiler_params=params(v.size * 4, 5),
         cost_estimate=pl.CostEstimate(flops=20 * v.size, bytes_accessed=12 * v.size, transcendentals=0),
-    )(me, taps, v, chip, n)
+    )(me, taps, v, side, n)
 
 
 def planes_kernel(me_ref, v_ref, y_ref, power_ref, n_in_ref, n_ref, keep_ref, send_ref, tile_ref, ends_ref):
@@ -316,21 +321,16 @@
             tile_ref[c, j, hi : hi + 1] = y_ref[c, 3 * j + 1, lo + 1 : hi]
             tile_ref[c, j, hi + 1 :] = y_ref[c, 3 * j + 2, lo:hi]
 
-    @pl.loop(0, radial // LANES)
-    def column(k):
-        lanes = pl.ds(pl.multiple_of(k * LANES, LANES), LANES)
-        decay = power_ref[1:2, lanes]
+    decay = power_ref[1:2]
+    ends_ref[...] = jnp.zeros_like(ends_ref)
+    for t in range(points):
         for c in range(comps):
-            low = high = None
-            for t in range(points):
-                tile = y_ref[c, t, :, lanes] if t < carriers else tile_ref[c, t - carriers, :, lanes]
-                n = n_in_ref[c, t, :, lanes] + v_ref[2, t, :, lanes] * axial_part(tile, weights)
-                n_ref[c, t, :, lanes] = n
-                right_side = v_ref[c, t, :, lanes] - STEP_WEIGHT * n
-                low = right_side if t == 0 else decay * low + right_side
-                high = right_side if t == 0 else high + power_ref[t : t + 1, lanes] * right_side
-            ends_ref[0, c, :, lanes] = low
-            ends_ref[1, c, :, lanes] = high
+            tile = y_ref[c, t] if t < carriers else tile_ref[c, t - carriers]
+            n = n_in_ref[c, t] + v_ref[2, t] * axial_part(tile, weights)
+            n_ref[c, t] = n
+            right_side = v_ref[c, t] - STEP_WEIGHT * n
+            ends_ref[0, c] = decay * ends_ref[0, c] + right_side
+            ends_ref[1, c] = ends_ref[1, c] + power_ref[t : t + 1] * right_side
 
     half = radial // 2
     core = me_ref[0] % 2
@@ -574,16 +574,17 @@
 
     velocity, planes_out = load(pltpu.with_memory_space_constraint(velocity, pltpu.HBM))
     planes_in = swap(planes_out, "gz", 1)
-    chip_out = pack_side(me, velocity, planes_out, reach, False)
+    mirror_out = pack_mirror(velocity, planes_out, width)
+    mirror_in = swap(mirror_out, "theta", sectors // 2)
+    chip_out = pack_side(me, velocity, mirror_out, reach, False)
     chip_in = swap_across(chip_out, "theta")
-    mirror_out = pack_mirror(velocity, chip_out, width)
-    mirror_in = swap(mirror_out, "theta", sectors // 2)
-    core_out = pack_side(me, velocity, mirror_out, reach, True)
+    core_out = pack_side(me, velocity, chip_out, reach, True)
     core_in = swap(core_out, "theta", 1)
     power, taps = table(me, viscous_factor, azimuth_stencil, points, sectors, planes, radial)
-    n = inner_terms(taps, velocity, op)
-    n = early_terms(me, taps, velocity, op, core_in, mirror_in, n)
-    n = late_terms(me, taps, velocity, chip_in, n)
+    n = mirror_terms(velocity, op, mirror_in)
+    n = inner_terms(taps, velocity, op, n)
+    n = side_terms(core_kernel, "core_terms", me, taps, velocity, core_in, n)
+    n = side_terms(late_kernel, "late_terms", me, taps, velocity, chip_in, n)
     n, own, send = planes_terms(me, velocity, planes_in, power, n)
     other = swap(send, "theta", 1)
     s, nonlinear = sweep(velocity, n, power)

time: 37.7 us -> 39.2 us (1.040)
  waiting for transfers between devices: 12.7 us -> 15.3 us
  starting transfers between devices: 14.8 us -> 14 us
    ppermute x1, waiting for transfers between devices: 0.01 us -> 4.79 us  [swap_across(): return lax.ppermute(block, axis, route)]
    ppermute x1, starting transfers between devices: 4.63 us -> 1.23 us  [swap_across(): return lax.ppermute(block, axis, route)]
    ppermute x8, starting transfers between devices: 10.2 us -> 12.7 us  [swap(): return lax.ppermute(block, axis, [(i, i ^ bit) for i in range(size)])]
    ppermute x8, waiting for transfers between devices: 12.7 us -> 10.5 us  [swap(): return lax.ppermute(block, axis, [(i, i ^ bit) for i in range(size)])]
    pallas_call x1, Pallas kernels: 1.13 us -> 0.72 us  [planes_terms(): pl.pallas_call(planes_kernel, name='planes_terms', out_shape=(held(*v.sha...]
    pallas_call x2 -> x3, Pallas kernels: 1.28 us -> 1.47 us  [the longest x2 1.01 us: side_terms(): pl.pallas_call(kernel, name=name, out_shape=held(*v.shape), in_specs=[SME...]
where the time goes in v8:
time: 39.2 us; the launch traced here: 39.1 us
  waiting for transfers between devices  15.3 us (39%)
  starting transfers between devices  14 us (36%)
  Pallas kernels  8.35 us (21%)
  between operations  1.45 us (4%)
    ppermute x8, starting transfers between devices, swap(): return lax.ppermute(block, axis, [(i, i ^ bit) for i in range(size)])  12.7 us
    ppermute x8, waiting for transfers between devices, swap(): return lax.ppermute(block, axis, [(i, i ^ bit) for i in range(size)])  10.5 us
    ppermute x1, waiting for transfers between devices, swap_across(): return lax.ppermute(block, axis, route)  4.79 us
    pallas_call x1, Pallas kernels, inner_terms(): pl.pallas_call(inner_kernel, name='inner_terms', out_shape=held(*v.shape)...  2.24 us
    ppermute x1, starting transfers between devices, swap_across(): return lax.ppermute(block, axis, route)  1.23 us
    pallas_call x1, Pallas kernels, load(): pl.pallas_call(load_kernel, name='load', out_shape=(held(*v.shape), held(...  1.17 us
    pallas_call x2, Pallas kernels, side_terms(): pl.pallas_call(kernel, name=name, out_shape=held(*v.shape), in_specs=[SME...  1.01 us
    pallas_call x1, Pallas kernels, close(): pl.pallas_call(close_kernel, name='close', out_shape=jax.ShapeDtypeStruct...  0.97 us
  transfers between devices with their start and end apart: 9, of which 6 were waited for; matrix products, arithmetic and copies ran while one was open for 0% of the time, Pallas kernels for 14%

profile of v8, /device:TPU:0, one launch (start us, length us, event | category | flops | bytes accessed | tf_op | source)
XLA Modules:
  0.0 39.1 jit_solution(14231518695923672005)
XLA Ops:
  0.6 1.2 %load.1 = (f32[3,16,8,512]{3,2,1,0:T(8,128)S(1)}, f32[3,12,8,512]{3,2,1,0:T(8,128)S(1)}) custom-call(f32[3,16,8,512]{3,2,1,0:T(8,128)} %hbm_ref.1), custom_call_target="tpu_custom_call" | custom-call | tf_op jit(solution)/shard_map/load/pallas_call | solution.py:89
  1.8 3.0 %collective-permute-start = (f32[3,12,8,512]{3,2,1,0:T(8,128)S(1)}, f32[3,12,8,512]{3,2,1,0:T(8,128)S(1)}, u32[]{:S(2)}, u32[]{:S(2)}) collective-permute-start(f32[3,12,8,512]{3,2,1,0:T(8,128)S(1)} %get-tuple-element.20.first_ref), channel_id=1, source_target_pairs={{0,1},{1,0},{2,3},{3,2},{4,5},{5,4},{6,7},{7,6},{8,9},{9,8},{10,11... | collective-permute-start | bytes 1769480 | tf_op jit(solution)/shard_map/ppermute | solution.py:42
  4.8 0.1 pack_mirror.1.first_ref
  4.9 2.7 %collective-permute-start.3 = (f32[3,4,8,128]{3,2,1,0:T(8,128)S(1)}, f32[3,4,8,128]{3,2,1,0:T(8,128)S(1)}, u32[]{:S(2)}, u32[]{:S(2)}) collective-permute-start(f32[3,4,8,128]{3,2,1,0:T(8,128)S(1)} %pack_mirror.1.first_ref), channel_id=1, source_target_pairs={{0,16},{2,18},{4,20},{6,22},{8,24},{10,26},{12,28},{14,30},{16,0},... | collective-permute-start | bytes 147464 | tf_op jit(solution)/shard_map/ppermute | solution.py:42
  7.7 1.2 %collective-permute-start.1 = (f32[3,10,8,512]{3,2,1,0:T(8,128)S(1)}, f32[3,10,8,512]{3,2,1,0:T(8,128)S(1)}, u32[]{:S(2)}, u32[]{:S(2)}) collective-permute-start(f32[3,10,8,512]{3,2,1,0:T(8,128)S(1)} %pack_chip.1.first_ref), channel_id=1, source_target_pairs={{2,4},{4,2},{6,8},{8,6},{10,12},{12,10},{14,16},{16,14},{18,20},{2... | collective-permute-start | bytes 1474568 | tf_op jit(solution)/shard_map/ppermute | solution.py:50
  8.9 0.5 %collective-permute-start.2 = (f32[3,10,8,512]{3,2,1,0:T(8,128)S(1)}, f32[3,10,8,512]{3,2,1,0:T(8,128)S(1)}, u32[]{:S(2)}, u32[]{:S(2)}) collective-permute-start(f32[3,10,8,512]{3,2,1,0:T(8,128)S(1)} %pack_core.1), channel_id=1, source_target_pairs={{0,2},{2,0},{4,6},{6,4},{8,10},{10,8},{12,14},{14,12},{16,18},{18,... | collective-permute-start | bytes 1474568 | tf_op jit(solution)/shard_map/ppermute | solution.py:42
  10.1 0.6 %table.1 = (f32[30,512]{1,0:T(8,128)S(1)}, f32[21,8,128]{2,1,0:T(8,128)S(1)}) custom-call(s32[1]{0:T(128)} %bitcast.me_ref, f32[1]{0:T(128)S(6)} %copy.14.factor_ref, f32[21]{0:T(128)S(1)} %copy-done.1), custom_call_target="tpu_custom_call" | custom-call | flops 512000 | bytes 204800 | tf_op jit(solution)/shard_map/table/pallas_call | solution.py:392
  10.7 0.5 %mirror_terms.1.n_in_ref = f32[3,16,8,512]{3,2,1,0:T(8,128)S(1)} custom-call(f32[3,16,8,512]{3,2,1,0:T(8,128)S(1)} %get-tuple-element.19.v_ref, f32[544,512]{1,0:T(8,128)S(1)} %bitcast.2, f32[3,4,8,128]{3,2,1,0:T(8,128)S(1)} %collective-permute-done.3.mirror_ref), custom_call_target="tpu_custom_call" | custom-call | flops 50331648 | bytes 3145728 | tf_op jit(solution)/shard_map/mirror_terms/pallas_call | solution.py:205
  11.2 2.2 %inner_terms.1.n_in_ref = f32[3,16,8,512]{3,2,1,0:T(8,128)S(1)} custom-call(f32[21,8,128]{2,1,0:T(8,128)S(1)} %get-tuple-element.22.tap_ref, f32[3,16,8,512]{3,2,1,0:T(8,128)S(1)} %get-tuple-element.19.v_ref, f32[544,512]{1,0:T(8,128)S(1)} %bitcast.3, f32[3,16,8,512]{3,2,1,0:T(8,128)S(1)} %mirror_terms.1.n_in_ref), custom_call_target="tpu_custom_call", output_to_operand_aliasing={{}: (3, {})} | custom-call | flops 5368709120 | bytes 3145728 | tf_op jit(solution)/shard_map/inner_terms/pallas_call | solution.py:249
  13.5 0.5 %core_terms.1.n_in_ref = f32[3,16,8,512]{3,2,1,0:T(8,128)S(1)} custom-call(s32[1]{0:T(128)} %bitcast.me_ref, f32[21,8,128]{2,1,0:T(8,128)S(1)} %get-tuple-element.22.tap_ref, f32[3,16,8,512]{3,2,1,0:T(8,128)S(1)} %get-tuple-element.19.v_ref, f32[3,10,8,512]{3,2,1,0:T(8,128)S(1)} %collective-permute-done.2.core_ref, ...), custom_call_target="tpu_custom_call", output_to_operand_aliasing={{}: (4, {})} | custom-call | flops 3932160 | bytes 2359296 | tf_op jit(solution)/shard_map/core_terms/pallas_call | solution.py:299
  14.0 4.8 %collective-permute-done.1.chip_ref = f32[3,10,8,512]{3,2,1,0:T(8,128)S(1)} collective-permute-done((f32[3,10,8,512]{3,2,1,0:T(8,128)S(1)}, f32[3,10,8,512]{3,2,1,0:T(8,128)S(1)}, u32[]{:S(2)}, u32[]{:S(2)}) %collective-permute-start.1) | collective-permute-done | bytes 491552 | tf_op jit(solution)/shard_map/ppermute | solution.py:50
  18.8 0.5 %late_terms.1.n_in_ref = f32[3,16,8,512]{3,2,1,0:T(8,128)S(1)} custom-call(s32[1]{0:T(128)} %bitcast.me_ref, f32[21,8,128]{2,1,0:T(8,128)S(1)} %get-tuple-element.22.tap_ref, f32[3,16,8,512]{3,2,1,0:T(8,128)S(1)} %get-tuple-element.19.v_ref, f32[3,10,8,512]{3,2,1,0:T(8,128)S(1)} %collective-permute-done.1.chip_ref, ...), custom_call_target="tpu_custom_call", output_to_operand_aliasing={{}: (4, {})} | custom-call | flops 3932160 | bytes 2359296 | tf_op jit(solution)/shard_map/late_terms/pallas_call | solution.py:299
  19.3 0.7 %planes_terms.1 = (f32[3,16,8,512]{3,2,1,0:T(8,128)S(1)}, f32[2,3,8,256]{3,2,1,0:T(8,128)S(1)}, f32[2,3,8,256]{3,2,1,0:T(8,128)S(1)}) custom-call(s32[1]{0:T(128)} %bitcast.me_ref, f32[3,16,8,512]{3,2,1,0:T(8,128)S(1)} %get-tuple-element.19.v_ref, f32[3,12,8,512]{3,2,1,0:T(8,128)S(1)} %collective-permute-done.y_ref, ...), custom_call_target="tpu_custom_call", output_to_operand_aliasing={{0}: (4, {})} | custom-call | flops 3932160 | bytes 3145728 | tf_op jit(solution)/shard_map/planes_terms/pallas_call | solution.py:344
  20.0 2.4 %collective-permute-start.4 = (f32[2,3,8,256]{3,2,1,0:T(8,128)S(1)}, f32[2,3,8,256]{3,2,1,0:T(8,128)S(1)}, u32[]{:S(2)}, u32[]{:S(2)}) collective-permute-start(f32[2,3,8,256]{3,2,1,0:T(8,128)S(1)} %get-tuple-element.26), channel_id=1, source_target_pairs={{0,2},{2,0},{4,6},{6,4},{8,10},{10,8},{12,14},{14,12},{16,18},{18,... | collective-permute-start | bytes 147464 | tf_op jit(solution)/shard_map/ppermute | solution.py:42
  22.4 0.9 %collective-permute-done.4.other_ref = f32[2,3,8,256]{3,2,1,0:T(8,128)S(1)} collective-permute-done((f32[2,3,8,256]{3,2,1,0:T(8,128)S(1)}, f32[2,3,8,256]{3,2,1,0:T(8,128)S(1)}, u32[]{:S(2)}, u32[]{:S(2)}) %collective-permute-start.4) | collective-permute-done | bytes 49184 | tf_op jit(solution)/shard_map/ppermute | solution.py:42
  23.3 2.0 %collective-permute-start.5 = (f32[2,3,8,256]{3,2,1,0:T(8,128)S(1)}, f32[2,3,8,256]{3,2,1,0:T(8,128)S(1)}, u32[]{:S(2)}, u32[]{:S(2)}) collective-permute-start(f32[2,3,8,256]{3,2,1,0:T(8,128)S(1)} %pair.1.block_ref), channel_id=1, source_target_pairs={{0,4},{2,6},{4,0},{6,2},{8,12},{10,14},{12,8},{14,10},{16,20},{18,... | collective-permute-start | bytes 147464 | tf_op jit(solution)/shard_map/ppermute | solution.py:42
  25.4 2.1 %collective-permute-done.5.other_ref = f32[2,3,8,256]{3,2,1,0:T(8,128)S(1)} collective-permute-done((f32[2,3,8,256]{3,2,1,0:T(8,128)S(1)}, f32[2,3,8,256]{3,2,1,0:T(8,128)S(1)}, u32[]{:S(2)}, u32[]{:S(2)}) %collective-permute-start.5) | collective-permute-done | bytes 49184 | tf_op jit(solution)/shard_map/ppermute | solution.py:42
  27.5 1.6 %collective-permute-start.6 = (f32[2,3,8,256]{3,2,1,0:T(8,128)S(1)}, f32[2,3,8,256]{3,2,1,0:T(8,128)S(1)}, u32[]{:S(2)}, u32[]{:S(2)}) collective-permute-start(f32[2,3,8,256]{3,2,1,0:T(8,128)S(1)} %get-tuple-element.27.block_ref), channel_id=1, source_target_pairs={{0,8},{2,10},{4,12},{6,14},{8,0},{10,2},{12,4},{14,6},{16,24},{18,... | collective-permute-start | bytes 147464 | tf_op jit(solution)/shard_map/ppermute | solution.py:42
  29.2 2.5 %collective-permute-done.6.other_ref = f32[2,3,8,256]{3,2,1,0:T(8,128)S(1)} collective-permute-done((f32[2,3,8,256]{3,2,1,0:T(8,128)S(1)}, f32[2,3,8,256]{3,2,1,0:T(8,128)S(1)}, u32[]{:S(2)}, u32[]{:S(2)}) %collective-permute-start.6) | collective-permute-done | bytes 49184 | tf_op jit(solution)/shard_map/ppermute | solution.py:42
  31.7 0.4 %collective-permute-start.7 = (f32[2,3,8,256]{3,2,1,0:T(8,128)S(1)}, f32[2,3,8,256]{3,2,1,0:T(8,128)S(1)}, u32[]{:S(2)}, u32[]{:S(2)}) collective-permute-start(f32[2,3,8,256]{3,2,1,0:T(8,128)S(1)} %get-tuple-element.29.block_ref), channel_id=1, source_target_pairs={{0,16},{2,18},{4,20},{6,22},{8,24},{10,26},{12,28},{14,30},{16,0},... | collective-permute-start | bytes 147464 | tf_op jit(solution)/shard_map/ppermute | solution.py:42
  32.1 0.9 %sweep.1 = (f32[3,16,8,512]{3,2,1,0:T(8,128)S(1)}, f32[3,16,8,512]{3,2,1,0:T(8,128)}) custom-call(f32[3,16,8,512]{3,2,1,0:T(8,128)S(1)} %get-tuple-element.19.v_ref, f32[3,16,8,512]{3,2,1,0:T(8,128)S(1)} %get-tuple-element.23.n_ref, f32[30,512]{1,0:T(8,128)S(1)} %get-tuple-element.21.power_ref), custom_call_target="tpu_custom_call" | custom-call | flops 1966080 | bytes 2359296 | tf_op jit(solution)/shard_map/sweep/pallas_call | solution.py:432
  33.0 3.8 %collective-permute-done.7.other_ref = f32[2,3,8,256]{3,2,1,0:T(8,128)S(1)} collective-permute-done((f32[2,3,8,256]{3,2,1,0:T(8,128)S(1)}, f32[2,3,8,256]{3,2,1,0:T(8,128)S(1)}, u32[]{:S(2)}, u32[]{:S(2)}) %collective-permute-start.7) | collective-permute-done | bytes 49184 | tf_op jit(solution)/shard_map/ppermute | solution.py:42
  36.9 1.2 %collective-permute-done.8.got_ref = f32[2,3,8,256]{3,2,1,0:T(8,128)S(1)} collective-permute-done((f32[2,3,8,256]{3,2,1,0:T(8,128)S(1)}, f32[2,3,8,256]{3,2,1,0:T(8,128)S(1)}, u32[]{:S(2)}, u32[]{:S(2)}) %collective-permute-start.8) | collective-permute-done | bytes 49184 | tf_op jit(solution)/shard_map/ppermute | solution.py:42
  38.1 1.0 %close.1 = f32[3,16,8,512]{3,2,1,0:T(8,128)} custom-call(s32[1]{0:T(128)} %bitcast.me_ref, f32[3,16,8,512]{3,2,1,0:T(8,128)S(1)} %get-tuple-element.24.ready_ref.s_ref, f32[30,512]{1,0:T(8,128)S(1)} %get-tuple-element.21.power_ref, f32[2,3,8,256]{3,2,1,0:T(8,128)S(1)} %get-tuple-element.33.mine_ref, f32[2,3,8,256]{3,2,1,0:T(8,128)S(1)} %collective-permute-done.8.got_ref), custom_call_target="tpu_custom_call" | custom-call | tf_op jit(solution)/shard_map/close/pallas_call | solution.py:552
  (15 shorter events, 0.3 us)
Async XLA Ops:
  1.8 17.5 %collective-permute-start = (f32[3,12,8,512]{3,2,1,0:T(8,128)S(1)}, f32[3,12,8,512]{3,2,1,0:T(8,128)S(1)}, u32[]{:S(2)}, u32[]{:S(2)}) collective-permute-start(f32[3,12,8,512]{3,2,1,0:T(8,128)S(1)} %get-tuple-element.20.first_ref), channel_id=1, source_target_pairs={{0,1},{1,0},{2,3},{3,2},{4,5},{5,4},{6,7},{7,6},{8,9},{9,8},{10,11... | collective-permute-start | bytes 1769480 | tf_op jit(solution)/shard_map/ppermute | solution.py:42
  4.9 5.8 %collective-permute-start.3 = (f32[3,4,8,128]{3,2,1,0:T(8,128)S(1)}, f32[3,4,8,128]{3,2,1,0:T(8,128)S(1)}, u32[]{:S(2)}, u32[]{:S(2)}) collective-permute-start(f32[3,4,8,128]{3,2,1,0:T(8,128)S(1)} %pack_mirror.1.first_ref), channel_id=1, source_target_pairs={{0,16},{2,18},{4,20},{6,22},{8,24},{10,26},{12,28},{14,30},{16,0},... | collective-permute-start | bytes 147464 | tf_op jit(solution)/shard_map/ppermute | solution.py:42
  7.6 2.5 %copy-start.1 = (f32[21]{0:T(128)S(1)}, f32[21]{0:T(128)}, u32[]{:S(2)}) copy-start(f32[21]{0:T(128)} %stencil_ref.1) | copy-start | bytes 256
  7.6 3.1 %copy-start = (f32[512,544]{0,1:T(8,128)S(1)}, f32[512,544]{0,1:T(8,128)}, u32[]{:S(2)}) copy-start(f32[512,544]{0,1:T(8,128)} %param.5) | copy-start | bytes 3342340
  7.7 11.1 %collective-permute-start.1 = (f32[3,10,8,512]{3,2,1,0:T(8,128)S(1)}, f32[3,10,8,512]{3,2,1,0:T(8,128)S(1)}, u32[]{:S(2)}, u32[]{:S(2)}) collective-permute-start(f32[3,10,8,512]{3,2,1,0:T(8,128)S(1)} %pack_chip.1.first_ref), channel_id=1, source_target_pairs={{2,4},{4,2},{6,8},{8,6},{10,12},{12,10},{14,16},{16,14},{18,20},{2... | collective-permute-start | bytes 1474568 | tf_op jit(solution)/shard_map/ppermute | solution.py:50
  8.9 4.5 %collective-permute-start.2 = (f32[3,10,8,512]{3,2,1,0:T(8,128)S(1)}, f32[3,10,8,512]{3,2,1,0:T(8,128)S(1)}, u32[]{:S(2)}, u32[]{:S(2)}) collective-permute-start(f32[3,10,8,512]{3,2,1,0:T(8,128)S(1)} %pack_core.1), channel_id=1, source_target_pairs={{0,2},{2,0},{4,6},{6,4},{8,10},{10,8},{12,14},{14,12},{16,18},{18,... | collective-permute-start | bytes 1474568 | tf_op jit(solution)/shard_map/ppermute | solution.py:42
  20.0 3.3 %collective-permute-start.4 = (f32[2,3,8,256]{3,2,1,0:T(8,128)S(1)}, f32[2,3,8,256]{3,2,1,0:T(8,128)S(1)}, u32[]{:S(2)}, u32[]{:S(2)}) collective-permute-start(f32[2,3,8,256]{3,2,1,0:T(8,128)S(1)} %get-tuple-element.26), channel_id=1, source_target_pairs={{0,2},{2,0},{4,6},{6,4},{8,10},{10,8},{12,14},{14,12},{16,18},{18,... | collective-permute-start | bytes 147464 | tf_op jit(solution)/shard_map/ppermute | solution.py:42
  23.3 4.2 %collective-permute-start.5 = (f32[2,3,8,256]{3,2,1,0:T(8,128)S(1)}, f32[2,3,8,256]{3,2,1,0:T(8,128)S(1)}, u32[]{:S(2)}, u32[]{:S(2)}) collective-permute-start(f32[2,3,8,256]{3,2,1,0:T(8,128)S(1)} %pair.1.block_ref), channel_id=1, source_target_pairs={{0,4},{2,6},{4,0},{6,2},{8,12},{10,14},{12,8},{14,10},{16,20},{18,... | collective-permute-start | bytes 147464 | tf_op jit(solution)/shard_map/ppermute | solution.py:42
  27.5 4.2 %collective-permute-start.6 = (f32[2,3,8,256]{3,2,1,0:T(8,128)S(1)}, f32[2,3,8,256]{3,2,1,0:T(8,128)S(1)}, u32[]{:S(2)}, u32[]{:S(2)}) collective-permute-start(f32[2,3,8,256]{3,2,1,0:T(8,128)S(1)} %get-tuple-element.27.block_ref), channel_id=1, source_target_pairs={{0,8},{2,10},{4,12},{6,14},{8,0},{10,2},{12,4},{14,6},{16,24},{18,... | collective-permute-start | bytes 147464 | tf_op jit(solution)/shard_map/ppermute | solution.py:42
  31.7 5.1 %collective-permute-start.7 = (f32[2,3,8,256]{3,2,1,0:T(8,128)S(1)}, f32[2,3,8,256]{3,2,1,0:T(8,128)S(1)}, u32[]{:S(2)}, u32[]{:S(2)}) collective-permute-start(f32[2,3,8,256]{3,2,1,0:T(8,128)S(1)} %get-tuple-element.29.block_ref), channel_id=1, source_target_pairs={{0,16},{2,18},{4,20},{6,22},{8,24},{10,26},{12,28},{14,30},{16,0},... | collective-permute-start | bytes 147464 | tf_op jit(solution)/shard_map/ppermute | solution.py:42
  36.8 1.3 %collective-permute-start.8 = (f32[2,3,8,256]{3,2,1,0:T(8,128)S(1)}, f32[2,3,8,256]{3,2,1,0:T(8,128)S(1)}, u32[]{:S(2)}, u32[]{:S(2)}) collective-permute-start(f32[2,3,8,256]{3,2,1,0:T(8,128)S(1)} %get-tuple-element.34), channel_id=1, source_target_pairs={{0,2},{2,0},{4,6},{6,4},{8,10},{10,8},{12,14},{14,12},{16,18},{18,... | collective-permute-start | bytes 147464 | tf_op jit(solution)/shard_map/ppermute | solution.py:42

commit v9 on v8

--- a/solution.py
+++ b/solution.py
@@ -14,6 +14,8 @@
 LANES = 128
 UNROLL = 16
 INNER = 10 << 29
+MIRROR = 1 << 26
+SIDE = 1 << 26
 
 VMEM = pl.BlockSpec(memory_space=pltpu.VMEM)
 SMEM = pl.BlockSpec(memory_space=pltpu.SMEM)
@@ -175,7 +177,7 @@
     return total
 
 
-def mirror_kernel(v_ref, op_ref, mirror_ref, n_ref, grad_ref):
+def mirror_kernel(v_ref, op_ref, mirror_ref, n_in_ref, n_ref, grad_ref):
     comps, points, planes, radial = v_ref.shape
     tiles = mirror_ref.shape[1]
     count = points // tiles
@@ -196,25 +198,26 @@
     def finish(t):
         for c in range(comps):
             start = pl.multiple_of((c * points + t) * planes, planes)
-            n_ref[c, t] = v_ref[0, t] * grad_ref[pl.ds(start, planes)]
+            n_ref[c, t] = n_in_ref[c, t] + v_ref[0, t] * grad_ref[pl.ds(start, planes)]
 
     each(points, finish)
 
 
-def mirror_terms(v, op, mirror):
+def mirror_terms(v, op, mirror, n):
     return pl.pallas_call(
         mirror_kernel,
         name="mirror_terms",
         out_shape=held(*v.shape),
-        in_specs=[VMEM, VMEM, VMEM],
+        in_specs=[VMEM] * 4,
         out_specs=VMEM,
         scratch_shapes=[pltpu.VMEM((v.size // v.shape[3], v.shape[3]), jnp.float32)],
+        input_output_aliases={3: 0},
         compiler_params=params(v.size * 4, 8),
-        cost_estimate=pl.CostEstimate(flops=2 * v.size * LANES, bytes_accessed=16 * v.size, transcendentals=0),
-    )(v, op, mirror)
-
-
-def inner_kernel(tap_ref, v_ref, op_ref, n_in_ref, n_ref, grad_ref):
+        cost_estimate=pl.CostEstimate(flops=MIRROR, bytes_accessed=16 * v.size, transcendentals=0),
+    )(v, op, mirror, n)
+
+
+def inner_kernel(tap_ref, v_ref, op_ref, n_ref, grad_ref):
     comps, points, planes, radial = v_ref.shape
     reach = (tap_ref.shape[0] - 1) // 2
     rows = points * planes
@@ -237,7 +240,7 @@
                     around = term if around is None else around + term
                 start = c * rows + t * planes
                 n = a * grad_ref[start : start + planes, lanes] + b_inv * around
-                n = n + e * axial_part(v_ref[c, t, :, lanes], weights) + n_in_ref[c, t, :, lanes]
+                n = n + e * axial_part(v_ref[c, t, :, lanes], weights)
                 if c == 0:
                     n = n - b_inv * b
                 elif c == 1:
@@ -245,18 +248,17 @@
                 n_ref[c, t, :, lanes] = n
 
 
-def inner_terms(taps, v, op, n):
+def inner_terms(taps, v, op):
     return pl.pallas_call(
         inner_kernel,
         name="inner_terms",
         out_shape=held(*v.shape),
-        in_specs=[VMEM] * 4,
+        in_specs=[VMEM] * 3,
         out_specs=VMEM,
         scratch_shapes=[pltpu.VMEM((v.size // v.shape[3], v.shape[3]), jnp.float32)],
-        input_output_aliases={3: 0},
         compiler_params=params(v.size * 4, 7),
         cost_estimate=pl.CostEstimate(flops=INNER, bytes_accessed=16 * v.size, transcendentals=0),
-    )(taps, v, op, n)
+    )(taps, v, op)
 
 
 def add_side(tap_ref, v_ref, side_ref, n_in_ref, n_ref, before):
@@ -304,7 +306,7 @@
         out_specs=VMEM,
         input_output_aliases={4: 0},
         compiler_params=params(v.size * 4, 5),
-        cost_estimate=pl.CostEstimate(flops=20 * v.size, bytes_accessed=12 * v.size, transcendentals=0),
+        cost_estimate=pl.CostEstimate(flops=SIDE, bytes_accessed=12 * v.size, transcendentals=0),
     )(me, taps, v, side, n)
 
 
@@ -574,17 +576,17 @@
 
     velocity, planes_out = load(pltpu.with_memory_space_constraint(velocity, pltpu.HBM))
     planes_in = swap(planes_out, "gz", 1)
-    mirror_out = pack_mirror(velocity, planes_out, width)
+    chip_out = pack_side(me, velocity, planes_out, reach, False)
+    chip_in = swap_across(chip_out, "theta")
+    mirror_out = pack_mirror(velocity, chip_out, width)
     mirror_in = swap(mirror_out, "theta", sectors // 2)
-    chip_out = pack_side(me, velocity, mirror_out, reach, False)
-    chip_in = swap_across(chip_out, "theta")
-    core_out = pack_side(me, velocity, chip_out, reach, True)
+    core_out = pack_side(me, velocity, mirror_out, reach, True)
     core_in = swap(core_out, "theta", 1)
     power, taps = table(me, viscous_factor, azimuth_stencil, points, sectors, planes, radial)
-    n = mirror_terms(velocity, op, mirror_in)
-    n = inner_terms(taps, velocity, op, n)
+    n = inner_terms(taps, velocity, op)
     n = side_terms(core_kernel, "core_terms", me, taps, velocity, core_in, n)
     n = side_terms(late_kernel, "late_terms", me, taps, velocity, chip_in, n)
+    n = mirror_terms(velocity, op, mirror_in, n)
     n, own, send = planes_terms(me, velocity, planes_in, power, n)
     other = swap(send, "theta", 1)
     s, nonlinear = sweep(velocity, n, power)

time: 39.2 us -> 37 us (0.944)
  waiting for transfers between devices: 15.3 us -> 11.9 us
  starting transfers between devices: 14 us -> 15.1 us
    ppermute x1, starting transfers between devices: 1.23 us -> 3.76 us  [swap_across(): return lax.ppermute(block, axis, route)]
    ppermute x8, waiting for transfers between devices: 10.5 us -> 8.49 us  [swap(): return lax.ppermute(block, axis, [(i, i ^ bit) for i in range(size)])]
    ppermute x1, waiting for transfers between devices: 4.79 us -> 3.39 us  [swap_across(): return lax.ppermute(block, axis, route)]
    ppermute x8, starting transfers between devices: 12.7 us -> 11.4 us  [swap(): return lax.ppermute(block, axis, [(i, i ^ bit) for i in range(size)])]
  transfers between devices with their start and end apart: 9 -> 9, of which waited for: 6 -> 7; matrix products, arithmetic and copies ran while one was open for 0% -> 0% of each run, Pallas kernels for 14% -> 15%
where the time goes in v9:
time: 37 us; the launch traced here: 36.8 us
  starting transfers between devices  15.1 us (41%)
  waiting for transfers between devices  11.9 us (32%)
  Pallas kernels  8.38 us (23%)
  between operations  1.45 us (4%)
    ppermute x8, starting transfers between devices, swap(): return lax.ppermute(block, axis, [(i, i ^ bit) for i in range(size)])  11.4 us
    ppermute x8, waiting for transfers between devices, swap(): return lax.ppermute(block, axis, [(i, i ^ bit) for i in range(size)])  8.49 us
    ppermute x1, starting transfers between devices, swap_across(): return lax.ppermute(block, axis, route)  3.76 us
    ppermute x1, waiting for transfers between devices, swap_across(): return lax.ppermute(block, axis, route)  3.39 us
    pallas_call x1, Pallas kernels, inner_terms(): pl.pallas_call(inner_kernel, name='inner_terms', out_shape=held(*v.shape)...  2.21 us
    pallas_call x1, Pallas kernels, load(): pl.pallas_call(load_kernel, name='load', out_shape=(held(*v.shape), held(...  1.17 us
    pallas_call x2, Pallas kernels, side_terms(): pl.pallas_call(kernel, name=name, out_shape=held(*v.shape), in_specs=[SME...  1.01 us
    pallas_call x1, Pallas kernels, close(): pl.pallas_call(close_kernel, name='close', out_shape=jax.ShapeDtypeStruct...  0.97 us
  transfers between devices with their start and end apart: 9, of which 7 were waited for; matrix products, arithmetic and copies ran while one was open for 0% of the time, Pallas kernels for 15%

profile of v9, /device:TPU:0, one launch (start us, length us, event | category | flops | bytes accessed | tf_op | source)
XLA Modules:
  0.0 36.8 jit_solution(3469161889235983413)
XLA Ops:
  0.6 1.2 %load.1 = (f32[3,16,8,512]{3,2,1,0:T(8,128)S(1)}, f32[3,12,8,512]{3,2,1,0:T(8,128)S(1)}) custom-call(f32[3,16,8,512]{3,2,1,0:T(8,128)} %hbm_ref.1), custom_call_target="tpu_custom_call" | custom-call | tf_op jit(solution)/shard_map/load/pallas_call | solution.py:91
  1.8 3.0 %collective-permute-start = (f32[3,12,8,512]{3,2,1,0:T(8,128)S(1)}, f32[3,12,8,512]{3,2,1,0:T(8,128)S(1)}, u32[]{:S(2)}, u32[]{:S(2)}) collective-permute-start(f32[3,12,8,512]{3,2,1,0:T(8,128)S(1)} %get-tuple-element.20.first_ref), channel_id=1, source_target_pairs={{0,1},{1,0},{2,3},{3,2},{4,5},{5,4},{6,7},{7,6},{8,9},{9,8},{10,11... | collective-permute-start | bytes 1769480 | tf_op jit(solution)/shard_map/ppermute | solution.py:44
  4.9 3.8 %collective-permute-start.2 = (f32[3,10,8,512]{3,2,1,0:T(8,128)S(1)}, f32[3,10,8,512]{3,2,1,0:T(8,128)S(1)}, u32[]{:S(2)}, u32[]{:S(2)}) collective-permute-start(f32[3,10,8,512]{3,2,1,0:T(8,128)S(1)} %pack_chip.1.first_ref), channel_id=1, source_target_pairs={{2,4},{4,2},{6,8},{8,6},{10,12},{12,10},{14,16},{16,14},{18,20},{2... | collective-permute-start | bytes 1474568 | tf_op jit(solution)/shard_map/ppermute | solution.py:52
  8.7 0.1 pack_mirror.1.first_ref
  8.9 0.3 collective-permute-start.3
  9.8 0.6 %table.1 = (f32[30,512]{1,0:T(8,128)S(1)}, f32[21,8,128]{2,1,0:T(8,128)S(1)}) custom-call(s32[1]{0:T(128)} %bitcast.me_ref, f32[1]{0:T(128)S(6)} %copy.14.factor_ref, f32[21]{0:T(128)S(1)} %copy-done.1), custom_call_target="tpu_custom_call" | custom-call | flops 512000 | bytes 204800 | tf_op jit(solution)/shard_map/table/pallas_call | solution.py:394
  10.5 2.2 %inner_terms.1.n_in_ref = f32[3,16,8,512]{3,2,1,0:T(8,128)S(1)} custom-call(f32[21,8,128]{2,1,0:T(8,128)S(1)} %get-tuple-element.22.tap_ref, f32[3,16,8,512]{3,2,1,0:T(8,128)S(1)} %get-tuple-element.19.v_ref, f32[544,512]{1,0:T(8,128)S(1)} %bitcast.2), custom_call_target="tpu_custom_call" | custom-call | flops 5368709120 | bytes 3145728 | tf_op jit(solution)/shard_map/inner_terms/pallas_call | solution.py:252
  12.7 0.5 %core_terms.1.n_in_ref = f32[3,16,8,512]{3,2,1,0:T(8,128)S(1)} custom-call(s32[1]{0:T(128)} %bitcast.me_ref, f32[21,8,128]{2,1,0:T(8,128)S(1)} %get-tuple-element.22.tap_ref, f32[3,16,8,512]{3,2,1,0:T(8,128)S(1)} %get-tuple-element.19.v_ref, f32[3,10,8,512]{3,2,1,0:T(8,128)S(1)} %collective-permute-done.3.core_ref, ...), custom_call_target="tpu_custom_call", output_to_operand_aliasing={{}: (4, {})} | custom-call | flops 67108864 | bytes 2359296 | tf_op jit(solution)/shard_map/core_terms/pallas_call | solution.py:301
  13.2 3.4 %collective-permute-done.2.chip_ref = f32[3,10,8,512]{3,2,1,0:T(8,128)S(1)} collective-permute-done((f32[3,10,8,512]{3,2,1,0:T(8,128)S(1)}, f32[3,10,8,512]{3,2,1,0:T(8,128)S(1)}, u32[]{:S(2)}, u32[]{:S(2)}) %collective-permute-start.2) | collective-permute-done | bytes 491552 | tf_op jit(solution)/shard_map/ppermute | solution.py:52
  16.6 0.5 %late_terms.1.n_in_ref = f32[3,16,8,512]{3,2,1,0:T(8,128)S(1)} custom-call(s32[1]{0:T(128)} %bitcast.me_ref, f32[21,8,128]{2,1,0:T(8,128)S(1)} %get-tuple-element.22.tap_ref, f32[3,16,8,512]{3,2,1,0:T(8,128)S(1)} %get-tuple-element.19.v_ref, f32[3,10,8,512]{3,2,1,0:T(8,128)S(1)} %collective-permute-done.2.chip_ref, ...), custom_call_target="tpu_custom_call", output_to_operand_aliasing={{}: (4, {})} | custom-call | flops 67108864 | bytes 2359296 | tf_op jit(solution)/shard_map/late_terms/pallas_call | solution.py:301
  17.1 0.5 %mirror_terms.1.n_in_ref = f32[3,16,8,512]{3,2,1,0:T(8,128)S(1)} custom-call(f32[3,16,8,512]{3,2,1,0:T(8,128)S(1)} %get-tuple-element.19.v_ref, f32[544,512]{1,0:T(8,128)S(1)} %bitcast.3, f32[3,4,8,128]{3,2,1,0:T(8,128)S(1)} %collective-permute-done.1.mirror_ref, f32[3,16,8,512]{3,2,1,0:T(8,128)S(1)} %late_terms.1.n_in_ref), custom_call_target="tpu_custom_call", output_to_operand_aliasing={{}: (3, {})} | custom-call | flops 67108864 | bytes 3145728 | tf_op jit(solution)/shard_map/mirror_terms/pallas_call | solution.py:207
  17.6 0.5 %collective-permute-done.y_ref = f32[3,12,8,512]{3,2,1,0:T(8,128)S(1)} collective-permute-done((f32[3,12,8,512]{3,2,1,0:T(8,128)S(1)}, f32[3,12,8,512]{3,2,1,0:T(8,128)S(1)}, u32[]{:S(2)}, u32[]{:S(2)}) %collective-permute-start) | collective-permute-done | bytes 589856 | tf_op jit(solution)/shard_map/ppermute | solution.py:44
  18.2 0.7 %planes_terms.1 = (f32[3,16,8,512]{3,2,1,0:T(8,128)S(1)}, f32[2,3,8,256]{3,2,1,0:T(8,128)S(1)}, f32[2,3,8,256]{3,2,1,0:T(8,128)S(1)}) custom-call(s32[1]{0:T(128)} %bitcast.me_ref, f32[3,16,8,512]{3,2,1,0:T(8,128)S(1)} %get-tuple-element.19.v_ref, f32[3,12,8,512]{3,2,1,0:T(8,128)S(1)} %collective-permute-done.y_ref, ...), custom_call_target="tpu_custom_call", output_to_operand_aliasing={{0}: (4, {})} | custom-call | flops 3932160 | bytes 3145728 | tf_op jit(solution)/shard_map/planes_terms/pallas_call | solution.py:346
  18.9 1.3 %collective-permute-start.4 = (f32[2,3,8,256]{3,2,1,0:T(8,128)S(1)}, f32[2,3,8,256]{3,2,1,0:T(8,128)S(1)}, u32[]{:S(2)}, u32[]{:S(2)}) collective-permute-start(f32[2,3,8,256]{3,2,1,0:T(8,128)S(1)} %get-tuple-element.26), channel_id=1, source_target_pairs={{0,2},{2,0},{4,6},{6,4},{8,10},{10,8},{12,14},{14,12},{16,18},{18,... | collective-permute-start | bytes 147464 | tf_op jit(solution)/shard_map/ppermute | solution.py:44
  20.2 0.9 %collective-permute-done.4.other_ref = f32[2,3,8,256]{3,2,1,0:T(8,128)S(1)} collective-permute-done((f32[2,3,8,256]{3,2,1,0:T(8,128)S(1)}, f32[2,3,8,256]{3,2,1,0:T(8,128)S(1)}, u32[]{:S(2)}, u32[]{:S(2)}) %collective-permute-start.4) | collective-permute-done | bytes 49184 | tf_op jit(solution)/shard_map/ppermute | solution.py:44
  21.1 2.0 %collective-permute-start.5 = (f32[2,3,8,256]{3,2,1,0:T(8,128)S(1)}, f32[2,3,8,256]{3,2,1,0:T(8,128)S(1)}, u32[]{:S(2)}, u32[]{:S(2)}) collective-permute-start(f32[2,3,8,256]{3,2,1,0:T(8,128)S(1)} %pair.1.block_ref), channel_id=1, source_target_pairs={{0,4},{2,6},{4,0},{6,2},{8,12},{10,14},{12,8},{14,10},{16,20},{18,... | collective-permute-start | bytes 147464 | tf_op jit(solution)/shard_map/ppermute | solution.py:44
  23.1 2.1 %collective-permute-done.5.other_ref = f32[2,3,8,256]{3,2,1,0:T(8,128)S(1)} collective-permute-done((f32[2,3,8,256]{3,2,1,0:T(8,128)S(1)}, f32[2,3,8,256]{3,2,1,0:T(8,128)S(1)}, u32[]{:S(2)}, u32[]{:S(2)}) %collective-permute-start.5) | collective-permute-done | bytes 49184 | tf_op jit(solution)/shard_map/ppermute | solution.py:44
  25.3 1.8 %collective-permute-start.6 = (f32[2,3,8,256]{3,2,1,0:T(8,128)S(1)}, f32[2,3,8,256]{3,2,1,0:T(8,128)S(1)}, u32[]{:S(2)}, u32[]{:S(2)}) collective-permute-start(f32[2,3,8,256]{3,2,1,0:T(8,128)S(1)} %get-tuple-element.27.block_ref), channel_id=1, source_target_pairs={{0,8},{2,10},{4,12},{6,14},{8,0},{10,2},{12,4},{14,6},{16,24},{18,... | collective-permute-start | bytes 147464 | tf_op jit(solution)/shard_map/ppermute | solution.py:44
  27.1 2.4 %collective-permute-done.6.other_ref = f32[2,3,8,256]{3,2,1,0:T(8,128)S(1)} collective-permute-done((f32[2,3,8,256]{3,2,1,0:T(8,128)S(1)}, f32[2,3,8,256]{3,2,1,0:T(8,128)S(1)}, u32[]{:S(2)}, u32[]{:S(2)}) %collective-permute-start.6) | collective-permute-done | bytes 49184 | tf_op jit(solution)/shard_map/ppermute | solution.py:44
  29.5 2.8 %collective-permute-start.7 = (f32[2,3,8,256]{3,2,1,0:T(8,128)S(1)}, f32[2,3,8,256]{3,2,1,0:T(8,128)S(1)}, u32[]{:S(2)}, u32[]{:S(2)}) collective-permute-start(f32[2,3,8,256]{3,2,1,0:T(8,128)S(1)} %get-tuple-element.29.block_ref), channel_id=1, source_target_pairs={{0,16},{2,18},{4,20},{6,22},{8,24},{10,26},{12,28},{14,30},{16,0},... | collective-permute-start | bytes 147464 | tf_op jit(solution)/shard_map/ppermute | solution.py:44
  32.3 0.9 %sweep.1 = (f32[3,16,8,512]{3,2,1,0:T(8,128)S(1)}, f32[3,16,8,512]{3,2,1,0:T(8,128)}) custom-call(f32[3,16,8,512]{3,2,1,0:T(8,128)S(1)} %get-tuple-element.19.v_ref, f32[3,16,8,512]{3,2,1,0:T(8,128)S(1)} %get-tuple-element.23.n_ref, f32[30,512]{1,0:T(8,128)S(1)} %get-tuple-element.21.power_ref), custom_call_target="tpu_custom_call" | custom-call | flops 1966080 | bytes 2359296 | tf_op jit(solution)/shard_map/sweep/pallas_call | solution.py:434
  33.2 1.4 %collective-permute-done.7.other_ref = f32[2,3,8,256]{3,2,1,0:T(8,128)S(1)} collective-permute-done((f32[2,3,8,256]{3,2,1,0:T(8,128)S(1)}, f32[2,3,8,256]{3,2,1,0:T(8,128)S(1)}, u32[]{:S(2)}, u32[]{:S(2)}) %collective-permute-start.7) | collective-permute-done | bytes 49184 | tf_op jit(solution)/shard_map/ppermute | solution.py:44
  34.6 1.2 %collective-permute-done.8.got_ref = f32[2,3,8,256]{3,2,1,0:T(8,128)S(1)} collective-permute-done((f32[2,3,8,256]{3,2,1,0:T(8,128)S(1)}, f32[2,3,8,256]{3,2,1,0:T(8,128)S(1)}, u32[]{:S(2)}, u32[]{:S(2)}) %collective-permute-start.8) | collective-permute-done | bytes 49184 | tf_op jit(solution)/shard_map/ppermute | solution.py:44
  35.9 1.0 %close.1 = f32[3,16,8,512]{3,2,1,0:T(8,128)} custom-call(s32[1]{0:T(128)} %bitcast.me_ref, f32[3,16,8,512]{3,2,1,0:T(8,128)S(1)} %get-tuple-element.24.ready_ref.s_ref, f32[30,512]{1,0:T(8,128)S(1)} %get-tuple-element.21.power_ref, f32[2,3,8,256]{3,2,1,0:T(8,128)S(1)} %get-tuple-element.33.mine_ref, f32[2,3,8,256]{3,2,1,0:T(8,128)S(1)} %collective-permute-done.8.got_ref), custom_call_target="tpu_custom_call" | custom-call | tf_op jit(solution)/shard_map/close/pallas_call | solution.py:554
  (15 shorter events, 0.3 us)
Async XLA Ops:
  1.8 16.4 %collective-permute-start = (f32[3,12,8,512]{3,2,1,0:T(8,128)S(1)}, f32[3,12,8,512]{3,2,1,0:T(8,128)S(1)}, u32[]{:S(2)}, u32[]{:S(2)}) collective-permute-start(f32[3,12,8,512]{3,2,1,0:T(8,128)S(1)} %get-tuple-element.20.first_ref), channel_id=1, source_target_pairs={{0,1},{1,0},{2,3},{3,2},{4,5},{5,4},{6,7},{7,6},{8,9},{9,8},{10,11... | collective-permute-start | bytes 1769480 | tf_op jit(solution)/shard_map/ppermute | solution.py:44
  4.9 4.9 %copy-start.1 = (f32[21]{0:T(128)S(1)}, f32[21]{0:T(128)}, u32[]{:S(2)}) copy-start(f32[21]{0:T(128)} %stencil_ref.1) | copy-start | bytes 256
  4.9 5.6 %copy-start = (f32[512,544]{0,1:T(8,128)S(1)}, f32[512,544]{0,1:T(8,128)}, u32[]{:S(2)}) copy-start(f32[512,544]{0,1:T(8,128)} %param.5) | copy-start | bytes 3342340
  4.9 11.7 %collective-permute-start.2 = (f32[3,10,8,512]{3,2,1,0:T(8,128)S(1)}, f32[3,10,8,512]{3,2,1,0:T(8,128)S(1)}, u32[]{:S(2)}, u32[]{:S(2)}) collective-permute-start(f32[3,10,8,512]{3,2,1,0:T(8,128)S(1)} %pack_chip.1.first_ref), channel_id=1, source_target_pairs={{2,4},{4,2},{6,8},{8,6},{10,12},{12,10},{14,16},{16,14},{18,20},{2... | collective-permute-start | bytes 1474568 | tf_op jit(solution)/shard_map/ppermute | solution.py:52
  8.8 8.3 %collective-permute-start.1 = (f32[3,4,8,128]{3,2,1,0:T(8,128)S(1)}, f32[3,4,8,128]{3,2,1,0:T(8,128)S(1)}, u32[]{:S(2)}, u32[]{:S(2)}) collective-permute-start(f32[3,4,8,128]{3,2,1,0:T(8,128)S(1)} %pack_mirror.1.first_ref), channel_id=1, source_target_pairs={{0,16},{2,18},{4,20},{6,22},{8,24},{10,26},{12,28},{14,30},{16,0},... | collective-permute-start | bytes 147464 | tf_op jit(solution)/shard_map/ppermute | solution.py:44
  8.9 3.8 %collective-permute-start.3 = (f32[3,10,8,512]{3,2,1,0:T(8,128)S(1)}, f32[3,10,8,512]{3,2,1,0:T(8,128)S(1)}, u32[]{:S(2)}, u32[]{:S(2)}) collective-permute-start(f32[3,10,8,512]{3,2,1,0:T(8,128)S(1)} %pack_core.1), channel_id=1, source_target_pairs={{0,2},{2,0},{4,6},{6,4},{8,10},{10,8},{12,14},{14,12},{16,18},{18,... | collective-permute-start | bytes 1474568 | tf_op jit(solution)/shard_map/ppermute | solution.py:44
  18.9 2.2 %collective-permute-start.4 = (f32[2,3,8,256]{3,2,1,0:T(8,128)S(1)}, f32[2,3,8,256]{3,2,1,0:T(8,128)S(1)}, u32[]{:S(2)}, u32[]{:S(2)}) collective-permute-start(f32[2,3,8,256]{3,2,1,0:T(8,128)S(1)} %get-tuple-element.26), channel_id=1, source_target_pairs={{0,2},{2,0},{4,6},{6,4},{8,10},{10,8},{12,14},{14,12},{16,18},{18,... | collective-permute-start | bytes 147464 | tf_op jit(solution)/shard_map/ppermute | solution.py:44
  21.1 4.2 %collective-permute-start.5 = (f32[2,3,8,256]{3,2,1,0:T(8,128)S(1)}, f32[2,3,8,256]{3,2,1,0:T(8,128)S(1)}, u32[]{:S(2)}, u32[]{:S(2)}) collective-permute-start(f32[2,3,8,256]{3,2,1,0:T(8,128)S(1)} %pair.1.block_ref), channel_id=1, source_target_pairs={{0,4},{2,6},{4,0},{6,2},{8,12},{10,14},{12,8},{14,10},{16,20},{18,... | collective-permute-start | bytes 147464 | tf_op jit(solution)/shard_map/ppermute | solution.py:44
  25.3 4.2 %collective-permute-start.6 = (f32[2,3,8,256]{3,2,1,0:T(8,128)S(1)}, f32[2,3,8,256]{3,2,1,0:T(8,128)S(1)}, u32[]{:S(2)}, u32[]{:S(2)}) collective-permute-start(f32[2,3,8,256]{3,2,1,0:T(8,128)S(1)} %get-tuple-element.27.block_ref), channel_id=1, source_target_pairs={{0,8},{2,10},{4,12},{6,14},{8,0},{10,2},{12,4},{14,6},{16,24},{18,... | collective-permute-start | bytes 147464 | tf_op jit(solution)/shard_map/ppermute | solution.py:44
  29.5 5.1 %collective-permute-start.7 = (f32[2,3,8,256]{3,2,1,0:T(8,128)S(1)}, f32[2,3,8,256]{3,2,1,0:T(8,128)S(1)}, u32[]{:S(2)}, u32[]{:S(2)}) collective-permute-start(f32[2,3,8,256]{3,2,1,0:T(8,128)S(1)} %get-tuple-element.29.block_ref), channel_id=1, source_target_pairs={{0,16},{2,18},{4,20},{6,22},{8,24},{10,26},{12,28},{14,30},{16,0},... | collective-permute-start | bytes 147464 | tf_op jit(solution)/shard_map/ppermute | solution.py:44
  34.6 1.3 %collective-permute-start.8 = (f32[2,3,8,256]{3,2,1,0:T(8,128)S(1)}, f32[2,3,8,256]{3,2,1,0:T(8,128)S(1)}, u32[]{:S(2)}, u32[]{:S(2)}) collective-permute-start(f32[2,3,8,256]{3,2,1,0:T(8,128)S(1)} %get-tuple-element.34), channel_id=1, source_target_pairs={{0,2},{2,0},{4,6},{6,4},{8,10},{10,8},{12,14},{14,12},{16,18},{18,... | collective-permute-start | bytes 147464 | tf_op jit(solution)/shard_map/ppermute | solution.py:44

commit v10 on v9

--- a/solution.py
+++ b/solution.py
@@ -66,14 +66,16 @@
     comps, points, planes, _ = v_ref.shape
     carriers = y_ref.shape[1]
     lo, hi = AXIAL_REACH, planes - AXIAL_REACH
-    loads = [pltpu.make_async_copy(hbm_ref.at[c], v_ref.at[c], sems.at[c]) for c in range(comps)]
-    for load in loads:
-        load.start()
-    for c in range(comps):
-        loads[c].wait()
-
-        def carry(t):
-            y_ref[c, t] = v_ref[c, t]
+    loads = []
+    for c in range(comps):
+        ways = ((hbm_ref.at[c], v_ref.at[c]), (hbm_ref.at[c, pl.ds(0, carriers)], y_ref.at[c]))
+        loads.append([pltpu.make_async_copy(*way, sems.at[k, c]) for k, way in enumerate(ways)])
+    for c in range(comps):
+        for way in loads[c]:
+            way.start()
+    for c in range(comps):
+        for way in loads[c]:
+            way.wait()
 
         def ride(j):
             t = carriers + j
@@ -82,7 +84,6 @@
             y_ref[c, 3 * j + 1, lo + 1 : hi] = v_ref[c, t, hi : hi + 1]
             y_ref[c, 3 * j + 2, lo:hi] = v_ref[c, t, hi + 1 :]
 
-        each(carriers, carry)
         each(points - carriers, ride)
 
 
@@ -94,7 +95,7 @@
         out_shape=(held(*v.shape), held(comps, points - points // 4, planes, radial)),
         in_specs=[HBM],
         out_specs=(VMEM, VMEM),
-        scratch_shapes=[pltpu.SemaphoreType.DMA((comps,))],
+        scratch_shapes=[pltpu.SemaphoreType.DMA((2, comps))],
         compiler_params=params(v.size * 4, 2),
     )(v)
 
@@ -310,49 +311,41 @@
     )(me, taps, v, side, n)
 
 
-def planes_kernel(me_ref, v_ref, y_ref, power_ref, n_in_ref, n_ref, keep_ref, send_ref, tile_ref, ends_ref):
+def planes_kernel(me_ref, v_ref, y_ref, power_ref, n_in_ref, n_ref, ends_ref, tile_ref, *, own):
     comps, points, planes, radial = v_ref.shape
+    half = radial // 2
     carriers = y_ref.shape[1]
     lo, hi = AXIAL_REACH, planes - AXIAL_REACH
     weights = axial_weights(planes, False)
+    lanes = half_lanes(me_ref, half, own)
     for c in range(comps):
         for j in range(points - carriers):
-            tile_ref[c, j, 0:2] = y_ref[c, 3 * j, lo:hi]
-            tile_ref[c, j, 2:3] = y_ref[c, 3 * j + 1, lo : lo + 1]
-            tile_ref[c, j, lo:hi] = jnp.zeros((hi - lo, radial), jnp.float32)
-            tile_ref[c, j, hi : hi + 1] = y_ref[c, 3 * j + 1, lo + 1 : hi]
-            tile_ref[c, j, hi + 1 :] = y_ref[c, 3 * j + 2, lo:hi]
-
-    decay = power_ref[1:2]
+            tile_ref[c, j, 0:2] = y_ref[c, 3 * j, lo:hi, lanes]
+            tile_ref[c, j, 2:3] = y_ref[c, 3 * j + 1, lo : lo + 1, lanes]
+            tile_ref[c, j, lo:hi] = jnp.zeros((hi - lo, half), jnp.float32)
+            tile_ref[c, j, hi : hi + 1] = y_ref[c, 3 * j + 1, lo + 1 : hi, lanes]
+            tile_ref[c, j, hi + 1 :] = y_ref[c, 3 * j + 2, lo:hi, lanes]
+    decay = power_ref[1:2, lanes]
     ends_ref[...] = jnp.zeros_like(ends_ref)
     for t in range(points):
         for c in range(comps):
-            tile = y_ref[c, t] if t < carriers else tile_ref[c, t - carriers]
-            n = n_in_ref[c, t] + v_ref[2, t] * axial_part(tile, weights)
-            n_ref[c, t] = n
-            right_side = v_ref[c, t] - STEP_WEIGHT * n
+            tile = y_ref[c, t, :, lanes] if t < carriers else tile_ref[c, t - carriers]
+            n = n_in_ref[c, t, :, lanes] + v_ref[2, t, :, lanes] * axial_part(tile, weights)
+            n_ref[c, t, :, lanes] = n
+            right_side = v_ref[c, t, :, lanes] - STEP_WEIGHT * n
             ends_ref[0, c] = decay * ends_ref[0, c] + right_side
-            ends_ref[1, c] = ends_ref[1, c] + power_ref[t : t + 1] * right_side
-
-    half = radial // 2
-    core = me_ref[0] % 2
-    keep_ref[...] = ends_ref[:, :, :, pl.ds(pl.multiple_of(core * half, half), half)]
-    send_ref[...] = ends_ref[:, :, :, pl.ds(pl.multiple_of((1 - core) * half, half), half)]
-
-
-def planes_terms(me, v, y, power, n):
+            ends_ref[1, c] = ends_ref[1, c] + power_ref[t : t + 1, lanes] * right_side
+
+
+def planes_terms(me, v, y, power, n, own):
     comps, points, planes, radial = v.shape
-    part = held(2, comps, planes, radial // 2)
-    return pl.pallas_call(
-        planes_kernel,
-        name="planes_terms",
-        out_shape=(held(*v.shape), part, part),
+    return pl.pallas_call(
+        functools.partial(planes_kernel, own=own),
+        name="planes_own" if own else "planes_other",
+        out_shape=(held(*v.shape), held(2, comps, planes, radial // 2)),
         in_specs=[SMEM] + [VMEM] * 4,
-        out_specs=(VMEM, VMEM, VMEM),
-        scratch_shapes=[
-            pltpu.VMEM((comps, points - y.shape[1], planes, radial), jnp.float32),
-            pltpu.VMEM((2, comps, planes, radial), jnp.float32),
-        ],
+        out_specs=(VMEM, VMEM),
+        scratch_shapes=[pltpu.VMEM((comps, points - y.shape[1], planes, radial // 2), jnp.float32)],
         input_output_aliases={4: 0},
         compiler_params=params(v.size * 4, 6),
         cost_estimate=pl.CostEstimate(flops=20 * v.size, bytes_accessed=16 * v.size, transcendentals=0),
@@ -443,14 +436,14 @@
     )(v, n, power)
 
 
-def my_lanes(me_ref, radial, half):
+def half_lanes(me_ref, half, own=True):
     core = me_ref[0] % 2
-    return pl.ds(pl.multiple_of(core * half, half), half)
+    return pl.ds(pl.multiple_of((core if own else 1 - core) * half, half), half)
 
 
 def pair_kernel(me_ref, power_ref, own_ref, other_ref, block_ref, *, points):
     half = own_ref.shape[3]
-    hop = power_ref[points : points + 1, my_lanes(me_ref, power_ref.shape[1], half)]
+    hop = power_ref[points : points + 1, half_lanes(me_ref, half)]
     odd = me_ref[0] % 2 == 1
     for c in range(own_ref.shape[1]):
         for side in range(2):
@@ -473,7 +466,7 @@
 def merge_kernel(me_ref, power_ref, block_ref, other_ref, *refs, points, bit):
     *entry_refs, block_out_ref, entry_out_ref = refs
     comps, half = block_ref.shape[1], block_ref.shape[3]
-    lanes = my_lanes(me_ref, power_ref.shape[1], half)
+    lanes = half_lanes(me_ref, half)
     first = points + 3 * bit
     across, before, after = [power_ref[first + k : first + k + 1, lanes] for k in range(3)]
     upper = (me_ref[0] >> bit) % 2 == 1
@@ -501,7 +494,7 @@
 
 def enter_kernel(me_ref, power_ref, block_ref, entry_ref, own_ref, other_ref, ready_ref, mine_ref, send_ref, *, points):
     comps, half = block_ref.shape[1], block_ref.shape[3]
-    lanes = my_lanes(me_ref, power_ref.shape[1], half)
+    lanes = half_lanes(me_ref, half)
     row = lambda k: power_ref[k : k + 1, lanes]
     hop, height, wrap = row(points), row(points + 1), row(points + 2)
     last = power_ref.shape[0]
@@ -530,40 +523,41 @@
     )(me, power, block, entry, own, other, ready)
 
 
-def close_kernel(me_ref, s_ref, power_ref, mine_ref, got_ref, out_ref, x_ref, both_ref, sems):
-    comps, points, planes, radial = s_ref.shape
-    half = mine_ref.shape[3]
-    core = me_ref[0] % 2
-    both_ref[:, :, :, pl.ds(pl.multiple_of(core * half, half), half)] = mine_ref[...]
-    both_ref[:, :, :, pl.ds(pl.multiple_of((1 - core) * half, half), half)] = got_ref[...]
+def close_kernel(me_ref, s_ref, power_ref, entry_ref, *refs, own):
+    out_ref, x_ref, sems = refs[-3:]
+    comps, points, _, _ = s_ref.shape
+    lanes = half_lanes(me_ref, entry_ref.shape[3], own)
     leaves = []
     for c in range(comps):
-        before, after = both_ref[0, c], both_ref[1, c]
+        before, after = entry_ref[0, c], entry_ref[1, c]
 
         def point(t):
-            x_ref[c, t] = s_ref[c, t] + power_ref[pl.ds(t + 1, 1)] * before + power_ref[pl.ds(points - t, 1)] * after
+            decayed = power_ref[pl.ds(t + 1, 1), lanes] * before + power_ref[pl.ds(points - t, 1), lanes] * after
+            x_ref[c, t] = s_ref[c, t, :, lanes] + decayed
 
         each(points, point)
-        leaves.append(pltpu.make_async_copy(x_ref.at[c], out_ref.at[c], sems.at[c]))
+        leaves.append(pltpu.make_async_copy(x_ref.at[c], out_ref.at[c, :, :, lanes], sems.at[c]))
         leaves[c].start()
     for leave in leaves:
         leave.wait()
 
 
-def close(me, s, power, mine, got):
-    return pl.pallas_call(
-        close_kernel,
-        name="close",
+def close(me, s, power, entry, out, own):
+    comps, points, planes, radial = s.shape
+    return pl.pallas_call(
+        functools.partial(close_kernel, own=own),
+        name="close_own" if own else "close_other",
         out_shape=jax.ShapeDtypeStruct(s.shape, s.dtype),
-        in_specs=[SMEM] + [VMEM] * 4,
+        in_specs=[SMEM] + [VMEM] * 3 + [ANY] * len(out),
         out_specs=ANY,
         scratch_shapes=[
-            pltpu.VMEM(s.shape, jnp.float32),
-            pltpu.VMEM((2,) + s.shape[:1] + s.shape[2:], jnp.float32),
-            pltpu.SemaphoreType.DMA((s.shape[0],)),
+            pltpu.VMEM((comps, points, planes, radial // 2), jnp.float32),
+            pltpu.SemaphoreType.DMA((comps,)),
         ],
+        input_output_aliases={4: 0} if out else {},
         compiler_params=params(s.size * 4, 5),
-    )(me, s, power, mine, got)
+        cost_estimate=pl.CostEstimate(flops=4 * s.size, bytes_accessed=8 * s.size, transcendentals=0),
+    )(me, s, power, entry, *out)
 
 
 def local(velocity, radial_op, azimuth_stencil, viscous_factor):
@@ -585,10 +579,11 @@
     power, taps = table(me, viscous_factor, azimuth_stencil, points, sectors, planes, radial)
     n = inner_terms(taps, velocity, op)
     n = side_terms(core_kernel, "core_terms", me, taps, velocity, core_in, n)
+    n = mirror_terms(velocity, op, mirror_in, n)
     n = side_terms(late_kernel, "late_terms", me, taps, velocity, chip_in, n)
-    n = mirror_terms(velocity, op, mirror_in, n)
-    n, own, send = planes_terms(me, velocity, planes_in, power, n)
+    n, send = planes_terms(me, velocity, planes_in, power, n, False)
     other = swap(send, "theta", 1)
+    n, own = planes_terms(me, velocity, planes_in, power, n, True)
     s, nonlinear = sweep(velocity, n, power)
     block = pair(me, power, own, other, points)
     entries = ()
@@ -596,7 +591,9 @@
         block, entry = merge(me, power, block, swap(block, "theta", 1 << bit), entries, points, bit)
         entries = (entry,)
     mine, send = enter(me, power, block, entry, own, other, s, points)
-    new_velocity = close(me, s, power, mine, swap(send, "theta", 1))
+    got = swap(send, "theta", 1)
+    new_velocity = close(me, s, power, mine, (), True)
+    new_velocity = close(me, s, power, got, (new_velocity,), False)
     return (new_velocity, nonlinear)
 
 

time: 37 us -> 36.2 us (0.978)
  waiting for transfers between devices: 11.9 us -> 10.7 us
  Pallas kernels: 8.38 us -> 9.26 us
  starting transfers between devices: 15.1 us -> 14.6 us
    ppermute x1, waiting for transfers between devices: 3.39 us -> 0.01 us  [swap_across(): return lax.ppermute(block, axis, route)]
    ppermute x8, waiting for transfers between devices: 8.49 us -> 10.7 us  [swap(): return lax.ppermute(block, axis, [(i, i ^ bit) for i in range(size)])]
    pallas_call x2 -> x4, Pallas kernels: 1.69 us -> 2.31 us  [the longest x2 1.59 us: close(): pl.pallas_call(functools.partial(close_kernel, own=own), name='close_own'...]
    ppermute x8, starting transfers between devices: 11.4 us -> 10.8 us  [swap(): return lax.ppermute(block, axis, [(i, i ^ bit) for i in range(size)])]
  transfers between devices with their start and end apart: 9 -> 9, of which waited for: 7 -> 7; matrix products, arithmetic and copies ran while one was open for 0% -> 0% of each run, Pallas kernels for 15% -> 18%
where the time goes in v10:
time: 36.2 us; the launch traced here: 36 us
  starting transfers between devices  14.6 us (40%)
  waiting for transfers between devices  10.7 us (30%)
  Pallas kernels  9.26 us (26%)
  between operations  1.46 us (4%)
    ppermute x8, starting transfers between devices, swap(): return lax.ppermute(block, axis, [(i, i ^ bit) for i in range(size)])  10.8 us
    ppermute x8, waiting for transfers between devices, swap(): return lax.ppermute(block, axis, [(i, i ^ bit) for i in range(size)])  10.7 us
    ppermute x1, starting transfers between devices, swap_across(): return lax.ppermute(block, axis, route)  3.76 us
    pallas_call x1, Pallas kernels, inner_terms(): pl.pallas_call(inner_kernel, name='inner_terms', out_shape=held(*v.shape)...  2.2 us
    pallas_call x2, Pallas kernels, close(): pl.pallas_call(functools.partial(close_kernel, own=own), name='close_own'...  1.59 us
    pallas_call x1, Pallas kernels, load(): pl.pallas_call(load_kernel, name='load', out_shape=(held(*v.shape), held(...  1.42 us
    pallas_call x2, Pallas kernels, side_terms(): pl.pallas_call(kernel, name=name, out_shape=held(*v.shape), in_specs=[SME...  1.02 us
    pallas_call x1, Pallas kernels, sweep(): pl.pallas_call(sweep_kernel, name='sweep', out_shape=(held(*v.shape), jax...  0.89 us
  transfers between devices with their start and end apart: 9, of which 7 were waited for; matrix products, arithmetic and copies ran while one was open for 0% of the time, Pallas kernels for 18%

profile of v10, /device:TPU:0, one launch (start us, length us, event | category | flops | bytes accessed | tf_op | source)
XLA Modules:
  0.0 36.0 jit_solution(16908584463363712317)
XLA Ops:
  0.6 1.4 %load.1 = (f32[3,16,8,512]{3,2,1,0:T(8,128)S(1)}, f32[3,12,8,512]{3,2,1,0:T(8,128)S(1)}) custom-call(f32[3,16,8,512]{3,2,1,0:T(8,128)} %hbm_ref.1), custom_call_target="tpu_custom_call" | custom-call | tf_op jit(solution)/shard_map/load/pallas_call | solution.py:92
  2.1 3.0 %collective-permute-start = (f32[3,12,8,512]{3,2,1,0:T(8,128)S(1)}, f32[3,12,8,512]{3,2,1,0:T(8,128)S(1)}, u32[]{:S(2)}, u32[]{:S(2)}) collective-permute-start(f32[3,12,8,512]{3,2,1,0:T(8,128)S(1)} %get-tuple-element.21.first_ref), channel_id=1, source_target_pairs={{0,1},{1,0},{2,3},{3,2},{4,5},{5,4},{6,7},{7,6},{8,9},{9,8},{10,11... | collective-permute-start | bytes 1769480 | tf_op jit(solution)/shard_map/ppermute | solution.py:44
  5.1 3.8 %collective-permute-start.1 = (f32[3,10,8,512]{3,2,1,0:T(8,128)S(1)}, f32[3,10,8,512]{3,2,1,0:T(8,128)S(1)}, u32[]{:S(2)}, u32[]{:S(2)}) collective-permute-start(f32[3,10,8,512]{3,2,1,0:T(8,128)S(1)} %pack_chip.1.first_ref), channel_id=1, source_target_pairs={{2,4},{4,2},{6,8},{8,6},{10,12},{12,10},{14,16},{16,14},{18,20},{2... | collective-permute-start | bytes 1474568 | tf_op jit(solution)/shard_map/ppermute | solution.py:52
  10.1 0.6 %table.1 = (f32[30,512]{1,0:T(8,128)S(1)}, f32[21,8,128]{2,1,0:T(8,128)S(1)}) custom-call(s32[1]{0:T(128)} %bitcast.me_ref, f32[1]{0:T(128)S(6)} %copy.18.factor_ref, f32[21]{0:T(128)S(1)} %copy-done.1), custom_call_target="tpu_custom_call" | custom-call | flops 512000 | bytes 204800 | tf_op jit(solution)/shard_map/table/pallas_call | solution.py:387
  10.7 2.2 %inner_terms.1.n_in_ref = f32[3,16,8,512]{3,2,1,0:T(8,128)S(1)} custom-call(f32[21,8,128]{2,1,0:T(8,128)S(1)} %get-tuple-element.23.tap_ref, f32[3,16,8,512]{3,2,1,0:T(8,128)S(1)} %get-tuple-element.20.v_ref, f32[544,512]{1,0:T(8,128)S(1)} %bitcast.2), custom_call_target="tpu_custom_call" | custom-call | flops 5368709120 | bytes 3145728 | tf_op jit(solution)/shard_map/inner_terms/pallas_call | solution.py:253
  12.9 0.5 %core_terms.1.n_in_ref = f32[3,16,8,512]{3,2,1,0:T(8,128)S(1)} custom-call(s32[1]{0:T(128)} %bitcast.me_ref, f32[21,8,128]{2,1,0:T(8,128)S(1)} %get-tuple-element.23.tap_ref, f32[3,16,8,512]{3,2,1,0:T(8,128)S(1)} %get-tuple-element.20.v_ref, f32[3,10,8,512]{3,2,1,0:T(8,128)S(1)} %collective-permute-done.3.core_ref, ...), custom_call_target="tpu_custom_call", output_to_operand_aliasing={{}: (4, {})} | custom-call | flops 67108864 | bytes 2359296 | tf_op jit(solution)/shard_map/core_terms/pallas_call | solution.py:302
  13.5 3.3 %collective-permute-done.2.mirror_ref = f32[3,4,8,128]{3,2,1,0:T(8,128)S(1)} collective-permute-done((f32[3,4,8,128]{3,2,1,0:T(8,128)S(1)}, f32[3,4,8,128]{3,2,1,0:T(8,128)S(1)}, u32[]{:S(2)}, u32[]{:S(2)}) %collective-permute-start.2) | collective-permute-done | bytes 49184 | tf_op jit(solution)/shard_map/ppermute | solution.py:44
  16.7 0.5 %mirror_terms.1.n_in_ref = f32[3,16,8,512]{3,2,1,0:T(8,128)S(1)} custom-call(f32[3,16,8,512]{3,2,1,0:T(8,128)S(1)} %get-tuple-element.20.v_ref, f32[544,512]{1,0:T(8,128)S(1)} %bitcast.3, f32[3,4,8,128]{3,2,1,0:T(8,128)S(1)} %collective-permute-done.2.mirror_ref, f32[3,16,8,512]{3,2,1,0:T(8,128)S(1)} %core_terms.1.n_in_ref), custom_call_target="tpu_custom_call", output_to_operand_aliasing={{}: (3, {})} | custom-call | flops 67108864 | bytes 3145728 | tf_op jit(solution)/shard_map/mirror_terms/pallas_call | solution.py:208
  17.3 0.5 %late_terms.1.n_in_ref = f32[3,16,8,512]{3,2,1,0:T(8,128)S(1)} custom-call(s32[1]{0:T(128)} %bitcast.me_ref, f32[21,8,128]{2,1,0:T(8,128)S(1)} %get-tuple-element.23.tap_ref, f32[3,16,8,512]{3,2,1,0:T(8,128)S(1)} %get-tuple-element.20.v_ref, f32[3,10,8,512]{3,2,1,0:T(8,128)S(1)} %collective-permute-done.1.chip_ref, ...), custom_call_target="tpu_custom_call", output_to_operand_aliasing={{}: (4, {})} | custom-call | flops 67108864 | bytes 2359296 | tf_op jit(solution)/shard_map/late_terms/pallas_call | solution.py:302
  17.8 0.6 %collective-permute-done.y_ref = f32[3,12,8,512]{3,2,1,0:T(8,128)S(1)} collective-permute-done((f32[3,12,8,512]{3,2,1,0:T(8,128)S(1)}, f32[3,12,8,512]{3,2,1,0:T(8,128)S(1)}, u32[]{:S(2)}, u32[]{:S(2)}) %collective-permute-start) | collective-permute-done | bytes 589856 | tf_op jit(solution)/shard_map/ppermute | solution.py:44
  18.4 0.4 planes_other.1
  18.8 0.8 %collective-permute-start.4 = (f32[2,3,8,256]{3,2,1,0:T(8,128)S(1)}, f32[2,3,8,256]{3,2,1,0:T(8,128)S(1)}, u32[]{:S(2)}, u32[]{:S(2)}) collective-permute-start(f32[2,3,8,256]{3,2,1,0:T(8,128)S(1)} %get-tuple-element.28), channel_id=1, source_target_pairs={{0,2},{2,0},{4,6},{6,4},{8,10},{10,8},{12,14},{14,12},{16,18},{18,... | collective-permute-start | bytes 147464 | tf_op jit(solution)/shard_map/ppermute | solution.py:44
  19.6 0.4 planes_own.1
  19.9 0.5 %collective-permute-done.4.other_ref = f32[2,3,8,256]{3,2,1,0:T(8,128)S(1)} collective-permute-done((f32[2,3,8,256]{3,2,1,0:T(8,128)S(1)}, f32[2,3,8,256]{3,2,1,0:T(8,128)S(1)}, u32[]{:S(2)}, u32[]{:S(2)}) %collective-permute-start.4) | collective-permute-done | bytes 49184 | tf_op jit(solution)/shard_map/ppermute | solution.py:44
  20.5 2.0 %collective-permute-start.5 = (f32[2,3,8,256]{3,2,1,0:T(8,128)S(1)}, f32[2,3,8,256]{3,2,1,0:T(8,128)S(1)}, u32[]{:S(2)}, u32[]{:S(2)}) collective-permute-start(f32[2,3,8,256]{3,2,1,0:T(8,128)S(1)} %pair.1.block_ref), channel_id=1, source_target_pairs={{0,4},{2,6},{4,0},{6,2},{8,12},{10,14},{12,8},{14,10},{16,20},{18,... | collective-permute-start | bytes 147464 | tf_op jit(solution)/shard_map/ppermute | solution.py:44
  22.5 2.1 %collective-permute-done.5.other_ref = f32[2,3,8,256]{3,2,1,0:T(8,128)S(1)} collective-permute-done((f32[2,3,8,256]{3,2,1,0:T(8,128)S(1)}, f32[2,3,8,256]{3,2,1,0:T(8,128)S(1)}, u32[]{:S(2)}, u32[]{:S(2)}) %collective-permute-start.5) | collective-permute-done | bytes 49184 | tf_op jit(solution)/shard_map/ppermute | solution.py:44
  24.6 1.8 %collective-permute-start.6 = (f32[2,3,8,256]{3,2,1,0:T(8,128)S(1)}, f32[2,3,8,256]{3,2,1,0:T(8,128)S(1)}, u32[]{:S(2)}, u32[]{:S(2)}) collective-permute-start(f32[2,3,8,256]{3,2,1,0:T(8,128)S(1)} %get-tuple-element.29.block_ref), channel_id=1, source_target_pairs={{0,8},{2,10},{4,12},{6,14},{8,0},{10,2},{12,4},{14,6},{16,24},{18,... | collective-permute-start | bytes 147464 | tf_op jit(solution)/shard_map/ppermute | solution.py:44
  26.4 2.4 %collective-permute-done.6.other_ref = f32[2,3,8,256]{3,2,1,0:T(8,128)S(1)} collective-permute-done((f32[2,3,8,256]{3,2,1,0:T(8,128)S(1)}, f32[2,3,8,256]{3,2,1,0:T(8,128)S(1)}, u32[]{:S(2)}, u32[]{:S(2)}) %collective-permute-start.6) | collective-permute-done | bytes 49184 | tf_op jit(solution)/shard_map/ppermute | solution.py:44
  28.8 2.8 %collective-permute-start.7 = (f32[2,3,8,256]{3,2,1,0:T(8,128)S(1)}, f32[2,3,8,256]{3,2,1,0:T(8,128)S(1)}, u32[]{:S(2)}, u32[]{:S(2)}) collective-permute-start(f32[2,3,8,256]{3,2,1,0:T(8,128)S(1)} %get-tuple-element.31.block_ref), channel_id=1, source_target_pairs={{0,16},{2,18},{4,20},{6,22},{8,24},{10,26},{12,28},{14,30},{16,0},... | collective-permute-start | bytes 147464 | tf_op jit(solution)/shard_map/ppermute | solution.py:44
  31.6 0.9 %sweep.1 = (f32[3,16,8,512]{3,2,1,0:T(8,128)S(1)}, f32[3,16,8,512]{3,2,1,0:T(8,128)}) custom-call(f32[3,16,8,512]{3,2,1,0:T(8,128)S(1)} %get-tuple-element.20.v_ref, f32[3,16,8,512]{3,2,1,0:T(8,128)S(1)} %get-tuple-element.25.n_ref, f32[30,512]{1,0:T(8,128)S(1)} %get-tuple-element.22.power_ref), custom_call_target="tpu_custom_call" | custom-call | flops 1966080 | bytes 2359296 | tf_op jit(solution)/shard_map/sweep/pallas_call | solution.py:427
  32.5 1.4 %collective-permute-done.7.other_ref = f32[2,3,8,256]{3,2,1,0:T(8,128)S(1)} collective-permute-done((f32[2,3,8,256]{3,2,1,0:T(8,128)S(1)}, f32[2,3,8,256]{3,2,1,0:T(8,128)S(1)}, u32[]{:S(2)}, u32[]{:S(2)}) %collective-permute-start.7) | collective-permute-done | bytes 49184 | tf_op jit(solution)/shard_map/ppermute | solution.py:44
  34.0 0.8 %close_own.1.refs_0_ = f32[3,16,8,512]{3,2,1,0:T(8,128)} custom-call(s32[1]{0:T(128)} %bitcast.me_ref, f32[3,16,8,512]{3,2,1,0:T(8,128)S(1)} %get-tuple-element.26.ready_ref.s_ref, f32[30,512]{1,0:T(8,128)S(1)} %get-tuple-element.22.power_ref, f32[2,3,8,256]{3,2,1,0:T(8,128)S(1)} %get-tuple-element.36.entry_ref), custom_call_target="tpu_custom_call" | custom-call | flops 786432 | bytes 1572864 | tf_op jit(solution)/shard_map/close_own/pallas_call | solution.py:547
  34.8 0.4 %collective-permute-done.8.entry_ref = f32[2,3,8,256]{3,2,1,0:T(8,128)S(1)} collective-permute-done((f32[2,3,8,256]{3,2,1,0:T(8,128)S(1)}, f32[2,3,8,256]{3,2,1,0:T(8,128)S(1)}, u32[]{:S(2)}, u32[]{:S(2)}) %collective-permute-start.8) | collective-permute-done | bytes 49184 | tf_op jit(solution)/shard_map/ppermute | solution.py:44
  35.2 0.8 %close_other.1 = f32[3,16,8,512]{3,2,1,0:T(8,128)} custom-call(s32[1]{0:T(128)} %bitcast.me_ref, f32[3,16,8,512]{3,2,1,0:T(8,128)S(1)} %get-tuple-element.26.ready_ref.s_ref, f32[30,512]{1,0:T(8,128)S(1)} %get-tuple-element.22.power_ref, f32[2,3,8,256]{3,2,1,0:T(8,128)S(1)} %collective-permute-done.8.entry_ref, ...), custom_call_target="tpu_custom_call", output_to_operand_aliasing={{}: (4, {})} | custom-call | flops 786432 | bytes 1572864 | tf_op jit(solution)/shard_map/close_other/pallas_call | solution.py:547
  (17 shorter events, 0.7 us)
Async XLA Ops:
  2.1 16.4 %collective-permute-start = (f32[3,12,8,512]{3,2,1,0:T(8,128)S(1)}, f32[3,12,8,512]{3,2,1,0:T(8,128)S(1)}, u32[]{:S(2)}, u32[]{:S(2)}) collective-permute-start(f32[3,12,8,512]{3,2,1,0:T(8,128)S(1)} %get-tuple-element.21.first_ref), channel_id=1, source_target_pairs={{0,1},{1,0},{2,3},{3,2},{4,5},{5,4},{6,7},{7,6},{8,9},{9,8},{10,11... | collective-permute-start | bytes 1769480 | tf_op jit(solution)/shard_map/ppermute | solution.py:44
  5.1 4.9 %copy-start.1 = (f32[21]{0:T(128)S(1)}, f32[21]{0:T(128)}, u32[]{:S(2)}) copy-start(f32[21]{0:T(128)} %stencil_ref.1) | copy-start | bytes 256
  5.1 5.6 %copy-start = (f32[512,544]{0,1:T(8,128)S(1)}, f32[512,544]{0,1:T(8,128)}, u32[]{:S(2)}) copy-start(f32[512,544]{0,1:T(8,128)} %param.5) | copy-start | bytes 3342340
  5.1 12.1 %collective-permute-start.1 = (f32[3,10,8,512]{3,2,1,0:T(8,128)S(1)}, f32[3,10,8,512]{3,2,1,0:T(8,128)S(1)}, u32[]{:S(2)}, u32[]{:S(2)}) collective-permute-start(f32[3,10,8,512]{3,2,1,0:T(8,128)S(1)} %pack_chip.1.first_ref), channel_id=1, source_target_pairs={{2,4},{4,2},{6,8},{8,6},{10,12},{12,10},{14,16},{16,14},{18,20},{2... | collective-permute-start | bytes 1474568 | tf_op jit(solution)/shard_map/ppermute | solution.py:52
  9.0 7.7 %collective-permute-start.2 = (f32[3,4,8,128]{3,2,1,0:T(8,128)S(1)}, f32[3,4,8,128]{3,2,1,0:T(8,128)S(1)}, u32[]{:S(2)}, u32[]{:S(2)}) collective-permute-start(f32[3,4,8,128]{3,2,1,0:T(8,128)S(1)} %pack_mirror.1.first_ref), channel_id=1, source_target_pairs={{0,16},{2,18},{4,20},{6,22},{8,24},{10,26},{12,28},{14,30},{16,0},... | collective-permute-start | bytes 147464 | tf_op jit(solution)/shard_map/ppermute | solution.py:44
  9.1 3.8 %collective-permute-start.3 = (f32[3,10,8,512]{3,2,1,0:T(8,128)S(1)}, f32[3,10,8,512]{3,2,1,0:T(8,128)S(1)}, u32[]{:S(2)}, u32[]{:S(2)}) collective-permute-start(f32[3,10,8,512]{3,2,1,0:T(8,128)S(1)} %pack_core.1), channel_id=1, source_target_pairs={{0,2},{2,0},{4,6},{6,4},{8,10},{10,8},{12,14},{14,12},{16,18},{18,... | collective-permute-start | bytes 1474568 | tf_op jit(solution)/shard_map/ppermute | solution.py:44
  18.8 1.7 %collective-permute-start.4 = (f32[2,3,8,256]{3,2,1,0:T(8,128)S(1)}, f32[2,3,8,256]{3,2,1,0:T(8,128)S(1)}, u32[]{:S(2)}, u32[]{:S(2)}) collective-permute-start(f32[2,3,8,256]{3,2,1,0:T(8,128)S(1)} %get-tuple-element.28), channel_id=1, source_target_pairs={{0,2},{2,0},{4,6},{6,4},{8,10},{10,8},{12,14},{14,12},{16,18},{18,... | collective-permute-start | bytes 147464 | tf_op jit(solution)/shard_map/ppermute | solution.py:44
  20.5 4.2 %collective-permute-start.5 = (f32[2,3,8,256]{3,2,1,0:T(8,128)S(1)}, f32[2,3,8,256]{3,2,1,0:T(8,128)S(1)}, u32[]{:S(2)}, u32[]{:S(2)}) collective-permute-start(f32[2,3,8,256]{3,2,1,0:T(8,128)S(1)} %pair.1.block_ref), channel_id=1, source_target_pairs={{0,4},{2,6},{4,0},{6,2},{8,12},{10,14},{12,8},{14,10},{16,20},{18,... | collective-permute-start | bytes 147464 | tf_op jit(solution)/shard_map/ppermute | solution.py:44
  24.6 4.2 %collective-permute-start.6 = (f32[2,3,8,256]{3,2,1,0:T(8,128)S(1)}, f32[2,3,8,256]{3,2,1,0:T(8,128)S(1)}, u32[]{:S(2)}, u32[]{:S(2)}) collective-permute-start(f32[2,3,8,256]{3,2,1,0:T(8,128)S(1)} %get-tuple-element.29.block_ref), channel_id=1, source_target_pairs={{0,8},{2,10},{4,12},{6,14},{8,0},{10,2},{12,4},{14,6},{16,24},{18,... | collective-permute-start | bytes 147464 | tf_op jit(solution)/shard_map/ppermute | solution.py:44
  28.8 5.1 %collective-permute-start.7 = (f32[2,3,8,256]{3,2,1,0:T(8,128)S(1)}, f32[2,3,8,256]{3,2,1,0:T(8,128)S(1)}, u32[]{:S(2)}, u32[]{:S(2)}) collective-permute-start(f32[2,3,8,256]{3,2,1,0:T(8,128)S(1)} %get-tuple-element.31.block_ref), channel_id=1, source_target_pairs={{0,16},{2,18},{4,20},{6,22},{8,24},{10,26},{12,28},{14,30},{16,0},... | collective-permute-start | bytes 147464 | tf_op jit(solution)/shard_map/ppermute | solution.py:44
  33.9 1.3 %collective-permute-start.8 = (f32[2,3,8,256]{3,2,1,0:T(8,128)S(1)}, f32[2,3,8,256]{3,2,1,0:T(8,128)S(1)}, u32[]{:S(2)}, u32[]{:S(2)}) collective-permute-start(f32[2,3,8,256]{3,2,1,0:T(8,128)S(1)} %get-tuple-element.35), channel_id=1, source_target_pairs={{0,2},{2,0},{4,6},{6,4},{8,10},{10,8},{12,14},{14,12},{16,18},{18,... | collective-permute-start | bytes 147464 | tf_op jit(solution)/shard_map/ppermute | solution.py:44

commit v11 on v10

--- a/solution.py
+++ b/solution.py
@@ -62,29 +62,48 @@
     return dot(left[0], right[0]) + (dot(left[0], right[1]) + dot(left[1], right[0]))
 
 
-def load_kernel(hbm_ref, v_ref, y_ref, sems):
-    comps, points, planes, _ = v_ref.shape
+def pack_tiles(v_ref, y_ref, comps):
+    points, planes = v_ref.shape[1:3]
     carriers = y_ref.shape[1]
     lo, hi = AXIAL_REACH, planes - AXIAL_REACH
-    loads = []
-    for c in range(comps):
-        ways = ((hbm_ref.at[c], v_ref.at[c]), (hbm_ref.at[c, pl.ds(0, carriers)], y_ref.at[c]))
-        loads.append([pltpu.make_async_copy(*way, sems.at[k, c]) for k, way in enumerate(ways)])
-    for c in range(comps):
-        for way in loads[c]:
-            way.start()
-    for c in range(comps):
-        for way in loads[c]:
-            way.wait()
+    for i, c in enumerate(comps):
+
+        def carry(t):
+            y_ref[i, t] = v_ref[c, t]
 
         def ride(j):
             t = carriers + j
-            y_ref[c, 3 * j, lo:hi] = v_ref[c, t, 0:2]
-            y_ref[c, 3 * j + 1, lo : lo + 1] = v_ref[c, t, 2:3]
-            y_ref[c, 3 * j + 1, lo + 1 : hi] = v_ref[c, t, hi : hi + 1]
-            y_ref[c, 3 * j + 2, lo:hi] = v_ref[c, t, hi + 1 :]
-
+            y_ref[i, 3 * j, lo:hi] = v_ref[c, t, 0:2]
+            y_ref[i, 3 * j + 1, lo : lo + 1] = v_ref[c, t, 2:3]
+            y_ref[i, 3 * j + 1, lo + 1 : hi] = v_ref[c, t, hi : hi + 1]
+            y_ref[i, 3 * j + 2, lo:hi] = v_ref[c, t, hi + 1 :]
+
+        each(carriers, carry)
         each(points - carriers, ride)
+
+
+def rebuild_tiles(y_ref, tile_ref):
+    carriers = y_ref.shape[1]
+    comps, riders, planes, radial = tile_ref.shape
+    lo, hi = AXIAL_REACH, planes - AXIAL_REACH
+    for c in range(comps):
+        for j in range(riders):
+            tile_ref[c, j, 0:2] = y_ref[c, 3 * j, lo:hi]
+            tile_ref[c, j, 2:3] = y_ref[c, 3 * j + 1, lo : lo + 1]
+            tile_ref[c, j, lo:hi] = jnp.zeros((hi - lo, radial), jnp.float32)
+            tile_ref[c, j, hi : hi + 1] = y_ref[c, 3 * j + 1, lo + 1 : hi]
+            tile_ref[c, j, hi + 1 :] = y_ref[c, 3 * j + 2, lo:hi]
+
+
+def load_kernel(hbm_ref, v_ref, y_ref, sems):
+    order = list(range(v_ref.shape[0]))
+    loads = [pltpu.make_async_copy(hbm_ref.at[c], v_ref.at[c], sems.at[c]) for c in order]
+    for c in reversed(order):
+        loads[c].start()
+    loads[-1].wait()
+    pack_tiles(v_ref, y_ref, order[-1:])
+    for c in order[:-1]:
+        loads[c].wait()
 
 
 def load(v):
@@ -92,12 +111,28 @@
     return pl.pallas_call(
         load_kernel,
         name="load",
-        out_shape=(held(*v.shape), held(comps, points - points // 4, planes, radial)),
+        out_shape=(held(*v.shape), held(1, points - points // 4, planes, radial)),
         in_specs=[HBM],
         out_specs=(VMEM, VMEM),
-        scratch_shapes=[pltpu.SemaphoreType.DMA((2, comps))],
+        scratch_shapes=[pltpu.SemaphoreType.DMA((comps,))],
         compiler_params=params(v.size * 4, 2),
     )(v)
+
+
+def pack_planes_kernel(v_ref, first_ref, y_ref):
+    pack_tiles(v_ref, y_ref, range(y_ref.shape[0]))
+
+
+def pack_planes(v, first):
+    comps, points, planes, radial = v.shape
+    return pl.pallas_call(
+        pack_planes_kernel,
+        name="pack_planes",
+        out_shape=held(comps - 1, points - points // 4, planes, radial),
+        in_specs=[VMEM, ANY],
+        out_specs=VMEM,
+        compiler_params=params(v.size * 4, 2),
+    )(v, first)
 
 
 def pack_side_kernel(me_ref, v_ref, first_ref, side_ref, *, after):
@@ -311,45 +346,89 @@
     )(me, taps, v, side, n)
 
 
-def planes_kernel(me_ref, v_ref, y_ref, power_ref, n_in_ref, n_ref, ends_ref, tile_ref, *, own):
+def share_kernel(v_ref, e_ref, power_ref, ends_ref, tile_ref):
     comps, points, planes, radial = v_ref.shape
-    half = radial // 2
-    carriers = y_ref.shape[1]
-    lo, hi = AXIAL_REACH, planes - AXIAL_REACH
+    carriers = e_ref.shape[1]
     weights = axial_weights(planes, False)
-    lanes = half_lanes(me_ref, half, own)
-    for c in range(comps):
-        for j in range(points - carriers):
-            tile_ref[c, j, 0:2] = y_ref[c, 3 * j, lo:hi, lanes]
-            tile_ref[c, j, 2:3] = y_ref[c, 3 * j + 1, lo : lo + 1, lanes]
-            tile_ref[c, j, lo:hi] = jnp.zeros((hi - lo, half), jnp.float32)
-            tile_ref[c, j, hi : hi + 1] = y_ref[c, 3 * j + 1, lo + 1 : hi, lanes]
-            tile_ref[c, j, hi + 1 :] = y_ref[c, 3 * j + 2, lo:hi, lanes]
-    decay = power_ref[1:2, lanes]
+    rebuild_tiles(e_ref, tile_ref)
+    decay = power_ref[1:2]
     ends_ref[...] = jnp.zeros_like(ends_ref)
     for t in range(points):
+        e = STEP_WEIGHT * (e_ref[0, t] if t < carriers else tile_ref[0, t - carriers])
         for c in range(comps):
-            tile = y_ref[c, t, :, lanes] if t < carriers else tile_ref[c, t - carriers]
-            n = n_in_ref[c, t, :, lanes] + v_ref[2, t, :, lanes] * axial_part(tile, weights)
-            n_ref[c, t, :, lanes] = n
-            right_side = v_ref[c, t, :, lanes] - STEP_WEIGHT * n
-            ends_ref[0, c] = decay * ends_ref[0, c] + right_side
-            ends_ref[1, c] = ends_ref[1, c] + power_ref[t : t + 1, lanes] * right_side
-
-
-def planes_terms(me, v, y, power, n, own):
+            right_side = e * axial_part(v_ref[c, t], weights)
+            ends_ref[0, c] = decay * ends_ref[0, c] - right_side
+            ends_ref[1, c] = ends_ref[1, c] - power_ref[t : t + 1] * right_side
+
+
+def share_terms(v, e, power):
     comps, points, planes, radial = v.shape
     return pl.pallas_call(
-        functools.partial(planes_kernel, own=own),
-        name="planes_own" if own else "planes_other",
-        out_shape=(held(*v.shape), held(2, comps, planes, radial // 2)),
+        share_kernel,
+        name="share_terms",
+        out_shape=held(2, comps, planes, radial),
+        in_specs=[VMEM] * 3,
+        out_specs=VMEM,
+        scratch_shapes=[pltpu.VMEM((1, points - e.shape[1], planes, radial), jnp.float32)],
+        compiler_params=params(v.size * 4, 4),
+        cost_estimate=pl.CostEstimate(flops=20 * v.size, bytes_accessed=8 * v.size, transcendentals=0),
+    )(v, e, power)
+
+
+def ends_kernel(me_ref, v_ref, share_ref, power_ref, n_ref, ends_ref, *, own):
+    comps, points, _, radial = v_ref.shape
+    lanes = half_lanes(me_ref, radial // 2, own)
+    decay = power_ref[1:2, lanes]
+    for c in range(comps):
+        low = high = None
+        for t in range(points):
+            right_side = v_ref[c, t, :, lanes] - STEP_WEIGHT * n_ref[c, t, :, lanes]
+            low = right_side if t == 0 else decay * low + right_side
+            high = right_side if t == 0 else high + power_ref[t : t + 1, lanes] * right_side
+        ends_ref[0, c] = low + share_ref[0, c, :, lanes]
+        ends_ref[1, c] = high + share_ref[1, c, :, lanes]
+
+
+def ends_terms(me, v, share, power, n, own):
+    comps, _, planes, radial = v.shape
+    return pl.pallas_call(
+        functools.partial(ends_kernel, own=own),
+        name="ends_own" if own else "ends_other",
+        out_shape=held(2, comps, planes, radial // 2),
         in_specs=[SMEM] + [VMEM] * 4,
-        out_specs=(VMEM, VMEM),
-        scratch_shapes=[pltpu.VMEM((comps, points - y.shape[1], planes, radial // 2), jnp.float32)],
+        out_specs=VMEM,
+        compiler_params=params(v.size * 4, 4),
+        cost_estimate=pl.CostEstimate(flops=20 * v.size, bytes_accessed=8 * v.size, transcendentals=0),
+    )(me, v, share, power, n)
+
+
+def planes_kernel(v_ref, y_ref, e_ref, ready_ref, n_in_ref, n_ref, y_tile_ref, e_tile_ref):
+    comps, points, planes, _ = v_ref.shape
+    carriers = y_ref.shape[1]
+    weights = axial_weights(planes, False)
+    rebuild_tiles(y_ref, y_tile_ref)
+    rebuild_tiles(e_ref, e_tile_ref)
+    for t in range(points):
+        for c in range(comps):
+            ref, tile_ref, i = (y_ref, y_tile_ref, c) if c < comps - 1 else (e_ref, e_tile_ref, 0)
+            tile = ref[i, t] if t < carriers else tile_ref[i, t - carriers]
+            n_ref[c, t] = n_in_ref[c, t] + v_ref[2, t] * axial_part(tile, weights)
+
+
+def planes_terms(v, y, e, ready, n):
+    comps, points, planes, radial = v.shape
+    riders = points - y.shape[1]
+    return pl.pallas_call(
+        planes_kernel,
+        name="planes_terms",
+        out_shape=held(*v.shape),
+        in_specs=[VMEM] * 3 + [ANY, VMEM],
+        out_specs=VMEM,
+        scratch_shapes=[pltpu.VMEM((k, riders, planes, radial), jnp.float32) for k in (comps - 1, 1)],
         input_output_aliases={4: 0},
         compiler_params=params(v.size * 4, 6),
         cost_estimate=pl.CostEstimate(flops=20 * v.size, bytes_accessed=16 * v.size, transcendentals=0),
-    )(me, v, y, power, n)
+    )(v, y, e, ready, n)
 
 
 def table_kernel(me_ref, factor_ref, stencil_ref, row_ref, tap_ref, *, points, sectors):
@@ -568,9 +647,9 @@
     me = lax.axis_index("theta").astype(jnp.int32).reshape(1)
     op = radial_op.T
 
-    velocity, planes_out = load(pltpu.with_memory_space_constraint(velocity, pltpu.HBM))
-    planes_in = swap(planes_out, "gz", 1)
-    chip_out = pack_side(me, velocity, planes_out, reach, False)
+    velocity, axial_out = load(pltpu.with_memory_space_constraint(velocity, pltpu.HBM))
+    axial_in = swap(axial_out, "gz", 1)
+    chip_out = pack_side(me, velocity, axial_out, reach, False)
     chip_in = swap_across(chip_out, "theta")
     mirror_out = pack_mirror(velocity, chip_out, width)
     mirror_in = swap(mirror_out, "theta", sectors // 2)
@@ -578,16 +657,22 @@
     core_in = swap(core_out, "theta", 1)
     power, taps = table(me, viscous_factor, azimuth_stencil, points, sectors, planes, radial)
     n = inner_terms(taps, velocity, op)
+    share_out = share_terms(velocity, axial_in, power)
+    share_in = swap(share_out, "gz", 1)
+    planes_in = swap(pack_planes(velocity, share_out), "gz", 1)
     n = side_terms(core_kernel, "core_terms", me, taps, velocity, core_in, n)
     n = mirror_terms(velocity, op, mirror_in, n)
     n = side_terms(late_kernel, "late_terms", me, taps, velocity, chip_in, n)
-    n, send = planes_terms(me, velocity, planes_in, power, n, False)
+    send = ends_terms(me, velocity, share_in, power, n, False)
     other = swap(send, "theta", 1)
-    n, own = planes_terms(me, velocity, planes_in, power, n, True)
-    s, nonlinear = sweep(velocity, n, power)
+    own = ends_terms(me, velocity, share_in, power, n, True)
     block = pair(me, power, own, other, points)
     entries = ()
-    for bit in range(1, sectors.bit_length() - 1):
+    last = sectors.bit_length() - 2
+    for bit in range(1, last + 1):
+        if bit == last:
+            n = planes_terms(velocity, planes_in, axial_in, block, n)
+            s, nonlinear = sweep(velocity, n, power)
         block, entry = merge(me, power, block, swap(block, "theta", 1 << bit), entries, points, bit)
         entries = (entry,)
     mine, send = enter(me, power, block, entry, own, other, s, points)

time: 36.2 us -> 35.9 us (level)
  waiting for transfers between devices: 10.7 us -> 7.52 us
  starting transfers between devices: 14.6 us -> 17.1 us
  Pallas kernels: 9.26 us -> 9.68 us
    ppermute x8 -> x10, waiting for transfers between devices: 10.7 us -> 7.52 us  [swap(): return lax.ppermute(block, axis, [(i, i ^ bit) for i in range(size)])]
    ppermute x8 -> x10, starting transfers between devices: 10.8 us -> 13.3 us  [swap(): return lax.ppermute(block, axis, [(i, i ^ bit) for i in range(size)])]
    pallas_call x2 -> x5, Pallas kernels: 0.72 us -> 1.42 us  [the longest x1 0.61 us: share_terms(): pl.pallas_call(share_kernel, name='share_terms', out_shape=held(2, comps,...]
  transfers between devices with their start and end apart: 9 -> 11, of which waited for: 7 -> 6; matrix products, arithmetic and copies ran while one was open for 0% -> 0% of each run, Pallas kernels for 18% -> 22%
where the time goes in v11:
time: 35.9 us; the launch traced here: 35.8 us
  starting transfers between devices  17.1 us (48%)
  Pallas kernels  9.68 us (27%)
  waiting for transfers between devices  7.52 us (21%)
  between operations  1.48 us (4%)
    ppermute x10, starting transfers between devices, swap(): return lax.ppermute(block, axis, [(i, i ^ bit) for i in range(size)])  13.3 us
    ppermute x10, waiting for transfers between devices, swap(): return lax.ppermute(block, axis, [(i, i ^ bit) for i in range(size)])  7.52 us
    ppermute x1, starting transfers between devices, swap_across(): return lax.ppermute(block, axis, route)  3.76 us
    pallas_call x1, Pallas kernels, inner_terms(): pl.pallas_call(inner_kernel, name='inner_terms', out_shape=held(*v.shape)...  2.2 us
    pallas_call x2, Pallas kernels, close(): pl.pallas_call(functools.partial(close_kernel, own=own), name='close_own'...  1.59 us
    pallas_call x1, Pallas kernels, load(): pl.pallas_call(load_kernel, name='load', out_shape=(held(*v.shape), held(...  1.14 us
    pallas_call x2, Pallas kernels, side_terms(): pl.pallas_call(kernel, name=name, out_shape=held(*v.shape), in_specs=[SME...  1.02 us
    pallas_call x1, Pallas kernels, sweep(): pl.pallas_call(sweep_kernel, name='sweep', out_shape=(held(*v.shape), jax...  0.89 us
  transfers between devices with their start and end apart: 11, of which 6 were waited for; matrix products, arithmetic and copies ran while one was open for 0% of the time, Pallas kernels for 22%

profile of v11, /device:TPU:0, one launch (start us, length us, event | category | flops | bytes accessed | tf_op | source)
XLA Modules:
  0.0 35.8 jit_solution(11389769181560845700)
XLA Ops:
  0.6 1.1 %load.1 = (f32[3,16,8,512]{3,2,1,0:T(8,128)S(1)}, f32[1,12,8,512]{3,2,1,0:T(8,128)S(1)}) custom-call(f32[3,16,8,512]{3,2,1,0:T(8,128)} %hbm_ref.1), custom_call_target="tpu_custom_call" | custom-call | tf_op jit(solution)/shard_map/load/pallas_call | solution.py:111
  1.8 3.0 %collective-permute-start = (f32[1,12,8,512]{3,2,1,0:T(8,128)S(1)}, f32[1,12,8,512]{3,2,1,0:T(8,128)S(1)}, u32[]{:S(2)}, u32[]{:S(2)}) collective-permute-start(f32[1,12,8,512]{3,2,1,0:T(8,128)S(1)} %get-tuple-element.17.first_ref), channel_id=1, source_target_pairs={{0,1},{1,0},{2,3},{3,2},{4,5},{5,4},{6,7},{7,6},{8,9},{9,8},{10,11... | collective-permute-start | bytes 589832 | tf_op jit(solution)/shard_map/ppermute | solution.py:44
  4.9 3.8 %collective-permute-start.3 = (f32[3,10,8,512]{3,2,1,0:T(8,128)S(1)}, f32[3,10,8,512]{3,2,1,0:T(8,128)S(1)}, u32[]{:S(2)}, u32[]{:S(2)}) collective-permute-start(f32[3,10,8,512]{3,2,1,0:T(8,128)S(1)} %pack_chip.1.first_ref), channel_id=1, source_target_pairs={{2,4},{4,2},{6,8},{8,6},{10,12},{12,10},{14,16},{16,14},{18,20},{2... | collective-permute-start | bytes 1474568 | tf_op jit(solution)/shard_map/ppermute | solution.py:52
  9.8 0.6 %table.1 = (f32[30,512]{1,0:T(8,128)S(1)}, f32[21,8,128]{2,1,0:T(8,128)S(1)}) custom-call(s32[1]{0:T(128)} %bitcast.me_ref, f32[1]{0:T(128)S(6)} %copy.16.factor_ref, f32[21]{0:T(128)S(1)} %copy-done.1), custom_call_target="tpu_custom_call" | custom-call | flops 512000 | bytes 204800 | tf_op jit(solution)/shard_map/table/pallas_call | solution.py:466
  10.4 0.6 %share_terms.1.first_ref = f32[2,3,8,512]{3,2,1,0:T(8,128)S(1)} custom-call(f32[3,16,8,512]{3,2,1,0:T(8,128)S(1)} %get-tuple-element.16.v_ref, f32[1,12,8,512]{3,2,1,0:T(8,128)S(1)} %collective-permute-done.e_ref, f32[30,512]{1,0:T(8,128)S(1)} %get-tuple-element.18.power_ref), custom_call_target="tpu_custom_call" | custom-call | flops 3932160 | bytes 1572864 | tf_op jit(solution)/shard_map/share_terms/pallas_call | solution.py:366
  11.0 1.1 %collective-permute-start.2 = (f32[2,3,8,512]{3,2,1,0:T(8,128)S(1)}, f32[2,3,8,512]{3,2,1,0:T(8,128)S(1)}, u32[]{:S(2)}, u32[]{:S(2)}) collective-permute-start(f32[2,3,8,512]{3,2,1,0:T(8,128)S(1)} %share_terms.1.first_ref), channel_id=1, source_target_pairs={{0,1},{1,0},{2,3},{3,2},{4,5},{5,4},{6,7},{7,6},{8,9},{9,8},{10,11... | collective-permute-start | bytes 294920 | tf_op jit(solution)/shard_map/ppermute | solution.py:44
  12.2 1.1 %collective-permute-start.1 = (f32[2,12,8,512]{3,2,1,0:T(8,128)S(1)}, f32[2,12,8,512]{3,2,1,0:T(8,128)S(1)}, u32[]{:S(2)}, u32[]{:S(2)}) collective-permute-start(f32[2,12,8,512]{3,2,1,0:T(8,128)S(1)} %pack_planes.1), channel_id=1, source_target_pairs={{0,1},{1,0},{2,3},{3,2},{4,5},{5,4},{6,7},{7,6},{8,9},{9,8},{10,11... | collective-permute-start | bytes 1179656 | tf_op jit(solution)/shard_map/ppermute | solution.py:44
  13.3 2.2 %inner_terms.1.n_in_ref = f32[3,16,8,512]{3,2,1,0:T(8,128)S(1)} custom-call(f32[21,8,128]{2,1,0:T(8,128)S(1)} %get-tuple-element.19.tap_ref, f32[3,16,8,512]{3,2,1,0:T(8,128)S(1)} %get-tuple-element.16.v_ref, f32[544,512]{1,0:T(8,128)S(1)} %bitcast.2), custom_call_target="tpu_custom_call" | custom-call | flops 5368709120 | bytes 3145728 | tf_op jit(solution)/shard_map/inner_terms/pallas_call | solution.py:288
  15.5 0.5 %core_terms.1.n_in_ref = f32[3,16,8,512]{3,2,1,0:T(8,128)S(1)} custom-call(s32[1]{0:T(128)} %bitcast.me_ref, f32[21,8,128]{2,1,0:T(8,128)S(1)} %get-tuple-element.19.tap_ref, f32[3,16,8,512]{3,2,1,0:T(8,128)S(1)} %get-tuple-element.16.v_ref, f32[3,10,8,512]{3,2,1,0:T(8,128)S(1)} %collective-permute-done.5.core_ref, ...), custom_call_target="tpu_custom_call", output_to_operand_aliasing={{}: (4, {})} | custom-call | flops 67108864 | bytes 2359296 | tf_op jit(solution)/shard_map/core_terms/pallas_call | solution.py:337
  16.0 0.4 %collective-permute-done.4.mirror_ref = f32[3,4,8,128]{3,2,1,0:T(8,128)S(1)} collective-permute-done((f32[3,4,8,128]{3,2,1,0:T(8,128)S(1)}, f32[3,4,8,128]{3,2,1,0:T(8,128)S(1)}, u32[]{:S(2)}, u32[]{:S(2)}) %collective-permute-start.4) | collective-permute-done | bytes 49184 | tf_op jit(solution)/shard_map/ppermute | solution.py:44
  16.4 0.5 %mirror_terms.1.n_in_ref = f32[3,16,8,512]{3,2,1,0:T(8,128)S(1)} custom-call(f32[3,16,8,512]{3,2,1,0:T(8,128)S(1)} %get-tuple-element.16.v_ref, f32[544,512]{1,0:T(8,128)S(1)} %bitcast.3, f32[3,4,8,128]{3,2,1,0:T(8,128)S(1)} %collective-permute-done.4.mirror_ref, f32[3,16,8,512]{3,2,1,0:T(8,128)S(1)} %core_terms.1.n_in_ref), custom_call_target="tpu_custom_call", output_to_operand_aliasing={{}: (3, {})} | custom-call | flops 67108864 | bytes 3145728 | tf_op jit(solution)/shard_map/mirror_terms/pallas_call | solution.py:243
  17.0 0.5 %late_terms.1.n_ref.n_in_ref = f32[3,16,8,512]{3,2,1,0:T(8,128)S(1)} custom-call(s32[1]{0:T(128)} %bitcast.me_ref, f32[21,8,128]{2,1,0:T(8,128)S(1)} %get-tuple-element.19.tap_ref, f32[3,16,8,512]{3,2,1,0:T(8,128)S(1)} %get-tuple-element.16.v_ref, f32[3,10,8,512]{3,2,1,0:T(8,128)S(1)} %collective-permute-done.3.chip_ref, ...), custom_call_target="tpu_custom_call", output_to_operand_aliasing={{}: (4, {})} | custom-call | flops 67108864 | bytes 2359296 | tf_op jit(solution)/shard_map/late_terms/pallas_call | solution.py:337
  17.6 1.7 %collective-permute-start.6 = (f32[2,3,8,256]{3,2,1,0:T(8,128)S(1)}, f32[2,3,8,256]{3,2,1,0:T(8,128)S(1)}, u32[]{:S(2)}, u32[]{:S(2)}) collective-permute-start(f32[2,3,8,256]{3,2,1,0:T(8,128)S(1)} %ends_other.1), channel_id=1, source_target_pairs={{0,2},{2,0},{4,6},{6,4},{8,10},{10,8},{12,14},{14,12},{16,18},{18,... | collective-permute-start | bytes 147464 | tf_op jit(solution)/shard_map/ppermute | solution.py:44
  19.4 0.8 %collective-permute-done.6.other_ref = f32[2,3,8,256]{3,2,1,0:T(8,128)S(1)} collective-permute-done((f32[2,3,8,256]{3,2,1,0:T(8,128)S(1)}, f32[2,3,8,256]{3,2,1,0:T(8,128)S(1)}, u32[]{:S(2)}, u32[]{:S(2)}) %collective-permute-start.6) | collective-permute-done | bytes 49184 | tf_op jit(solution)/shard_map/ppermute | solution.py:44
  20.2 1.7 %collective-permute-start.7 = (f32[2,3,8,256]{3,2,1,0:T(8,128)S(1)}, f32[2,3,8,256]{3,2,1,0:T(8,128)S(1)}, u32[]{:S(2)}, u32[]{:S(2)}) collective-permute-start(f32[2,3,8,256]{3,2,1,0:T(8,128)S(1)} %pair.1.block_ref), channel_id=1, source_target_pairs={{0,4},{2,6},{4,0},{6,2},{8,12},{10,14},{12,8},{14,10},{16,20},{18,... | collective-permute-start | bytes 147464 | tf_op jit(solution)/shard_map/ppermute | solution.py:44
  21.9 2.4 %collective-permute-done.7.other_ref = f32[2,3,8,256]{3,2,1,0:T(8,128)S(1)} collective-permute-done((f32[2,3,8,256]{3,2,1,0:T(8,128)S(1)}, f32[2,3,8,256]{3,2,1,0:T(8,128)S(1)}, u32[]{:S(2)}, u32[]{:S(2)}) %collective-permute-start.7) | collective-permute-done | bytes 49184 | tf_op jit(solution)/shard_map/ppermute | solution.py:44
  24.4 1.6 %collective-permute-start.8 = (f32[2,3,8,256]{3,2,1,0:T(8,128)S(1)}, f32[2,3,8,256]{3,2,1,0:T(8,128)S(1)}, u32[]{:S(2)}, u32[]{:S(2)}) collective-permute-start(f32[2,3,8,256]{3,2,1,0:T(8,128)S(1)} %get-tuple-element.20.block_ref), channel_id=1, source_target_pairs={{0,8},{2,10},{4,12},{6,14},{8,0},{10,2},{12,4},{14,6},{16,24},{18,... | collective-permute-start | bytes 147464 | tf_op jit(solution)/shard_map/ppermute | solution.py:44
  26.0 2.5 %collective-permute-done.8.other_ref = f32[2,3,8,256]{3,2,1,0:T(8,128)S(1)} collective-permute-done((f32[2,3,8,256]{3,2,1,0:T(8,128)S(1)}, f32[2,3,8,256]{3,2,1,0:T(8,128)S(1)}, u32[]{:S(2)}, u32[]{:S(2)}) %collective-permute-start.8) | collective-permute-done | bytes 49184 | tf_op jit(solution)/shard_map/ppermute | solution.py:44
  28.6 2.7 %collective-permute-start.9 = (f32[2,3,8,256]{3,2,1,0:T(8,128)S(1)}, f32[2,3,8,256]{3,2,1,0:T(8,128)S(1)}, u32[]{:S(2)}, u32[]{:S(2)}) collective-permute-start(f32[2,3,8,256]{3,2,1,0:T(8,128)S(1)} %get-tuple-element.22.ready_ref.block_ref), channel_id=1, source_target_pairs={{0,16},{2,18},{4,20},{6,22},{8,24},{10,26},{12,28},{14,30},{16,0},... | collective-permute-start | bytes 147464 | tf_op jit(solution)/shard_map/ppermute | solution.py:44
  31.2 0.5 %planes_terms.1.n_ref = f32[3,16,8,512]{3,2,1,0:T(8,128)S(1)} custom-call(f32[3,16,8,512]{3,2,1,0:T(8,128)S(1)} %get-tuple-element.16.v_ref, f32[2,12,8,512]{3,2,1,0:T(8,128)S(1)} %collective-permute-done.1.y_ref, f32[1,12,8,512]{3,2,1,0:T(8,128)S(1)} %collective-permute-done.e_ref, ...), custom_call_target="tpu_custom_call", output_to_operand_aliasing={{}: (4, {})} | custom-call | flops 3932160 | bytes 3145728 | tf_op jit(solution)/shard_map/planes_terms/pallas_call | solution.py:421
  31.8 0.9 %sweep.1 = (f32[3,16,8,512]{3,2,1,0:T(8,128)S(1)}, f32[3,16,8,512]{3,2,1,0:T(8,128)}) custom-call(f32[3,16,8,512]{3,2,1,0:T(8,128)S(1)} %get-tuple-element.16.v_ref, f32[3,16,8,512]{3,2,1,0:T(8,128)S(1)} %planes_terms.1.n_ref, f32[30,512]{1,0:T(8,128)S(1)} %get-tuple-element.18.power_ref), custom_call_target="tpu_custom_call" | custom-call | flops 1966080 | bytes 2359296 | tf_op jit(solution)/shard_map/sweep/pallas_call | solution.py:506
  32.7 0.9 %collective-permute-done.9.other_ref = f32[2,3,8,256]{3,2,1,0:T(8,128)S(1)} collective-permute-done((f32[2,3,8,256]{3,2,1,0:T(8,128)S(1)}, f32[2,3,8,256]{3,2,1,0:T(8,128)S(1)}, u32[]{:S(2)}, u32[]{:S(2)}) %collective-permute-start.9) | collective-permute-done | bytes 49184 | tf_op jit(solution)/shard_map/ppermute | solution.py:44
  33.8 0.8 %close_own.1.refs_0_ = f32[3,16,8,512]{3,2,1,0:T(8,128)} custom-call(s32[1]{0:T(128)} %bitcast.me_ref, f32[3,16,8,512]{3,2,1,0:T(8,128)S(1)} %get-tuple-element.23.ready_ref.s_ref, f32[30,512]{1,0:T(8,128)S(1)} %get-tuple-element.18.power_ref, f32[2,3,8,256]{3,2,1,0:T(8,128)S(1)} %get-tuple-element.28.entry_ref), custom_call_target="tpu_custom_call" | custom-call | flops 786432 | bytes 1572864 | tf_op jit(solution)/shard_map/close_own/pallas_call | solution.py:626
  35.0 0.8 %close_other.1 = f32[3,16,8,512]{3,2,1,0:T(8,128)} custom-call(s32[1]{0:T(128)} %bitcast.me_ref, f32[3,16,8,512]{3,2,1,0:T(8,128)S(1)} %get-tuple-element.23.ready_ref.s_ref, f32[30,512]{1,0:T(8,128)S(1)} %get-tuple-element.18.power_ref, f32[2,3,8,256]{3,2,1,0:T(8,128)S(1)} %collective-permute-done.10.entry_ref, ...), custom_call_target="tpu_custom_call", output_to_operand_aliasing={{}: (4, {})} | custom-call | flops 786432 | bytes 1572864 | tf_op jit(solution)/shard_map/close_other/pallas_call | solution.py:626
  (24 shorter events, 1.4 us)
Async XLA Ops:
  1.8 8.6 %collective-permute-start = (f32[1,12,8,512]{3,2,1,0:T(8,128)S(1)}, f32[1,12,8,512]{3,2,1,0:T(8,128)S(1)}, u32[]{:S(2)}, u32[]{:S(2)}) collective-permute-start(f32[1,12,8,512]{3,2,1,0:T(8,128)S(1)} %get-tuple-element.17.first_ref), channel_id=1, source_target_pairs={{0,1},{1,0},{2,3},{3,2},{4,5},{5,4},{6,7},{7,6},{8,9},{9,8},{10,11... | collective-permute-start | bytes 589832 | tf_op jit(solution)/shard_map/ppermute | solution.py:44
  4.8 4.9 %copy-start.1 = (f32[21]{0:T(128)S(1)}, f32[21]{0:T(128)}, u32[]{:S(2)}) copy-start(f32[21]{0:T(128)} %stencil_ref.1) | copy-start | bytes 256
  4.9 12.1 %collective-permute-start.3 = (f32[3,10,8,512]{3,2,1,0:T(8,128)S(1)}, f32[3,10,8,512]{3,2,1,0:T(8,128)S(1)}, u32[]{:S(2)}, u32[]{:S(2)}) collective-permute-start(f32[3,10,8,512]{3,2,1,0:T(8,128)S(1)} %pack_chip.1.first_ref), channel_id=1, source_target_pairs={{2,4},{4,2},{6,8},{8,6},{10,12},{12,10},{14,16},{16,14},{18,20},{2... | collective-permute-start | bytes 1474568 | tf_op jit(solution)/shard_map/ppermute | solution.py:52
  8.7 7.7 %collective-permute-start.4 = (f32[3,4,8,128]{3,2,1,0:T(8,128)S(1)}, f32[3,4,8,128]{3,2,1,0:T(8,128)S(1)}, u32[]{:S(2)}, u32[]{:S(2)}) collective-permute-start(f32[3,4,8,128]{3,2,1,0:T(8,128)S(1)} %pack_mirror.1.first_ref), channel_id=1, source_target_pairs={{0,16},{2,18},{4,20},{6,22},{8,24},{10,26},{12,28},{14,30},{16,0},... | collective-permute-start | bytes 147464 | tf_op jit(solution)/shard_map/ppermute | solution.py:44
  8.9 6.6 %collective-permute-start.5 = (f32[3,10,8,512]{3,2,1,0:T(8,128)S(1)}, f32[3,10,8,512]{3,2,1,0:T(8,128)S(1)}, u32[]{:S(2)}, u32[]{:S(2)}) collective-permute-start(f32[3,10,8,512]{3,2,1,0:T(8,128)S(1)} %pack_core.1), channel_id=1, source_target_pairs={{0,2},{2,0},{4,6},{6,4},{8,10},{10,8},{12,14},{14,12},{16,18},{18,... | collective-permute-start | bytes 1474568 | tf_op jit(solution)/shard_map/ppermute | solution.py:44
  10.4 2.9 %copy-start = (f32[512,544]{0,1:T(8,128)S(1)}, f32[512,544]{0,1:T(8,128)}, u32[]{:S(2)}) copy-start(f32[512,544]{0,1:T(8,128)} %param.5) | copy-start | bytes 3342340
  11.0 6.4 %collective-permute-start.2 = (f32[2,3,8,512]{3,2,1,0:T(8,128)S(1)}, f32[2,3,8,512]{3,2,1,0:T(8,128)S(1)}, u32[]{:S(2)}, u32[]{:S(2)}) collective-permute-start(f32[2,3,8,512]{3,2,1,0:T(8,128)S(1)} %share_terms.1.first_ref), channel_id=1, source_target_pairs={{0,1},{1,0},{2,3},{3,2},{4,5},{5,4},{6,7},{7,6},{8,9},{9,8},{10,11... | collective-permute-start | bytes 294920 | tf_op jit(solution)/shard_map/ppermute | solution.py:44
  12.2 19.0 %collective-permute-start.1 = (f32[2,12,8,512]{3,2,1,0:T(8,128)S(1)}, f32[2,12,8,512]{3,2,1,0:T(8,128)S(1)}, u32[]{:S(2)}, u32[]{:S(2)}) collective-permute-start(f32[2,12,8,512]{3,2,1,0:T(8,128)S(1)} %pack_planes.1), channel_id=1, source_target_pairs={{0,1},{1,0},{2,3},{3,2},{4,5},{5,4},{6,7},{7,6},{8,9},{9,8},{10,11... | collective-permute-start | bytes 1179656 | tf_op jit(solution)/shard_map/ppermute | solution.py:44
  17.6 2.6 %collective-permute-start.6 = (f32[2,3,8,256]{3,2,1,0:T(8,128)S(1)}, f32[2,3,8,256]{3,2,1,0:T(8,128)S(1)}, u32[]{:S(2)}, u32[]{:S(2)}) collective-permute-start(f32[2,3,8,256]{3,2,1,0:T(8,128)S(1)} %ends_other.1), channel_id=1, source_target_pairs={{0,2},{2,0},{4,6},{6,4},{8,10},{10,8},{12,14},{14,12},{16,18},{18,... | collective-permute-start | bytes 147464 | tf_op jit(solution)/shard_map/ppermute | solution.py:44
  20.2 4.2 %collective-permute-start.7 = (f32[2,3,8,256]{3,2,1,0:T(8,128)S(1)}, f32[2,3,8,256]{3,2,1,0:T(8,128)S(1)}, u32[]{:S(2)}, u32[]{:S(2)}) collective-permute-start(f32[2,3,8,256]{3,2,1,0:T(8,128)S(1)} %pair.1.block_ref), channel_id=1, source_target_pairs={{0,4},{2,6},{4,0},{6,2},{8,12},{10,14},{12,8},{14,10},{16,20},{18,... | collective-permute-start | bytes 147464 | tf_op jit(solution)/shard_map/ppermute | solution.py:44
  24.4 4.2 %collective-permute-start.8 = (f32[2,3,8,256]{3,2,1,0:T(8,128)S(1)}, f32[2,3,8,256]{3,2,1,0:T(8,128)S(1)}, u32[]{:S(2)}, u32[]{:S(2)}) collective-permute-start(f32[2,3,8,256]{3,2,1,0:T(8,128)S(1)} %get-tuple-element.20.block_ref), channel_id=1, source_target_pairs={{0,8},{2,10},{4,12},{6,14},{8,0},{10,2},{12,4},{14,6},{16,24},{18,... | collective-permute-start | bytes 147464 | tf_op jit(solution)/shard_map/ppermute | solution.py:44
  28.6 5.1 %collective-permute-start.9 = (f32[2,3,8,256]{3,2,1,0:T(8,128)S(1)}, f32[2,3,8,256]{3,2,1,0:T(8,128)S(1)}, u32[]{:S(2)}, u32[]{:S(2)}) collective-permute-start(f32[2,3,8,256]{3,2,1,0:T(8,128)S(1)} %get-tuple-element.22.ready_ref.block_ref), channel_id=1, source_target_pairs={{0,16},{2,18},{4,20},{6,22},{8,24},{10,26},{12,28},{14,30},{16,0},... | collective-permute-start | bytes 147464 | tf_op jit(solution)/shard_map/ppermute | solution.py:44
  33.7 1.3 %collective-permute-start.10 = (f32[2,3,8,256]{3,2,1,0:T(8,128)S(1)}, f32[2,3,8,256]{3,2,1,0:T(8,128)S(1)}, u32[]{:S(2)}, u32[]{:S(2)}) collective-permute-start(f32[2,3,8,256]{3,2,1,0:T(8,128)S(1)} %get-tuple-element.27), channel_id=1, source_target_pairs={{0,2},{2,0},{4,6},{6,4},{8,10},{10,8},{12,14},{14,12},{16,18},{18,... | collective-permute-start | bytes 147464 | tf_op jit(solution)/shard_map/ppermute | solution.py:44

commit v12 on v11

--- a/solution.py
+++ b/solution.py
@@ -11,9 +11,10 @@
 AXIAL_REACH = len(AXIAL_WEIGHTS)
 STEP_WEIGHT = 0.2
 MIRROR_SIGNS = (-1.0, -1.0, 1.0)
+CORE_PARTS = ((0, 1), (2,))
 LANES = 128
 UNROLL = 16
-INNER = 10 << 29
+INNER = 1 << 31
 MIRROR = 1 << 26
 SIDE = 1 << 26
 
@@ -135,13 +136,14 @@
     )(v, first)
 
 
-def pack_side_kernel(me_ref, v_ref, first_ref, side_ref, *, after):
-    points, reach = v_ref.shape[1], side_ref.shape[1]
+def pack_side_kernel(me_ref, v_ref, first_ref, *side_refs, after, parts):
+    points, reach = v_ref.shape[1], side_refs[0].shape[1]
 
     def put(start):
-        for c in range(v_ref.shape[0]):
-            for h in range(reach):
-                side_ref[c, h] = v_ref[c, start + h]
+        for side_ref, part in zip(side_refs, parts):
+            for i, c in enumerate(part):
+                for h in range(reach):
+                    side_ref[i, h] = v_ref[c, start + h]
 
     even = me_ref[0] % 2 == 0
     last = even if after else jnp.logical_not(even)
@@ -149,14 +151,14 @@
     pl.when(jnp.logical_not(last))(lambda: put(0))
 
 
-def pack_side(me, v, first, reach, after):
-    comps, _, planes, radial = v.shape
-    return pl.pallas_call(
-        functools.partial(pack_side_kernel, after=after),
+def pack_side(me, v, first, reach, after, parts):
+    _, _, planes, radial = v.shape
+    return pl.pallas_call(
+        functools.partial(pack_side_kernel, after=after, parts=parts),
         name="pack_core" if after else "pack_chip",
-        out_shape=held(comps, reach, planes, radial),
+        out_shape=tuple(held(len(part), reach, planes, radial) for part in parts),
         in_specs=[SMEM, VMEM, ANY],
-        out_specs=VMEM,
+        out_specs=(VMEM,) * len(parts),
         compiler_params=params(v.size * 4, 3),
     )(me, v, first)
 
@@ -297,9 +299,10 @@
     )(taps, v, op)
 
 
-def add_side(tap_ref, v_ref, side_ref, n_in_ref, n_ref, before):
+def add_side(tap_ref, v_ref, side_refs, n_in_ref, n_ref, before):
     comps, points, _, radial = v_ref.shape
-    reach = side_ref.shape[1]
+    reach = side_refs[0].shape[1]
+    sides = [(ref, i) for ref in side_refs for i in range(ref.shape[0])]
     first = 0 if before else reach + 1
 
     @pl.loop(0, radial // LANES)
@@ -308,7 +311,8 @@
         inv_r = inverse_radius(LANES, k * LANES)
         weights = [tap_ref[first + i] for i in range(reach)]
         for c in range(comps):
-            side = [side_ref[c, h, :, lanes] for h in range(reach)]
+            ref, i = sides[c]
+            side = [ref[i, h, :, lanes] for h in range(reach)]
             for u in range(reach):
                 t = u if before else points - reach + u
                 taps = [(h, h - u) for h in range(u, reach)] if before else [(h, reach - 1 + h - u) for h in range(u + 1)]
@@ -319,31 +323,33 @@
                 n_ref[c, t, :, lanes] = n_in_ref[c, t, :, lanes] + v_ref[1, t, :, lanes] * inv_r * around
 
 
-def core_kernel(me_ref, tap_ref, v_ref, core_ref, n_in_ref, n_ref):
+def core_kernel(me_ref, tap_ref, v_ref, *refs):
+    *core_refs, n_in_ref, n_ref = refs
     even = me_ref[0] % 2 == 0
-    add = functools.partial(add_side, tap_ref, v_ref, core_ref, n_in_ref, n_ref)
+    add = functools.partial(add_side, tap_ref, v_ref, core_refs, n_in_ref, n_ref)
     pl.when(even)(lambda: add(False))
     pl.when(jnp.logical_not(even))(lambda: add(True))
 
 
-def late_kernel(me_ref, tap_ref, v_ref, chip_ref, n_in_ref, n_ref):
+def late_kernel(me_ref, tap_ref, v_ref, *refs):
+    *chip_refs, n_in_ref, n_ref = refs
     even = me_ref[0] % 2 == 0
-    add = functools.partial(add_side, tap_ref, v_ref, chip_ref, n_in_ref, n_ref)
+    add = functools.partial(add_side, tap_ref, v_ref, chip_refs, n_in_ref, n_ref)
     pl.when(even)(lambda: add(True))
     pl.when(jnp.logical_not(even))(lambda: add(False))
 
 
-def side_terms(kernel, name, me, taps, v, side, n):
+def side_terms(kernel, name, me, taps, v, sides, n):
     return pl.pallas_call(
         kernel,
         name=name,
         out_shape=held(*v.shape),
-        in_specs=[SMEM, VMEM, VMEM, VMEM, VMEM],
-        out_specs=VMEM,
-        input_output_aliases={4: 0},
+        in_specs=[SMEM] + [VMEM] * (3 + len(sides)),
+        out_specs=VMEM,
+        input_output_aliases={3 + len(sides): 0},
         compiler_params=params(v.size * 4, 5),
         cost_estimate=pl.CostEstimate(flops=SIDE, bytes_accessed=12 * v.size, transcendentals=0),
-    )(me, taps, v, side, n)
+    )(me, taps, v, *sides, n)
 
 
 def share_kernel(v_ref, e_ref, power_ref, ends_ref, tile_ref):
@@ -649,12 +655,13 @@
 
     velocity, axial_out = load(pltpu.with_memory_space_constraint(velocity, pltpu.HBM))
     axial_in = swap(axial_out, "gz", 1)
-    chip_out = pack_side(me, velocity, axial_out, reach, False)
-    chip_in = swap_across(chip_out, "theta")
-    mirror_out = pack_mirror(velocity, chip_out, width)
+    everything = (tuple(range(comps)),)
+    chip_out = pack_side(me, velocity, axial_out, reach, False, everything)
+    chip_in = [swap_across(part, "theta") for part in chip_out]
+    mirror_out = pack_mirror(velocity, chip_out[0], width)
     mirror_in = swap(mirror_out, "theta", sectors // 2)
-    core_out = pack_side(me, velocity, mirror_out, reach, True)
-    core_in = swap(core_out, "theta", 1)
+    core_out = pack_side(me, velocity, mirror_out, reach, True, CORE_PARTS)
+    core_in = [swap(part, "theta", 1) for part in core_out]
     power, taps = table(me, viscous_factor, azimuth_stencil, points, sectors, planes, radial)
     n = inner_terms(taps, velocity, op)
     share_out = share_terms(velocity, axial_in, power)

time: 35.9 us -> 37.1 us (1.033)
  waiting for transfers between devices: 7.52 us -> 14 us
  starting transfers between devices: 17.1 us -> 11.8 us
    ppermute x10 -> x11, starting transfers between devices: 13.3 us -> 6.3 us  [swap(): return lax.ppermute(block, axis, [(i, i ^ bit) for i in range(size)])]
    ppermute x10 -> x11, waiting for transfers between devices: 7.52 us -> 14 us  [swap(): return lax.ppermute(block, axis, [(i, i ^ bit) for i in range(size)])]
    ppermute x1, starting transfers between devices: 3.76 us -> 5.48 us  [swap_across(): return lax.ppermute(block, axis, route)]
  transfers between devices with their start and end apart: 11 -> 12, of which waited for: 6 -> 6; matrix products, arithmetic and copies ran while one was open for 0% -> 0% of each run, Pallas kernels for 22% -> 21%
where the time goes in v12:
time: 37.1 us; the launch traced here: 36.9 us
  waiting for transfers between devices  14 us (38%)
  starting transfers between devices  11.8 us (32%)
  Pallas kernels  9.69 us (26%)
  between operations  1.51 us (4%)
    ppermute x11, waiting for transfers between devices, swap(): return lax.ppermute(block, axis, [(i, i ^ bit) for i in range(size)])  14 us
    ppermute x11, starting transfers between devices, swap(): return lax.ppermute(block, axis, [(i, i ^ bit) for i in range(size)])  6.3 us
    ppermute x1, starting transfers between devices, swap_across(): return lax.ppermute(block, axis, route)  5.48 us
    pallas_call x1, Pallas kernels, inner_terms(): pl.pallas_call(inner_kernel, name='inner_terms', out_shape=held(*v.shape)...  2.2 us
    pallas_call x2, Pallas kernels, close(): pl.pallas_call(functools.partial(close_kernel, own=own), name='close_own'...  1.59 us
    pallas_call x1, Pallas kernels, load(): pl.pallas_call(load_kernel, name='load', out_shape=(held(*v.shape), held(...  1.14 us
    pallas_call x2, Pallas kernels, side_terms(): pl.pallas_call(kernel, name=name, out_shape=held(*v.shape), in_specs=[SME...  1 us
    pallas_call x1, Pallas kernels, sweep(): pl.pallas_call(sweep_kernel, name='sweep', out_shape=(held(*v.shape), jax...  0.89 us
  transfers between devices with their start and end apart: 12, of which 6 were waited for; matrix products, arithmetic and copies ran while one was open for 0% of the time, Pallas kernels for 21%

profile of v12, /device:TPU:0, one launch (start us, length us, event | category | flops | bytes accessed | tf_op | source)
XLA Modules:
  0.0 36.9 jit_solution(5042523498443723306)
XLA Ops:
  0.6 1.1 %load.1 = (f32[3,16,8,512]{3,2,1,0:T(8,128)S(1)}, f32[1,12,8,512]{3,2,1,0:T(8,128)S(1)}) custom-call(f32[3,16,8,512]{3,2,1,0:T(8,128)} %hbm_ref.1), custom_call_target="tpu_custom_call" | custom-call | tf_op jit(solution)/shard_map/load/pallas_call | solution.py:112
  1.8 5.5 %collective-permute-start.3 = (f32[3,10,8,512]{3,2,1,0:T(8,128)S(1)}, f32[3,10,8,512]{3,2,1,0:T(8,128)S(1)}, u32[]{:S(2)}, u32[]{:S(2)}) collective-permute-start(f32[3,10,8,512]{3,2,1,0:T(8,128)S(1)} %pack_chip.1.first_ref), channel_id=1, source_target_pairs={{2,4},{4,2},{6,8},{8,6},{10,12},{12,10},{14,16},{16,14},{18,20},{2... | collective-permute-start | bytes 1474568 | tf_op jit(solution)/shard_map/ppermute | solution.py:53
  7.3 1.5 %collective-permute-start = (f32[1,12,8,512]{3,2,1,0:T(8,128)S(1)}, f32[1,12,8,512]{3,2,1,0:T(8,128)S(1)}, u32[]{:S(2)}, u32[]{:S(2)}) collective-permute-start(f32[1,12,8,512]{3,2,1,0:T(8,128)S(1)} %get-tuple-element.19.first_ref), channel_id=1, source_target_pairs={{0,1},{1,0},{2,3},{3,2},{4,5},{5,4},{6,7},{7,6},{8,9},{9,8},{10,11... | collective-permute-start | bytes 589832 | tf_op jit(solution)/shard_map/ppermute | solution.py:45
  9.1 0.5 %collective-permute-start.5 = (f32[2,10,8,512]{3,2,1,0:T(8,128)S(1)}, f32[2,10,8,512]{3,2,1,0:T(8,128)S(1)}, u32[]{:S(2)}, u32[]{:S(2)}) collective-permute-start(f32[2,10,8,512]{3,2,1,0:T(8,128)S(1)} %get-tuple-element.22), channel_id=1, source_target_pairs={{0,2},{2,0},{4,6},{6,4},{8,10},{10,8},{12,14},{14,12},{16,18},{18,... | collective-permute-start | bytes 983048 | tf_op jit(solution)/shard_map/ppermute | solution.py:45
  10.3 0.6 %table.1 = (f32[30,512]{1,0:T(8,128)S(1)}, f32[21,8,128]{2,1,0:T(8,128)S(1)}) custom-call(s32[1]{0:T(128)} %bitcast.me_ref, f32[1]{0:T(128)S(6)} %copy.16.factor_ref, f32[21]{0:T(128)S(1)} %copy-done.1), custom_call_target="tpu_custom_call" | custom-call | flops 512000 | bytes 204800 | tf_op jit(solution)/shard_map/table/pallas_call | solution.py:472
  10.9 2.1 %collective-permute-done.e_ref = f32[1,12,8,512]{3,2,1,0:T(8,128)S(1)} collective-permute-done((f32[1,12,8,512]{3,2,1,0:T(8,128)S(1)}, f32[1,12,8,512]{3,2,1,0:T(8,128)S(1)}, u32[]{:S(2)}, u32[]{:S(2)}) %collective-permute-start) | collective-permute-done | bytes 196640 | tf_op jit(solution)/shard_map/ppermute | solution.py:45
  13.0 0.6 %share_terms.1.first_ref = f32[2,3,8,512]{3,2,1,0:T(8,128)S(1)} custom-call(f32[3,16,8,512]{3,2,1,0:T(8,128)S(1)} %get-tuple-element.18.v_ref, f32[1,12,8,512]{3,2,1,0:T(8,128)S(1)} %collective-permute-done.e_ref, f32[30,512]{1,0:T(8,128)S(1)} %get-tuple-element.20.power_ref), custom_call_target="tpu_custom_call" | custom-call | flops 3932160 | bytes 1572864 | tf_op jit(solution)/shard_map/share_terms/pallas_call | solution.py:372
  13.6 1.6 %collective-permute-start.2 = (f32[2,3,8,512]{3,2,1,0:T(8,128)S(1)}, f32[2,3,8,512]{3,2,1,0:T(8,128)S(1)}, u32[]{:S(2)}, u32[]{:S(2)}) collective-permute-start(f32[2,3,8,512]{3,2,1,0:T(8,128)S(1)} %share_terms.1.first_ref), channel_id=1, source_target_pairs={{0,1},{1,0},{2,3},{3,2},{4,5},{5,4},{6,7},{7,6},{8,9},{9,8},{10,11... | collective-permute-start | bytes 294920 | tf_op jit(solution)/shard_map/ppermute | solution.py:45
  15.3 0.6 %collective-permute-start.1 = (f32[2,12,8,512]{3,2,1,0:T(8,128)S(1)}, f32[2,12,8,512]{3,2,1,0:T(8,128)S(1)}, u32[]{:S(2)}, u32[]{:S(2)}) collective-permute-start(f32[2,12,8,512]{3,2,1,0:T(8,128)S(1)} %pack_planes.1), channel_id=1, source_target_pairs={{0,1},{1,0},{2,3},{3,2},{4,5},{5,4},{6,7},{7,6},{8,9},{9,8},{10,11... | collective-permute-start | bytes 1179656 | tf_op jit(solution)/shard_map/ppermute | solution.py:45
  15.8 2.2 %inner_terms.1.refs_2_ = f32[3,16,8,512]{3,2,1,0:T(8,128)S(1)} custom-call(f32[21,8,128]{2,1,0:T(8,128)S(1)} %get-tuple-element.21.tap_ref, f32[3,16,8,512]{3,2,1,0:T(8,128)S(1)} %get-tuple-element.18.v_ref, f32[544,512]{1,0:T(8,128)S(1)} %bitcast.2), custom_call_target="tpu_custom_call" | custom-call | flops 2147483648 | bytes 3145728 | tf_op jit(solution)/shard_map/inner_terms/pallas_call | solution.py:290
  18.1 0.5 %core_terms.1.n_in_ref = f32[3,16,8,512]{3,2,1,0:T(8,128)S(1)} custom-call(s32[1]{0:T(128)} %bitcast.me_ref, f32[21,8,128]{2,1,0:T(8,128)S(1)} %get-tuple-element.21.tap_ref, f32[3,16,8,512]{3,2,1,0:T(8,128)S(1)} %get-tuple-element.18.v_ref, f32[2,10,8,512]{3,2,1,0:T(8,128)S(1)} %collective-permute-done.5.refs_0_, ...), custom_call_target="tpu_custom_call", output_to_operand_aliasing={{}: (5, {})} | custom-call | flops 67108864 | bytes 2359296 | tf_op jit(solution)/shard_map/core_terms/pallas_call | solution.py:343
  18.6 0.5 %mirror_terms.1.refs_1_ = f32[3,16,8,512]{3,2,1,0:T(8,128)S(1)} custom-call(f32[3,16,8,512]{3,2,1,0:T(8,128)S(1)} %get-tuple-element.18.v_ref, f32[544,512]{1,0:T(8,128)S(1)} %bitcast.3, f32[3,4,8,128]{3,2,1,0:T(8,128)S(1)} %collective-permute-done.4.mirror_ref, f32[3,16,8,512]{3,2,1,0:T(8,128)S(1)} %core_terms.1.n_in_ref), custom_call_target="tpu_custom_call", output_to_operand_aliasing={{}: (3, {})} | custom-call | flops 67108864 | bytes 3145728 | tf_op jit(solution)/shard_map/mirror_terms/pallas_call | solution.py:245
  19.1 0.5 %late_terms.1.n_ref.n_in_ref = f32[3,16,8,512]{3,2,1,0:T(8,128)S(1)} custom-call(s32[1]{0:T(128)} %bitcast.me_ref, f32[21,8,128]{2,1,0:T(8,128)S(1)} %get-tuple-element.21.tap_ref, f32[3,16,8,512]{3,2,1,0:T(8,128)S(1)} %get-tuple-element.18.v_ref, f32[3,10,8,512]{3,2,1,0:T(8,128)S(1)} %collective-permute-done.3.refs_0_, ...), custom_call_target="tpu_custom_call", output_to_operand_aliasing={{}: (4, {})} | custom-call | flops 67108864 | bytes 2359296 | tf_op jit(solution)/shard_map/late_terms/pallas_call | solution.py:343
  19.9 1.1 %collective-permute-done.7.other_ref = f32[2,3,8,256]{3,2,1,0:T(8,128)S(1)} collective-permute-done((f32[2,3,8,256]{3,2,1,0:T(8,128)S(1)}, f32[2,3,8,256]{3,2,1,0:T(8,128)S(1)}, u32[]{:S(2)}, u32[]{:S(2)}) %collective-permute-start.7) | collective-permute-done | bytes 49184 | tf_op jit(solution)/shard_map/ppermute | solution.py:45
  21.1 4.1 %collective-permute-done.8.other_ref = f32[2,3,8,256]{3,2,1,0:T(8,128)S(1)} collective-permute-done((f32[2,3,8,256]{3,2,1,0:T(8,128)S(1)}, f32[2,3,8,256]{3,2,1,0:T(8,128)S(1)}, u32[]{:S(2)}, u32[]{:S(2)}) %collective-permute-start.8) | collective-permute-done | bytes 49184 | tf_op jit(solution)/shard_map/ppermute | solution.py:45
  25.2 0.4 %collective-permute-start.9 = (f32[2,3,8,256]{3,2,1,0:T(8,128)S(1)}, f32[2,3,8,256]{3,2,1,0:T(8,128)S(1)}, u32[]{:S(2)}, u32[]{:S(2)}) collective-permute-start(f32[2,3,8,256]{3,2,1,0:T(8,128)S(1)} %get-tuple-element.24.block_ref), channel_id=1, source_target_pairs={{0,8},{2,10},{4,12},{6,14},{8,0},{10,2},{12,4},{14,6},{16,24},{18,... | collective-permute-start | bytes 147464 | tf_op jit(solution)/shard_map/ppermute | solution.py:45
  25.7 3.7 %collective-permute-done.9.other_ref = f32[2,3,8,256]{3,2,1,0:T(8,128)S(1)} collective-permute-done((f32[2,3,8,256]{3,2,1,0:T(8,128)S(1)}, f32[2,3,8,256]{3,2,1,0:T(8,128)S(1)}, u32[]{:S(2)}, u32[]{:S(2)}) %collective-permute-start.9) | collective-permute-done | bytes 49184 | tf_op jit(solution)/shard_map/ppermute | solution.py:45
  29.4 1.4 %collective-permute-start.10 = (f32[2,3,8,256]{3,2,1,0:T(8,128)S(1)}, f32[2,3,8,256]{3,2,1,0:T(8,128)S(1)}, u32[]{:S(2)}, u32[]{:S(2)}) collective-permute-start(f32[2,3,8,256]{3,2,1,0:T(8,128)S(1)} %get-tuple-element.26.ready_ref.block_ref), channel_id=1, source_target_pairs={{0,16},{2,18},{4,20},{6,22},{8,24},{10,26},{12,28},{14,30},{16,0},... | collective-permute-start | bytes 147464 | tf_op jit(solution)/shard_map/ppermute | solution.py:45
  30.8 0.5 %planes_terms.1.n_ref = f32[3,16,8,512]{3,2,1,0:T(8,128)S(1)} custom-call(f32[3,16,8,512]{3,2,1,0:T(8,128)S(1)} %get-tuple-element.18.v_ref, f32[2,12,8,512]{3,2,1,0:T(8,128)S(1)} %collective-permute-done.1.y_ref, f32[1,12,8,512]{3,2,1,0:T(8,128)S(1)} %collective-permute-done.e_ref, ...), custom_call_target="tpu_custom_call", output_to_operand_aliasing={{}: (4, {})} | custom-call | flops 3932160 | bytes 3145728 | tf_op jit(solution)/shard_map/planes_terms/pallas_call | solution.py:427
  31.4 0.9 %sweep.1 = (f32[3,16,8,512]{3,2,1,0:T(8,128)S(1)}, f32[3,16,8,512]{3,2,1,0:T(8,128)}) custom-call(f32[3,16,8,512]{3,2,1,0:T(8,128)S(1)} %get-tuple-element.18.v_ref, f32[3,16,8,512]{3,2,1,0:T(8,128)S(1)} %planes_terms.1.n_ref, f32[30,512]{1,0:T(8,128)S(1)} %get-tuple-element.20.power_ref), custom_call_target="tpu_custom_call" | custom-call | flops 1966080 | bytes 2359296 | tf_op jit(solution)/shard_map/sweep/pallas_call | solution.py:512
  32.3 2.5 %collective-permute-done.10.other_ref = f32[2,3,8,256]{3,2,1,0:T(8,128)S(1)} collective-permute-done((f32[2,3,8,256]{3,2,1,0:T(8,128)S(1)}, f32[2,3,8,256]{3,2,1,0:T(8,128)S(1)}, u32[]{:S(2)}, u32[]{:S(2)}) %collective-permute-start.10) | collective-permute-done | bytes 49184 | tf_op jit(solution)/shard_map/ppermute | solution.py:45
  34.9 0.8 %close_own.1.refs_0_ = f32[3,16,8,512]{3,2,1,0:T(8,128)} custom-call(s32[1]{0:T(128)} %bitcast.me_ref, f32[3,16,8,512]{3,2,1,0:T(8,128)S(1)} %get-tuple-element.27.ready_ref.s_ref, f32[30,512]{1,0:T(8,128)S(1)} %get-tuple-element.20.power_ref, f32[2,3,8,256]{3,2,1,0:T(8,128)S(1)} %get-tuple-element.32.entry_ref), custom_call_target="tpu_custom_call" | custom-call | flops 786432 | bytes 1572864 | tf_op jit(solution)/shard_map/close_own/pallas_call | solution.py:632
  35.7 0.4 %collective-permute-done.11.entry_ref = f32[2,3,8,256]{3,2,1,0:T(8,128)S(1)} collective-permute-done((f32[2,3,8,256]{3,2,1,0:T(8,128)S(1)}, f32[2,3,8,256]{3,2,1,0:T(8,128)S(1)}, u32[]{:S(2)}, u32[]{:S(2)}) %collective-permute-start.11) | collective-permute-done | bytes 49184 | tf_op jit(solution)/shard_map/ppermute | solution.py:45
  36.1 0.8 %close_other.1 = f32[3,16,8,512]{3,2,1,0:T(8,128)} custom-call(s32[1]{0:T(128)} %bitcast.me_ref, f32[3,16,8,512]{3,2,1,0:T(8,128)S(1)} %get-tuple-element.27.ready_ref.s_ref, f32[30,512]{1,0:T(8,128)S(1)} %get-tuple-element.20.power_ref, f32[2,3,8,256]{3,2,1,0:T(8,128)S(1)} %collective-permute-done.11.entry_ref, ...), custom_call_target="tpu_custom_call", output_to_operand_aliasing={{}: (4, {})} | custom-call | flops 786432 | bytes 1572864 | tf_op jit(solution)/shard_map/close_other/pallas_call | solution.py:632
  (26 shorter events, 0.9 us)
Async XLA Ops:
  1.8 8.4 %copy-start.1 = (f32[21]{0:T(128)S(1)}, f32[21]{0:T(128)}, u32[]{:S(2)}) copy-start(f32[21]{0:T(128)} %stencil_ref.1) | copy-start | bytes 256
  1.8 17.3 %collective-permute-start.3 = (f32[3,10,8,512]{3,2,1,0:T(8,128)S(1)}, f32[3,10,8,512]{3,2,1,0:T(8,128)S(1)}, u32[]{:S(2)}, u32[]{:S(2)}) collective-permute-start(f32[3,10,8,512]{3,2,1,0:T(8,128)S(1)} %pack_chip.1.first_ref), channel_id=1, source_target_pairs={{2,4},{4,2},{6,8},{8,6},{10,12},{12,10},{14,16},{16,14},{18,20},{2... | collective-permute-start | bytes 1474568 | tf_op jit(solution)/shard_map/ppermute | solution.py:53
  7.3 5.7 %collective-permute-start = (f32[1,12,8,512]{3,2,1,0:T(8,128)S(1)}, f32[1,12,8,512]{3,2,1,0:T(8,128)S(1)}, u32[]{:S(2)}, u32[]{:S(2)}) collective-permute-start(f32[1,12,8,512]{3,2,1,0:T(8,128)S(1)} %get-tuple-element.19.first_ref), channel_id=1, source_target_pairs={{0,1},{1,0},{2,3},{3,2},{4,5},{5,4},{6,7},{7,6},{8,9},{9,8},{10,11... | collective-permute-start | bytes 589832 | tf_op jit(solution)/shard_map/ppermute | solution.py:45
  9.0 6.3 %collective-permute-start.6 = (f32[1,10,8,512]{3,2,1,0:T(8,128)S(1)}, f32[1,10,8,512]{3,2,1,0:T(8,128)S(1)}, u32[]{:S(2)}, u32[]{:S(2)}) collective-permute-start(f32[1,10,8,512]{3,2,1,0:T(8,128)S(1)} %get-tuple-element.23), channel_id=1, source_target_pairs={{0,2},{2,0},{4,6},{6,4},{8,10},{10,8},{12,14},{14,12},{16,18},{18,... | collective-permute-start | bytes 491528 | tf_op jit(solution)/shard_map/ppermute | solution.py:45
  9.1 9.0 %collective-permute-start.5 = (f32[2,10,8,512]{3,2,1,0:T(8,128)S(1)}, f32[2,10,8,512]{3,2,1,0:T(8,128)S(1)}, u32[]{:S(2)}, u32[]{:S(2)}) collective-permute-start(f32[2,10,8,512]{3,2,1,0:T(8,128)S(1)} %get-tuple-element.22), channel_id=1, source_target_pairs={{0,2},{2,0},{4,6},{6,4},{8,10},{10,8},{12,14},{14,12},{16,18},{18,... | collective-permute-start | bytes 983048 | tf_op jit(solution)/shard_map/ppermute | solution.py:45
  9.6 9.0 %collective-permute-start.4 = (f32[3,4,8,128]{3,2,1,0:T(8,128)S(1)}, f32[3,4,8,128]{3,2,1,0:T(8,128)S(1)}, u32[]{:S(2)}, u32[]{:S(2)}) collective-permute-start(f32[3,4,8,128]{3,2,1,0:T(8,128)S(1)} %pack_mirror.1.first_ref), channel_id=1, source_target_pairs={{0,16},{2,18},{4,20},{6,22},{8,24},{10,26},{12,28},{14,30},{16,0},... | collective-permute-start | bytes 147464 | tf_op jit(solution)/shard_map/ppermute | solution.py:45
  13.0 2.8 %copy-start = (f32[512,544]{0,1:T(8,128)S(1)}, f32[512,544]{0,1:T(8,128)}, u32[]{:S(2)}) copy-start(f32[512,544]{0,1:T(8,128)} %param.5) | copy-start | bytes 3342340
  13.6 6.0 %collective-permute-start.2 = (f32[2,3,8,512]{3,2,1,0:T(8,128)S(1)}, f32[2,3,8,512]{3,2,1,0:T(8,128)S(1)}, u32[]{:S(2)}, u32[]{:S(2)}) collective-permute-start(f32[2,3,8,512]{3,2,1,0:T(8,128)S(1)} %share_terms.1.first_ref), channel_id=1, source_target_pairs={{0,1},{1,0},{2,3},{3,2},{4,5},{5,4},{6,7},{7,6},{8,9},{9,8},{10,11... | collective-permute-start | bytes 294920 | tf_op jit(solution)/shard_map/ppermute | solution.py:45
  15.3 15.6 %collective-permute-start.1 = (f32[2,12,8,512]{3,2,1,0:T(8,128)S(1)}, f32[2,12,8,512]{3,2,1,0:T(8,128)S(1)}, u32[]{:S(2)}, u32[]{:S(2)}) collective-permute-start(f32[2,12,8,512]{3,2,1,0:T(8,128)S(1)} %pack_planes.1), channel_id=1, source_target_pairs={{0,1},{1,0},{2,3},{3,2},{4,5},{5,4},{6,7},{7,6},{8,9},{9,8},{10,11... | collective-permute-start | bytes 1179656 | tf_op jit(solution)/shard_map/ppermute | solution.py:45
  19.7 1.3 %collective-permute-start.7 = (f32[2,3,8,256]{3,2,1,0:T(8,128)S(1)}, f32[2,3,8,256]{3,2,1,0:T(8,128)S(1)}, u32[]{:S(2)}, u32[]{:S(2)}) collective-permute-start(f32[2,3,8,256]{3,2,1,0:T(8,128)S(1)} %ends_other.1), channel_id=1, source_target_pairs={{0,2},{2,0},{4,6},{6,4},{8,10},{10,8},{12,14},{14,12},{16,18},{18,... | collective-permute-start | bytes 147464 | tf_op jit(solution)/shard_map/ppermute | solution.py:45
  21.1 4.2 %collective-permute-start.8 = (f32[2,3,8,256]{3,2,1,0:T(8,128)S(1)}, f32[2,3,8,256]{3,2,1,0:T(8,128)S(1)}, u32[]{:S(2)}, u32[]{:S(2)}) collective-permute-start(f32[2,3,8,256]{3,2,1,0:T(8,128)S(1)} %pair.1.block_ref), channel_id=1, source_target_pairs={{0,4},{2,6},{4,0},{6,2},{8,12},{10,14},{12,8},{14,10},{16,20},{18,... | collective-permute-start | bytes 147464 | tf_op jit(solution)/shard_map/ppermute | solution.py:45
  25.2 4.2 %collective-permute-start.9 = (f32[2,3,8,256]{3,2,1,0:T(8,128)S(1)}, f32[2,3,8,256]{3,2,1,0:T(8,128)S(1)}, u32[]{:S(2)}, u32[]{:S(2)}) collective-permute-start(f32[2,3,8,256]{3,2,1,0:T(8,128)S(1)} %get-tuple-element.24.block_ref), channel_id=1, source_target_pairs={{0,8},{2,10},{4,12},{6,14},{8,0},{10,2},{12,4},{14,6},{16,24},{18,... | collective-permute-start | bytes 147464 | tf_op jit(solution)/shard_map/ppermute | solution.py:45
  29.4 5.4 %collective-permute-start.10 = (f32[2,3,8,256]{3,2,1,0:T(8,128)S(1)}, f32[2,3,8,256]{3,2,1,0:T(8,128)S(1)}, u32[]{:S(2)}, u32[]{:S(2)}) collective-permute-start(f32[2,3,8,256]{3,2,1,0:T(8,128)S(1)} %get-tuple-element.26.ready_ref.block_ref), channel_id=1, source_target_pairs={{0,16},{2,18},{4,20},{6,22},{8,24},{10,26},{12,28},{14,30},{16,0},... | collective-permute-start | bytes 147464 | tf_op jit(solution)/shard_map/ppermute | solution.py:45
  34.9 1.3 %collective-permute-start.11 = (f32[2,3,8,256]{3,2,1,0:T(8,128)S(1)}, f32[2,3,8,256]{3,2,1,0:T(8,128)S(1)}, u32[]{:S(2)}, u32[]{:S(2)}) collective-permute-start(f32[2,3,8,256]{3,2,1,0:T(8,128)S(1)} %get-tuple-element.31), channel_id=1, source_target_pairs={{0,2},{2,0},{4,6},{6,4},{8,10},{10,8},{12,14},{14,12},{16,18},{18,... | collective-permute-start | bytes 147464 | tf_op jit(solution)/shard_map/ppermute | solution.py:45

commit v13 on v12

--- a/solution.py
+++ b/solution.py
@@ -14,9 +14,10 @@
 CORE_PARTS = ((0, 1), (2,))
 LANES = 128
 UNROLL = 16
-INNER = 1 << 31
-MIRROR = 1 << 26
-SIDE = 1 << 26
+INNER = 1 << 20
+MIRROR = 25 << 26
+SIDE = 1 << 20
+LATE = 1 << 30
 
 VMEM = pl.BlockSpec(memory_space=pltpu.VMEM)
 SMEM = pl.BlockSpec(memory_space=pltpu.SMEM)
@@ -332,27 +333,27 @@
 
 
 def late_kernel(me_ref, tap_ref, v_ref, *refs):
-    *chip_refs, n_in_ref, n_ref = refs
+    *chip_refs, n_in_ref, _, n_ref = refs
     even = me_ref[0] % 2 == 0
     add = functools.partial(add_side, tap_ref, v_ref, chip_refs, n_in_ref, n_ref)
     pl.when(even)(lambda: add(True))
     pl.when(jnp.logical_not(even))(lambda: add(False))
 
 
-def side_terms(kernel, name, me, taps, v, sides, n):
+def side_terms(kernel, name, me, taps, v, sides, n, ready=(), flops=SIDE):
     return pl.pallas_call(
         kernel,
         name=name,
         out_shape=held(*v.shape),
-        in_specs=[SMEM] + [VMEM] * (3 + len(sides)),
+        in_specs=[SMEM] + [VMEM] * (3 + len(sides)) + [ANY] * len(ready),
         out_specs=VMEM,
         input_output_aliases={3 + len(sides): 0},
         compiler_params=params(v.size * 4, 5),
-        cost_estimate=pl.CostEstimate(flops=SIDE, bytes_accessed=12 * v.size, transcendentals=0),
-    )(me, taps, v, *sides, n)
-
-
-def share_kernel(v_ref, e_ref, power_ref, ends_ref, tile_ref):
+        cost_estimate=pl.CostEstimate(flops=flops, bytes_accessed=12 * v.size, transcendentals=0),
+    )(me, taps, v, *sides, n, *ready)
+
+
+def share_kernel(v_ref, e_ref, power_ref, ready_ref, ends_ref, tile_ref):
     comps, points, planes, radial = v_ref.shape
     carriers = e_ref.shape[1]
     weights = axial_weights(planes, False)
@@ -367,18 +368,18 @@
             ends_ref[1, c] = ends_ref[1, c] - power_ref[t : t + 1] * right_side
 
 
-def share_terms(v, e, power):
+def share_terms(v, e, power, ready):
     comps, points, planes, radial = v.shape
     return pl.pallas_call(
         share_kernel,
         name="share_terms",
         out_shape=held(2, comps, planes, radial),
-        in_specs=[VMEM] * 3,
+        in_specs=[VMEM] * 3 + [ANY],
         out_specs=VMEM,
         scratch_shapes=[pltpu.VMEM((1, points - e.shape[1], planes, radial), jnp.float32)],
         compiler_params=params(v.size * 4, 4),
         cost_estimate=pl.CostEstimate(flops=20 * v.size, bytes_accessed=8 * v.size, transcendentals=0),
-    )(v, e, power)
+    )(v, e, power, ready)
 
 
 def ends_kernel(me_ref, v_ref, share_ref, power_ref, n_ref, ends_ref, *, own):
@@ -664,12 +665,12 @@
     core_in = [swap(part, "theta", 1) for part in core_out]
     power, taps = table(me, viscous_factor, azimuth_stencil, points, sectors, planes, radial)
     n = inner_terms(taps, velocity, op)
-    share_out = share_terms(velocity, axial_in, power)
+    share_out = share_terms(velocity, axial_in, power, n)
     share_in = swap(share_out, "gz", 1)
     planes_in = swap(pack_planes(velocity, share_out), "gz", 1)
     n = side_terms(core_kernel, "core_terms", me, taps, velocity, core_in, n)
     n = mirror_terms(velocity, op, mirror_in, n)
-    n = side_terms(late_kernel, "late_terms", me, taps, velocity, chip_in, n)
+    n = side_terms(late_kernel, "late_terms", me, taps, velocity, chip_in, n, (share_in,), LATE)
     send = ends_terms(me, velocity, share_in, power, n, False)
     other = swap(send, "theta", 1)
     own = ends_terms(me, velocity, share_in, power, n, True)

time: 37.1 us -> 38.8 us (1.046)
  waiting for transfers between devices: 14 us -> 16.7 us
  starting transfers between devices: 11.8 us -> 10.8 us
    ppermute x11, waiting for transfers between devices: 14 us -> 16.7 us  [swap(): return lax.ppermute(block, axis, [(i, i ^ bit) for i in range(size)])]
    ppermute x11, starting transfers between devices: 6.3 us -> 5.28 us  [swap(): return lax.ppermute(block, axis, [(i, i ^ bit) for i in range(size)])]
  transfers between devices with their start and end apart: 12 -> 12, of which waited for: 6 -> 7; matrix products, arithmetic and copies ran while one was open for 0% -> 0% of each run, Pallas kernels for 21% -> 20%
where the time goes in v13:
time: 38.8 us; the launch traced here: 38.7 us
  waiting for transfers between devices  16.7 us (43%)
  starting transfers between devices  10.8 us (28%)
  Pallas kernels  9.66 us (25%)
  between operations  1.51 us (4%)
    ppermute x11, waiting for transfers between devices, swap(): return lax.ppermute(block, axis, [(i, i ^ bit) for i in range(size)])  16.7 us
    ppermute x1, starting transfers between devices, swap_across(): return lax.ppermute(block, axis, route)  5.48 us
    ppermute x11, starting transfers between devices, swap(): return lax.ppermute(block, axis, [(i, i ^ bit) for i in range(size)])  5.28 us
    pallas_call x1, Pallas kernels, inner_terms(): pl.pallas_call(inner_kernel, name='inner_terms', out_shape=held(*v.shape)...  2.2 us
    pallas_call x2, Pallas kernels, close(): pl.pallas_call(functools.partial(close_kernel, own=own), name='close_own'...  1.59 us
    pallas_call x1, Pallas kernels, load(): pl.pallas_call(load_kernel, name='load', out_shape=(held(*v.shape), held(...  1.14 us
    pallas_call x2, Pallas kernels, side_terms(): pl.pallas_call(kernel, name=name, out_shape=held(*v.shape), in_specs=[SME...  0.98 us
    pallas_call x1, Pallas kernels, sweep(): pl.pallas_call(sweep_kernel, name='sweep', out_shape=(held(*v.shape), jax...  0.89 us
  transfers between devices with their start and end apart: 12, of which 7 were waited for; matrix products, arithmetic and copies ran while one was open for 0% of the time, Pallas kernels for 20%

profile of v13, /device:TPU:0, one launch (start us, length us, event | category | flops | bytes accessed | tf_op | source)
XLA Modules:
  0.0 38.7 jit_solution(8862814425779437299)
XLA Ops:
  0.6 1.1 %load.1 = (f32[3,16,8,512]{3,2,1,0:T(8,128)S(1)}, f32[1,12,8,512]{3,2,1,0:T(8,128)S(1)}) custom-call(f32[3,16,8,512]{3,2,1,0:T(8,128)} %hbm_ref.1), custom_call_target="tpu_custom_call" | custom-call | tf_op jit(solution)/shard_map/load/pallas_call | solution.py:113
  1.9 5.5 %collective-permute-start.3 = (f32[3,10,8,512]{3,2,1,0:T(8,128)S(1)}, f32[3,10,8,512]{3,2,1,0:T(8,128)S(1)}, u32[]{:S(2)}, u32[]{:S(2)}) collective-permute-start(f32[3,10,8,512]{3,2,1,0:T(8,128)S(1)} %pack_chip.1.first_ref), channel_id=1, source_target_pairs={{2,4},{4,2},{6,8},{8,6},{10,12},{12,10},{14,16},{16,14},{18,20},{2... | collective-permute-start | bytes 1474568 | tf_op jit(solution)/shard_map/ppermute | solution.py:54
  7.6 1.6 %collective-permute-start = (f32[1,12,8,512]{3,2,1,0:T(8,128)S(1)}, f32[1,12,8,512]{3,2,1,0:T(8,128)S(1)}, u32[]{:S(2)}, u32[]{:S(2)}) collective-permute-start(f32[1,12,8,512]{3,2,1,0:T(8,128)S(1)} %get-tuple-element.19.first_ref), channel_id=1, source_target_pairs={{0,1},{1,0},{2,3},{3,2},{4,5},{5,4},{6,7},{7,6},{8,9},{9,8},{10,11... | collective-permute-start | bytes 589832 | tf_op jit(solution)/shard_map/ppermute | solution.py:46
  9.2 0.2 collective-permute-start.6
  10.0 0.6 %table.1 = (f32[30,512]{1,0:T(8,128)S(1)}, f32[21,8,128]{2,1,0:T(8,128)S(1)}) custom-call(s32[1]{0:T(128)} %bitcast.me_ref, f32[1]{0:T(128)S(6)} %copy.16.factor_ref, f32[21]{0:T(128)S(1)} %copy-done.1), custom_call_target="tpu_custom_call" | custom-call | flops 512000 | bytes 204800 | tf_op jit(solution)/shard_map/table/pallas_call | solution.py:473
  10.6 2.2 %inner_terms.1.ready_ref.refs_2_ = f32[3,16,8,512]{3,2,1,0:T(8,128)S(1)} custom-call(f32[21,8,128]{2,1,0:T(8,128)S(1)} %get-tuple-element.21.tap_ref, f32[3,16,8,512]{3,2,1,0:T(8,128)S(1)} %get-tuple-element.18.v_ref, f32[544,512]{1,0:T(8,128)S(1)} %bitcast.2), custom_call_target="tpu_custom_call" | custom-call | flops 1048576 | bytes 3145728 | tf_op jit(solution)/shard_map/inner_terms/pallas_call | solution.py:291
  12.8 2.1 %collective-permute-done.e_ref = f32[1,12,8,512]{3,2,1,0:T(8,128)S(1)} collective-permute-done((f32[1,12,8,512]{3,2,1,0:T(8,128)S(1)}, f32[1,12,8,512]{3,2,1,0:T(8,128)S(1)}, u32[]{:S(2)}, u32[]{:S(2)}) %collective-permute-start) | collective-permute-done | bytes 196640 | tf_op jit(solution)/shard_map/ppermute | solution.py:46
  14.9 0.6 %share_terms.1.first_ref = f32[2,3,8,512]{3,2,1,0:T(8,128)S(1)} custom-call(f32[3,16,8,512]{3,2,1,0:T(8,128)S(1)} %get-tuple-element.18.v_ref, f32[1,12,8,512]{3,2,1,0:T(8,128)S(1)} %collective-permute-done.e_ref, f32[30,512]{1,0:T(8,128)S(1)} %get-tuple-element.20.power_ref, f32[3,16,8,512]{3,2,1,0:T(8,128)S(1)} %inner_terms.1.ready_ref.refs_2_), custom_call_target="tpu_custom_call" | custom-call | flops 3932160 | bytes 1572864 | tf_op jit(solution)/shard_map/share_terms/pallas_call | solution.py:373
  15.5 1.6 %collective-permute-start.2 = (f32[2,3,8,512]{3,2,1,0:T(8,128)S(1)}, f32[2,3,8,512]{3,2,1,0:T(8,128)S(1)}, u32[]{:S(2)}, u32[]{:S(2)}) collective-permute-start(f32[2,3,8,512]{3,2,1,0:T(8,128)S(1)} %share_terms.1.first_ref), channel_id=1, source_target_pairs={{0,1},{1,0},{2,3},{3,2},{4,5},{5,4},{6,7},{7,6},{8,9},{9,8},{10,11... | collective-permute-start | bytes 294920 | tf_op jit(solution)/shard_map/ppermute | solution.py:46
  17.2 0.6 %collective-permute-start.1 = (f32[2,12,8,512]{3,2,1,0:T(8,128)S(1)}, f32[2,12,8,512]{3,2,1,0:T(8,128)S(1)}, u32[]{:S(2)}, u32[]{:S(2)}) collective-permute-start(f32[2,12,8,512]{3,2,1,0:T(8,128)S(1)} %pack_planes.1), channel_id=1, source_target_pairs={{0,1},{1,0},{2,3},{3,2},{4,5},{5,4},{6,7},{7,6},{8,9},{9,8},{10,11... | collective-permute-start | bytes 1179656 | tf_op jit(solution)/shard_map/ppermute | solution.py:46
  17.7 0.5 %core_terms.1.n_in_ref = f32[3,16,8,512]{3,2,1,0:T(8,128)S(1)} custom-call(s32[1]{0:T(128)} %bitcast.me_ref, f32[21,8,128]{2,1,0:T(8,128)S(1)} %get-tuple-element.21.tap_ref, f32[3,16,8,512]{3,2,1,0:T(8,128)S(1)} %get-tuple-element.18.v_ref, f32[2,10,8,512]{3,2,1,0:T(8,128)S(1)} %collective-permute-done.5.refs_0_, ...), custom_call_target="tpu_custom_call", output_to_operand_aliasing={{}: (5, {})} | custom-call | flops 1048576 | bytes 2359296 | tf_op jit(solution)/shard_map/core_terms/pallas_call | solution.py:344
  18.3 0.5 %mirror_terms.1.refs_1_ = f32[3,16,8,512]{3,2,1,0:T(8,128)S(1)} custom-call(f32[3,16,8,512]{3,2,1,0:T(8,128)S(1)} %get-tuple-element.18.v_ref, f32[544,512]{1,0:T(8,128)S(1)} %bitcast.3, f32[3,4,8,128]{3,2,1,0:T(8,128)S(1)} %collective-permute-done.4.mirror_ref, f32[3,16,8,512]{3,2,1,0:T(8,128)S(1)} %core_terms.1.n_in_ref), custom_call_target="tpu_custom_call", output_to_operand_aliasing={{}: (3, {})} | custom-call | flops 1677721600 | bytes 3145728 | tf_op jit(solution)/shard_map/mirror_terms/pallas_call | solution.py:246
  18.8 2.4 %collective-permute-done.2.refs_2_.share_ref = f32[2,3,8,512]{3,2,1,0:T(8,128)S(1)} collective-permute-done((f32[2,3,8,512]{3,2,1,0:T(8,128)S(1)}, f32[2,3,8,512]{3,2,1,0:T(8,128)S(1)}, u32[]{:S(2)}, u32[]{:S(2)}) %collective-permute-start.2) | collective-permute-done | bytes 98336 | tf_op jit(solution)/shard_map/ppermute | solution.py:46
  21.2 0.5 %late_terms.1.n_ref.n_in_ref = f32[3,16,8,512]{3,2,1,0:T(8,128)S(1)} custom-call(s32[1]{0:T(128)} %bitcast.me_ref, f32[21,8,128]{2,1,0:T(8,128)S(1)} %get-tuple-element.21.tap_ref, f32[3,16,8,512]{3,2,1,0:T(8,128)S(1)} %get-tuple-element.18.v_ref, f32[3,10,8,512]{3,2,1,0:T(8,128)S(1)} %collective-permute-done.3.refs_0_, ...), custom_call_target="tpu_custom_call", output_to_operand_aliasing={{}: (4, {})} | custom-call | flops 1073741824 | bytes 2359296 | tf_op jit(solution)/shard_map/late_terms/pallas_call | solution.py:344
  22.0 1.1 %collective-permute-done.7.other_ref = f32[2,3,8,256]{3,2,1,0:T(8,128)S(1)} collective-permute-done((f32[2,3,8,256]{3,2,1,0:T(8,128)S(1)}, f32[2,3,8,256]{3,2,1,0:T(8,128)S(1)}, u32[]{:S(2)}, u32[]{:S(2)}) %collective-permute-start.7) | collective-permute-done | bytes 49184 | tf_op jit(solution)/shard_map/ppermute | solution.py:46
  23.2 4.1 %collective-permute-done.8.other_ref = f32[2,3,8,256]{3,2,1,0:T(8,128)S(1)} collective-permute-done((f32[2,3,8,256]{3,2,1,0:T(8,128)S(1)}, f32[2,3,8,256]{3,2,1,0:T(8,128)S(1)}, u32[]{:S(2)}, u32[]{:S(2)}) %collective-permute-start.8) | collective-permute-done | bytes 49184 | tf_op jit(solution)/shard_map/ppermute | solution.py:46
  27.3 4.1 %collective-permute-done.9.other_ref = f32[2,3,8,256]{3,2,1,0:T(8,128)S(1)} collective-permute-done((f32[2,3,8,256]{3,2,1,0:T(8,128)S(1)}, f32[2,3,8,256]{3,2,1,0:T(8,128)S(1)}, u32[]{:S(2)}, u32[]{:S(2)}) %collective-permute-start.9) | collective-permute-done | bytes 49184 | tf_op jit(solution)/shard_map/ppermute | solution.py:46
  31.4 1.0 %collective-permute-start.10 = (f32[2,3,8,256]{3,2,1,0:T(8,128)S(1)}, f32[2,3,8,256]{3,2,1,0:T(8,128)S(1)}, u32[]{:S(2)}, u32[]{:S(2)}) collective-permute-start(f32[2,3,8,256]{3,2,1,0:T(8,128)S(1)} %get-tuple-element.26.ready_ref.block_ref), channel_id=1, source_target_pairs={{0,16},{2,18},{4,20},{6,22},{8,24},{10,26},{12,28},{14,30},{16,0},... | collective-permute-start | bytes 147464 | tf_op jit(solution)/shard_map/ppermute | solution.py:46
  32.5 0.5 %planes_terms.1.n_ref = f32[3,16,8,512]{3,2,1,0:T(8,128)S(1)} custom-call(f32[3,16,8,512]{3,2,1,0:T(8,128)S(1)} %get-tuple-element.18.v_ref, f32[2,12,8,512]{3,2,1,0:T(8,128)S(1)} %collective-permute-done.1.y_ref, f32[1,12,8,512]{3,2,1,0:T(8,128)S(1)} %collective-permute-done.e_ref, ...), custom_call_target="tpu_custom_call", output_to_operand_aliasing={{}: (4, {})} | custom-call | flops 3932160 | bytes 3145728 | tf_op jit(solution)/shard_map/planes_terms/pallas_call | solution.py:428
  33.0 0.9 %sweep.1 = (f32[3,16,8,512]{3,2,1,0:T(8,128)S(1)}, f32[3,16,8,512]{3,2,1,0:T(8,128)}) custom-call(f32[3,16,8,512]{3,2,1,0:T(8,128)S(1)} %get-tuple-element.18.v_ref, f32[3,16,8,512]{3,2,1,0:T(8,128)S(1)} %planes_terms.1.n_ref, f32[30,512]{1,0:T(8,128)S(1)} %get-tuple-element.20.power_ref), custom_call_target="tpu_custom_call" | custom-call | flops 1966080 | bytes 2359296 | tf_op jit(solution)/shard_map/sweep/pallas_call | solution.py:513
  33.9 2.6 %collective-permute-done.10.other_ref = f32[2,3,8,256]{3,2,1,0:T(8,128)S(1)} collective-permute-done((f32[2,3,8,256]{3,2,1,0:T(8,128)S(1)}, f32[2,3,8,256]{3,2,1,0:T(8,128)S(1)}, u32[]{:S(2)}, u32[]{:S(2)}) %collective-permute-start.10) | collective-permute-done | bytes 49184 | tf_op jit(solution)/shard_map/ppermute | solution.py:46
  36.6 0.8 %close_own.1.refs_0_ = f32[3,16,8,512]{3,2,1,0:T(8,128)} custom-call(s32[1]{0:T(128)} %bitcast.me_ref, f32[3,16,8,512]{3,2,1,0:T(8,128)S(1)} %get-tuple-element.27.ready_ref.s_ref, f32[30,512]{1,0:T(8,128)S(1)} %get-tuple-element.20.power_ref, f32[2,3,8,256]{3,2,1,0:T(8,128)S(1)} %get-tuple-element.32.entry_ref), custom_call_target="tpu_custom_call" | custom-call | flops 786432 | bytes 1572864 | tf_op jit(solution)/shard_map/close_own/pallas_call | solution.py:633
  37.5 0.4 %collective-permute-done.11.entry_ref = f32[2,3,8,256]{3,2,1,0:T(8,128)S(1)} collective-permute-done((f32[2,3,8,256]{3,2,1,0:T(8,128)S(1)}, f32[2,3,8,256]{3,2,1,0:T(8,128)S(1)}, u32[]{:S(2)}, u32[]{:S(2)}) %collective-permute-start.11) | collective-permute-done | bytes 49184 | tf_op jit(solution)/shard_map/ppermute | solution.py:46
  37.9 0.8 %close_other.1 = f32[3,16,8,512]{3,2,1,0:T(8,128)} custom-call(s32[1]{0:T(128)} %bitcast.me_ref, f32[3,16,8,512]{3,2,1,0:T(8,128)S(1)} %get-tuple-element.27.ready_ref.s_ref, f32[30,512]{1,0:T(8,128)S(1)} %get-tuple-element.20.power_ref, f32[2,3,8,256]{3,2,1,0:T(8,128)S(1)} %collective-permute-done.11.entry_ref, ...), custom_call_target="tpu_custom_call", output_to_operand_aliasing={{}: (4, {})} | custom-call | flops 786432 | bytes 1572864 | tf_op jit(solution)/shard_map/close_other/pallas_call | solution.py:633
  (26 shorter events, 1.0 us)
Async XLA Ops:
  1.8 8.2 %copy-start.1 = (f32[21]{0:T(128)S(1)}, f32[21]{0:T(128)}, u32[]{:S(2)}) copy-start(f32[21]{0:T(128)} %stencil_ref.1) | copy-start | bytes 256
  1.8 8.8 %copy-start = (f32[512,544]{0,1:T(8,128)S(1)}, f32[512,544]{0,1:T(8,128)}, u32[]{:S(2)}) copy-start(f32[512,544]{0,1:T(8,128)} %param.5) | copy-start | bytes 3342340
  1.9 19.3 %collective-permute-start.3 = (f32[3,10,8,512]{3,2,1,0:T(8,128)S(1)}, f32[3,10,8,512]{3,2,1,0:T(8,128)S(1)}, u32[]{:S(2)}, u32[]{:S(2)}) collective-permute-start(f32[3,10,8,512]{3,2,1,0:T(8,128)S(1)} %pack_chip.1.first_ref), channel_id=1, source_target_pairs={{2,4},{4,2},{6,8},{8,6},{10,12},{12,10},{14,16},{16,14},{18,20},{2... | collective-permute-start | bytes 1474568 | tf_op jit(solution)/shard_map/ppermute | solution.py:54
  7.5 10.2 %collective-permute-start.5 = (f32[2,10,8,512]{3,2,1,0:T(8,128)S(1)}, f32[2,10,8,512]{3,2,1,0:T(8,128)S(1)}, u32[]{:S(2)}, u32[]{:S(2)}) collective-permute-start(f32[2,10,8,512]{3,2,1,0:T(8,128)S(1)} %get-tuple-element.22), channel_id=1, source_target_pairs={{0,2},{2,0},{4,6},{6,4},{8,10},{10,8},{12,14},{14,12},{16,18},{18,... | collective-permute-start | bytes 983048 | tf_op jit(solution)/shard_map/ppermute | solution.py:46
  7.6 7.3 %collective-permute-start = (f32[1,12,8,512]{3,2,1,0:T(8,128)S(1)}, f32[1,12,8,512]{3,2,1,0:T(8,128)S(1)}, u32[]{:S(2)}, u32[]{:S(2)}) collective-permute-start(f32[1,12,8,512]{3,2,1,0:T(8,128)S(1)} %get-tuple-element.19.first_ref), channel_id=1, source_target_pairs={{0,1},{1,0},{2,3},{3,2},{4,5},{5,4},{6,7},{7,6},{8,9},{9,8},{10,11... | collective-permute-start | bytes 589832 | tf_op jit(solution)/shard_map/ppermute | solution.py:46
  9.2 8.0 %collective-permute-start.6 = (f32[1,10,8,512]{3,2,1,0:T(8,128)S(1)}, f32[1,10,8,512]{3,2,1,0:T(8,128)S(1)}, u32[]{:S(2)}, u32[]{:S(2)}) collective-permute-start(f32[1,10,8,512]{3,2,1,0:T(8,128)S(1)} %get-tuple-element.23), channel_id=1, source_target_pairs={{0,2},{2,0},{4,6},{6,4},{8,10},{10,8},{12,14},{14,12},{16,18},{18,... | collective-permute-start | bytes 491528 | tf_op jit(solution)/shard_map/ppermute | solution.py:46
  9.3 8.9 %collective-permute-start.4 = (f32[3,4,8,128]{3,2,1,0:T(8,128)S(1)}, f32[3,4,8,128]{3,2,1,0:T(8,128)S(1)}, u32[]{:S(2)}, u32[]{:S(2)}) collective-permute-start(f32[3,4,8,128]{3,2,1,0:T(8,128)S(1)} %pack_mirror.1.first_ref), channel_id=1, source_target_pairs={{0,16},{2,18},{4,20},{6,22},{8,24},{10,26},{12,28},{14,30},{16,0},... | collective-permute-start | bytes 147464 | tf_op jit(solution)/shard_map/ppermute | solution.py:46
  15.5 5.7 %collective-permute-start.2 = (f32[2,3,8,512]{3,2,1,0:T(8,128)S(1)}, f32[2,3,8,512]{3,2,1,0:T(8,128)S(1)}, u32[]{:S(2)}, u32[]{:S(2)}) collective-permute-start(f32[2,3,8,512]{3,2,1,0:T(8,128)S(1)} %share_terms.1.first_ref), channel_id=1, source_target_pairs={{0,1},{1,0},{2,3},{3,2},{4,5},{5,4},{6,7},{7,6},{8,9},{9,8},{10,11... | collective-permute-start | bytes 294920 | tf_op jit(solution)/shard_map/ppermute | solution.py:46
  17.2 15.3 %collective-permute-start.1 = (f32[2,12,8,512]{3,2,1,0:T(8,128)S(1)}, f32[2,12,8,512]{3,2,1,0:T(8,128)S(1)}, u32[]{:S(2)}, u32[]{:S(2)}) collective-permute-start(f32[2,12,8,512]{3,2,1,0:T(8,128)S(1)} %pack_planes.1), channel_id=1, source_target_pairs={{0,1},{1,0},{2,3},{3,2},{4,5},{5,4},{6,7},{7,6},{8,9},{9,8},{10,11... | collective-permute-start | bytes 1179656 | tf_op jit(solution)/shard_map/ppermute | solution.py:46
  21.8 1.3 %collective-permute-start.7 = (f32[2,3,8,256]{3,2,1,0:T(8,128)S(1)}, f32[2,3,8,256]{3,2,1,0:T(8,128)S(1)}, u32[]{:S(2)}, u32[]{:S(2)}) collective-permute-start(f32[2,3,8,256]{3,2,1,0:T(8,128)S(1)} %ends_other.1), channel_id=1, source_target_pairs={{0,2},{2,0},{4,6},{6,4},{8,10},{10,8},{12,14},{14,12},{16,18},{18,... | collective-permute-start | bytes 147464 | tf_op jit(solution)/shard_map/ppermute | solution.py:46
  23.1 4.2 %collective-permute-start.8 = (f32[2,3,8,256]{3,2,1,0:T(8,128)S(1)}, f32[2,3,8,256]{3,2,1,0:T(8,128)S(1)}, u32[]{:S(2)}, u32[]{:S(2)}) collective-permute-start(f32[2,3,8,256]{3,2,1,0:T(8,128)S(1)} %pair.1.block_ref), channel_id=1, source_target_pairs={{0,4},{2,6},{4,0},{6,2},{8,12},{10,14},{12,8},{14,10},{16,20},{18,... | collective-permute-start | bytes 147464 | tf_op jit(solution)/shard_map/ppermute | solution.py:46
  27.3 4.2 %collective-permute-start.9 = (f32[2,3,8,256]{3,2,1,0:T(8,128)S(1)}, f32[2,3,8,256]{3,2,1,0:T(8,128)S(1)}, u32[]{:S(2)}, u32[]{:S(2)}) collective-permute-start(f32[2,3,8,256]{3,2,1,0:T(8,128)S(1)} %get-tuple-element.24.block_ref), channel_id=1, source_target_pairs={{0,8},{2,10},{4,12},{6,14},{8,0},{10,2},{12,4},{14,6},{16,24},{18,... | collective-permute-start | bytes 147464 | tf_op jit(solution)/shard_map/ppermute | solution.py:46
  31.4 5.1 %collective-permute-start.10 = (f32[2,3,8,256]{3,2,1,0:T(8,128)S(1)}, f32[2,3,8,256]{3,2,1,0:T(8,128)S(1)}, u32[]{:S(2)}, u32[]{:S(2)}) collective-permute-start(f32[2,3,8,256]{3,2,1,0:T(8,128)S(1)} %get-tuple-element.26.ready_ref.block_ref), channel_id=1, source_target_pairs={{0,16},{2,18},{4,20},{6,22},{8,24},{10,26},{12,28},{14,30},{16,0},... | collective-permute-start | bytes 147464 | tf_op jit(solution)/shard_map/ppermute | solution.py:46
  36.6 1.3 %collective-permute-start.11 = (f32[2,3,8,256]{3,2,1,0:T(8,128)S(1)}, f32[2,3,8,256]{3,2,1,0:T(8,128)S(1)}, u32[]{:S(2)}, u32[]{:S(2)}) collective-permute-start(f32[2,3,8,256]{3,2,1,0:T(8,128)S(1)} %get-tuple-element.31), channel_id=1, source_target_pairs={{0,2},{2,0},{4,6},{6,4},{8,10},{10,8},{12,14},{14,12},{16,18},{18,... | collective-permute-start | bytes 147464 | tf_op jit(solution)/shard_map/ppermute | solution.py:46

commit v14 on v13

--- a/solution.py
+++ b/solution.py
@@ -300,20 +300,23 @@
     )(taps, v, op)
 
 
-def add_side(tap_ref, v_ref, side_refs, n_in_ref, n_ref, before):
+def add_side(tap_ref, v_ref, side_refs, n_in_ref, n_ref, before, columns):
     comps, points, _, radial = v_ref.shape
     reach = side_refs[0].shape[1]
     sides = [(ref, i) for ref in side_refs for i in range(ref.shape[0])]
     first = 0 if before else reach + 1
 
-    @pl.loop(0, radial // LANES)
-    def column(k):
+    start, count = columns
+
+    @pl.loop(0, count)
+    def column(i):
+        k = start + i
         lanes = pl.ds(pl.multiple_of(k * LANES, LANES), LANES)
         inv_r = inverse_radius(LANES, k * LANES)
         weights = [tap_ref[first + i] for i in range(reach)]
         for c in range(comps):
-            ref, i = sides[c]
-            side = [ref[i, h, :, lanes] for h in range(reach)]
+            ref, part = sides[c]
+            side = [ref[part, h, :, lanes] for h in range(reach)]
             for u in range(reach):
                 t = u if before else points - reach + u
                 taps = [(h, h - u) for h in range(u, reach)] if before else [(h, reach - 1 + h - u) for h in range(u + 1)]
@@ -327,17 +330,20 @@
 def core_kernel(me_ref, tap_ref, v_ref, *refs):
     *core_refs, n_in_ref, n_ref = refs
     even = me_ref[0] % 2 == 0
-    add = functools.partial(add_side, tap_ref, v_ref, core_refs, n_in_ref, n_ref)
-    pl.when(even)(lambda: add(False))
-    pl.when(jnp.logical_not(even))(lambda: add(True))
-
-
-def late_kernel(me_ref, tap_ref, v_ref, *refs):
+    columns = (0, v_ref.shape[3] // LANES)
+    add = functools.partial(add_side, tap_ref, v_ref, core_refs, n_in_ref, n_ref, columns=columns)
+    pl.when(even)(lambda: add(before=False))
+    pl.when(jnp.logical_not(even))(lambda: add(before=True))
+
+
+def late_kernel(me_ref, tap_ref, v_ref, *refs, own):
     *chip_refs, n_in_ref, _, n_ref = refs
-    even = me_ref[0] % 2 == 0
-    add = functools.partial(add_side, tap_ref, v_ref, chip_refs, n_in_ref, n_ref)
-    pl.when(even)(lambda: add(True))
-    pl.when(jnp.logical_not(even))(lambda: add(False))
+    core = me_ref[0] % 2
+    count = v_ref.shape[3] // (2 * LANES)
+    columns = ((core if own else 1 - core) * count, count)
+    add = functools.partial(add_side, tap_ref, v_ref, chip_refs, n_in_ref, n_ref, columns=columns)
+    pl.when(core == 0)(lambda: add(before=True))
+    pl.when(core == 1)(lambda: add(before=False))
 
 
 def side_terms(kernel, name, me, taps, v, sides, n, ready=(), flops=SIDE):
@@ -549,8 +555,8 @@
     )(me, power, own, other)
 
 
-def merge_kernel(me_ref, power_ref, block_ref, other_ref, *refs, points, bit):
-    *entry_refs, block_out_ref, entry_out_ref = refs
+def merge_kernel(me_ref, power_ref, block_ref, other_ref, *refs, points, bit, entries):
+    entry_refs, (block_out_ref, entry_out_ref) = refs[:entries], refs[-2:]
     comps, half = block_ref.shape[1], block_ref.shape[3]
     lanes = half_lanes(me_ref, half)
     first = points + 3 * bit
@@ -567,15 +573,15 @@
             entry_out_ref[side, c] = entry_refs[0][side, c] + enters if entry_refs else enters
 
 
-def merge(me, power, block, other, entries, points, bit):
-    return pl.pallas_call(
-        functools.partial(merge_kernel, points=points, bit=bit),
+def merge(me, power, block, other, entries, ready, points, bit):
+    return pl.pallas_call(
+        functools.partial(merge_kernel, points=points, bit=bit, entries=len(entries)),
         name="merge",
         out_shape=(held(*block.shape), held(*block.shape)),
-        in_specs=[SMEM] + [VMEM] * (3 + len(entries)),
+        in_specs=[SMEM] + [VMEM] * (3 + len(entries)) + [ANY] * len(ready),
         out_specs=(VMEM, VMEM),
         compiler_params=params(block.size * 4, 8),
-    )(me, power, block, other, *entries)
+    )(me, power, block, other, *entries, *ready)
 
 
 def enter_kernel(me_ref, power_ref, block_ref, entry_ref, own_ref, other_ref, ready_ref, mine_ref, send_ref, *, points):
@@ -667,21 +673,25 @@
     n = inner_terms(taps, velocity, op)
     share_out = share_terms(velocity, axial_in, power, n)
     share_in = swap(share_out, "gz", 1)
-    planes_in = swap(pack_planes(velocity, share_out), "gz", 1)
     n = side_terms(core_kernel, "core_terms", me, taps, velocity, core_in, n)
     n = mirror_terms(velocity, op, mirror_in, n)
-    n = side_terms(late_kernel, "late_terms", me, taps, velocity, chip_in, n, (share_in,), LATE)
+    late = functools.partial(late_kernel, own=False)
+    n = side_terms(late, "late_other", me, taps, velocity, chip_in, n, (share_in,), LATE)
     send = ends_terms(me, velocity, share_in, power, n, False)
     other = swap(send, "theta", 1)
+    late = functools.partial(late_kernel, own=True)
+    n = side_terms(late, "late_own", me, taps, velocity, chip_in, n, (send,))
     own = ends_terms(me, velocity, share_in, power, n, True)
     block = pair(me, power, own, other, points)
-    entries = ()
+    planes_in = swap(pack_planes(velocity, block), "gz", 1)
+    entries, ready = (), ()
     last = sectors.bit_length() - 2
     for bit in range(1, last + 1):
         if bit == last:
             n = planes_terms(velocity, planes_in, axial_in, block, n)
             s, nonlinear = sweep(velocity, n, power)
-        block, entry = merge(me, power, block, swap(block, "theta", 1 << bit), entries, points, bit)
+            ready = (s,)
+        block, entry = merge(me, power, block, swap(block, "theta", 1 << bit), entries, ready, points, bit)
         entries = (entry,)
     mine, send = enter(me, power, block, entry, own, other, s, points)
     got = swap(send, "theta", 1)

time: 38.8 us -> 39.2 us (1.010)
  waiting for transfers between devices: 16.7 us -> 17.1 us
    pallas_call x2 -> x3, Pallas kernels: 0.98 us -> 1 us  [side_terms(): pl.pallas_call(kernel, name=name, out_shape=held(*v.shape), in_specs=[SME...]
  transfers between devices with their start and end apart: 12 -> 12, of which waited for: 7 -> 8; matrix products, arithmetic and copies ran while one was open for 0% -> 0% of each run, Pallas kernels for 20% -> 19%
where the time goes in v14:
time: 39.2 us; the launch traced here: 39 us
  waiting for transfers between devices  17.1 us (44%)
  starting transfers between devices  10.8 us (28%)
  Pallas kernels  9.69 us (25%)
  between operations  1.5 us (4%)
    ppermute x11, waiting for transfers between devices, swap(): return lax.ppermute(block, axis, [(i, i ^ bit) for i in range(size)])  17.1 us
    ppermute x1, starting transfers between devices, swap_across(): return lax.ppermute(block, axis, route)  5.48 us
    ppermute x11, starting transfers between devices, swap(): return lax.ppermute(block, axis, [(i, i ^ bit) for i in range(size)])  5.29 us
    pallas_call x1, Pallas kernels, inner_terms(): pl.pallas_call(inner_kernel, name='inner_terms', out_shape=held(*v.shape)...  2.2 us
    pallas_call x2, Pallas kernels, close(): pl.pallas_call(functools.partial(close_kernel, own=own), name='close_own'...  1.59 us
    pallas_call x1, Pallas kernels, load(): pl.pallas_call(load_kernel, name='load', out_shape=(held(*v.shape), held(...  1.14 us
    pallas_call x3, Pallas kernels, side_terms(): pl.pallas_call(kernel, name=name, out_shape=held(*v.shape), in_specs=[SME...  1 us
    pallas_call x1, Pallas kernels, sweep(): pl.pallas_call(sweep_kernel, name='sweep', out_shape=(held(*v.shape), jax...  0.89 us
  transfers between devices with their start and end apart: 12, of which 8 were waited for; matrix products, arithmetic and copies ran while one was open for 0% of the time, Pallas kernels for 19%

profile of v14, /device:TPU:0, one launch (start us, length us, event | category | flops | bytes accessed | tf_op | source)
XLA Modules:
  0.0 39.0 jit_solution(11442645231683730084)
XLA Ops:
  0.6 1.1 %load.1 = (f32[3,16,8,512]{3,2,1,0:T(8,128)S(1)}, f32[1,12,8,512]{3,2,1,0:T(8,128)S(1)}) custom-call(f32[3,16,8,512]{3,2,1,0:T(8,128)} %hbm_ref.1), custom_call_target="tpu_custom_call" | custom-call | tf_op jit(solution)/shard_map/load/pallas_call | solution.py:113
  1.9 5.5 %collective-permute-start.2 = (f32[3,10,8,512]{3,2,1,0:T(8,128)S(1)}, f32[3,10,8,512]{3,2,1,0:T(8,128)S(1)}, u32[]{:S(2)}, u32[]{:S(2)}) collective-permute-start(f32[3,10,8,512]{3,2,1,0:T(8,128)S(1)} %pack_chip.1.first_ref), channel_id=1, source_target_pairs={{2,4},{4,2},{6,8},{8,6},{10,12},{12,10},{14,16},{16,14},{18,20},{2... | collective-permute-start | bytes 1474568 | tf_op jit(solution)/shard_map/ppermute | solution.py:54
  7.6 1.6 %collective-permute-start = (f32[1,12,8,512]{3,2,1,0:T(8,128)S(1)}, f32[1,12,8,512]{3,2,1,0:T(8,128)S(1)}, u32[]{:S(2)}, u32[]{:S(2)}) collective-permute-start(f32[1,12,8,512]{3,2,1,0:T(8,128)S(1)} %get-tuple-element.20.first_ref), channel_id=1, source_target_pairs={{0,1},{1,0},{2,3},{3,2},{4,5},{5,4},{6,7},{7,6},{8,9},{9,8},{10,11... | collective-permute-start | bytes 589832 | tf_op jit(solution)/shard_map/ppermute | solution.py:46
  10.0 0.6 %table.1 = (f32[30,512]{1,0:T(8,128)S(1)}, f32[21,8,128]{2,1,0:T(8,128)S(1)}) custom-call(s32[1]{0:T(128)} %bitcast.me_ref, f32[1]{0:T(128)S(6)} %copy.18.factor_ref, f32[21]{0:T(128)S(1)} %copy-done.1), custom_call_target="tpu_custom_call" | custom-call | flops 512000 | bytes 204800 | tf_op jit(solution)/shard_map/table/pallas_call | solution.py:479
  10.6 2.2 %inner_terms.1.ready_ref.refs_2_ = f32[3,16,8,512]{3,2,1,0:T(8,128)S(1)} custom-call(f32[21,8,128]{2,1,0:T(8,128)S(1)} %get-tuple-element.21.tap_ref, f32[3,16,8,512]{3,2,1,0:T(8,128)S(1)} %get-tuple-element.18.v_ref, f32[544,512]{1,0:T(8,128)S(1)} %bitcast.2), custom_call_target="tpu_custom_call" | custom-call | flops 1048576 | bytes 3145728 | tf_op jit(solution)/shard_map/inner_terms/pallas_call | solution.py:291
  12.8 2.1 %collective-permute-done.e_ref = f32[1,12,8,512]{3,2,1,0:T(8,128)S(1)} collective-permute-done((f32[1,12,8,512]{3,2,1,0:T(8,128)S(1)}, f32[1,12,8,512]{3,2,1,0:T(8,128)S(1)}, u32[]{:S(2)}, u32[]{:S(2)}) %collective-permute-start) | collective-permute-done | bytes 196640 | tf_op jit(solution)/shard_map/ppermute | solution.py:46
  14.9 0.6 %share_terms.1 = f32[2,3,8,512]{3,2,1,0:T(8,128)S(1)} custom-call(f32[3,16,8,512]{3,2,1,0:T(8,128)S(1)} %get-tuple-element.18.v_ref, f32[1,12,8,512]{3,2,1,0:T(8,128)S(1)} %collective-permute-done.e_ref, f32[30,512]{1,0:T(8,128)S(1)} %get-tuple-element.19.power_ref, f32[3,16,8,512]{3,2,1,0:T(8,128)S(1)} %inner_terms.1.ready_ref.refs_2_), custom_call_target="tpu_custom_call" | custom-call | flops 3932160 | bytes 1572864 | tf_op jit(solution)/shard_map/share_terms/pallas_call | solution.py:379
  15.5 1.6 %collective-permute-start.1 = (f32[2,3,8,512]{3,2,1,0:T(8,128)S(1)}, f32[2,3,8,512]{3,2,1,0:T(8,128)S(1)}, u32[]{:S(2)}, u32[]{:S(2)}) collective-permute-start(f32[2,3,8,512]{3,2,1,0:T(8,128)S(1)} %share_terms.1), channel_id=1, source_target_pairs={{0,1},{1,0},{2,3},{3,2},{4,5},{5,4},{6,7},{7,6},{8,9},{9,8},{10,11... | collective-permute-start | bytes 294920 | tf_op jit(solution)/shard_map/ppermute | solution.py:46
  17.1 0.5 %core_terms.1.n_in_ref = f32[3,16,8,512]{3,2,1,0:T(8,128)S(1)} custom-call(s32[1]{0:T(128)} %bitcast.me_ref, f32[21,8,128]{2,1,0:T(8,128)S(1)} %get-tuple-element.21.tap_ref, f32[3,16,8,512]{3,2,1,0:T(8,128)S(1)} %get-tuple-element.18.v_ref, f32[2,10,8,512]{3,2,1,0:T(8,128)S(1)} %collective-permute-done.4.refs_0_, ...), custom_call_target="tpu_custom_call", output_to_operand_aliasing={{}: (5, {})} | custom-call | flops 1048576 | bytes 2359296 | tf_op jit(solution)/shard_map/core_terms/pallas_call | solution.py:350
  17.6 0.5 %mirror_terms.1.refs_1_ = f32[3,16,8,512]{3,2,1,0:T(8,128)S(1)} custom-call(f32[3,16,8,512]{3,2,1,0:T(8,128)S(1)} %get-tuple-element.18.v_ref, f32[544,512]{1,0:T(8,128)S(1)} %bitcast.3, f32[3,4,8,128]{3,2,1,0:T(8,128)S(1)} %collective-permute-done.3.mirror_ref, f32[3,16,8,512]{3,2,1,0:T(8,128)S(1)} %core_terms.1.n_in_ref), custom_call_target="tpu_custom_call", output_to_operand_aliasing={{}: (3, {})} | custom-call | flops 1677721600 | bytes 3145728 | tf_op jit(solution)/shard_map/mirror_terms/pallas_call | solution.py:246
  18.1 2.1 %collective-permute-done.1.refs_2_.share_ref = f32[2,3,8,512]{3,2,1,0:T(8,128)S(1)} collective-permute-done((f32[2,3,8,512]{3,2,1,0:T(8,128)S(1)}, f32[2,3,8,512]{3,2,1,0:T(8,128)S(1)}, u32[]{:S(2)}, u32[]{:S(2)}) %collective-permute-start.1) | collective-permute-done | bytes 98336 | tf_op jit(solution)/shard_map/ppermute | solution.py:46
  20.2 0.2 late_other.1.n_ref.refs_1_
  20.6 0.3 late_own.1.n_ref.n_in_ref
  21.0 0.8 %collective-permute-done.6.other_ref = f32[2,3,8,256]{3,2,1,0:T(8,128)S(1)} collective-permute-done((f32[2,3,8,256]{3,2,1,0:T(8,128)S(1)}, f32[2,3,8,256]{3,2,1,0:T(8,128)S(1)}, u32[]{:S(2)}, u32[]{:S(2)}) %collective-permute-start.6) | collective-permute-done | bytes 49184 | tf_op jit(solution)/shard_map/ppermute | solution.py:46
  21.9 1.6 %collective-permute-start.7 = (f32[2,12,8,512]{3,2,1,0:T(8,128)S(1)}, f32[2,12,8,512]{3,2,1,0:T(8,128)S(1)}, u32[]{:S(2)}, u32[]{:S(2)}) collective-permute-start(f32[2,12,8,512]{3,2,1,0:T(8,128)S(1)} %pack_planes.1), channel_id=1, source_target_pairs={{0,1},{1,0},{2,3},{3,2},{4,5},{5,4},{6,7},{7,6},{8,9},{9,8},{10,11... | collective-permute-start | bytes 1179656 | tf_op jit(solution)/shard_map/ppermute | solution.py:46
  23.5 4.1 %collective-permute-done.8.other_ref = f32[2,3,8,256]{3,2,1,0:T(8,128)S(1)} collective-permute-done((f32[2,3,8,256]{3,2,1,0:T(8,128)S(1)}, f32[2,3,8,256]{3,2,1,0:T(8,128)S(1)}, u32[]{:S(2)}, u32[]{:S(2)}) %collective-permute-start.8) | collective-permute-done | bytes 49184 | tf_op jit(solution)/shard_map/ppermute | solution.py:46
  27.7 4.1 %collective-permute-done.9.other_ref = f32[2,3,8,256]{3,2,1,0:T(8,128)S(1)} collective-permute-done((f32[2,3,8,256]{3,2,1,0:T(8,128)S(1)}, f32[2,3,8,256]{3,2,1,0:T(8,128)S(1)}, u32[]{:S(2)}, u32[]{:S(2)}) %collective-permute-start.9) | collective-permute-done | bytes 49184 | tf_op jit(solution)/shard_map/ppermute | solution.py:46
  31.9 1.3 %collective-permute-done.7.y_ref = f32[2,12,8,512]{3,2,1,0:T(8,128)S(1)} collective-permute-done((f32[2,12,8,512]{3,2,1,0:T(8,128)S(1)}, f32[2,12,8,512]{3,2,1,0:T(8,128)S(1)}, u32[]{:S(2)}, u32[]{:S(2)}) %collective-permute-start.7) | collective-permute-done | bytes 393248 | tf_op jit(solution)/shard_map/ppermute | solution.py:46
  33.2 0.5 %planes_terms.1.n_ref = f32[3,16,8,512]{3,2,1,0:T(8,128)S(1)} custom-call(f32[3,16,8,512]{3,2,1,0:T(8,128)S(1)} %get-tuple-element.18.v_ref, f32[2,12,8,512]{3,2,1,0:T(8,128)S(1)} %collective-permute-done.7.y_ref, f32[1,12,8,512]{3,2,1,0:T(8,128)S(1)} %collective-permute-done.e_ref, ...), custom_call_target="tpu_custom_call", output_to_operand_aliasing={{}: (4, {})} | custom-call | flops 3932160 | bytes 3145728 | tf_op jit(solution)/shard_map/planes_terms/pallas_call | solution.py:434
  33.7 0.9 %sweep.1 = (f32[3,16,8,512]{3,2,1,0:T(8,128)S(1)}, f32[3,16,8,512]{3,2,1,0:T(8,128)}) custom-call(f32[3,16,8,512]{3,2,1,0:T(8,128)S(1)} %get-tuple-element.18.v_ref, f32[3,16,8,512]{3,2,1,0:T(8,128)S(1)} %planes_terms.1.n_ref, f32[30,512]{1,0:T(8,128)S(1)} %get-tuple-element.19.power_ref), custom_call_target="tpu_custom_call" | custom-call | flops 1966080 | bytes 2359296 | tf_op jit(solution)/shard_map/sweep/pallas_call | solution.py:519
  34.6 2.2 %collective-permute-done.10.other_ref = f32[2,3,8,256]{3,2,1,0:T(8,128)S(1)} collective-permute-done((f32[2,3,8,256]{3,2,1,0:T(8,128)S(1)}, f32[2,3,8,256]{3,2,1,0:T(8,128)S(1)}, u32[]{:S(2)}, u32[]{:S(2)}) %collective-permute-start.10) | collective-permute-done | bytes 49184 | tf_op jit(solution)/shard_map/ppermute | solution.py:46
  37.0 0.8 %close_own.1.refs_0_ = f32[3,16,8,512]{3,2,1,0:T(8,128)} custom-call(s32[1]{0:T(128)} %bitcast.me_ref, f32[3,16,8,512]{3,2,1,0:T(8,128)S(1)} %get-tuple-element.27.refs_1_.ready_ref.s_ref, f32[30,512]{1,0:T(8,128)S(1)} %get-tuple-element.19.power_ref, f32[2,3,8,256]{3,2,1,0:T(8,128)S(1)} %get-tuple-element.32.entry_ref), custom_call_target="tpu_custom_call" | custom-call | flops 786432 | bytes 1572864 | tf_op jit(solution)/shard_map/close_own/pallas_call | solution.py:639
  37.8 0.4 %collective-permute-done.11.entry_ref = f32[2,3,8,256]{3,2,1,0:T(8,128)S(1)} collective-permute-done((f32[2,3,8,256]{3,2,1,0:T(8,128)S(1)}, f32[2,3,8,256]{3,2,1,0:T(8,128)S(1)}, u32[]{:S(2)}, u32[]{:S(2)}) %collective-permute-start.11) | collective-permute-done | bytes 49184 | tf_op jit(solution)/shard_map/ppermute | solution.py:46
  38.2 0.8 %close_other.1 = f32[3,16,8,512]{3,2,1,0:T(8,128)} custom-call(s32[1]{0:T(128)} %bitcast.me_ref, f32[3,16,8,512]{3,2,1,0:T(8,128)S(1)} %get-tuple-element.27.refs_1_.ready_ref.s_ref, f32[30,512]{1,0:T(8,128)S(1)} %get-tuple-element.19.power_ref, f32[2,3,8,256]{3,2,1,0:T(8,128)S(1)} %collective-permute-done.11.entry_ref, ...), custom_call_target="tpu_custom_call", output_to_operand_aliasing={{}: (4, {})} | custom-call | flops 786432 | bytes 1572864 | tf_op jit(solution)/shard_map/close_other/pallas_call | solution.py:639
  (27 shorter events, 1.1 us)
Async XLA Ops:
  1.8 8.2 %copy-start.1 = (f32[21]{0:T(128)S(1)}, f32[21]{0:T(128)}, u32[]{:S(2)}) copy-start(f32[21]{0:T(128)} %stencil_ref.1) | copy-start | bytes 256
  1.8 8.8 %copy-start = (f32[512,544]{0,1:T(8,128)S(1)}, f32[512,544]{0,1:T(8,128)}, u32[]{:S(2)}) copy-start(f32[512,544]{0,1:T(8,128)} %param.5) | copy-start | bytes 3342340
  1.9 18.3 %collective-permute-start.2 = (f32[3,10,8,512]{3,2,1,0:T(8,128)S(1)}, f32[3,10,8,512]{3,2,1,0:T(8,128)S(1)}, u32[]{:S(2)}, u32[]{:S(2)}) collective-permute-start(f32[3,10,8,512]{3,2,1,0:T(8,128)S(1)} %pack_chip.1.first_ref), channel_id=1, source_target_pairs={{2,4},{4,2},{6,8},{8,6},{10,12},{12,10},{14,16},{16,14},{18,20},{2... | collective-permute-start | bytes 1474568 | tf_op jit(solution)/shard_map/ppermute | solution.py:54
  7.5 9.6 %collective-permute-start.4 = (f32[2,10,8,512]{3,2,1,0:T(8,128)S(1)}, f32[2,10,8,512]{3,2,1,0:T(8,128)S(1)}, u32[]{:S(2)}, u32[]{:S(2)}) collective-permute-start(f32[2,10,8,512]{3,2,1,0:T(8,128)S(1)} %get-tuple-element.22), channel_id=1, source_target_pairs={{0,2},{2,0},{4,6},{6,4},{8,10},{10,8},{12,14},{14,12},{16,18},{18,... | collective-permute-start | bytes 983048 | tf_op jit(solution)/shard_map/ppermute | solution.py:46
  7.6 7.3 %collective-permute-start = (f32[1,12,8,512]{3,2,1,0:T(8,128)S(1)}, f32[1,12,8,512]{3,2,1,0:T(8,128)S(1)}, u32[]{:S(2)}, u32[]{:S(2)}) collective-permute-start(f32[1,12,8,512]{3,2,1,0:T(8,128)S(1)} %get-tuple-element.20.first_ref), channel_id=1, source_target_pairs={{0,1},{1,0},{2,3},{3,2},{4,5},{5,4},{6,7},{7,6},{8,9},{9,8},{10,11... | collective-permute-start | bytes 589832 | tf_op jit(solution)/shard_map/ppermute | solution.py:46
  9.2 7.9 %collective-permute-start.5 = (f32[1,10,8,512]{3,2,1,0:T(8,128)S(1)}, f32[1,10,8,512]{3,2,1,0:T(8,128)S(1)}, u32[]{:S(2)}, u32[]{:S(2)}) collective-permute-start(f32[1,10,8,512]{3,2,1,0:T(8,128)S(1)} %get-tuple-element.23), channel_id=1, source_target_pairs={{0,2},{2,0},{4,6},{6,4},{8,10},{10,8},{12,14},{14,12},{16,18},{18,... | collective-permute-start | bytes 491528 | tf_op jit(solution)/shard_map/ppermute | solution.py:46
  9.3 8.3 %collective-permute-start.3 = (f32[3,4,8,128]{3,2,1,0:T(8,128)S(1)}, f32[3,4,8,128]{3,2,1,0:T(8,128)S(1)}, u32[]{:S(2)}, u32[]{:S(2)}) collective-permute-start(f32[3,4,8,128]{3,2,1,0:T(8,128)S(1)} %pack_mirror.1.first_ref), channel_id=1, source_target_pairs={{0,16},{2,18},{4,20},{6,22},{8,24},{10,26},{12,28},{14,30},{16,0},... | collective-permute-start | bytes 147464 | tf_op jit(solution)/shard_map/ppermute | solution.py:46
  15.5 4.7 %collective-permute-start.1 = (f32[2,3,8,512]{3,2,1,0:T(8,128)S(1)}, f32[2,3,8,512]{3,2,1,0:T(8,128)S(1)}, u32[]{:S(2)}, u32[]{:S(2)}) collective-permute-start(f32[2,3,8,512]{3,2,1,0:T(8,128)S(1)} %share_terms.1), channel_id=1, source_target_pairs={{0,1},{1,0},{2,3},{3,2},{4,5},{5,4},{6,7},{7,6},{8,9},{9,8},{10,11... | collective-permute-start | bytes 294920 | tf_op jit(solution)/shard_map/ppermute | solution.py:46
  20.6 1.3 %collective-permute-start.6 = (f32[2,3,8,256]{3,2,1,0:T(8,128)S(1)}, f32[2,3,8,256]{3,2,1,0:T(8,128)S(1)}, u32[]{:S(2)}, u32[]{:S(2)}) collective-permute-start(f32[2,3,8,256]{3,2,1,0:T(8,128)S(1)} %ends_other.1.refs_2_), channel_id=1, source_target_pairs={{0,2},{2,0},{4,6},{6,4},{8,10},{10,8},{12,14},{14,12},{16,18},{18,... | collective-permute-start | bytes 147464 | tf_op jit(solution)/shard_map/ppermute | solution.py:46
  21.9 11.2 %collective-permute-start.7 = (f32[2,12,8,512]{3,2,1,0:T(8,128)S(1)}, f32[2,12,8,512]{3,2,1,0:T(8,128)S(1)}, u32[]{:S(2)}, u32[]{:S(2)}) collective-permute-start(f32[2,12,8,512]{3,2,1,0:T(8,128)S(1)} %pack_planes.1), channel_id=1, source_target_pairs={{0,1},{1,0},{2,3},{3,2},{4,5},{5,4},{6,7},{7,6},{8,9},{9,8},{10,11... | collective-permute-start | bytes 1179656 | tf_op jit(solution)/shard_map/ppermute | solution.py:46
  23.5 4.1 %collective-permute-start.8 = (f32[2,3,8,256]{3,2,1,0:T(8,128)S(1)}, f32[2,3,8,256]{3,2,1,0:T(8,128)S(1)}, u32[]{:S(2)}, u32[]{:S(2)}) collective-permute-start(f32[2,3,8,256]{3,2,1,0:T(8,128)S(1)} %pair.1.first_ref.block_ref), channel_id=1, source_target_pairs={{0,4},{2,6},{4,0},{6,2},{8,12},{10,14},{12,8},{14,10},{16,20},{18,... | collective-permute-start | bytes 147464 | tf_op jit(solution)/shard_map/ppermute | solution.py:46
  27.6 4.2 %collective-permute-start.9 = (f32[2,3,8,256]{3,2,1,0:T(8,128)S(1)}, f32[2,3,8,256]{3,2,1,0:T(8,128)S(1)}, u32[]{:S(2)}, u32[]{:S(2)}) collective-permute-start(f32[2,3,8,256]{3,2,1,0:T(8,128)S(1)} %get-tuple-element.24.block_ref), channel_id=1, source_target_pairs={{0,8},{2,10},{4,12},{6,14},{8,0},{10,2},{12,4},{14,6},{16,24},{18,... | collective-permute-start | bytes 147464 | tf_op jit(solution)/shard_map/ppermute | solution.py:46
  31.8 5.1 %collective-permute-start.10 = (f32[2,3,8,256]{3,2,1,0:T(8,128)S(1)}, f32[2,3,8,256]{3,2,1,0:T(8,128)S(1)}, u32[]{:S(2)}, u32[]{:S(2)}) collective-permute-start(f32[2,3,8,256]{3,2,1,0:T(8,128)S(1)} %get-tuple-element.26.ready_ref.block_ref), channel_id=1, source_target_pairs={{0,16},{2,18},{4,20},{6,22},{8,24},{10,26},{12,28},{14,30},{16,0},... | collective-permute-start | bytes 147464 | tf_op jit(solution)/shard_map/ppermute | solution.py:46
  36.9 1.3 %collective-permute-start.11 = (f32[2,3,8,256]{3,2,1,0:T(8,128)S(1)}, f32[2,3,8,256]{3,2,1,0:T(8,128)S(1)}, u32[]{:S(2)}, u32[]{:S(2)}) collective-permute-start(f32[2,3,8,256]{3,2,1,0:T(8,128)S(1)} %get-tuple-element.31), channel_id=1, source_target_pairs={{0,2},{2,0},{4,6},{6,4},{8,10},{10,8},{12,14},{14,12},{16,18},{18,... | collective-permute-start | bytes 147464 | tf_op jit(solution)/shard_map/ppermute | solution.py:46

commit v15 on v11

--- a/solution.py
+++ b/solution.py
@@ -297,13 +297,16 @@
     )(taps, v, op)
 
 
-def add_side(tap_ref, v_ref, side_ref, n_in_ref, n_ref, before):
+def add_side(tap_ref, v_ref, side_ref, n_in_ref, n_ref, before, columns):
     comps, points, _, radial = v_ref.shape
     reach = side_ref.shape[1]
     first = 0 if before else reach + 1
 
-    @pl.loop(0, radial // LANES)
-    def column(k):
+    start, count = columns
+
+    @pl.loop(0, count)
+    def column(i):
+        k = start + i
         lanes = pl.ds(pl.multiple_of(k * LANES, LANES), LANES)
         inv_r = inverse_radius(LANES, k * LANES)
         weights = [tap_ref[first + i] for i in range(reach)]
@@ -321,29 +324,32 @@
 
 def core_kernel(me_ref, tap_ref, v_ref, core_ref, n_in_ref, n_ref):
     even = me_ref[0] % 2 == 0
-    add = functools.partial(add_side, tap_ref, v_ref, core_ref, n_in_ref, n_ref)
-    pl.when(even)(lambda: add(False))
-    pl.when(jnp.logical_not(even))(lambda: add(True))
-
-
-def late_kernel(me_ref, tap_ref, v_ref, chip_ref, n_in_ref, n_ref):
-    even = me_ref[0] % 2 == 0
-    add = functools.partial(add_side, tap_ref, v_ref, chip_ref, n_in_ref, n_ref)
-    pl.when(even)(lambda: add(True))
-    pl.when(jnp.logical_not(even))(lambda: add(False))
-
-
-def side_terms(kernel, name, me, taps, v, side, n):
+    columns = (0, v_ref.shape[3] // LANES)
+    add = functools.partial(add_side, tap_ref, v_ref, core_ref, n_in_ref, n_ref, columns=columns)
+    pl.when(even)(lambda: add(before=False))
+    pl.when(jnp.logical_not(even))(lambda: add(before=True))
+
+
+def late_kernel(me_ref, tap_ref, v_ref, chip_ref, n_in_ref, ready_ref, n_ref, *, own):
+    core = me_ref[0] % 2
+    count = v_ref.shape[3] // (2 * LANES)
+    columns = ((core if own else 1 - core) * count, count)
+    add = functools.partial(add_side, tap_ref, v_ref, chip_ref, n_in_ref, n_ref, columns=columns)
+    pl.when(core == 0)(lambda: add(before=True))
+    pl.when(core == 1)(lambda: add(before=False))
+
+
+def side_terms(kernel, name, me, taps, v, side, n, ready=()):
     return pl.pallas_call(
         kernel,
         name=name,
         out_shape=held(*v.shape),
-        in_specs=[SMEM, VMEM, VMEM, VMEM, VMEM],
+        in_specs=[SMEM] + [VMEM] * 4 + [ANY] * len(ready),
         out_specs=VMEM,
         input_output_aliases={4: 0},
         compiler_params=params(v.size * 4, 5),
         cost_estimate=pl.CostEstimate(flops=SIDE, bytes_accessed=12 * v.size, transcendentals=0),
-    )(me, taps, v, side, n)
+    )(me, taps, v, side, n, *ready)
 
 
 def share_kernel(v_ref, e_ref, power_ref, ends_ref, tile_ref):
@@ -653,7 +659,7 @@
     chip_in = swap_across(chip_out, "theta")
     mirror_out = pack_mirror(velocity, chip_out, width)
     mirror_in = swap(mirror_out, "theta", sectors // 2)
-    core_out = pack_side(me, velocity, mirror_out, reach, True)
+    core_out = pack_side(me, velocity, axial_in, reach, True)
     core_in = swap(core_out, "theta", 1)
     power, taps = table(me, viscous_factor, azimuth_stencil, points, sectors, planes, radial)
     n = inner_terms(taps, velocity, op)
@@ -662,9 +668,12 @@
     planes_in = swap(pack_planes(velocity, share_out), "gz", 1)
     n = side_terms(core_kernel, "core_terms", me, taps, velocity, core_in, n)
     n = mirror_terms(velocity, op, mirror_in, n)
-    n = side_terms(late_kernel, "late_terms", me, taps, velocity, chip_in, n)
+    late = functools.partial(late_kernel, own=False)
+    n = side_terms(late, "late_other", me, taps, velocity, chip_in, n, (share_in,))
     send = ends_terms(me, velocity, share_in, power, n, False)
     other = swap(send, "theta", 1)
+    late = functools.partial(late_kernel, own=True)
+    n = side_terms(late, "late_own", me, taps, velocity, chip_in, n, (send,))
     own = ends_terms(me, velocity, share_in, power, n, True)
     block = pair(me, power, own, other, points)
     entries = ()

time: 35.9 us -> 35.7 us (level)
    pallas_call x2 -> x3, Pallas kernels: 1.02 us -> 1.03 us  [side_terms(): pl.pallas_call(kernel, name=name, out_shape=held(*v.shape), in_specs=[SME...]
where the time goes in v15:
time: 35.7 us; the launch traced here: 35.5 us
  starting transfers between devices  16.9 us (47%)
  Pallas kernels  9.7 us (27%)
  waiting for transfers between devices  7.42 us (21%)
  between operations  1.49 us (4%)
    ppermute x10, starting transfers between devices, swap(): return lax.ppermute(block, axis, [(i, i ^ bit) for i in range(size)])  13.1 us
    ppermute x10, waiting for transfers between devices, swap(): return lax.ppermute(block, axis, [(i, i ^ bit) for i in range(size)])  7.42 us
    ppermute x1, starting transfers between devices, swap_across(): return lax.ppermute(block, axis, route)  3.76 us
    pallas_call x1, Pallas kernels, inner_terms(): pl.pallas_call(inner_kernel, name='inner_terms', out_shape=held(*v.shape)...  2.2 us
    pallas_call x2, Pallas kernels, close(): pl.pallas_call(functools.partial(close_kernel, own=own), name='close_own'...  1.59 us
    pallas_call x1, Pallas kernels, load(): pl.pallas_call(load_kernel, name='load', out_shape=(held(*v.shape), held(...  1.14 us
    pallas_call x3, Pallas kernels, side_terms(): pl.pallas_call(kernel, name=name, out_shape=held(*v.shape), in_specs=[SME...  1.03 us
    pallas_call x1, Pallas kernels, sweep(): pl.pallas_call(sweep_kernel, name='sweep', out_shape=(held(*v.shape), jax...  0.89 us
  transfers between devices with their start and end apart: 11, of which 6 were waited for; matrix products, arithmetic and copies ran while one was open for 0% of the time, Pallas kernels for 22%

profile of v15, /device:TPU:0, one launch (start us, length us, event | category | flops | bytes accessed | tf_op | source)
XLA Modules:
  0.0 35.5 jit_solution(7053220385342191863)
XLA Ops:
  0.6 1.1 %load.1 = (f32[3,16,8,512]{3,2,1,0:T(8,128)S(1)}, f32[1,12,8,512]{3,2,1,0:T(8,128)S(1)}) custom-call(f32[3,16,8,512]{3,2,1,0:T(8,128)} %hbm_ref.1), custom_call_target="tpu_custom_call" | custom-call | tf_op jit(solution)/shard_map/load/pallas_call | solution.py:111
  1.8 3.0 %collective-permute-start = (f32[1,12,8,512]{3,2,1,0:T(8,128)S(1)}, f32[1,12,8,512]{3,2,1,0:T(8,128)S(1)}, u32[]{:S(2)}, u32[]{:S(2)}) collective-permute-start(f32[1,12,8,512]{3,2,1,0:T(8,128)S(1)} %get-tuple-element.17.first_ref), channel_id=1, source_target_pairs={{0,1},{1,0},{2,3},{3,2},{4,5},{5,4},{6,7},{7,6},{8,9},{9,8},{10,11... | collective-permute-start | bytes 589832 | tf_op jit(solution)/shard_map/ppermute | solution.py:44
  4.8 3.8 %collective-permute-start.3 = (f32[3,10,8,512]{3,2,1,0:T(8,128)S(1)}, f32[3,10,8,512]{3,2,1,0:T(8,128)S(1)}, u32[]{:S(2)}, u32[]{:S(2)}) collective-permute-start(f32[3,10,8,512]{3,2,1,0:T(8,128)S(1)} %pack_chip.1.first_ref), channel_id=1, source_target_pairs={{2,4},{4,2},{6,8},{8,6},{10,12},{12,10},{14,16},{16,14},{18,20},{2... | collective-permute-start | bytes 1474568 | tf_op jit(solution)/shard_map/ppermute | solution.py:52
  9.4 0.6 %table.1 = (f32[30,512]{1,0:T(8,128)S(1)}, f32[21,8,128]{2,1,0:T(8,128)S(1)}) custom-call(s32[1]{0:T(128)} %bitcast.me_ref, f32[1]{0:T(128)S(6)} %copy.18.factor_ref, f32[21]{0:T(128)S(1)} %copy-done.1), custom_call_target="tpu_custom_call" | custom-call | flops 512000 | bytes 204800 | tf_op jit(solution)/shard_map/table/pallas_call | solution.py:472
  10.1 0.6 %share_terms.1.first_ref = f32[2,3,8,512]{3,2,1,0:T(8,128)S(1)} custom-call(f32[3,16,8,512]{3,2,1,0:T(8,128)S(1)} %get-tuple-element.16.v_ref, f32[1,12,8,512]{3,2,1,0:T(8,128)S(1)} %collective-permute-done.e_ref.first_ref, f32[30,512]{1,0:T(8,128)S(1)} %get-tuple-element.18.power_ref), custom_call_target="tpu_custom_call" | custom-call | flops 3932160 | bytes 1572864 | tf_op jit(solution)/shard_map/share_terms/pallas_call | solution.py:372
  10.7 1.4 %collective-permute-start.2 = (f32[2,3,8,512]{3,2,1,0:T(8,128)S(1)}, f32[2,3,8,512]{3,2,1,0:T(8,128)S(1)}, u32[]{:S(2)}, u32[]{:S(2)}) collective-permute-start(f32[2,3,8,512]{3,2,1,0:T(8,128)S(1)} %share_terms.1.first_ref), channel_id=1, source_target_pairs={{0,1},{1,0},{2,3},{3,2},{4,5},{5,4},{6,7},{7,6},{8,9},{9,8},{10,11... | collective-permute-start | bytes 294920 | tf_op jit(solution)/shard_map/ppermute | solution.py:44
  12.3 0.7 %collective-permute-start.1 = (f32[2,12,8,512]{3,2,1,0:T(8,128)S(1)}, f32[2,12,8,512]{3,2,1,0:T(8,128)S(1)}, u32[]{:S(2)}, u32[]{:S(2)}) collective-permute-start(f32[2,12,8,512]{3,2,1,0:T(8,128)S(1)} %pack_planes.1), channel_id=1, source_target_pairs={{0,1},{1,0},{2,3},{3,2},{4,5},{5,4},{6,7},{7,6},{8,9},{9,8},{10,11... | collective-permute-start | bytes 1179656 | tf_op jit(solution)/shard_map/ppermute | solution.py:44
  13.1 2.2 %inner_terms.1.n_in_ref = f32[3,16,8,512]{3,2,1,0:T(8,128)S(1)} custom-call(f32[21,8,128]{2,1,0:T(8,128)S(1)} %get-tuple-element.19.tap_ref, f32[3,16,8,512]{3,2,1,0:T(8,128)S(1)} %get-tuple-element.16.v_ref, f32[544,512]{1,0:T(8,128)S(1)} %bitcast.2), custom_call_target="tpu_custom_call" | custom-call | flops 5368709120 | bytes 3145728 | tf_op jit(solution)/shard_map/inner_terms/pallas_call | solution.py:288
  15.3 0.5 %core_terms.1.n_in_ref = f32[3,16,8,512]{3,2,1,0:T(8,128)S(1)} custom-call(s32[1]{0:T(128)} %bitcast.me_ref, f32[21,8,128]{2,1,0:T(8,128)S(1)} %get-tuple-element.19.tap_ref, f32[3,16,8,512]{3,2,1,0:T(8,128)S(1)} %get-tuple-element.16.v_ref, f32[3,10,8,512]{3,2,1,0:T(8,128)S(1)} %collective-permute-done.5.core_ref, ...), custom_call_target="tpu_custom_call", output_to_operand_aliasing={{}: (4, {})} | custom-call | flops 67108864 | bytes 2359296 | tf_op jit(solution)/shard_map/core_terms/pallas_call | solution.py:343
  15.8 0.6 %collective-permute-done.4.mirror_ref = f32[3,4,8,128]{3,2,1,0:T(8,128)S(1)} collective-permute-done((f32[3,4,8,128]{3,2,1,0:T(8,128)S(1)}, f32[3,4,8,128]{3,2,1,0:T(8,128)S(1)}, u32[]{:S(2)}, u32[]{:S(2)}) %collective-permute-start.4) | collective-permute-done | bytes 49184 | tf_op jit(solution)/shard_map/ppermute | solution.py:44
  16.4 0.5 %mirror_terms.1.n_in_ref = f32[3,16,8,512]{3,2,1,0:T(8,128)S(1)} custom-call(f32[3,16,8,512]{3,2,1,0:T(8,128)S(1)} %get-tuple-element.16.v_ref, f32[544,512]{1,0:T(8,128)S(1)} %bitcast.3, f32[3,4,8,128]{3,2,1,0:T(8,128)S(1)} %collective-permute-done.4.mirror_ref, f32[3,16,8,512]{3,2,1,0:T(8,128)S(1)} %core_terms.1.n_in_ref), custom_call_target="tpu_custom_call", output_to_operand_aliasing={{}: (3, {})} | custom-call | flops 67108864 | bytes 3145728 | tf_op jit(solution)/shard_map/mirror_terms/pallas_call | solution.py:243
  17.3 1.7 %collective-permute-start.6 = (f32[2,3,8,256]{3,2,1,0:T(8,128)S(1)}, f32[2,3,8,256]{3,2,1,0:T(8,128)S(1)}, u32[]{:S(2)}, u32[]{:S(2)}) collective-permute-start(f32[2,3,8,256]{3,2,1,0:T(8,128)S(1)} %ends_other.1.ready_ref), channel_id=1, source_target_pairs={{0,2},{2,0},{4,6},{6,4},{8,10},{10,8},{12,14},{14,12},{16,18},{18,... | collective-permute-start | bytes 147464 | tf_op jit(solution)/shard_map/ppermute | solution.py:44
  19.4 0.5 %collective-permute-done.6.other_ref = f32[2,3,8,256]{3,2,1,0:T(8,128)S(1)} collective-permute-done((f32[2,3,8,256]{3,2,1,0:T(8,128)S(1)}, f32[2,3,8,256]{3,2,1,0:T(8,128)S(1)}, u32[]{:S(2)}, u32[]{:S(2)}) %collective-permute-start.6) | collective-permute-done | bytes 49184 | tf_op jit(solution)/shard_map/ppermute | solution.py:44
  19.9 1.7 %collective-permute-start.7 = (f32[2,3,8,256]{3,2,1,0:T(8,128)S(1)}, f32[2,3,8,256]{3,2,1,0:T(8,128)S(1)}, u32[]{:S(2)}, u32[]{:S(2)}) collective-permute-start(f32[2,3,8,256]{3,2,1,0:T(8,128)S(1)} %pair.1.block_ref), channel_id=1, source_target_pairs={{0,4},{2,6},{4,0},{6,2},{8,12},{10,14},{12,8},{14,10},{16,20},{18,... | collective-permute-start | bytes 147464 | tf_op jit(solution)/shard_map/ppermute | solution.py:44
  21.7 2.4 %collective-permute-done.7.other_ref = f32[2,3,8,256]{3,2,1,0:T(8,128)S(1)} collective-permute-done((f32[2,3,8,256]{3,2,1,0:T(8,128)S(1)}, f32[2,3,8,256]{3,2,1,0:T(8,128)S(1)}, u32[]{:S(2)}, u32[]{:S(2)}) %collective-permute-start.7) | collective-permute-done | bytes 49184 | tf_op jit(solution)/shard_map/ppermute | solution.py:44
  24.1 1.6 %collective-permute-start.8 = (f32[2,3,8,256]{3,2,1,0:T(8,128)S(1)}, f32[2,3,8,256]{3,2,1,0:T(8,128)S(1)}, u32[]{:S(2)}, u32[]{:S(2)}) collective-permute-start(f32[2,3,8,256]{3,2,1,0:T(8,128)S(1)} %get-tuple-element.20.block_ref), channel_id=1, source_target_pairs={{0,8},{2,10},{4,12},{6,14},{8,0},{10,2},{12,4},{14,6},{16,24},{18,... | collective-permute-start | bytes 147464 | tf_op jit(solution)/shard_map/ppermute | solution.py:44
  25.7 2.5 %collective-permute-done.8.other_ref = f32[2,3,8,256]{3,2,1,0:T(8,128)S(1)} collective-permute-done((f32[2,3,8,256]{3,2,1,0:T(8,128)S(1)}, f32[2,3,8,256]{3,2,1,0:T(8,128)S(1)}, u32[]{:S(2)}, u32[]{:S(2)}) %collective-permute-start.8) | collective-permute-done | bytes 49184 | tf_op jit(solution)/shard_map/ppermute | solution.py:44
  28.3 2.7 %collective-permute-start.9 = (f32[2,3,8,256]{3,2,1,0:T(8,128)S(1)}, f32[2,3,8,256]{3,2,1,0:T(8,128)S(1)}, u32[]{:S(2)}, u32[]{:S(2)}) collective-permute-start(f32[2,3,8,256]{3,2,1,0:T(8,128)S(1)} %get-tuple-element.22.ready_ref.block_ref), channel_id=1, source_target_pairs={{0,16},{2,18},{4,20},{6,22},{8,24},{10,26},{12,28},{14,30},{16,0},... | collective-permute-start | bytes 147464 | tf_op jit(solution)/shard_map/ppermute | solution.py:44
  30.9 0.5 %planes_terms.1.n_ref = f32[3,16,8,512]{3,2,1,0:T(8,128)S(1)} custom-call(f32[3,16,8,512]{3,2,1,0:T(8,128)S(1)} %get-tuple-element.16.v_ref, f32[2,12,8,512]{3,2,1,0:T(8,128)S(1)} %collective-permute-done.1.y_ref, f32[1,12,8,512]{3,2,1,0:T(8,128)S(1)} %collective-permute-done.e_ref.first_ref, ...), custom_call_target="tpu_custom_call", output_to_operand_aliasing={{}: (4, {})} | custom-call | flops 3932160 | bytes 3145728 | tf_op jit(solution)/shard_map/planes_terms/pallas_call | solution.py:427
  31.5 0.9 %sweep.1 = (f32[3,16,8,512]{3,2,1,0:T(8,128)S(1)}, f32[3,16,8,512]{3,2,1,0:T(8,128)}) custom-call(f32[3,16,8,512]{3,2,1,0:T(8,128)S(1)} %get-tuple-element.16.v_ref, f32[3,16,8,512]{3,2,1,0:T(8,128)S(1)} %planes_terms.1.n_ref, f32[30,512]{1,0:T(8,128)S(1)} %get-tuple-element.18.power_ref), custom_call_target="tpu_custom_call" | custom-call | flops 1966080 | bytes 2359296 | tf_op jit(solution)/shard_map/sweep/pallas_call | solution.py:512
  32.4 0.9 %collective-permute-done.9.other_ref = f32[2,3,8,256]{3,2,1,0:T(8,128)S(1)} collective-permute-done((f32[2,3,8,256]{3,2,1,0:T(8,128)S(1)}, f32[2,3,8,256]{3,2,1,0:T(8,128)S(1)}, u32[]{:S(2)}, u32[]{:S(2)}) %collective-permute-start.9) | collective-permute-done | bytes 49184 | tf_op jit(solution)/shard_map/ppermute | solution.py:44
  33.5 0.8 %close_own.1.refs_0_ = f32[3,16,8,512]{3,2,1,0:T(8,128)} custom-call(s32[1]{0:T(128)} %bitcast.me_ref, f32[3,16,8,512]{3,2,1,0:T(8,128)S(1)} %get-tuple-element.23.ready_ref.s_ref, f32[30,512]{1,0:T(8,128)S(1)} %get-tuple-element.18.power_ref, f32[2,3,8,256]{3,2,1,0:T(8,128)S(1)} %get-tuple-element.28.entry_ref), custom_call_target="tpu_custom_call" | custom-call | flops 786432 | bytes 1572864 | tf_op jit(solution)/shard_map/close_own/pallas_call | solution.py:632
  34.3 0.4 %collective-permute-done.10.entry_ref = f32[2,3,8,256]{3,2,1,0:T(8,128)S(1)} collective-permute-done((f32[2,3,8,256]{3,2,1,0:T(8,128)S(1)}, f32[2,3,8,256]{3,2,1,0:T(8,128)S(1)}, u32[]{:S(2)}, u32[]{:S(2)}) %collective-permute-start.10) | collective-permute-done | bytes 49184 | tf_op jit(solution)/shard_map/ppermute | solution.py:44
  34.7 0.8 %close_other.1 = f32[3,16,8,512]{3,2,1,0:T(8,128)} custom-call(s32[1]{0:T(128)} %bitcast.me_ref, f32[3,16,8,512]{3,2,1,0:T(8,128)S(1)} %get-tuple-element.23.ready_ref.s_ref, f32[30,512]{1,0:T(8,128)S(1)} %get-tuple-element.18.power_ref, f32[2,3,8,256]{3,2,1,0:T(8,128)S(1)} %collective-permute-done.10.entry_ref, ...), custom_call_target="tpu_custom_call", output_to_operand_aliasing={{}: (4, {})} | custom-call | flops 786432 | bytes 1572864 | tf_op jit(solution)/shard_map/close_other/pallas_call | solution.py:632
  (25 shorter events, 1.3 us)
Async XLA Ops:
  1.8 8.3 %collective-permute-start = (f32[1,12,8,512]{3,2,1,0:T(8,128)S(1)}, f32[1,12,8,512]{3,2,1,0:T(8,128)S(1)}, u32[]{:S(2)}, u32[]{:S(2)}) collective-permute-start(f32[1,12,8,512]{3,2,1,0:T(8,128)S(1)} %get-tuple-element.17.first_ref), channel_id=1, source_target_pairs={{0,1},{1,0},{2,3},{3,2},{4,5},{5,4},{6,7},{7,6},{8,9},{9,8},{10,11... | collective-permute-start | bytes 589832 | tf_op jit(solution)/shard_map/ppermute | solution.py:44
  4.8 4.6 %copy-start.1 = (f32[21]{0:T(128)S(1)}, f32[21]{0:T(128)}, u32[]{:S(2)}) copy-start(f32[21]{0:T(128)} %stencil_ref.1) | copy-start | bytes 256
  4.8 12.1 %collective-permute-start.3 = (f32[3,10,8,512]{3,2,1,0:T(8,128)S(1)}, f32[3,10,8,512]{3,2,1,0:T(8,128)S(1)}, u32[]{:S(2)}, u32[]{:S(2)}) collective-permute-start(f32[3,10,8,512]{3,2,1,0:T(8,128)S(1)} %pack_chip.1.first_ref), channel_id=1, source_target_pairs={{2,4},{4,2},{6,8},{8,6},{10,12},{12,10},{14,16},{16,14},{18,20},{2... | collective-permute-start | bytes 1474568 | tf_op jit(solution)/shard_map/ppermute | solution.py:52
  8.7 7.7 %collective-permute-start.4 = (f32[3,4,8,128]{3,2,1,0:T(8,128)S(1)}, f32[3,4,8,128]{3,2,1,0:T(8,128)S(1)}, u32[]{:S(2)}, u32[]{:S(2)}) collective-permute-start(f32[3,4,8,128]{3,2,1,0:T(8,128)S(1)} %pack_mirror.1), channel_id=1, source_target_pairs={{0,16},{2,18},{4,20},{6,22},{8,24},{10,26},{12,28},{14,30},{16,0},... | collective-permute-start | bytes 147464 | tf_op jit(solution)/shard_map/ppermute | solution.py:44
  10.7 2.4 %copy-start = (f32[512,544]{0,1:T(8,128)S(1)}, f32[512,544]{0,1:T(8,128)}, u32[]{:S(2)}) copy-start(f32[512,544]{0,1:T(8,128)} %param.5) | copy-start | bytes 3342340
  10.7 6.2 %collective-permute-start.2 = (f32[2,3,8,512]{3,2,1,0:T(8,128)S(1)}, f32[2,3,8,512]{3,2,1,0:T(8,128)S(1)}, u32[]{:S(2)}, u32[]{:S(2)}) collective-permute-start(f32[2,3,8,512]{3,2,1,0:T(8,128)S(1)} %share_terms.1.first_ref), channel_id=1, source_target_pairs={{0,1},{1,0},{2,3},{3,2},{4,5},{5,4},{6,7},{7,6},{8,9},{9,8},{10,11... | collective-permute-start | bytes 294920 | tf_op jit(solution)/shard_map/ppermute | solution.py:44
  12.3 3.0 %collective-permute-start.5 = (f32[3,10,8,512]{3,2,1,0:T(8,128)S(1)}, f32[3,10,8,512]{3,2,1,0:T(8,128)S(1)}, u32[]{:S(2)}, u32[]{:S(2)}) collective-permute-start(f32[3,10,8,512]{3,2,1,0:T(8,128)S(1)} %pack_core.1), channel_id=1, source_target_pairs={{0,2},{2,0},{4,6},{6,4},{8,10},{10,8},{12,14},{14,12},{16,18},{18,... | collective-permute-start | bytes 1474568 | tf_op jit(solution)/shard_map/ppermute | solution.py:44
  12.3 18.6 %collective-permute-start.1 = (f32[2,12,8,512]{3,2,1,0:T(8,128)S(1)}, f32[2,12,8,512]{3,2,1,0:T(8,128)S(1)}, u32[]{:S(2)}, u32[]{:S(2)}) collective-permute-start(f32[2,12,8,512]{3,2,1,0:T(8,128)S(1)} %pack_planes.1), channel_id=1, source_target_pairs={{0,1},{1,0},{2,3},{3,2},{4,5},{5,4},{6,7},{7,6},{8,9},{9,8},{10,11... | collective-permute-start | bytes 1179656 | tf_op jit(solution)/shard_map/ppermute | solution.py:44
  17.3 2.6 %collective-permute-start.6 = (f32[2,3,8,256]{3,2,1,0:T(8,128)S(1)}, f32[2,3,8,256]{3,2,1,0:T(8,128)S(1)}, u32[]{:S(2)}, u32[]{:S(2)}) collective-permute-start(f32[2,3,8,256]{3,2,1,0:T(8,128)S(1)} %ends_other.1.ready_ref), channel_id=1, source_target_pairs={{0,2},{2,0},{4,6},{6,4},{8,10},{10,8},{12,14},{14,12},{16,18},{18,... | collective-permute-start | bytes 147464 | tf_op jit(solution)/shard_map/ppermute | solution.py:44
  19.9 4.2 %collective-permute-start.7 = (f32[2,3,8,256]{3,2,1,0:T(8,128)S(1)}, f32[2,3,8,256]{3,2,1,0:T(8,128)S(1)}, u32[]{:S(2)}, u32[]{:S(2)}) collective-permute-start(f32[2,3,8,256]{3,2,1,0:T(8,128)S(1)} %pair.1.block_ref), channel_id=1, source_target_pairs={{0,4},{2,6},{4,0},{6,2},{8,12},{10,14},{12,8},{14,10},{16,20},{18,... | collective-permute-start | bytes 147464 | tf_op jit(solution)/shard_map/ppermute | solution.py:44
  24.1 4.2 %collective-permute-start.8 = (f32[2,3,8,256]{3,2,1,0:T(8,128)S(1)}, f32[2,3,8,256]{3,2,1,0:T(8,128)S(1)}, u32[]{:S(2)}, u32[]{:S(2)}) collective-permute-start(f32[2,3,8,256]{3,2,1,0:T(8,128)S(1)} %get-tuple-element.20.block_ref), channel_id=1, source_target_pairs={{0,8},{2,10},{4,12},{6,14},{8,0},{10,2},{12,4},{14,6},{16,24},{18,... | collective-permute-start | bytes 147464 | tf_op jit(solution)/shard_map/ppermute | solution.py:44
  28.3 5.1 %collective-permute-start.9 = (f32[2,3,8,256]{3,2,1,0:T(8,128)S(1)}, f32[2,3,8,256]{3,2,1,0:T(8,128)S(1)}, u32[]{:S(2)}, u32[]{:S(2)}) collective-permute-start(f32[2,3,8,256]{3,2,1,0:T(8,128)S(1)} %get-tuple-element.22.ready_ref.block_ref), channel_id=1, source_target_pairs={{0,16},{2,18},{4,20},{6,22},{8,24},{10,26},{12,28},{14,30},{16,0},... | collective-permute-start | bytes 147464 | tf_op jit(solution)/shard_map/ppermute | solution.py:44
  33.4 1.3 %collective-permute-start.10 = (f32[2,3,8,256]{3,2,1,0:T(8,128)S(1)}, f32[2,3,8,256]{3,2,1,0:T(8,128)S(1)}, u32[]{:S(2)}, u32[]{:S(2)}) collective-permute-start(f32[2,3,8,256]{3,2,1,0:T(8,128)S(1)} %get-tuple-element.27), channel_id=1, source_target_pairs={{0,2},{2,0},{4,6},{6,4},{8,10},{10,8},{12,14},{14,12},{16,18},{18,... | collective-permute-start | bytes 147464 | tf_op jit(solution)/shard_map/ppermute | solution.py:44

commit v16 on v15

--- a/solution.py
+++ b/solution.py
@@ -14,7 +14,7 @@
 LANES = 128
 UNROLL = 16
 INNER = 10 << 29
-MIRROR = 1 << 26
+MIRROR = 1 << 31
 SIDE = 1 << 26
 
 VMEM = pl.BlockSpec(memory_space=pltpu.VMEM)
@@ -119,20 +119,21 @@
     )(v)
 
 
-def pack_planes_kernel(v_ref, first_ref, y_ref):
+def pack_planes_kernel(v_ref, *refs):
+    y_ref = refs[-1]
     pack_tiles(v_ref, y_ref, range(y_ref.shape[0]))
 
 
-def pack_planes(v, first):
+def pack_planes(v, *first):
     comps, points, planes, radial = v.shape
     return pl.pallas_call(
         pack_planes_kernel,
         name="pack_planes",
         out_shape=held(comps - 1, points - points // 4, planes, radial),
-        in_specs=[VMEM, ANY],
+        in_specs=[VMEM] + [ANY] * len(first),
         out_specs=VMEM,
         compiler_params=params(v.size * 4, 2),
-    )(v, first)
+    )(v, *first)
 
 
 def pack_side_kernel(me_ref, v_ref, first_ref, side_ref, *, after):
@@ -253,7 +254,7 @@
     )(v, op, mirror, n)
 
 
-def inner_kernel(tap_ref, v_ref, op_ref, n_ref, grad_ref):
+def inner_kernel(tap_ref, v_ref, op_ref, ready_ref, n_ref, grad_ref):
     comps, points, planes, radial = v_ref.shape
     reach = (tap_ref.shape[0] - 1) // 2
     rows = points * planes
@@ -284,17 +285,17 @@
                 n_ref[c, t, :, lanes] = n
 
 
-def inner_terms(taps, v, op):
+def inner_terms(taps, v, op, ready):
     return pl.pallas_call(
         inner_kernel,
         name="inner_terms",
         out_shape=held(*v.shape),
-        in_specs=[VMEM] * 3,
+        in_specs=[VMEM] * 3 + [ANY],
         out_specs=VMEM,
         scratch_shapes=[pltpu.VMEM((v.size // v.shape[3], v.shape[3]), jnp.float32)],
         compiler_params=params(v.size * 4, 7),
         cost_estimate=pl.CostEstimate(flops=INNER, bytes_accessed=16 * v.size, transcendentals=0),
-    )(taps, v, op)
+    )(taps, v, op, ready)
 
 
 def add_side(tap_ref, v_ref, side_ref, n_in_ref, n_ref, before, columns):
@@ -322,30 +323,32 @@
                 n_ref[c, t, :, lanes] = n_in_ref[c, t, :, lanes] + v_ref[1, t, :, lanes] * inv_r * around
 
 
-def core_kernel(me_ref, tap_ref, v_ref, core_ref, n_in_ref, n_ref):
+def core_kernel(me_ref, tap_ref, v_ref, core_ref, n_in_ref, n_ref, done_ref):
     even = me_ref[0] % 2 == 0
     columns = (0, v_ref.shape[3] // LANES)
     add = functools.partial(add_side, tap_ref, v_ref, core_ref, n_in_ref, n_ref, columns=columns)
     pl.when(even)(lambda: add(before=False))
     pl.when(jnp.logical_not(even))(lambda: add(before=True))
-
-
-def late_kernel(me_ref, tap_ref, v_ref, chip_ref, n_in_ref, ready_ref, n_ref, *, own):
+    done_ref[...] = jnp.zeros_like(done_ref)
+
+
+def late_kernel(me_ref, tap_ref, v_ref, chip_ref, n_in_ref, ready_ref, n_ref, done_ref, *, own):
     core = me_ref[0] % 2
     count = v_ref.shape[3] // (2 * LANES)
     columns = ((core if own else 1 - core) * count, count)
     add = functools.partial(add_side, tap_ref, v_ref, chip_ref, n_in_ref, n_ref, columns=columns)
     pl.when(core == 0)(lambda: add(before=True))
     pl.when(core == 1)(lambda: add(before=False))
+    done_ref[...] = jnp.zeros_like(done_ref)
 
 
 def side_terms(kernel, name, me, taps, v, side, n, ready=()):
     return pl.pallas_call(
         kernel,
         name=name,
-        out_shape=held(*v.shape),
+        out_shape=(held(*v.shape), held(8, LANES)),
         in_specs=[SMEM] + [VMEM] * 4 + [ANY] * len(ready),
-        out_specs=VMEM,
+        out_specs=(VMEM, VMEM),
         input_output_aliases={4: 0},
         compiler_params=params(v.size * 4, 5),
         cost_estimate=pl.CostEstimate(flops=SIDE, bytes_accessed=12 * v.size, transcendentals=0),
@@ -662,18 +665,18 @@
     core_out = pack_side(me, velocity, axial_in, reach, True)
     core_in = swap(core_out, "theta", 1)
     power, taps = table(me, viscous_factor, azimuth_stencil, points, sectors, planes, radial)
-    n = inner_terms(taps, velocity, op)
     share_out = share_terms(velocity, axial_in, power)
     share_in = swap(share_out, "gz", 1)
-    planes_in = swap(pack_planes(velocity, share_out), "gz", 1)
-    n = side_terms(core_kernel, "core_terms", me, taps, velocity, core_in, n)
+    n = inner_terms(taps, velocity, op, share_out)
+    n, done = side_terms(core_kernel, "core_terms", me, taps, velocity, core_in, n)
+    planes_in = swap(pack_planes(velocity, done), "gz", 1)
     n = mirror_terms(velocity, op, mirror_in, n)
     late = functools.partial(late_kernel, own=False)
-    n = side_terms(late, "late_other", me, taps, velocity, chip_in, n, (share_in,))
+    n, _ = side_terms(late, "late_other", me, taps, velocity, chip_in, n, (share_in,))
     send = ends_terms(me, velocity, share_in, power, n, False)
     other = swap(send, "theta", 1)
     late = functools.partial(late_kernel, own=True)
-    n = side_terms(late, "late_own", me, taps, velocity, chip_in, n, (send,))
+    n, _ = side_terms(late, "late_own", me, taps, velocity, chip_in, n, (send,))
     own = ends_terms(me, velocity, share_in, power, n, True)
     block = pair(me, power, own, other, points)
     entries = ()

time: 35.7 us -> 37.5 us (1.050)
  Pallas kernels: 9.7 us -> 10.9 us
  waiting for transfers between devices: 7.42 us -> 7.94 us
    pallas_call x3, Pallas kernels: 1.03 us -> 2.21 us  [side_terms(): pl.pallas_call(kernel, name=name, out_shape=(held(*v.shape), held(8, LANE...]
    ppermute x10, waiting for transfers between devices: 7.42 us -> 7.93 us  [swap(): return lax.ppermute(block, axis, [(i, i ^ bit) for i in range(size)])]
  transfers between devices with their start and end apart: 11 -> 11, of which waited for: 6 -> 5; matrix products, arithmetic and copies ran while one was open for 0% -> 0% of each run, Pallas kernels for 22% -> 20%
where the time goes in v16:
time: 37.5 us; the launch traced here: 37.3 us
  starting transfers between devices  17 us (45%)
  Pallas kernels  10.9 us (29%)
  waiting for transfers between devices  7.94 us (21%)
  between operations  1.48 us (4%)
    ppermute x10, starting transfers between devices, swap(): return lax.ppermute(block, axis, [(i, i ^ bit) for i in range(size)])  13.3 us
    ppermute x10, waiting for transfers between devices, swap(): return lax.ppermute(block, axis, [(i, i ^ bit) for i in range(size)])  7.93 us
    ppermute x1, starting transfers between devices, swap_across(): return lax.ppermute(block, axis, route)  3.76 us
    pallas_call x3, Pallas kernels, side_terms(): pl.pallas_call(kernel, name=name, out_shape=(held(*v.shape), held(8, LANE...  2.21 us
    pallas_call x1, Pallas kernels, inner_terms(): pl.pallas_call(inner_kernel, name='inner_terms', out_shape=held(*v.shape)...  2.2 us
    pallas_call x2, Pallas kernels, close(): pl.pallas_call(functools.partial(close_kernel, own=own), name='close_own'...  1.59 us
    pallas_call x1, Pallas kernels, load(): pl.pallas_call(load_kernel, name='load', out_shape=(held(*v.shape), held(...  1.14 us
    pallas_call x1, Pallas kernels, sweep(): pl.pallas_call(sweep_kernel, name='sweep', out_shape=(held(*v.shape), jax...  0.89 us
  transfers between devices with their start and end apart: 11, of which 5 were waited for; matrix products, arithmetic and copies ran while one was open for 0% of the time, Pallas kernels for 20%

profile of v16, /device:TPU:0, one launch (start us, length us, event | category | flops | bytes accessed | tf_op | source)
XLA Modules:
  0.0 37.3 jit_solution(11739661486025855108)
XLA Ops:
  0.6 1.1 %load.1 = (f32[3,16,8,512]{3,2,1,0:T(8,128)S(1)}, f32[1,12,8,512]{3,2,1,0:T(8,128)S(1)}) custom-call(f32[3,16,8,512]{3,2,1,0:T(8,128)} %hbm_ref.1), custom_call_target="tpu_custom_call" | custom-call | tf_op jit(solution)/shard_map/load/pallas_call | solution.py:111
  1.8 3.0 %collective-permute-start = (f32[1,12,8,512]{3,2,1,0:T(8,128)S(1)}, f32[1,12,8,512]{3,2,1,0:T(8,128)S(1)}, u32[]{:S(2)}, u32[]{:S(2)}) collective-permute-start(f32[1,12,8,512]{3,2,1,0:T(8,128)S(1)} %get-tuple-element.22.first_ref), channel_id=1, source_target_pairs={{0,1},{1,0},{2,3},{3,2},{4,5},{5,4},{6,7},{7,6},{8,9},{9,8},{10,11... | collective-permute-start | bytes 589832 | tf_op jit(solution)/shard_map/ppermute | solution.py:44
  4.8 3.8 %collective-permute-start.4 = (f32[3,10,8,512]{3,2,1,0:T(8,128)S(1)}, f32[3,10,8,512]{3,2,1,0:T(8,128)S(1)}, u32[]{:S(2)}, u32[]{:S(2)}) collective-permute-start(f32[3,10,8,512]{3,2,1,0:T(8,128)S(1)} %pack_chip.1.first_ref), channel_id=1, source_target_pairs={{2,4},{4,2},{6,8},{8,6},{10,12},{12,10},{14,16},{16,14},{18,20},{2... | collective-permute-start | bytes 1474568 | tf_op jit(solution)/shard_map/ppermute | solution.py:52
  9.4 0.6 %table.1 = (f32[30,512]{1,0:T(8,128)S(1)}, f32[21,8,128]{2,1,0:T(8,128)S(1)}) custom-call(s32[1]{0:T(128)} %bitcast.me_ref, f32[1]{0:T(128)S(6)} %copy.18.factor_ref, f32[21]{0:T(128)S(1)} %copy-done.1), custom_call_target="tpu_custom_call" | custom-call | flops 512000 | bytes 204800 | tf_op jit(solution)/shard_map/table/pallas_call | solution.py:475
  10.4 0.6 %share_terms.1.ready_ref = f32[2,3,8,512]{3,2,1,0:T(8,128)S(1)} custom-call(f32[3,16,8,512]{3,2,1,0:T(8,128)S(1)} %get-tuple-element.20.v_ref, f32[1,12,8,512]{3,2,1,0:T(8,128)S(1)} %collective-permute-done.first_ref.e_ref, f32[30,512]{1,0:T(8,128)S(1)} %get-tuple-element.23.power_ref), custom_call_target="tpu_custom_call" | custom-call | flops 3932160 | bytes 1572864 | tf_op jit(solution)/shard_map/share_terms/pallas_call | solution.py:375
  11.0 1.2 %collective-permute-start.3 = (f32[2,3,8,512]{3,2,1,0:T(8,128)S(1)}, f32[2,3,8,512]{3,2,1,0:T(8,128)S(1)}, u32[]{:S(2)}, u32[]{:S(2)}) collective-permute-start(f32[2,3,8,512]{3,2,1,0:T(8,128)S(1)} %share_terms.1.ready_ref), channel_id=1, source_target_pairs={{0,1},{1,0},{2,3},{3,2},{4,5},{5,4},{6,7},{7,6},{8,9},{9,8},{10,11... | collective-permute-start | bytes 294920 | tf_op jit(solution)/shard_map/ppermute | solution.py:44
  12.2 2.2 %inner_terms.1.n_in_ref = f32[3,16,8,512]{3,2,1,0:T(8,128)S(1)} custom-call(f32[21,8,128]{2,1,0:T(8,128)S(1)} %get-tuple-element.21.tap_ref, f32[3,16,8,512]{3,2,1,0:T(8,128)S(1)} %get-tuple-element.20.v_ref, f32[544,512]{1,0:T(8,128)S(1)} %bitcast.2, f32[2,3,8,512]{3,2,1,0:T(8,128)S(1)} %share_terms.1.ready_ref), custom_call_target="tpu_custom_call" | custom-call | flops 5368709120 | bytes 3145728 | tf_op jit(solution)/shard_map/inner_terms/pallas_call | solution.py:289
  14.5 0.5 %core_terms.1 = (f32[3,16,8,512]{3,2,1,0:T(8,128)S(1)}, f32[8,128]{1,0:T(8,128)S(1)}) custom-call(s32[1]{0:T(128)} %bitcast.me_ref, f32[21,8,128]{2,1,0:T(8,128)S(1)} %get-tuple-element.21.tap_ref, f32[3,16,8,512]{3,2,1,0:T(8,128)S(1)} %get-tuple-element.20.v_ref, ...), custom_call_target="tpu_custom_call", output_to_operand_aliasing={{0}: (4, {})} | custom-call | flops 67108864 | bytes 2359296 | tf_op jit(solution)/shard_map/core_terms/pallas_call | solution.py:346
  15.1 0.9 %collective-permute-start.2 = (f32[2,12,8,512]{3,2,1,0:T(8,128)S(1)}, f32[2,12,8,512]{3,2,1,0:T(8,128)S(1)}, u32[]{:S(2)}, u32[]{:S(2)}) collective-permute-start(f32[2,12,8,512]{3,2,1,0:T(8,128)S(1)} %pack_planes.1), channel_id=1, source_target_pairs={{0,1},{1,0},{2,3},{3,2},{4,5},{5,4},{6,7},{7,6},{8,9},{9,8},{10,11... | collective-permute-start | bytes 1179656 | tf_op jit(solution)/shard_map/ppermute | solution.py:44
  16.4 0.5 %mirror_terms.1.n_in_ref = f32[3,16,8,512]{3,2,1,0:T(8,128)S(1)} custom-call(f32[3,16,8,512]{3,2,1,0:T(8,128)S(1)} %get-tuple-element.20.v_ref, f32[544,512]{1,0:T(8,128)S(1)} %bitcast.3, f32[3,4,8,128]{3,2,1,0:T(8,128)S(1)} %collective-permute-done.5.mirror_ref, f32[3,16,8,512]{3,2,1,0:T(8,128)S(1)} %get-tuple-element.25.n_in_ref), custom_call_target="tpu_custom_call", output_to_operand_aliasing={{}: (3, {})} | custom-call | flops 2147483648 | bytes 3145728 | tf_op jit(solution)/shard_map/mirror_terms/pallas_call | solution.py:244
  17.0 0.8 %late_other.1 = (f32[3,16,8,512]{3,2,1,0:T(8,128)S(1)}, f32[8,128]{1,0:T(8,128)}) custom-call(s32[1]{0:T(128)} %bitcast.me_ref, f32[21,8,128]{2,1,0:T(8,128)S(1)} %get-tuple-element.21.tap_ref, f32[3,16,8,512]{3,2,1,0:T(8,128)S(1)} %get-tuple-element.20.v_ref, ...), custom_call_target="tpu_custom_call", output_to_operand_aliasing={{0}: (4, {})} | custom-call | flops 67108864 | bytes 2359296 | tf_op jit(solution)/shard_map/late_other/pallas_call | solution.py:346
  17.9 1.4 %collective-permute-start.6 = (f32[2,3,8,256]{3,2,1,0:T(8,128)S(1)}, f32[2,3,8,256]{3,2,1,0:T(8,128)S(1)}, u32[]{:S(2)}, u32[]{:S(2)}) collective-permute-start(f32[2,3,8,256]{3,2,1,0:T(8,128)S(1)} %ends_other.1.ready_ref), channel_id=1, source_target_pairs={{0,2},{2,0},{4,6},{6,4},{8,10},{10,8},{12,14},{14,12},{16,18},{18,... | collective-permute-start | bytes 147464 | tf_op jit(solution)/shard_map/ppermute | solution.py:44
  19.3 0.8 %late_own.1 = (f32[3,16,8,512]{3,2,1,0:T(8,128)S(1)}, f32[8,128]{1,0:T(8,128)}) custom-call(s32[1]{0:T(128)} %bitcast.me_ref, f32[21,8,128]{2,1,0:T(8,128)S(1)} %get-tuple-element.21.tap_ref, f32[3,16,8,512]{3,2,1,0:T(8,128)S(1)} %get-tuple-element.20.v_ref, f32[3,10,8,512]{3,2,1,0:T(8,128)S(1)} %collective-permute-done.4.chip_ref, ...), custom_call_target="tpu_custom_call", output_to_operand_aliasing={{0}: (4, {})} | custom-call | flops 67108864 | bytes 2359296 | tf_op jit(solution)/shard_map/late_own/pallas_call | solution.py:346
  20.3 2.0 %collective-permute-start.7 = (f32[2,3,8,256]{3,2,1,0:T(8,128)S(1)}, f32[2,3,8,256]{3,2,1,0:T(8,128)S(1)}, u32[]{:S(2)}, u32[]{:S(2)}) collective-permute-start(f32[2,3,8,256]{3,2,1,0:T(8,128)S(1)} %pair.1.block_ref), channel_id=1, source_target_pairs={{0,4},{2,6},{4,0},{6,2},{8,12},{10,14},{12,8},{14,10},{16,20},{18,... | collective-permute-start | bytes 147464 | tf_op jit(solution)/shard_map/ppermute | solution.py:44
  22.2 2.2 %collective-permute-done.7.other_ref = f32[2,3,8,256]{3,2,1,0:T(8,128)S(1)} collective-permute-done((f32[2,3,8,256]{3,2,1,0:T(8,128)S(1)}, f32[2,3,8,256]{3,2,1,0:T(8,128)S(1)}, u32[]{:S(2)}, u32[]{:S(2)}) %collective-permute-start.7) | collective-permute-done | bytes 49184 | tf_op jit(solution)/shard_map/ppermute | solution.py:44
  24.5 1.6 %collective-permute-start.8 = (f32[2,3,8,256]{3,2,1,0:T(8,128)S(1)}, f32[2,3,8,256]{3,2,1,0:T(8,128)S(1)}, u32[]{:S(2)}, u32[]{:S(2)}) collective-permute-start(f32[2,3,8,256]{3,2,1,0:T(8,128)S(1)} %get-tuple-element.28.block_ref), channel_id=1, source_target_pairs={{0,8},{2,10},{4,12},{6,14},{8,0},{10,2},{12,4},{14,6},{16,24},{18,... | collective-permute-start | bytes 147464 | tf_op jit(solution)/shard_map/ppermute | solution.py:44
  26.1 2.5 %collective-permute-done.8.other_ref = f32[2,3,8,256]{3,2,1,0:T(8,128)S(1)} collective-permute-done((f32[2,3,8,256]{3,2,1,0:T(8,128)S(1)}, f32[2,3,8,256]{3,2,1,0:T(8,128)S(1)}, u32[]{:S(2)}, u32[]{:S(2)}) %collective-permute-start.8) | collective-permute-done | bytes 49184 | tf_op jit(solution)/shard_map/ppermute | solution.py:44
  28.6 2.7 %collective-permute-start.9 = (f32[2,3,8,256]{3,2,1,0:T(8,128)S(1)}, f32[2,3,8,256]{3,2,1,0:T(8,128)S(1)}, u32[]{:S(2)}, u32[]{:S(2)}) collective-permute-start(f32[2,3,8,256]{3,2,1,0:T(8,128)S(1)} %get-tuple-element.30.ready_ref.block_ref), channel_id=1, source_target_pairs={{0,16},{2,18},{4,20},{6,22},{8,24},{10,26},{12,28},{14,30},{16,0},... | collective-permute-start | bytes 147464 | tf_op jit(solution)/shard_map/ppermute | solution.py:44
  31.3 2.4 %collective-permute-done.9.other_ref = f32[2,3,8,256]{3,2,1,0:T(8,128)S(1)} collective-permute-done((f32[2,3,8,256]{3,2,1,0:T(8,128)S(1)}, f32[2,3,8,256]{3,2,1,0:T(8,128)S(1)}, u32[]{:S(2)}, u32[]{:S(2)}) %collective-permute-start.9) | collective-permute-done | bytes 49184 | tf_op jit(solution)/shard_map/ppermute | solution.py:44
  33.7 0.6 %planes_terms.1.n_ref = f32[3,16,8,512]{3,2,1,0:T(8,128)S(1)} custom-call(f32[3,16,8,512]{3,2,1,0:T(8,128)S(1)} %get-tuple-element.20.v_ref, f32[2,12,8,512]{3,2,1,0:T(8,128)S(1)} %collective-permute-done.2.y_ref, f32[1,12,8,512]{3,2,1,0:T(8,128)S(1)} %collective-permute-done.first_ref.e_ref, ...), custom_call_target="tpu_custom_call", output_to_operand_aliasing={{}: (4, {})} | custom-call | flops 3932160 | bytes 3145728 | tf_op jit(solution)/shard_map/planes_terms/pallas_call | solution.py:430
  34.3 0.9 %sweep.1 = (f32[3,16,8,512]{3,2,1,0:T(8,128)S(1)}, f32[3,16,8,512]{3,2,1,0:T(8,128)}) custom-call(f32[3,16,8,512]{3,2,1,0:T(8,128)S(1)} %get-tuple-element.20.v_ref, f32[3,16,8,512]{3,2,1,0:T(8,128)S(1)} %planes_terms.1.n_ref, f32[30,512]{1,0:T(8,128)S(1)} %get-tuple-element.23.power_ref), custom_call_target="tpu_custom_call" | custom-call | flops 1966080 | bytes 2359296 | tf_op jit(solution)/shard_map/sweep/pallas_call | solution.py:515
  35.3 0.8 %close_own.1.refs_0_ = f32[3,16,8,512]{3,2,1,0:T(8,128)} custom-call(s32[1]{0:T(128)} %bitcast.me_ref, f32[3,16,8,512]{3,2,1,0:T(8,128)S(1)} %get-tuple-element.31.ready_ref.s_ref, f32[30,512]{1,0:T(8,128)S(1)} %get-tuple-element.23.power_ref, f32[2,3,8,256]{3,2,1,0:T(8,128)S(1)} %get-tuple-element.36.entry_ref), custom_call_target="tpu_custom_call" | custom-call | flops 786432 | bytes 1572864 | tf_op jit(solution)/shard_map/close_own/pallas_call | solution.py:635
  36.1 0.4 %collective-permute-done.10.entry_ref = f32[2,3,8,256]{3,2,1,0:T(8,128)S(1)} collective-permute-done((f32[2,3,8,256]{3,2,1,0:T(8,128)S(1)}, f32[2,3,8,256]{3,2,1,0:T(8,128)S(1)}, u32[]{:S(2)}, u32[]{:S(2)}) %collective-permute-start.10) | collective-permute-done | bytes 49184 | tf_op jit(solution)/shard_map/ppermute | solution.py:44
  36.5 0.8 %close_other.1 = f32[3,16,8,512]{3,2,1,0:T(8,128)} custom-call(s32[1]{0:T(128)} %bitcast.me_ref, f32[3,16,8,512]{3,2,1,0:T(8,128)S(1)} %get-tuple-element.31.ready_ref.s_ref, f32[30,512]{1,0:T(8,128)S(1)} %get-tuple-element.23.power_ref, f32[2,3,8,256]{3,2,1,0:T(8,128)S(1)} %collective-permute-done.10.entry_ref, ...), custom_call_target="tpu_custom_call", output_to_operand_aliasing={{}: (4, {})} | custom-call | flops 786432 | bytes 1572864 | tf_op jit(solution)/shard_map/close_other/pallas_call | solution.py:635
  (25 shorter events, 1.4 us)
Async XLA Ops:
  1.8 8.3 %collective-permute-start = (f32[1,12,8,512]{3,2,1,0:T(8,128)S(1)}, f32[1,12,8,512]{3,2,1,0:T(8,128)S(1)}, u32[]{:S(2)}, u32[]{:S(2)}) collective-permute-start(f32[1,12,8,512]{3,2,1,0:T(8,128)S(1)} %get-tuple-element.22.first_ref), channel_id=1, source_target_pairs={{0,1},{1,0},{2,3},{3,2},{4,5},{5,4},{6,7},{7,6},{8,9},{9,8},{10,11... | collective-permute-start | bytes 589832 | tf_op jit(solution)/shard_map/ppermute | solution.py:44
  4.8 4.6 %copy-start.1 = (f32[21]{0:T(128)S(1)}, f32[21]{0:T(128)}, u32[]{:S(2)}) copy-start(f32[21]{0:T(128)} %stencil_ref.1) | copy-start | bytes 256
  4.8 12.1 %collective-permute-start.4 = (f32[3,10,8,512]{3,2,1,0:T(8,128)S(1)}, f32[3,10,8,512]{3,2,1,0:T(8,128)S(1)}, u32[]{:S(2)}, u32[]{:S(2)}) collective-permute-start(f32[3,10,8,512]{3,2,1,0:T(8,128)S(1)} %pack_chip.1.first_ref), channel_id=1, source_target_pairs={{2,4},{4,2},{6,8},{8,6},{10,12},{12,10},{14,16},{16,14},{18,20},{2... | collective-permute-start | bytes 1474568 | tf_op jit(solution)/shard_map/ppermute | solution.py:52
  8.7 7.7 %collective-permute-start.5 = (f32[3,4,8,128]{3,2,1,0:T(8,128)S(1)}, f32[3,4,8,128]{3,2,1,0:T(8,128)S(1)}, u32[]{:S(2)}, u32[]{:S(2)}) collective-permute-start(f32[3,4,8,128]{3,2,1,0:T(8,128)S(1)} %pack_mirror.1), channel_id=1, source_target_pairs={{0,16},{2,18},{4,20},{6,22},{8,24},{10,26},{12,28},{14,30},{16,0},... | collective-permute-start | bytes 147464 | tf_op jit(solution)/shard_map/ppermute | solution.py:44
  10.1 2.2 %copy-start = (f32[512,544]{0,1:T(8,128)S(1)}, f32[512,544]{0,1:T(8,128)}, u32[]{:S(2)}) copy-start(f32[512,544]{0,1:T(8,128)} %param.5) | copy-start | bytes 3342340
  10.2 4.3 %collective-permute-start.1 = (f32[3,10,8,512]{3,2,1,0:T(8,128)S(1)}, f32[3,10,8,512]{3,2,1,0:T(8,128)S(1)}, u32[]{:S(2)}, u32[]{:S(2)}) collective-permute-start(f32[3,10,8,512]{3,2,1,0:T(8,128)S(1)} %pack_core.1), channel_id=1, source_target_pairs={{0,2},{2,0},{4,6},{6,4},{8,10},{10,8},{12,14},{14,12},{16,18},{18,... | collective-permute-start | bytes 1474568 | tf_op jit(solution)/shard_map/ppermute | solution.py:44
  11.0 5.9 %collective-permute-start.3 = (f32[2,3,8,512]{3,2,1,0:T(8,128)S(1)}, f32[2,3,8,512]{3,2,1,0:T(8,128)S(1)}, u32[]{:S(2)}, u32[]{:S(2)}) collective-permute-start(f32[2,3,8,512]{3,2,1,0:T(8,128)S(1)} %share_terms.1.ready_ref), channel_id=1, source_target_pairs={{0,1},{1,0},{2,3},{3,2},{4,5},{5,4},{6,7},{7,6},{8,9},{9,8},{10,11... | collective-permute-start | bytes 294920 | tf_op jit(solution)/shard_map/ppermute | solution.py:44
  15.1 18.6 %collective-permute-start.2 = (f32[2,12,8,512]{3,2,1,0:T(8,128)S(1)}, f32[2,12,8,512]{3,2,1,0:T(8,128)S(1)}, u32[]{:S(2)}, u32[]{:S(2)}) collective-permute-start(f32[2,12,8,512]{3,2,1,0:T(8,128)S(1)} %pack_planes.1), channel_id=1, source_target_pairs={{0,1},{1,0},{2,3},{3,2},{4,5},{5,4},{6,7},{7,6},{8,9},{9,8},{10,11... | collective-permute-start | bytes 1179656 | tf_op jit(solution)/shard_map/ppermute | solution.py:44
  17.9 2.3 %collective-permute-start.6 = (f32[2,3,8,256]{3,2,1,0:T(8,128)S(1)}, f32[2,3,8,256]{3,2,1,0:T(8,128)S(1)}, u32[]{:S(2)}, u32[]{:S(2)}) collective-permute-start(f32[2,3,8,256]{3,2,1,0:T(8,128)S(1)} %ends_other.1.ready_ref), channel_id=1, source_target_pairs={{0,2},{2,0},{4,6},{6,4},{8,10},{10,8},{12,14},{14,12},{16,18},{18,... | collective-permute-start | bytes 147464 | tf_op jit(solution)/shard_map/ppermute | solution.py:44
  20.3 4.2 %collective-permute-start.7 = (f32[2,3,8,256]{3,2,1,0:T(8,128)S(1)}, f32[2,3,8,256]{3,2,1,0:T(8,128)S(1)}, u32[]{:S(2)}, u32[]{:S(2)}) collective-permute-start(f32[2,3,8,256]{3,2,1,0:T(8,128)S(1)} %pair.1.block_ref), channel_id=1, source_target_pairs={{0,4},{2,6},{4,0},{6,2},{8,12},{10,14},{12,8},{14,10},{16,20},{18,... | collective-permute-start | bytes 147464 | tf_op jit(solution)/shard_map/ppermute | solution.py:44
  24.5 4.2 %collective-permute-start.8 = (f32[2,3,8,256]{3,2,1,0:T(8,128)S(1)}, f32[2,3,8,256]{3,2,1,0:T(8,128)S(1)}, u32[]{:S(2)}, u32[]{:S(2)}) collective-permute-start(f32[2,3,8,256]{3,2,1,0:T(8,128)S(1)} %get-tuple-element.28.block_ref), channel_id=1, source_target_pairs={{0,8},{2,10},{4,12},{6,14},{8,0},{10,2},{12,4},{14,6},{16,24},{18,... | collective-permute-start | bytes 147464 | tf_op jit(solution)/shard_map/ppermute | solution.py:44
  28.6 5.1 %collective-permute-start.9 = (f32[2,3,8,256]{3,2,1,0:T(8,128)S(1)}, f32[2,3,8,256]{3,2,1,0:T(8,128)S(1)}, u32[]{:S(2)}, u32[]{:S(2)}) collective-permute-start(f32[2,3,8,256]{3,2,1,0:T(8,128)S(1)} %get-tuple-element.30.ready_ref.block_ref), channel_id=1, source_target_pairs={{0,16},{2,18},{4,20},{6,22},{8,24},{10,26},{12,28},{14,30},{16,0},... | collective-permute-start | bytes 147464 | tf_op jit(solution)/shard_map/ppermute | solution.py:44
  35.2 1.3 %collective-permute-start.10 = (f32[2,3,8,256]{3,2,1,0:T(8,128)S(1)}, f32[2,3,8,256]{3,2,1,0:T(8,128)S(1)}, u32[]{:S(2)}, u32[]{:S(2)}) collective-permute-start(f32[2,3,8,256]{3,2,1,0:T(8,128)S(1)} %get-tuple-element.35), channel_id=1, source_target_pairs={{0,2},{2,0},{4,6},{6,4},{8,10},{10,8},{12,14},{14,12},{16,18},{18,... | collective-permute-start | bytes 147464 | tf_op jit(solution)/shard_map/ppermute | solution.py:44

commit v17 on v15

--- a/solution.py
+++ b/solution.py
@@ -13,9 +13,10 @@
 MIRROR_SIGNS = (-1.0, -1.0, 1.0)
 LANES = 128
 UNROLL = 16
-INNER = 10 << 29
-MIRROR = 1 << 26
-SIDE = 1 << 26
+INNER = 1 << 20
+MIRROR = 25 << 26
+SIDE = 1 << 20
+LATE = 1 << 30
 
 VMEM = pl.BlockSpec(memory_space=pltpu.VMEM)
 SMEM = pl.BlockSpec(memory_space=pltpu.SMEM)
@@ -62,21 +63,21 @@
     return dot(left[0], right[0]) + (dot(left[0], right[1]) + dot(left[1], right[0]))
 
 
-def pack_tiles(v_ref, y_ref, comps):
+def pack_tiles(v_ref, y_ref, comps, lanes=slice(None)):
     points, planes = v_ref.shape[1:3]
     carriers = y_ref.shape[1]
     lo, hi = AXIAL_REACH, planes - AXIAL_REACH
     for i, c in enumerate(comps):
 
         def carry(t):
-            y_ref[i, t] = v_ref[c, t]
+            y_ref[i, t] = v_ref[c, t, :, lanes]
 
         def ride(j):
             t = carriers + j
-            y_ref[i, 3 * j, lo:hi] = v_ref[c, t, 0:2]
-            y_ref[i, 3 * j + 1, lo : lo + 1] = v_ref[c, t, 2:3]
-            y_ref[i, 3 * j + 1, lo + 1 : hi] = v_ref[c, t, hi : hi + 1]
-            y_ref[i, 3 * j + 2, lo:hi] = v_ref[c, t, hi + 1 :]
+            y_ref[i, 3 * j, lo:hi] = v_ref[c, t, 0:2, lanes]
+            y_ref[i, 3 * j + 1, lo : lo + 1] = v_ref[c, t, 2:3, lanes]
+            y_ref[i, 3 * j + 1, lo + 1 : hi] = v_ref[c, t, hi : hi + 1, lanes]
+            y_ref[i, 3 * j + 2, lo:hi] = v_ref[c, t, hi + 1 :, lanes]
 
         each(carriers, carry)
         each(points - carriers, ride)
@@ -95,28 +96,31 @@
             tile_ref[c, j, hi + 1 :] = y_ref[c, 3 * j + 2, lo:hi]
 
 
-def load_kernel(hbm_ref, v_ref, y_ref, sems):
+def load_kernel(me_ref, hbm_ref, v_ref, other_ref, own_ref, sems):
     order = list(range(v_ref.shape[0]))
     loads = [pltpu.make_async_copy(hbm_ref.at[c], v_ref.at[c], sems.at[c]) for c in order]
     for c in reversed(order):
         loads[c].start()
     loads[-1].wait()
-    pack_tiles(v_ref, y_ref, order[-1:])
+    half = other_ref.shape[3]
+    pack_tiles(v_ref, other_ref, order[-1:], half_lanes(me_ref, half, False))
+    pack_tiles(v_ref, own_ref, order[-1:], half_lanes(me_ref, half, True))
     for c in order[:-1]:
         loads[c].wait()
 
 
-def load(v):
+def load(me, v):
     comps, points, planes, radial = v.shape
+    part = held(1, points - points // 4, planes, radial // 2)
     return pl.pallas_call(
         load_kernel,
         name="load",
-        out_shape=(held(*v.shape), held(1, points - points // 4, planes, radial)),
-        in_specs=[HBM],
-        out_specs=(VMEM, VMEM),
+        out_shape=(held(*v.shape), part, part),
+        in_specs=[SMEM, HBM],
+        out_specs=(VMEM, VMEM, VMEM),
         scratch_shapes=[pltpu.SemaphoreType.DMA((comps,))],
         compiler_params=params(v.size * 4, 2),
-    )(v)
+    )(me, v)
 
 
 def pack_planes_kernel(v_ref, first_ref, y_ref):
@@ -339,7 +343,7 @@
     pl.when(core == 1)(lambda: add(before=False))
 
 
-def side_terms(kernel, name, me, taps, v, side, n, ready=()):
+def side_terms(kernel, name, me, taps, v, side, n, ready=(), flops=SIDE):
     return pl.pallas_call(
         kernel,
         name=name,
@@ -348,37 +352,38 @@
         out_specs=VMEM,
         input_output_aliases={4: 0},
         compiler_params=params(v.size * 4, 5),
-        cost_estimate=pl.CostEstimate(flops=SIDE, bytes_accessed=12 * v.size, transcendentals=0),
+        cost_estimate=pl.CostEstimate(flops=flops, bytes_accessed=12 * v.size, transcendentals=0),
     )(me, taps, v, side, n, *ready)
 
 
-def share_kernel(v_ref, e_ref, power_ref, ends_ref, tile_ref):
+def share_kernel(me_ref, v_ref, e_ref, power_ref, ready_ref, ends_ref, tile_ref, *, own):
     comps, points, planes, radial = v_ref.shape
+    lanes = half_lanes(me_ref, radial // 2, own)
     carriers = e_ref.shape[1]
     weights = axial_weights(planes, False)
     rebuild_tiles(e_ref, tile_ref)
-    decay = power_ref[1:2]
+    decay = power_ref[1:2, lanes]
     ends_ref[...] = jnp.zeros_like(ends_ref)
     for t in range(points):
         e = STEP_WEIGHT * (e_ref[0, t] if t < carriers else tile_ref[0, t - carriers])
         for c in range(comps):
-            right_side = e * axial_part(v_ref[c, t], weights)
+            right_side = e * axial_part(v_ref[c, t, :, lanes], weights)
             ends_ref[0, c] = decay * ends_ref[0, c] - right_side
-            ends_ref[1, c] = ends_ref[1, c] - power_ref[t : t + 1] * right_side
-
-
-def share_terms(v, e, power):
+            ends_ref[1, c] = ends_ref[1, c] - power_ref[t : t + 1, lanes] * right_side
+
+
+def share_terms(me, v, e, power, ready, own):
     comps, points, planes, radial = v.shape
     return pl.pallas_call(
-        share_kernel,
-        name="share_terms",
-        out_shape=held(2, comps, planes, radial),
-        in_specs=[VMEM] * 3,
-        out_specs=VMEM,
-        scratch_shapes=[pltpu.VMEM((1, points - e.shape[1], planes, radial), jnp.float32)],
+        functools.partial(share_kernel, own=own),
+        name="share_own" if own else "share_other",
+        out_shape=held(2, comps, planes, radial // 2),
+        in_specs=[SMEM] + [VMEM] * 3 + [ANY],
+        out_specs=VMEM,
+        scratch_shapes=[pltpu.VMEM((1, points - e.shape[1], planes, radial // 2), jnp.float32)],
         compiler_params=params(v.size * 4, 4),
         cost_estimate=pl.CostEstimate(flops=20 * v.size, bytes_accessed=8 * v.size, transcendentals=0),
-    )(v, e, power)
+    )(me, v, e, power, ready)
 
 
 def ends_kernel(me_ref, v_ref, share_ref, power_ref, n_ref, ends_ref, *, own):
@@ -391,8 +396,8 @@
             right_side = v_ref[c, t, :, lanes] - STEP_WEIGHT * n_ref[c, t, :, lanes]
             low = right_side if t == 0 else decay * low + right_side
             high = right_side if t == 0 else high + power_ref[t : t + 1, lanes] * right_side
-        ends_ref[0, c] = low + share_ref[0, c, :, lanes]
-        ends_ref[1, c] = high + share_ref[1, c, :, lanes]
+        ends_ref[0, c] = low + share_ref[0, c]
+        ends_ref[1, c] = high + share_ref[1, c]
 
 
 def ends_terms(me, v, share, power, n, own):
@@ -408,33 +413,43 @@
     )(me, v, share, power, n)
 
 
-def planes_kernel(v_ref, y_ref, e_ref, ready_ref, n_in_ref, n_ref, y_tile_ref, e_tile_ref):
-    comps, points, planes, _ = v_ref.shape
+def planes_kernel(me_ref, v_ref, y_ref, other_ref, own_ref, ready_ref, n_in_ref, n_ref, y_tile_ref, half_ref, e_ref):
+    comps, points, planes, radial = v_ref.shape
     carriers = y_ref.shape[1]
     weights = axial_weights(planes, False)
     rebuild_tiles(y_ref, y_tile_ref)
-    rebuild_tiles(e_ref, e_tile_ref)
+    for own, part_ref in ((False, other_ref), (True, own_ref)):
+        lanes = half_lanes(me_ref, radial // 2, own)
+        rebuild_tiles(part_ref, half_ref)
+        for t in range(points):
+            e_ref[t, :, lanes] = part_ref[0, t] if t < carriers else half_ref[0, t - carriers]
     for t in range(points):
         for c in range(comps):
-            ref, tile_ref, i = (y_ref, y_tile_ref, c) if c < comps - 1 else (e_ref, e_tile_ref, 0)
-            tile = ref[i, t] if t < carriers else tile_ref[i, t - carriers]
+            if c == comps - 1:
+                tile = e_ref[t]
+            else:
+                tile = y_ref[c, t] if t < carriers else y_tile_ref[c, t - carriers]
             n_ref[c, t] = n_in_ref[c, t] + v_ref[2, t] * axial_part(tile, weights)
 
 
-def planes_terms(v, y, e, ready, n):
+def planes_terms(me, v, y, other, own, ready, n):
     comps, points, planes, radial = v.shape
     riders = points - y.shape[1]
     return pl.pallas_call(
         planes_kernel,
         name="planes_terms",
         out_shape=held(*v.shape),
-        in_specs=[VMEM] * 3 + [ANY, VMEM],
-        out_specs=VMEM,
-        scratch_shapes=[pltpu.VMEM((k, riders, planes, radial), jnp.float32) for k in (comps - 1, 1)],
-        input_output_aliases={4: 0},
-        compiler_params=params(v.size * 4, 6),
+        in_specs=[SMEM] + [VMEM] * 4 + [ANY, VMEM],
+        out_specs=VMEM,
+        scratch_shapes=[
+            pltpu.VMEM((comps - 1, riders, planes, radial), jnp.float32),
+            pltpu.VMEM((1, riders, planes, radial // 2), jnp.float32),
+            pltpu.VMEM((points, planes, radial), jnp.float32),
+        ],
+        input_output_aliases={6: 0},
+        compiler_params=params(v.size * 4, 8),
         cost_estimate=pl.CostEstimate(flops=20 * v.size, bytes_accessed=16 * v.size, transcendentals=0),
-    )(v, y, e, ready, n)
+    )(me, v, y, other, own, ready, n)
 
 
 def table_kernel(me_ref, factor_ref, stencil_ref, row_ref, tap_ref, *, points, sectors):
@@ -653,34 +668,37 @@
     me = lax.axis_index("theta").astype(jnp.int32).reshape(1)
     op = radial_op.T
 
-    velocity, axial_out = load(pltpu.with_memory_space_constraint(velocity, pltpu.HBM))
-    axial_in = swap(axial_out, "gz", 1)
-    chip_out = pack_side(me, velocity, axial_out, reach, False)
+    velocity, other_out, own_out = load(me, pltpu.with_memory_space_constraint(velocity, pltpu.HBM))
+    chip_out = pack_side(me, velocity, other_out, reach, False)
     chip_in = swap_across(chip_out, "theta")
+    other_in = swap(other_out, "gz", 1)
+    own_in = swap(own_out, "gz", 1)
     mirror_out = pack_mirror(velocity, chip_out, width)
     mirror_in = swap(mirror_out, "theta", sectors // 2)
-    core_out = pack_side(me, velocity, axial_in, reach, True)
+    core_out = pack_side(me, velocity, mirror_out, reach, True)
     core_in = swap(core_out, "theta", 1)
     power, taps = table(me, viscous_factor, azimuth_stencil, points, sectors, planes, radial)
     n = inner_terms(taps, velocity, op)
-    share_out = share_terms(velocity, axial_in, power)
-    share_in = swap(share_out, "gz", 1)
-    planes_in = swap(pack_planes(velocity, share_out), "gz", 1)
+    share_other_out = share_terms(me, velocity, other_in, power, n, False)
+    share_other = swap(share_other_out, "gz", 1)
+    share_own_out = share_terms(me, velocity, own_in, power, share_other_out, True)
+    share_own = swap(share_own_out, "gz", 1)
+    planes_in = swap(pack_planes(velocity, share_own_out), "gz", 1)
     n = side_terms(core_kernel, "core_terms", me, taps, velocity, core_in, n)
     n = mirror_terms(velocity, op, mirror_in, n)
     late = functools.partial(late_kernel, own=False)
-    n = side_terms(late, "late_other", me, taps, velocity, chip_in, n, (share_in,))
-    send = ends_terms(me, velocity, share_in, power, n, False)
+    n = side_terms(late, "late_other", me, taps, velocity, chip_in, n, (share_other,), LATE)
+    send = ends_terms(me, velocity, share_other, power, n, False)
     other = swap(send, "theta", 1)
     late = functools.partial(late_kernel, own=True)
     n = side_terms(late, "late_own", me, taps, velocity, chip_in, n, (send,))
-    own = ends_terms(me, velocity, share_in, power, n, True)
+    own = ends_terms(me, velocity, share_own, power, n, True)
     block = pair(me, power, own, other, points)
     entries = ()
     last = sectors.bit_length() - 2
     for bit in range(1, last + 1):
         if bit == last:
-            n = planes_terms(velocity, planes_in, axial_in, block, n)
+            n = planes_terms(me, velocity, planes_in, other_in, own_in, block, n)
             s, nonlinear = sweep(velocity, n, power)
         block, entry = merge(me, power, block, swap(block, "theta", 1 << bit), entries, points, bit)
         entries = (entry,)

time: 35.7 us -> 36.7 us (1.028)
  waiting for transfers between devices: 7.42 us -> 8.97 us
  starting transfers between devices: 16.9 us -> 16.3 us
    ppermute x10 -> x12, starting transfers between devices: 13.1 us -> 10.6 us  [swap(): return lax.ppermute(block, axis, [(i, i ^ bit) for i in range(size)])]
    ppermute x1, starting transfers between devices: 3.76 us -> 5.64 us  [swap_across(): return lax.ppermute(block, axis, route)]
    ppermute x10 -> x12, waiting for transfers between devices: 7.42 us -> 8.97 us  [swap(): return lax.ppermute(block, axis, [(i, i ^ bit) for i in range(size)])]
    pallas_call x2 -> x3, Pallas kernels: 1.74 us -> 1.74 us  [the longest x1 1.14 us: load(): pl.pallas_call(load_kernel, name='load', out_shape=(held(*v.shape), part,...]
  transfers between devices with their start and end apart: 11 -> 13, of which waited for: 6 -> 6; matrix products, arithmetic and copies ran while one was open for 0% -> 0% of each run, Pallas kernels for 22% -> 21%
where the time goes in v17:
time: 36.7 us; the launch traced here: 36.5 us
  starting transfers between devices  16.3 us (44%)
  Pallas kernels  9.74 us (27%)
  waiting for transfers between devices  8.97 us (24%)
  between operations  1.52 us (4%)
    ppermute x12, starting transfers between devices, swap(): return lax.ppermute(block, axis, [(i, i ^ bit) for i in range(size)])  10.6 us
    ppermute x12, waiting for transfers between devices, swap(): return lax.ppermute(block, axis, [(i, i ^ bit) for i in range(size)])  8.97 us
    ppermute x1, starting transfers between devices, swap_across(): return lax.ppermute(block, axis, route)  5.64 us
    pallas_call x1, Pallas kernels, inner_terms(): pl.pallas_call(inner_kernel, name='inner_terms', out_shape=held(*v.shape)...  2.21 us
    pallas_call x2, Pallas kernels, close(): pl.pallas_call(functools.partial(close_kernel, own=own), name='close_own'...  1.59 us
    pallas_call x1, Pallas kernels, load(): pl.pallas_call(load_kernel, name='load', out_shape=(held(*v.shape), part,...  1.14 us
    pallas_call x3, Pallas kernels, side_terms(): pl.pallas_call(kernel, name=name, out_shape=held(*v.shape), in_specs=[SME...  1.03 us
    pallas_call x1, Pallas kernels, sweep(): pl.pallas_call(sweep_kernel, name='sweep', out_shape=(held(*v.shape), jax...  0.89 us
  transfers between devices with their start and end apart: 13, of which 6 were waited for; matrix products, arithmetic and copies ran while one was open for 0% of the time, Pallas kernels for 21%

profile of v17, /device:TPU:0, one launch (start us, length us, event | category | flops | bytes accessed | tf_op | source)
XLA Modules:
  0.0 36.5 jit_solution(169239482939717627)
XLA Ops:
  0.6 1.1 %load.1 = (f32[3,16,8,512]{3,2,1,0:T(8,128)S(1)}, f32[1,12,8,256]{3,2,1,0:T(8,128)S(1)}, f32[1,12,8,256]{3,2,1,0:T(8,128)S(1)}) custom-call(s32[1]{0:T(128)} %bitcast.me_ref, f32[3,16,8,512]{3,2,1,0:T(8,128)} %hbm_ref.1), custom_call_target="tpu_custom_call" | custom-call | tf_op jit(solution)/shard_map/load/pallas_call | solution.py:115
  2.0 0.5 %collective-permute-start.6 = (f32[3,10,8,512]{3,2,1,0:T(8,128)S(1)}, f32[3,10,8,512]{3,2,1,0:T(8,128)S(1)}, u32[]{:S(2)}, u32[]{:S(2)}) collective-permute-start(f32[3,10,8,512]{3,2,1,0:T(8,128)S(1)} %pack_core.1), channel_id=1, source_target_pairs={{0,2},{2,0},{4,6},{6,4},{8,10},{10,8},{12,14},{14,12},{16,18},{18,... | collective-permute-start | bytes 1474568 | tf_op jit(solution)/shard_map/ppermute | solution.py:45
  2.5 5.6 %collective-permute-start.4 = (f32[3,10,8,512]{3,2,1,0:T(8,128)S(1)}, f32[3,10,8,512]{3,2,1,0:T(8,128)S(1)}, u32[]{:S(2)}, u32[]{:S(2)}) collective-permute-start(f32[3,10,8,512]{3,2,1,0:T(8,128)S(1)} %pack_chip.1.first_ref), channel_id=1, source_target_pairs={{2,4},{4,2},{6,8},{8,6},{10,12},{12,10},{14,16},{16,14},{18,20},{2... | collective-permute-start | bytes 1474568 | tf_op jit(solution)/shard_map/ppermute | solution.py:53
  8.2 1.5 %collective-permute-start.1 = (f32[1,12,8,256]{3,2,1,0:T(8,128)S(1)}, f32[1,12,8,256]{3,2,1,0:T(8,128)S(1)}, u32[]{:S(2)}, u32[]{:S(2)}) collective-permute-start(f32[1,12,8,256]{3,2,1,0:T(8,128)S(1)} %get-tuple-element.20.first_ref), channel_id=1, source_target_pairs={{0,1},{1,0},{2,3},{3,2},{4,5},{5,4},{6,7},{7,6},{8,9},{9,8},{10,11... | collective-permute-start | bytes 294920 | tf_op jit(solution)/shard_map/ppermute | solution.py:45
  9.7 0.5 %collective-permute-start = (f32[1,12,8,256]{3,2,1,0:T(8,128)S(1)}, f32[1,12,8,256]{3,2,1,0:T(8,128)S(1)}, u32[]{:S(2)}, u32[]{:S(2)}) collective-permute-start(f32[1,12,8,256]{3,2,1,0:T(8,128)S(1)} %get-tuple-element.18), channel_id=1, source_target_pairs={{0,1},{1,0},{2,3},{3,2},{4,5},{5,4},{6,7},{7,6},{8,9},{9,8},{10,11... | collective-permute-start | bytes 294920 | tf_op jit(solution)/shard_map/ppermute | solution.py:45
  10.9 0.6 %table.1 = (f32[30,512]{1,0:T(8,128)S(1)}, f32[21,8,128]{2,1,0:T(8,128)S(1)}) custom-call(s32[1]{0:T(128)} %bitcast.me_ref, f32[1]{0:T(128)S(6)} %copy.18.factor_ref, f32[21]{0:T(128)S(1)} %copy-done.1), custom_call_target="tpu_custom_call" | custom-call | flops 512000 | bytes 204800 | tf_op jit(solution)/shard_map/table/pallas_call | solution.py:487
  11.5 2.2 %inner_terms.1.ready_ref.n_in_ref = f32[3,16,8,512]{3,2,1,0:T(8,128)S(1)} custom-call(f32[21,8,128]{2,1,0:T(8,128)S(1)} %get-tuple-element.21.tap_ref, f32[3,16,8,512]{3,2,1,0:T(8,128)S(1)} %get-tuple-element.17.v_ref, f32[544,512]{1,0:T(8,128)S(1)} %bitcast.2), custom_call_target="tpu_custom_call" | custom-call | flops 1048576 | bytes 3145728 | tf_op jit(solution)/shard_map/inner_terms/pallas_call | solution.py:292
  13.7 0.3 share_other.1.ready_ref
  14.1 1.6 %collective-permute-start.7 = (f32[2,3,8,256]{3,2,1,0:T(8,128)S(1)}, f32[2,3,8,256]{3,2,1,0:T(8,128)S(1)}, u32[]{:S(2)}, u32[]{:S(2)}) collective-permute-start(f32[2,3,8,256]{3,2,1,0:T(8,128)S(1)} %share_other.1.ready_ref), channel_id=1, source_target_pairs={{0,1},{1,0},{2,3},{3,2},{4,5},{5,4},{6,7},{7,6},{8,9},{9,8},{10,11... | collective-permute-start | bytes 147464 | tf_op jit(solution)/shard_map/ppermute | solution.py:45
  15.9 0.6 %collective-permute-start.3 = (f32[2,3,8,256]{3,2,1,0:T(8,128)S(1)}, f32[2,3,8,256]{3,2,1,0:T(8,128)S(1)}, u32[]{:S(2)}, u32[]{:S(2)}) collective-permute-start(f32[2,3,8,256]{3,2,1,0:T(8,128)S(1)} %share_own.1.first_ref), channel_id=1, source_target_pairs={{0,1},{1,0},{2,3},{3,2},{4,5},{5,4},{6,7},{7,6},{8,9},{9,8},{10,11... | collective-permute-start | bytes 147464 | tf_op jit(solution)/shard_map/ppermute | solution.py:45
  16.6 1.6 %collective-permute-start.2 = (f32[2,12,8,512]{3,2,1,0:T(8,128)S(1)}, f32[2,12,8,512]{3,2,1,0:T(8,128)S(1)}, u32[]{:S(2)}, u32[]{:S(2)}) collective-permute-start(f32[2,12,8,512]{3,2,1,0:T(8,128)S(1)} %pack_planes.1), channel_id=1, source_target_pairs={{0,1},{1,0},{2,3},{3,2},{4,5},{5,4},{6,7},{7,6},{8,9},{9,8},{10,11... | collective-permute-start | bytes 1179656 | tf_op jit(solution)/shard_map/ppermute | solution.py:45
  18.2 0.5 %core_terms.1.n_in_ref = f32[3,16,8,512]{3,2,1,0:T(8,128)S(1)} custom-call(s32[1]{0:T(128)} %bitcast.me_ref, f32[21,8,128]{2,1,0:T(8,128)S(1)} %get-tuple-element.21.tap_ref, f32[3,16,8,512]{3,2,1,0:T(8,128)S(1)} %get-tuple-element.17.v_ref, f32[3,10,8,512]{3,2,1,0:T(8,128)S(1)} %collective-permute-done.6.core_ref, ...), custom_call_target="tpu_custom_call", output_to_operand_aliasing={{}: (4, {})} | custom-call | flops 1048576 | bytes 2359296 | tf_op jit(solution)/shard_map/core_terms/pallas_call | solution.py:347
  18.7 0.5 %mirror_terms.1.n_in_ref = f32[3,16,8,512]{3,2,1,0:T(8,128)S(1)} custom-call(f32[3,16,8,512]{3,2,1,0:T(8,128)S(1)} %get-tuple-element.17.v_ref, f32[544,512]{1,0:T(8,128)S(1)} %bitcast.3, f32[3,4,8,128]{3,2,1,0:T(8,128)S(1)} %collective-permute-done.5.mirror_ref, f32[3,16,8,512]{3,2,1,0:T(8,128)S(1)} %core_terms.1.n_in_ref), custom_call_target="tpu_custom_call", output_to_operand_aliasing={{}: (3, {})} | custom-call | flops 1677721600 | bytes 3145728 | tf_op jit(solution)/shard_map/mirror_terms/pallas_call | solution.py:247
  20.0 0.7 %collective-permute-done.3.share_ref = f32[2,3,8,256]{3,2,1,0:T(8,128)S(1)} collective-permute-done((f32[2,3,8,256]{3,2,1,0:T(8,128)S(1)}, f32[2,3,8,256]{3,2,1,0:T(8,128)S(1)}, u32[]{:S(2)}, u32[]{:S(2)}) %collective-permute-start.3) | collective-permute-done | bytes 49184 | tf_op jit(solution)/shard_map/ppermute | solution.py:45
  21.1 4.0 %collective-permute-done.9.other_ref = f32[2,3,8,256]{3,2,1,0:T(8,128)S(1)} collective-permute-done((f32[2,3,8,256]{3,2,1,0:T(8,128)S(1)}, f32[2,3,8,256]{3,2,1,0:T(8,128)S(1)}, u32[]{:S(2)}, u32[]{:S(2)}) %collective-permute-start.9) | collective-permute-done | bytes 49184 | tf_op jit(solution)/shard_map/ppermute | solution.py:45
  25.1 1.1 %collective-permute-start.10 = (f32[2,3,8,256]{3,2,1,0:T(8,128)S(1)}, f32[2,3,8,256]{3,2,1,0:T(8,128)S(1)}, u32[]{:S(2)}, u32[]{:S(2)}) collective-permute-start(f32[2,3,8,256]{3,2,1,0:T(8,128)S(1)} %get-tuple-element.22.block_ref), channel_id=1, source_target_pairs={{0,8},{2,10},{4,12},{6,14},{8,0},{10,2},{12,4},{14,6},{16,24},{18,... | collective-permute-start | bytes 147464 | tf_op jit(solution)/shard_map/ppermute | solution.py:45
  26.2 3.1 %collective-permute-done.10.other_ref = f32[2,3,8,256]{3,2,1,0:T(8,128)S(1)} collective-permute-done((f32[2,3,8,256]{3,2,1,0:T(8,128)S(1)}, f32[2,3,8,256]{3,2,1,0:T(8,128)S(1)}, u32[]{:S(2)}, u32[]{:S(2)}) %collective-permute-start.10) | collective-permute-done | bytes 49184 | tf_op jit(solution)/shard_map/ppermute | solution.py:45
  29.3 3.0 %collective-permute-start.11 = (f32[2,3,8,256]{3,2,1,0:T(8,128)S(1)}, f32[2,3,8,256]{3,2,1,0:T(8,128)S(1)}, u32[]{:S(2)}, u32[]{:S(2)}) collective-permute-start(f32[2,3,8,256]{3,2,1,0:T(8,128)S(1)} %get-tuple-element.24.ready_ref.block_ref), channel_id=1, source_target_pairs={{0,16},{2,18},{4,20},{6,22},{8,24},{10,26},{12,28},{14,30},{16,0},... | collective-permute-start | bytes 147464 | tf_op jit(solution)/shard_map/ppermute | solution.py:45
  32.3 0.6 %planes_terms.1.n_ref = f32[3,16,8,512]{3,2,1,0:T(8,128)S(1)} custom-call(s32[1]{0:T(128)} %bitcast.me_ref, f32[3,16,8,512]{3,2,1,0:T(8,128)S(1)} %get-tuple-element.17.v_ref, f32[2,12,8,512]{3,2,1,0:T(8,128)S(1)} %collective-permute-done.2.y_ref, f32[1,12,8,256]{3,2,1,0:T(8,128)S(1)} %collective-permute-done.1.e_ref.other_ref, ...), custom_call_target="tpu_custom_call", output_to_operand_aliasing={{}: (6, {})} | custom-call | flops 3932160 | bytes 3145728 | tf_op jit(solution)/shard_map/planes_terms/pallas_call | solution.py:438
  32.9 0.9 %sweep.1 = (f32[3,16,8,512]{3,2,1,0:T(8,128)S(1)}, f32[3,16,8,512]{3,2,1,0:T(8,128)}) custom-call(f32[3,16,8,512]{3,2,1,0:T(8,128)S(1)} %get-tuple-element.17.v_ref, f32[3,16,8,512]{3,2,1,0:T(8,128)S(1)} %planes_terms.1.n_ref, f32[30,512]{1,0:T(8,128)S(1)} %get-tuple-element.19.power_ref), custom_call_target="tpu_custom_call" | custom-call | flops 1966080 | bytes 2359296 | tf_op jit(solution)/shard_map/sweep/pallas_call | solution.py:527
  33.8 0.6 %collective-permute-done.11.other_ref = f32[2,3,8,256]{3,2,1,0:T(8,128)S(1)} collective-permute-done((f32[2,3,8,256]{3,2,1,0:T(8,128)S(1)}, f32[2,3,8,256]{3,2,1,0:T(8,128)S(1)}, u32[]{:S(2)}, u32[]{:S(2)}) %collective-permute-start.11) | collective-permute-done | bytes 49184 | tf_op jit(solution)/shard_map/ppermute | solution.py:45
  34.5 0.8 %close_own.1.refs_0_ = f32[3,16,8,512]{3,2,1,0:T(8,128)} custom-call(s32[1]{0:T(128)} %bitcast.me_ref, f32[3,16,8,512]{3,2,1,0:T(8,128)S(1)} %get-tuple-element.25.ready_ref.s_ref, f32[30,512]{1,0:T(8,128)S(1)} %get-tuple-element.19.power_ref, f32[2,3,8,256]{3,2,1,0:T(8,128)S(1)} %get-tuple-element.30.entry_ref), custom_call_target="tpu_custom_call" | custom-call | flops 786432 | bytes 1572864 | tf_op jit(solution)/shard_map/close_own/pallas_call | solution.py:647
  35.3 0.4 %collective-permute-done.12.entry_ref = f32[2,3,8,256]{3,2,1,0:T(8,128)S(1)} collective-permute-done((f32[2,3,8,256]{3,2,1,0:T(8,128)S(1)}, f32[2,3,8,256]{3,2,1,0:T(8,128)S(1)}, u32[]{:S(2)}, u32[]{:S(2)}) %collective-permute-start.12) | collective-permute-done | bytes 49184 | tf_op jit(solution)/shard_map/ppermute | solution.py:45
  35.7 0.8 %close_other.1 = f32[3,16,8,512]{3,2,1,0:T(8,128)} custom-call(s32[1]{0:T(128)} %bitcast.me_ref, f32[3,16,8,512]{3,2,1,0:T(8,128)S(1)} %get-tuple-element.25.ready_ref.s_ref, f32[30,512]{1,0:T(8,128)S(1)} %get-tuple-element.19.power_ref, f32[2,3,8,256]{3,2,1,0:T(8,128)S(1)} %collective-permute-done.12.entry_ref, ...), custom_call_target="tpu_custom_call", output_to_operand_aliasing={{}: (4, {})} | custom-call | flops 786432 | bytes 1572864 | tf_op jit(solution)/shard_map/close_other/pallas_call | solution.py:647
  (30 shorter events, 1.9 us)
Async XLA Ops:
  1.8 9.0 %copy-start.1 = (f32[21]{0:T(128)S(1)}, f32[21]{0:T(128)}, u32[]{:S(2)}) copy-start(f32[21]{0:T(128)} %stencil_ref.1) | copy-start | bytes 256
  1.8 9.7 %copy-start = (f32[512,544]{0,1:T(8,128)S(1)}, f32[512,544]{0,1:T(8,128)}, u32[]{:S(2)}) copy-start(f32[512,544]{0,1:T(8,128)} %param.5) | copy-start | bytes 3342340
  2.0 14.6 %collective-permute-start.6 = (f32[3,10,8,512]{3,2,1,0:T(8,128)S(1)}, f32[3,10,8,512]{3,2,1,0:T(8,128)S(1)}, u32[]{:S(2)}, u32[]{:S(2)}) collective-permute-start(f32[3,10,8,512]{3,2,1,0:T(8,128)S(1)} %pack_core.1), channel_id=1, source_target_pairs={{0,2},{2,0},{4,6},{6,4},{8,10},{10,8},{12,14},{14,12},{16,18},{18,... | collective-permute-start | bytes 1474568 | tf_op jit(solution)/shard_map/ppermute | solution.py:45
  2.5 16.7 %collective-permute-start.4 = (f32[3,10,8,512]{3,2,1,0:T(8,128)S(1)}, f32[3,10,8,512]{3,2,1,0:T(8,128)S(1)}, u32[]{:S(2)}, u32[]{:S(2)}) collective-permute-start(f32[3,10,8,512]{3,2,1,0:T(8,128)S(1)} %pack_chip.1.first_ref), channel_id=1, source_target_pairs={{2,4},{4,2},{6,8},{8,6},{10,12},{12,10},{14,16},{16,14},{18,20},{2... | collective-permute-start | bytes 1474568 | tf_op jit(solution)/shard_map/ppermute | solution.py:53
  8.2 5.6 %collective-permute-start.1 = (f32[1,12,8,256]{3,2,1,0:T(8,128)S(1)}, f32[1,12,8,256]{3,2,1,0:T(8,128)S(1)}, u32[]{:S(2)}, u32[]{:S(2)}) collective-permute-start(f32[1,12,8,256]{3,2,1,0:T(8,128)S(1)} %get-tuple-element.20.first_ref), channel_id=1, source_target_pairs={{0,1},{1,0},{2,3},{3,2},{4,5},{5,4},{6,7},{7,6},{8,9},{9,8},{10,11... | collective-permute-start | bytes 294920 | tf_op jit(solution)/shard_map/ppermute | solution.py:45
  9.7 5.9 %collective-permute-start = (f32[1,12,8,256]{3,2,1,0:T(8,128)S(1)}, f32[1,12,8,256]{3,2,1,0:T(8,128)S(1)}, u32[]{:S(2)}, u32[]{:S(2)}) collective-permute-start(f32[1,12,8,256]{3,2,1,0:T(8,128)S(1)} %get-tuple-element.18), channel_id=1, source_target_pairs={{0,1},{1,0},{2,3},{3,2},{4,5},{5,4},{6,7},{7,6},{8,9},{9,8},{10,11... | collective-permute-start | bytes 294920 | tf_op jit(solution)/shard_map/ppermute | solution.py:45
  10.2 8.5 %collective-permute-start.5 = (f32[3,4,8,128]{3,2,1,0:T(8,128)S(1)}, f32[3,4,8,128]{3,2,1,0:T(8,128)S(1)}, u32[]{:S(2)}, u32[]{:S(2)}) collective-permute-start(f32[3,4,8,128]{3,2,1,0:T(8,128)S(1)} %pack_mirror.1.first_ref), channel_id=1, source_target_pairs={{0,16},{2,18},{4,20},{6,22},{8,24},{10,26},{12,28},{14,30},{16,0},... | collective-permute-start | bytes 147464 | tf_op jit(solution)/shard_map/ppermute | solution.py:45
  14.1 5.2 %collective-permute-start.7 = (f32[2,3,8,256]{3,2,1,0:T(8,128)S(1)}, f32[2,3,8,256]{3,2,1,0:T(8,128)S(1)}, u32[]{:S(2)}, u32[]{:S(2)}) collective-permute-start(f32[2,3,8,256]{3,2,1,0:T(8,128)S(1)} %share_other.1.ready_ref), channel_id=1, source_target_pairs={{0,1},{1,0},{2,3},{3,2},{4,5},{5,4},{6,7},{7,6},{8,9},{9,8},{10,11... | collective-permute-start | bytes 147464 | tf_op jit(solution)/shard_map/ppermute | solution.py:45
  15.9 4.7 %collective-permute-start.3 = (f32[2,3,8,256]{3,2,1,0:T(8,128)S(1)}, f32[2,3,8,256]{3,2,1,0:T(8,128)S(1)}, u32[]{:S(2)}, u32[]{:S(2)}) collective-permute-start(f32[2,3,8,256]{3,2,1,0:T(8,128)S(1)} %share_own.1.first_ref), channel_id=1, source_target_pairs={{0,1},{1,0},{2,3},{3,2},{4,5},{5,4},{6,7},{7,6},{8,9},{9,8},{10,11... | collective-permute-start | bytes 147464 | tf_op jit(solution)/shard_map/ppermute | solution.py:45
  16.6 15.7 %collective-permute-start.2 = (f32[2,12,8,512]{3,2,1,0:T(8,128)S(1)}, f32[2,12,8,512]{3,2,1,0:T(8,128)S(1)}, u32[]{:S(2)}, u32[]{:S(2)}) collective-permute-start(f32[2,12,8,512]{3,2,1,0:T(8,128)S(1)} %pack_planes.1), channel_id=1, source_target_pairs={{0,1},{1,0},{2,3},{3,2},{4,5},{5,4},{6,7},{7,6},{8,9},{9,8},{10,11... | collective-permute-start | bytes 1179656 | tf_op jit(solution)/shard_map/ppermute | solution.py:45
  19.6 1.3 %collective-permute-start.8 = (f32[2,3,8,256]{3,2,1,0:T(8,128)S(1)}, f32[2,3,8,256]{3,2,1,0:T(8,128)S(1)}, u32[]{:S(2)}, u32[]{:S(2)}) collective-permute-start(f32[2,3,8,256]{3,2,1,0:T(8,128)S(1)} %ends_other.1.ready_ref), channel_id=1, source_target_pairs={{0,2},{2,0},{4,6},{6,4},{8,10},{10,8},{12,14},{14,12},{16,18},{18,... | collective-permute-start | bytes 147464 | tf_op jit(solution)/shard_map/ppermute | solution.py:45
  20.9 4.2 %collective-permute-start.9 = (f32[2,3,8,256]{3,2,1,0:T(8,128)S(1)}, f32[2,3,8,256]{3,2,1,0:T(8,128)S(1)}, u32[]{:S(2)}, u32[]{:S(2)}) collective-permute-start(f32[2,3,8,256]{3,2,1,0:T(8,128)S(1)} %pair.1.block_ref), channel_id=1, source_target_pairs={{0,4},{2,6},{4,0},{6,2},{8,12},{10,14},{12,8},{14,10},{16,20},{18,... | collective-permute-start | bytes 147464 | tf_op jit(solution)/shard_map/ppermute | solution.py:45
  25.1 4.2 %collective-permute-start.10 = (f32[2,3,8,256]{3,2,1,0:T(8,128)S(1)}, f32[2,3,8,256]{3,2,1,0:T(8,128)S(1)}, u32[]{:S(2)}, u32[]{:S(2)}) collective-permute-start(f32[2,3,8,256]{3,2,1,0:T(8,128)S(1)} %get-tuple-element.22.block_ref), channel_id=1, source_target_pairs={{0,8},{2,10},{4,12},{6,14},{8,0},{10,2},{12,4},{14,6},{16,24},{18,... | collective-permute-start | bytes 147464 | tf_op jit(solution)/shard_map/ppermute | solution.py:45
  29.3 5.1 %collective-permute-start.11 = (f32[2,3,8,256]{3,2,1,0:T(8,128)S(1)}, f32[2,3,8,256]{3,2,1,0:T(8,128)S(1)}, u32[]{:S(2)}, u32[]{:S(2)}) collective-permute-start(f32[2,3,8,256]{3,2,1,0:T(8,128)S(1)} %get-tuple-element.24.ready_ref.block_ref), channel_id=1, source_target_pairs={{0,16},{2,18},{4,20},{6,22},{8,24},{10,26},{12,28},{14,30},{16,0},... | collective-permute-start | bytes 147464 | tf_op jit(solution)/shard_map/ppermute | solution.py:45
  34.4 1.3 %collective-permute-start.12 = (f32[2,3,8,256]{3,2,1,0:T(8,128)S(1)}, f32[2,3,8,256]{3,2,1,0:T(8,128)S(1)}, u32[]{:S(2)}, u32[]{:S(2)}) collective-permute-start(f32[2,3,8,256]{3,2,1,0:T(8,128)S(1)} %get-tuple-element.29), channel_id=1, source_target_pairs={{0,2},{2,0},{4,6},{6,4},{8,10},{10,8},{12,14},{14,12},{16,18},{18,... | collective-permute-start | bytes 147464 | tf_op jit(solution)/shard_map/ppermute | solution.py:45

commit v18 on v15

--- a/solution.py
+++ b/solution.py
@@ -11,9 +11,10 @@
 AXIAL_REACH = len(AXIAL_WEIGHTS)
 STEP_WEIGHT = 0.2
 MIRROR_SIGNS = (-1.0, -1.0, 1.0)
+CHIP_PARTS = 2
 LANES = 128
 UNROLL = 16
-INNER = 10 << 29
+INNER = 1 << 31
 MIRROR = 1 << 26
 SIDE = 1 << 26
 
@@ -135,13 +136,16 @@
     )(v, first)
 
 
-def pack_side_kernel(me_ref, v_ref, first_ref, side_ref, *, after):
-    points, reach = v_ref.shape[1], side_ref.shape[1]
+def pack_side_kernel(me_ref, v_ref, first_ref, *side_refs, after):
+    points = v_ref.shape[1]
+    each_part = side_refs[0].shape[1]
+    reach = each_part * len(side_refs)
 
     def put(start):
-        for c in range(v_ref.shape[0]):
-            for h in range(reach):
-                side_ref[c, h] = v_ref[c, start + h]
+        for k, side_ref in enumerate(side_refs):
+            for c in range(v_ref.shape[0]):
+                for h in range(each_part):
+                    side_ref[c, h] = v_ref[c, start + k * each_part + h]
 
     even = me_ref[0] % 2 == 0
     last = even if after else jnp.logical_not(even)
@@ -149,14 +153,15 @@
     pl.when(jnp.logical_not(last))(lambda: put(0))
 
 
-def pack_side(me, v, first, reach, after):
+def pack_side(me, v, first, reach, after, parts):
     comps, _, planes, radial = v.shape
+    parts = parts if reach % parts == 0 else 1
     return pl.pallas_call(
         functools.partial(pack_side_kernel, after=after),
         name="pack_core" if after else "pack_chip",
-        out_shape=held(comps, reach, planes, radial),
+        out_shape=(held(comps, reach // parts, planes, radial),) * parts,
         in_specs=[SMEM, VMEM, ANY],
-        out_specs=VMEM,
+        out_specs=(VMEM,) * parts,
         compiler_params=params(v.size * 4, 3),
     )(me, v, first)
 
@@ -297,9 +302,10 @@
     )(taps, v, op)
 
 
-def add_side(tap_ref, v_ref, side_ref, n_in_ref, n_ref, before, columns):
+def add_side(tap_ref, v_ref, side_refs, n_in_ref, n_ref, before, columns):
     comps, points, _, radial = v_ref.shape
-    reach = side_ref.shape[1]
+    each_part = side_refs[0].shape[1]
+    reach = each_part * len(side_refs)
     first = 0 if before else reach + 1
 
     start, count = columns
@@ -311,7 +317,7 @@
         inv_r = inverse_radius(LANES, k * LANES)
         weights = [tap_ref[first + i] for i in range(reach)]
         for c in range(comps):
-            side = [side_ref[c, h, :, lanes] for h in range(reach)]
+            side = [side_refs[h // each_part][c, h % each_part, :, lanes] for h in range(reach)]
             for u in range(reach):
                 t = u if before else points - reach + u
                 taps = [(h, h - u) for h in range(u, reach)] if before else [(h, reach - 1 + h - u) for h in range(u + 1)]
@@ -322,34 +328,36 @@
                 n_ref[c, t, :, lanes] = n_in_ref[c, t, :, lanes] + v_ref[1, t, :, lanes] * inv_r * around
 
 
-def core_kernel(me_ref, tap_ref, v_ref, core_ref, n_in_ref, n_ref):
+def core_kernel(me_ref, tap_ref, v_ref, *refs):
+    *core_refs, n_in_ref, n_ref = refs
     even = me_ref[0] % 2 == 0
     columns = (0, v_ref.shape[3] // LANES)
-    add = functools.partial(add_side, tap_ref, v_ref, core_ref, n_in_ref, n_ref, columns=columns)
+    add = functools.partial(add_side, tap_ref, v_ref, core_refs, n_in_ref, n_ref, columns=columns)
     pl.when(even)(lambda: add(before=False))
     pl.when(jnp.logical_not(even))(lambda: add(before=True))
 
 
-def late_kernel(me_ref, tap_ref, v_ref, chip_ref, n_in_ref, ready_ref, n_ref, *, own):
+def late_kernel(me_ref, tap_ref, v_ref, *refs, own):
+    *chip_refs, n_in_ref, _, n_ref = refs
     core = me_ref[0] % 2
     count = v_ref.shape[3] // (2 * LANES)
     columns = ((core if own else 1 - core) * count, count)
-    add = functools.partial(add_side, tap_ref, v_ref, chip_ref, n_in_ref, n_ref, columns=columns)
+    add = functools.partial(add_side, tap_ref, v_ref, chip_refs, n_in_ref, n_ref, columns=columns)
     pl.when(core == 0)(lambda: add(before=True))
     pl.when(core == 1)(lambda: add(before=False))
 
 
-def side_terms(kernel, name, me, taps, v, side, n, ready=()):
+def side_terms(kernel, name, me, taps, v, sides, n, ready=()):
     return pl.pallas_call(
         kernel,
         name=name,
         out_shape=held(*v.shape),
-        in_specs=[SMEM] + [VMEM] * 4 + [ANY] * len(ready),
-        out_specs=VMEM,
-        input_output_aliases={4: 0},
+        in_specs=[SMEM] + [VMEM] * (3 + len(sides)) + [ANY] * len(ready),
+        out_specs=VMEM,
+        input_output_aliases={3 + len(sides): 0},
         compiler_params=params(v.size * 4, 5),
         cost_estimate=pl.CostEstimate(flops=SIDE, bytes_accessed=12 * v.size, transcendentals=0),
-    )(me, taps, v, side, n, *ready)
+    )(me, taps, v, *sides, n, *ready)
 
 
 def share_kernel(v_ref, e_ref, power_ref, ends_ref, tile_ref):
@@ -655,12 +663,12 @@
 
     velocity, axial_out = load(pltpu.with_memory_space_constraint(velocity, pltpu.HBM))
     axial_in = swap(axial_out, "gz", 1)
-    chip_out = pack_side(me, velocity, axial_out, reach, False)
-    chip_in = swap_across(chip_out, "theta")
-    mirror_out = pack_mirror(velocity, chip_out, width)
+    chip_out = pack_side(me, velocity, axial_out, reach, False, CHIP_PARTS)
+    chip_in = [swap_across(part, "theta") for part in chip_out]
+    mirror_out = pack_mirror(velocity, chip_out[0], width)
     mirror_in = swap(mirror_out, "theta", sectors // 2)
-    core_out = pack_side(me, velocity, axial_in, reach, True)
-    core_in = swap(core_out, "theta", 1)
+    core_out = pack_side(me, velocity, mirror_out, reach, True, 1)
+    core_in = [swap(part, "theta", 1) for part in core_out]
     power, taps = table(me, viscous_factor, azimuth_stencil, points, sectors, planes, radial)
     n = inner_terms(taps, velocity, op)
     share_out = share_terms(velocity, axial_in, power)

time: 35.7 us -> 36.2 us (1.014)
  starting transfers between devices: 16.9 us -> 17.5 us
    ppermute x1 -> x2, starting transfers between devices: 3.76 us -> 4.44 us  [swap_across(): return lax.ppermute(block, axis, route)]
  transfers between devices with their start and end apart: 11 -> 12, of which waited for: 6 -> 6; matrix products, arithmetic and copies ran while one was open for 0% -> 0% of each run, Pallas kernels for 22% -> 21%
where the time goes in v18:
time: 36.2 us; the launch traced here: 36 us
  starting transfers between devices  17.5 us (48%)
  Pallas kernels  9.7 us (27%)
  waiting for transfers between devices  7.29 us (20%)
  between operations  1.5 us (4%)
    ppermute x10, starting transfers between devices, swap(): return lax.ppermute(block, axis, [(i, i ^ bit) for i in range(size)])  13.1 us
    ppermute x10, waiting for transfers between devices, swap(): return lax.ppermute(block, axis, [(i, i ^ bit) for i in range(size)])  7.24 us
    ppermute x2, starting transfers between devices, swap_across(): return lax.ppermute(block, axis, route)  4.44 us
    pallas_call x1, Pallas kernels, inner_terms(): pl.pallas_call(inner_kernel, name='inner_terms', out_shape=held(*v.shape)...  2.2 us
    pallas_call x2, Pallas kernels, close(): pl.pallas_call(functools.partial(close_kernel, own=own), name='close_own'...  1.59 us
    pallas_call x1, Pallas kernels, load(): pl.pallas_call(load_kernel, name='load', out_shape=(held(*v.shape), held(...  1.14 us
    pallas_call x3, Pallas kernels, side_terms(): pl.pallas_call(kernel, name=name, out_shape=held(*v.shape), in_specs=[SME...  1.01 us
    pallas_call x1, Pallas kernels, sweep(): pl.pallas_call(sweep_kernel, name='sweep', out_shape=(held(*v.shape), jax...  0.89 us
  transfers between devices with their start and end apart: 12, of which 6 were waited for; matrix products, arithmetic and copies ran while one was open for 0% of the time, Pallas kernels for 21%

profile of v18, /device:TPU:0, one launch (start us, length us, event | category | flops | bytes accessed | tf_op | source)
XLA Modules:
  0.0 36.0 jit_solution(8815300089595886898)
XLA Ops:
  0.6 1.1 %load.1 = (f32[3,16,8,512]{3,2,1,0:T(8,128)S(1)}, f32[1,12,8,512]{3,2,1,0:T(8,128)S(1)}) custom-call(f32[3,16,8,512]{3,2,1,0:T(8,128)} %hbm_ref.1), custom_call_target="tpu_custom_call" | custom-call | tf_op jit(solution)/shard_map/load/pallas_call | solution.py:112
  2.0 0.5 %collective-permute-start.6 = (f32[3,10,8,512]{3,2,1,0:T(8,128)S(1)}, f32[3,10,8,512]{3,2,1,0:T(8,128)S(1)}, u32[]{:S(2)}, u32[]{:S(2)}) collective-permute-start(f32[3,10,8,512]{3,2,1,0:T(8,128)S(1)} %pack_core.1), channel_id=1, source_target_pairs={{0,2},{2,0},{4,6},{6,4},{8,10},{10,8},{12,14},{14,12},{16,18},{18,... | collective-permute-start | bytes 1474568 | tf_op jit(solution)/shard_map/ppermute | solution.py:45
  2.5 2.6 %collective-permute-start = (f32[1,12,8,512]{3,2,1,0:T(8,128)S(1)}, f32[1,12,8,512]{3,2,1,0:T(8,128)S(1)}, u32[]{:S(2)}, u32[]{:S(2)}) collective-permute-start(f32[1,12,8,512]{3,2,1,0:T(8,128)S(1)} %get-tuple-element.19.first_ref), channel_id=1, source_target_pairs={{0,1},{1,0},{2,3},{3,2},{4,5},{5,4},{6,7},{7,6},{8,9},{9,8},{10,11... | collective-permute-start | bytes 589832 | tf_op jit(solution)/shard_map/ppermute | solution.py:45
  5.1 4.3 %collective-permute-start.3 = (f32[3,5,8,512]{3,2,1,0:T(8,128)S(1)}, f32[3,5,8,512]{3,2,1,0:T(8,128)S(1)}, u32[]{:S(2)}, u32[]{:S(2)}) collective-permute-start(f32[3,5,8,512]{3,2,1,0:T(8,128)S(1)} %get-tuple-element.22.first_ref), channel_id=1, source_target_pairs={{2,4},{4,2},{6,8},{8,6},{10,12},{12,10},{14,16},{16,14},{18,20},{2... | collective-permute-start | bytes 737288 | tf_op jit(solution)/shard_map/ppermute | solution.py:53
  9.6 0.8 %collective-permute-start.5 = (f32[3,4,8,128]{3,2,1,0:T(8,128)S(1)}, f32[3,4,8,128]{3,2,1,0:T(8,128)S(1)}, u32[]{:S(2)}, u32[]{:S(2)}) collective-permute-start(f32[3,4,8,128]{3,2,1,0:T(8,128)S(1)} %pack_mirror.1.first_ref), channel_id=1, source_target_pairs={{0,16},{2,18},{4,20},{6,22},{8,24},{10,26},{12,28},{14,30},{16,0},... | collective-permute-start | bytes 147464 | tf_op jit(solution)/shard_map/ppermute | solution.py:45
  11.0 0.6 %table.1 = (f32[30,512]{1,0:T(8,128)S(1)}, f32[21,8,128]{2,1,0:T(8,128)S(1)}) custom-call(s32[1]{0:T(128)} %bitcast.me_ref, f32[1]{0:T(128)S(6)} %copy.18.factor_ref, f32[21]{0:T(128)S(1)} %copy-done.1), custom_call_target="tpu_custom_call" | custom-call | flops 512000 | bytes 204800 | tf_op jit(solution)/shard_map/table/pallas_call | solution.py:480
  11.7 0.6 %share_terms.1.first_ref = f32[2,3,8,512]{3,2,1,0:T(8,128)S(1)} custom-call(f32[3,16,8,512]{3,2,1,0:T(8,128)S(1)} %get-tuple-element.18.v_ref, f32[1,12,8,512]{3,2,1,0:T(8,128)S(1)} %collective-permute-done.e_ref, f32[30,512]{1,0:T(8,128)S(1)} %get-tuple-element.20.power_ref), custom_call_target="tpu_custom_call" | custom-call | flops 3932160 | bytes 1572864 | tf_op jit(solution)/shard_map/share_terms/pallas_call | solution.py:380
  12.3 0.8 %collective-permute-start.2 = (f32[2,3,8,512]{3,2,1,0:T(8,128)S(1)}, f32[2,3,8,512]{3,2,1,0:T(8,128)S(1)}, u32[]{:S(2)}, u32[]{:S(2)}) collective-permute-start(f32[2,3,8,512]{3,2,1,0:T(8,128)S(1)} %share_terms.1.first_ref), channel_id=1, source_target_pairs={{0,1},{1,0},{2,3},{3,2},{4,5},{5,4},{6,7},{7,6},{8,9},{9,8},{10,11... | collective-permute-start | bytes 294920 | tf_op jit(solution)/shard_map/ppermute | solution.py:45
  13.1 1.4 %collective-permute-start.1 = (f32[2,12,8,512]{3,2,1,0:T(8,128)S(1)}, f32[2,12,8,512]{3,2,1,0:T(8,128)S(1)}, u32[]{:S(2)}, u32[]{:S(2)}) collective-permute-start(f32[2,12,8,512]{3,2,1,0:T(8,128)S(1)} %pack_planes.1), channel_id=1, source_target_pairs={{0,1},{1,0},{2,3},{3,2},{4,5},{5,4},{6,7},{7,6},{8,9},{9,8},{10,11... | collective-permute-start | bytes 1179656 | tf_op jit(solution)/shard_map/ppermute | solution.py:45
  14.5 2.2 %inner_terms.1.refs_1_ = f32[3,16,8,512]{3,2,1,0:T(8,128)S(1)} custom-call(f32[21,8,128]{2,1,0:T(8,128)S(1)} %get-tuple-element.21.tap_ref, f32[3,16,8,512]{3,2,1,0:T(8,128)S(1)} %get-tuple-element.18.v_ref, f32[544,512]{1,0:T(8,128)S(1)} %bitcast.2), custom_call_target="tpu_custom_call" | custom-call | flops 2147483648 | bytes 3145728 | tf_op jit(solution)/shard_map/inner_terms/pallas_call | solution.py:293
  16.7 0.5 %core_terms.1.n_in_ref = f32[3,16,8,512]{3,2,1,0:T(8,128)S(1)} custom-call(s32[1]{0:T(128)} %bitcast.me_ref, f32[21,8,128]{2,1,0:T(8,128)S(1)} %get-tuple-element.21.tap_ref, f32[3,16,8,512]{3,2,1,0:T(8,128)S(1)} %get-tuple-element.18.v_ref, f32[3,10,8,512]{3,2,1,0:T(8,128)S(1)} %collective-permute-done.6.refs_0_, ...), custom_call_target="tpu_custom_call", output_to_operand_aliasing={{}: (4, {})} | custom-call | flops 67108864 | bytes 2359296 | tf_op jit(solution)/shard_map/core_terms/pallas_call | solution.py:351
  17.3 0.5 %mirror_terms.1.refs_2_ = f32[3,16,8,512]{3,2,1,0:T(8,128)S(1)} custom-call(f32[3,16,8,512]{3,2,1,0:T(8,128)S(1)} %get-tuple-element.18.v_ref, f32[544,512]{1,0:T(8,128)S(1)} %bitcast.3, f32[3,4,8,128]{3,2,1,0:T(8,128)S(1)} %collective-permute-done.5.mirror_ref, f32[3,16,8,512]{3,2,1,0:T(8,128)S(1)} %core_terms.1.n_in_ref), custom_call_target="tpu_custom_call", output_to_operand_aliasing={{}: (3, {})} | custom-call | flops 67108864 | bytes 3145728 | tf_op jit(solution)/shard_map/mirror_terms/pallas_call | solution.py:248
  18.3 1.2 %collective-permute-start.7 = (f32[2,3,8,256]{3,2,1,0:T(8,128)S(1)}, f32[2,3,8,256]{3,2,1,0:T(8,128)S(1)}, u32[]{:S(2)}, u32[]{:S(2)}) collective-permute-start(f32[2,3,8,256]{3,2,1,0:T(8,128)S(1)} %ends_other.1.refs_3_), channel_id=1, source_target_pairs={{0,2},{2,0},{4,6},{6,4},{8,10},{10,8},{12,14},{14,12},{16,18},{18,... | collective-permute-start | bytes 147464 | tf_op jit(solution)/shard_map/ppermute | solution.py:45
  19.9 0.5 %collective-permute-done.7.other_ref = f32[2,3,8,256]{3,2,1,0:T(8,128)S(1)} collective-permute-done((f32[2,3,8,256]{3,2,1,0:T(8,128)S(1)}, f32[2,3,8,256]{3,2,1,0:T(8,128)S(1)}, u32[]{:S(2)}, u32[]{:S(2)}) %collective-permute-start.7) | collective-permute-done | bytes 49184 | tf_op jit(solution)/shard_map/ppermute | solution.py:45
  20.4 1.4 %collective-permute-start.8 = (f32[2,3,8,256]{3,2,1,0:T(8,128)S(1)}, f32[2,3,8,256]{3,2,1,0:T(8,128)S(1)}, u32[]{:S(2)}, u32[]{:S(2)}) collective-permute-start(f32[2,3,8,256]{3,2,1,0:T(8,128)S(1)} %pair.1.block_ref), channel_id=1, source_target_pairs={{0,4},{2,6},{4,0},{6,2},{8,12},{10,14},{12,8},{14,10},{16,20},{18,... | collective-permute-start | bytes 147464 | tf_op jit(solution)/shard_map/ppermute | solution.py:45
  21.9 2.7 %collective-permute-done.8.other_ref = f32[2,3,8,256]{3,2,1,0:T(8,128)S(1)} collective-permute-done((f32[2,3,8,256]{3,2,1,0:T(8,128)S(1)}, f32[2,3,8,256]{3,2,1,0:T(8,128)S(1)}, u32[]{:S(2)}, u32[]{:S(2)}) %collective-permute-start.8) | collective-permute-done | bytes 49184 | tf_op jit(solution)/shard_map/ppermute | solution.py:45
  24.6 1.6 %collective-permute-start.9 = (f32[2,3,8,256]{3,2,1,0:T(8,128)S(1)}, f32[2,3,8,256]{3,2,1,0:T(8,128)S(1)}, u32[]{:S(2)}, u32[]{:S(2)}) collective-permute-start(f32[2,3,8,256]{3,2,1,0:T(8,128)S(1)} %get-tuple-element.24.block_ref), channel_id=1, source_target_pairs={{0,8},{2,10},{4,12},{6,14},{8,0},{10,2},{12,4},{14,6},{16,24},{18,... | collective-permute-start | bytes 147464 | tf_op jit(solution)/shard_map/ppermute | solution.py:45
  26.3 2.5 %collective-permute-done.9.other_ref = f32[2,3,8,256]{3,2,1,0:T(8,128)S(1)} collective-permute-done((f32[2,3,8,256]{3,2,1,0:T(8,128)S(1)}, f32[2,3,8,256]{3,2,1,0:T(8,128)S(1)}, u32[]{:S(2)}, u32[]{:S(2)}) %collective-permute-start.9) | collective-permute-done | bytes 49184 | tf_op jit(solution)/shard_map/ppermute | solution.py:45
  28.8 2.7 %collective-permute-start.10 = (f32[2,3,8,256]{3,2,1,0:T(8,128)S(1)}, f32[2,3,8,256]{3,2,1,0:T(8,128)S(1)}, u32[]{:S(2)}, u32[]{:S(2)}) collective-permute-start(f32[2,3,8,256]{3,2,1,0:T(8,128)S(1)} %get-tuple-element.26.ready_ref.block_ref), channel_id=1, source_target_pairs={{0,16},{2,18},{4,20},{6,22},{8,24},{10,26},{12,28},{14,30},{16,0},... | collective-permute-start | bytes 147464 | tf_op jit(solution)/shard_map/ppermute | solution.py:45
  31.5 0.5 %planes_terms.1.n_ref = f32[3,16,8,512]{3,2,1,0:T(8,128)S(1)} custom-call(f32[3,16,8,512]{3,2,1,0:T(8,128)S(1)} %get-tuple-element.18.v_ref, f32[2,12,8,512]{3,2,1,0:T(8,128)S(1)} %collective-permute-done.1.y_ref, f32[1,12,8,512]{3,2,1,0:T(8,128)S(1)} %collective-permute-done.e_ref, ...), custom_call_target="tpu_custom_call", output_to_operand_aliasing={{}: (4, {})} | custom-call | flops 3932160 | bytes 3145728 | tf_op jit(solution)/shard_map/planes_terms/pallas_call | solution.py:435
  32.0 0.9 %sweep.1 = (f32[3,16,8,512]{3,2,1,0:T(8,128)S(1)}, f32[3,16,8,512]{3,2,1,0:T(8,128)}) custom-call(f32[3,16,8,512]{3,2,1,0:T(8,128)S(1)} %get-tuple-element.18.v_ref, f32[3,16,8,512]{3,2,1,0:T(8,128)S(1)} %planes_terms.1.n_ref, f32[30,512]{1,0:T(8,128)S(1)} %get-tuple-element.20.power_ref), custom_call_target="tpu_custom_call" | custom-call | flops 1966080 | bytes 2359296 | tf_op jit(solution)/shard_map/sweep/pallas_call | solution.py:520
  32.9 0.9 %collective-permute-done.10.other_ref = f32[2,3,8,256]{3,2,1,0:T(8,128)S(1)} collective-permute-done((f32[2,3,8,256]{3,2,1,0:T(8,128)S(1)}, f32[2,3,8,256]{3,2,1,0:T(8,128)S(1)}, u32[]{:S(2)}, u32[]{:S(2)}) %collective-permute-start.10) | collective-permute-done | bytes 49184 | tf_op jit(solution)/shard_map/ppermute | solution.py:45
  34.0 0.8 %close_own.1.refs_0_ = f32[3,16,8,512]{3,2,1,0:T(8,128)} custom-call(s32[1]{0:T(128)} %bitcast.me_ref, f32[3,16,8,512]{3,2,1,0:T(8,128)S(1)} %get-tuple-element.27.ready_ref.s_ref, f32[30,512]{1,0:T(8,128)S(1)} %get-tuple-element.20.power_ref, f32[2,3,8,256]{3,2,1,0:T(8,128)S(1)} %get-tuple-element.32.entry_ref), custom_call_target="tpu_custom_call" | custom-call | flops 786432 | bytes 1572864 | tf_op jit(solution)/shard_map/close_own/pallas_call | solution.py:640
  35.2 0.8 %close_other.1 = f32[3,16,8,512]{3,2,1,0:T(8,128)} custom-call(s32[1]{0:T(128)} %bitcast.me_ref, f32[3,16,8,512]{3,2,1,0:T(8,128)S(1)} %get-tuple-element.27.ready_ref.s_ref, f32[30,512]{1,0:T(8,128)S(1)} %get-tuple-element.20.power_ref, f32[2,3,8,256]{3,2,1,0:T(8,128)S(1)} %collective-permute-done.11.entry_ref, ...), custom_call_target="tpu_custom_call", output_to_operand_aliasing={{}: (4, {})} | custom-call | flops 786432 | bytes 1572864 | tf_op jit(solution)/shard_map/close_other/pallas_call | solution.py:640
  (27 shorter events, 1.9 us)
Async XLA Ops:
  1.8 9.2 %copy-start.1 = (f32[21]{0:T(128)S(1)}, f32[21]{0:T(128)}, u32[]{:S(2)}) copy-start(f32[21]{0:T(128)} %stencil_ref.1) | copy-start | bytes 256
  2.0 11.1 %collective-permute-start.6 = (f32[3,10,8,512]{3,2,1,0:T(8,128)S(1)}, f32[3,10,8,512]{3,2,1,0:T(8,128)S(1)}, u32[]{:S(2)}, u32[]{:S(2)}) collective-permute-start(f32[3,10,8,512]{3,2,1,0:T(8,128)S(1)} %pack_core.1), channel_id=1, source_target_pairs={{0,2},{2,0},{4,6},{6,4},{8,10},{10,8},{12,14},{14,12},{16,18},{18,... | collective-permute-start | bytes 1474568 | tf_op jit(solution)/shard_map/ppermute | solution.py:45
  2.5 9.1 %collective-permute-start = (f32[1,12,8,512]{3,2,1,0:T(8,128)S(1)}, f32[1,12,8,512]{3,2,1,0:T(8,128)S(1)}, u32[]{:S(2)}, u32[]{:S(2)}) collective-permute-start(f32[1,12,8,512]{3,2,1,0:T(8,128)S(1)} %get-tuple-element.19.first_ref), channel_id=1, source_target_pairs={{0,1},{1,0},{2,3},{3,2},{4,5},{5,4},{6,7},{7,6},{8,9},{9,8},{10,11... | collective-permute-start | bytes 589832 | tf_op jit(solution)/shard_map/ppermute | solution.py:45
  5.1 12.7 %collective-permute-start.3 = (f32[3,5,8,512]{3,2,1,0:T(8,128)S(1)}, f32[3,5,8,512]{3,2,1,0:T(8,128)S(1)}, u32[]{:S(2)}, u32[]{:S(2)}) collective-permute-start(f32[3,5,8,512]{3,2,1,0:T(8,128)S(1)} %get-tuple-element.22.first_ref), channel_id=1, source_target_pairs={{2,4},{4,2},{6,8},{8,6},{10,12},{12,10},{14,16},{16,14},{18,20},{2... | collective-permute-start | bytes 737288 | tf_op jit(solution)/shard_map/ppermute | solution.py:53
  9.4 8.4 %collective-permute-start.4 = (f32[3,5,8,512]{3,2,1,0:T(8,128)S(1)}, f32[3,5,8,512]{3,2,1,0:T(8,128)S(1)}, u32[]{:S(2)}, u32[]{:S(2)}) collective-permute-start(f32[3,5,8,512]{3,2,1,0:T(8,128)S(1)} %get-tuple-element.23), channel_id=1, source_target_pairs={{2,4},{4,2},{6,8},{8,6},{10,12},{12,10},{14,16},{16,14},{18,20},{2... | collective-permute-start | bytes 737288 | tf_op jit(solution)/shard_map/ppermute | solution.py:53
  9.6 7.7 %collective-permute-start.5 = (f32[3,4,8,128]{3,2,1,0:T(8,128)S(1)}, f32[3,4,8,128]{3,2,1,0:T(8,128)S(1)}, u32[]{:S(2)}, u32[]{:S(2)}) collective-permute-start(f32[3,4,8,128]{3,2,1,0:T(8,128)S(1)} %pack_mirror.1.first_ref), channel_id=1, source_target_pairs={{0,16},{2,18},{4,20},{6,22},{8,24},{10,26},{12,28},{14,30},{16,0},... | collective-permute-start | bytes 147464 | tf_op jit(solution)/shard_map/ppermute | solution.py:45
  11.7 2.9 %copy-start = (f32[512,544]{0,1:T(8,128)S(1)}, f32[512,544]{0,1:T(8,128)}, u32[]{:S(2)}) copy-start(f32[512,544]{0,1:T(8,128)} %param.5) | copy-start | bytes 3342340
  12.3 5.7 %collective-permute-start.2 = (f32[2,3,8,512]{3,2,1,0:T(8,128)S(1)}, f32[2,3,8,512]{3,2,1,0:T(8,128)S(1)}, u32[]{:S(2)}, u32[]{:S(2)}) collective-permute-start(f32[2,3,8,512]{3,2,1,0:T(8,128)S(1)} %share_terms.1.first_ref), channel_id=1, source_target_pairs={{0,1},{1,0},{2,3},{3,2},{4,5},{5,4},{6,7},{7,6},{8,9},{9,8},{10,11... | collective-permute-start | bytes 294920 | tf_op jit(solution)/shard_map/ppermute | solution.py:45
  13.1 18.3 %collective-permute-start.1 = (f32[2,12,8,512]{3,2,1,0:T(8,128)S(1)}, f32[2,12,8,512]{3,2,1,0:T(8,128)S(1)}, u32[]{:S(2)}, u32[]{:S(2)}) collective-permute-start(f32[2,12,8,512]{3,2,1,0:T(8,128)S(1)} %pack_planes.1), channel_id=1, source_target_pairs={{0,1},{1,0},{2,3},{3,2},{4,5},{5,4},{6,7},{7,6},{8,9},{9,8},{10,11... | collective-permute-start | bytes 1179656 | tf_op jit(solution)/shard_map/ppermute | solution.py:45
  18.3 2.1 %collective-permute-start.7 = (f32[2,3,8,256]{3,2,1,0:T(8,128)S(1)}, f32[2,3,8,256]{3,2,1,0:T(8,128)S(1)}, u32[]{:S(2)}, u32[]{:S(2)}) collective-permute-start(f32[2,3,8,256]{3,2,1,0:T(8,128)S(1)} %ends_other.1.refs_3_), channel_id=1, source_target_pairs={{0,2},{2,0},{4,6},{6,4},{8,10},{10,8},{12,14},{14,12},{16,18},{18,... | collective-permute-start | bytes 147464 | tf_op jit(solution)/shard_map/ppermute | solution.py:45
  20.4 4.2 %collective-permute-start.8 = (f32[2,3,8,256]{3,2,1,0:T(8,128)S(1)}, f32[2,3,8,256]{3,2,1,0:T(8,128)S(1)}, u32[]{:S(2)}, u32[]{:S(2)}) collective-permute-start(f32[2,3,8,256]{3,2,1,0:T(8,128)S(1)} %pair.1.block_ref), channel_id=1, source_target_pairs={{0,4},{2,6},{4,0},{6,2},{8,12},{10,14},{12,8},{14,10},{16,20},{18,... | collective-permute-start | bytes 147464 | tf_op jit(solution)/shard_map/ppermute | solution.py:45
  24.6 4.2 %collective-permute-start.9 = (f32[2,3,8,256]{3,2,1,0:T(8,128)S(1)}, f32[2,3,8,256]{3,2,1,0:T(8,128)S(1)}, u32[]{:S(2)}, u32[]{:S(2)}) collective-permute-start(f32[2,3,8,256]{3,2,1,0:T(8,128)S(1)} %get-tuple-element.24.block_ref), channel_id=1, source_target_pairs={{0,8},{2,10},{4,12},{6,14},{8,0},{10,2},{12,4},{14,6},{16,24},{18,... | collective-permute-start | bytes 147464 | tf_op jit(solution)/shard_map/ppermute | solution.py:45
  28.8 5.1 %collective-permute-start.10 = (f32[2,3,8,256]{3,2,1,0:T(8,128)S(1)}, f32[2,3,8,256]{3,2,1,0:T(8,128)S(1)}, u32[]{:S(2)}, u32[]{:S(2)}) collective-permute-start(f32[2,3,8,256]{3,2,1,0:T(8,128)S(1)} %get-tuple-element.26.ready_ref.block_ref), channel_id=1, source_target_pairs={{0,16},{2,18},{4,20},{6,22},{8,24},{10,26},{12,28},{14,30},{16,0},... | collective-permute-start | bytes 147464 | tf_op jit(solution)/shard_map/ppermute | solution.py:45
  33.9 1.3 %collective-permute-start.11 = (f32[2,3,8,256]{3,2,1,0:T(8,128)S(1)}, f32[2,3,8,256]{3,2,1,0:T(8,128)S(1)}, u32[]{:S(2)}, u32[]{:S(2)}) collective-permute-start(f32[2,3,8,256]{3,2,1,0:T(8,128)S(1)} %get-tuple-element.31), channel_id=1, source_target_pairs={{0,2},{2,0},{4,6},{6,4},{8,10},{10,8},{12,14},{14,12},{16,18},{18,... | collective-permute-start | bytes 147464 | tf_op jit(solution)/shard_map/ppermute | solution.py:45

commit v19 on v15

--- a/solution.py
+++ b/solution.py
@@ -95,26 +95,22 @@
             tile_ref[c, j, hi + 1 :] = y_ref[c, 3 * j + 2, lo:hi]
 
 
-def load_kernel(hbm_ref, v_ref, y_ref, sems):
-    order = list(range(v_ref.shape[0]))
-    loads = [pltpu.make_async_copy(hbm_ref.at[c], v_ref.at[c], sems.at[c]) for c in order]
-    for c in reversed(order):
-        loads[c].start()
-    loads[-1].wait()
-    pack_tiles(v_ref, y_ref, order[-1:])
-    for c in order[:-1]:
-        loads[c].wait()
-
-
-def load(v):
+def load_axial_kernel(hbm_ref, y_ref, e_ref, sem):
+    load = pltpu.make_async_copy(hbm_ref.at[pl.ds(hbm_ref.shape[0] - 1, 1)], e_ref, sem)
+    load.start()
+    load.wait()
+    pack_tiles(e_ref, y_ref, (0,))
+
+
+def load_axial(v):
     comps, points, planes, radial = v.shape
     return pl.pallas_call(
-        load_kernel,
-        name="load",
-        out_shape=(held(*v.shape), held(1, points - points // 4, planes, radial)),
+        load_axial_kernel,
+        name="load_axial",
+        out_shape=held(1, points - points // 4, planes, radial),
         in_specs=[HBM],
-        out_specs=(VMEM, VMEM),
-        scratch_shapes=[pltpu.SemaphoreType.DMA((comps,))],
+        out_specs=VMEM,
+        scratch_shapes=[pltpu.VMEM((1, points, planes, radial), jnp.float32), pltpu.SemaphoreType.DMA],
         compiler_params=params(v.size * 4, 2),
     )(v)
 
@@ -653,7 +649,7 @@
     me = lax.axis_index("theta").astype(jnp.int32).reshape(1)
     op = radial_op.T
 
-    velocity, axial_out = load(pltpu.with_memory_space_constraint(velocity, pltpu.HBM))
+    axial_out = load_axial(pltpu.with_memory_space_constraint(velocity, pltpu.HBM))
     axial_in = swap(axial_out, "gz", 1)
     chip_out = pack_side(me, velocity, axial_out, reach, False)
     chip_in = swap_across(chip_out, "theta")

time: 35.7 us -> 35.6 us (level)
  no operation moved by 1% of the time
where the time goes in v19:
time: 35.6 us; the launch traced here: 35.4 us
  starting transfers between devices  16.9 us (47%)
  Pallas kernels  9.63 us (27%)
  waiting for transfers between devices  7.42 us (21%)
  between operations  1.5 us (4%)
    ppermute x10, starting transfers between devices, swap(): return lax.ppermute(block, axis, [(i, i ^ bit) for i in range(size)])  13.1 us
    ppermute x10, waiting for transfers between devices, swap(): return lax.ppermute(block, axis, [(i, i ^ bit) for i in range(size)])  7.42 us
    ppermute x1, starting transfers between devices, swap_across(): return lax.ppermute(block, axis, route)  3.76 us
    pallas_call x1, Pallas kernels, inner_terms(): pl.pallas_call(inner_kernel, name='inner_terms', out_shape=held(*v.shape)...  2.2 us
    pallas_call x2, Pallas kernels, close(): pl.pallas_call(functools.partial(close_kernel, own=own), name='close_own'...  1.59 us
    pallas_call x1, Pallas kernels, load_axial(): pl.pallas_call(load_axial_kernel, name='load_axial', out_shape=held(1, po...  1.06 us
    pallas_call x3, Pallas kernels, side_terms(): pl.pallas_call(kernel, name=name, out_shape=held(*v.shape), in_specs=[SME...  1.03 us
    pallas_call x1, Pallas kernels, sweep(): pl.pallas_call(sweep_kernel, name='sweep', out_shape=(held(*v.shape), jax...  0.89 us
  transfers between devices with their start and end apart: 11, of which 6 were waited for; matrix products, arithmetic and copies ran while one was open for 0% of the time, Pallas kernels for 22%

profile of v19, /device:TPU:0, one launch (start us, length us, event | category | flops | bytes accessed | tf_op | source)
XLA Modules:
  0.0 35.4 jit_solution(4742338884500105996)
XLA Ops:
  0.6 1.1 %load_axial.1.first_ref = f32[1,12,8,512]{3,2,1,0:T(8,128)S(1)} custom-call(f32[3,16,8,512]{3,2,1,0:T(8,128)} %v_ref.27), custom_call_target="tpu_custom_call" | custom-call | tf_op jit(solution)/shard_map/load_axial/pallas_call | solution.py:107
  1.7 3.0 %collective-permute-start = (f32[1,12,8,512]{3,2,1,0:T(8,128)S(1)}, f32[1,12,8,512]{3,2,1,0:T(8,128)S(1)}, u32[]{:S(2)}, u32[]{:S(2)}) collective-permute-start(f32[1,12,8,512]{3,2,1,0:T(8,128)S(1)} %load_axial.1.first_ref), channel_id=1, source_target_pairs={{0,1},{1,0},{2,3},{3,2},{4,5},{5,4},{6,7},{7,6},{8,9},{9,8},{10,11... | collective-permute-start | bytes 589832 | tf_op jit(solution)/shard_map/ppermute | solution.py:44
  4.8 3.8 %collective-permute-start.3 = (f32[3,10,8,512]{3,2,1,0:T(8,128)S(1)}, f32[3,10,8,512]{3,2,1,0:T(8,128)S(1)}, u32[]{:S(2)}, u32[]{:S(2)}) collective-permute-start(f32[3,10,8,512]{3,2,1,0:T(8,128)S(1)} %pack_chip.1.first_ref), channel_id=1, source_target_pairs={{2,4},{4,2},{6,8},{8,6},{10,12},{12,10},{14,16},{16,14},{18,20},{2... | collective-permute-start | bytes 1474568 | tf_op jit(solution)/shard_map/ppermute | solution.py:52
  9.4 0.6 %table.1 = (f32[30,512]{1,0:T(8,128)S(1)}, f32[21,8,128]{2,1,0:T(8,128)S(1)}) custom-call(s32[1]{0:T(128)} %bitcast.me_ref, f32[1]{0:T(128)S(6)} %copy.18.factor_ref, f32[21]{0:T(128)S(1)} %copy-done.2), custom_call_target="tpu_custom_call" | custom-call | flops 512000 | bytes 204800 | tf_op jit(solution)/shard_map/table/pallas_call | solution.py:468
  10.0 0.6 %share_terms.1.first_ref = f32[2,3,8,512]{3,2,1,0:T(8,128)S(1)} custom-call(f32[3,16,8,512]{3,2,1,0:T(8,128)S(1)} %copy-done, f32[1,12,8,512]{3,2,1,0:T(8,128)S(1)} %collective-permute-done.e_ref.first_ref, f32[30,512]{1,0:T(8,128)S(1)} %get-tuple-element.14.power_ref), custom_call_target="tpu_custom_call" | custom-call | flops 3932160 | bytes 1572864 | tf_op jit(solution)/shard_map/share_terms/pallas_call | solution.py:368
  10.7 1.4 %collective-permute-start.2 = (f32[2,3,8,512]{3,2,1,0:T(8,128)S(1)}, f32[2,3,8,512]{3,2,1,0:T(8,128)S(1)}, u32[]{:S(2)}, u32[]{:S(2)}) collective-permute-start(f32[2,3,8,512]{3,2,1,0:T(8,128)S(1)} %share_terms.1.first_ref), channel_id=1, source_target_pairs={{0,1},{1,0},{2,3},{3,2},{4,5},{5,4},{6,7},{7,6},{8,9},{9,8},{10,11... | collective-permute-start | bytes 294920 | tf_op jit(solution)/shard_map/ppermute | solution.py:44
  12.3 0.7 %collective-permute-start.1 = (f32[2,12,8,512]{3,2,1,0:T(8,128)S(1)}, f32[2,12,8,512]{3,2,1,0:T(8,128)S(1)}, u32[]{:S(2)}, u32[]{:S(2)}) collective-permute-start(f32[2,12,8,512]{3,2,1,0:T(8,128)S(1)} %pack_planes.1), channel_id=1, source_target_pairs={{0,1},{1,0},{2,3},{3,2},{4,5},{5,4},{6,7},{7,6},{8,9},{9,8},{10,11... | collective-permute-start | bytes 1179656 | tf_op jit(solution)/shard_map/ppermute | solution.py:44
  13.0 2.2 %inner_terms.1.n_in_ref = f32[3,16,8,512]{3,2,1,0:T(8,128)S(1)} custom-call(f32[21,8,128]{2,1,0:T(8,128)S(1)} %get-tuple-element.15.tap_ref, f32[3,16,8,512]{3,2,1,0:T(8,128)S(1)} %copy-done, f32[544,512]{1,0:T(8,128)S(1)} %bitcast.2), custom_call_target="tpu_custom_call" | custom-call | flops 5368709120 | bytes 3145728 | tf_op jit(solution)/shard_map/inner_terms/pallas_call | solution.py:284
  15.2 0.5 %core_terms.1.n_in_ref = f32[3,16,8,512]{3,2,1,0:T(8,128)S(1)} custom-call(s32[1]{0:T(128)} %bitcast.me_ref, f32[21,8,128]{2,1,0:T(8,128)S(1)} %get-tuple-element.15.tap_ref, f32[3,16,8,512]{3,2,1,0:T(8,128)S(1)} %copy-done, f32[3,10,8,512]{3,2,1,0:T(8,128)S(1)} %collective-permute-done.5.core_ref, ...), custom_call_target="tpu_custom_call", output_to_operand_aliasing={{}: (4, {})} | custom-call | flops 67108864 | bytes 2359296 | tf_op jit(solution)/shard_map/core_terms/pallas_call | solution.py:339
  15.8 0.6 %collective-permute-done.4.mirror_ref = f32[3,4,8,128]{3,2,1,0:T(8,128)S(1)} collective-permute-done((f32[3,4,8,128]{3,2,1,0:T(8,128)S(1)}, f32[3,4,8,128]{3,2,1,0:T(8,128)S(1)}, u32[]{:S(2)}, u32[]{:S(2)}) %collective-permute-start.4) | collective-permute-done | bytes 49184 | tf_op jit(solution)/shard_map/ppermute | solution.py:44
  16.4 0.5 %mirror_terms.1.n_in_ref = f32[3,16,8,512]{3,2,1,0:T(8,128)S(1)} custom-call(f32[3,16,8,512]{3,2,1,0:T(8,128)S(1)} %copy-done, f32[544,512]{1,0:T(8,128)S(1)} %bitcast.3, f32[3,4,8,128]{3,2,1,0:T(8,128)S(1)} %collective-permute-done.4.mirror_ref, f32[3,16,8,512]{3,2,1,0:T(8,128)S(1)} %core_terms.1.n_in_ref), custom_call_target="tpu_custom_call", output_to_operand_aliasing={{}: (3, {})} | custom-call | flops 67108864 | bytes 3145728 | tf_op jit(solution)/shard_map/mirror_terms/pallas_call | solution.py:239
  17.3 1.7 %collective-permute-start.6 = (f32[2,3,8,256]{3,2,1,0:T(8,128)S(1)}, f32[2,3,8,256]{3,2,1,0:T(8,128)S(1)}, u32[]{:S(2)}, u32[]{:S(2)}) collective-permute-start(f32[2,3,8,256]{3,2,1,0:T(8,128)S(1)} %ends_other.1.ready_ref), channel_id=1, source_target_pairs={{0,2},{2,0},{4,6},{6,4},{8,10},{10,8},{12,14},{14,12},{16,18},{18,... | collective-permute-start | bytes 147464 | tf_op jit(solution)/shard_map/ppermute | solution.py:44
  19.3 0.5 %collective-permute-done.6.other_ref = f32[2,3,8,256]{3,2,1,0:T(8,128)S(1)} collective-permute-done((f32[2,3,8,256]{3,2,1,0:T(8,128)S(1)}, f32[2,3,8,256]{3,2,1,0:T(8,128)S(1)}, u32[]{:S(2)}, u32[]{:S(2)}) %collective-permute-start.6) | collective-permute-done | bytes 49184 | tf_op jit(solution)/shard_map/ppermute | solution.py:44
  19.9 1.7 %collective-permute-start.7 = (f32[2,3,8,256]{3,2,1,0:T(8,128)S(1)}, f32[2,3,8,256]{3,2,1,0:T(8,128)S(1)}, u32[]{:S(2)}, u32[]{:S(2)}) collective-permute-start(f32[2,3,8,256]{3,2,1,0:T(8,128)S(1)} %pair.1.block_ref), channel_id=1, source_target_pairs={{0,4},{2,6},{4,0},{6,2},{8,12},{10,14},{12,8},{14,10},{16,20},{18,... | collective-permute-start | bytes 147464 | tf_op jit(solution)/shard_map/ppermute | solution.py:44
  21.6 2.4 %collective-permute-done.7.other_ref = f32[2,3,8,256]{3,2,1,0:T(8,128)S(1)} collective-permute-done((f32[2,3,8,256]{3,2,1,0:T(8,128)S(1)}, f32[2,3,8,256]{3,2,1,0:T(8,128)S(1)}, u32[]{:S(2)}, u32[]{:S(2)}) %collective-permute-start.7) | collective-permute-done | bytes 49184 | tf_op jit(solution)/shard_map/ppermute | solution.py:44
  24.0 1.6 %collective-permute-start.8 = (f32[2,3,8,256]{3,2,1,0:T(8,128)S(1)}, f32[2,3,8,256]{3,2,1,0:T(8,128)S(1)}, u32[]{:S(2)}, u32[]{:S(2)}) collective-permute-start(f32[2,3,8,256]{3,2,1,0:T(8,128)S(1)} %get-tuple-element.16.block_ref), channel_id=1, source_target_pairs={{0,8},{2,10},{4,12},{6,14},{8,0},{10,2},{12,4},{14,6},{16,24},{18,... | collective-permute-start | bytes 147464 | tf_op jit(solution)/shard_map/ppermute | solution.py:44
  25.7 2.5 %collective-permute-done.8.other_ref = f32[2,3,8,256]{3,2,1,0:T(8,128)S(1)} collective-permute-done((f32[2,3,8,256]{3,2,1,0:T(8,128)S(1)}, f32[2,3,8,256]{3,2,1,0:T(8,128)S(1)}, u32[]{:S(2)}, u32[]{:S(2)}) %collective-permute-start.8) | collective-permute-done | bytes 49184 | tf_op jit(solution)/shard_map/ppermute | solution.py:44
  28.2 2.7 %collective-permute-start.9 = (f32[2,3,8,256]{3,2,1,0:T(8,128)S(1)}, f32[2,3,8,256]{3,2,1,0:T(8,128)S(1)}, u32[]{:S(2)}, u32[]{:S(2)}) collective-permute-start(f32[2,3,8,256]{3,2,1,0:T(8,128)S(1)} %get-tuple-element.18.ready_ref.block_ref), channel_id=1, source_target_pairs={{0,16},{2,18},{4,20},{6,22},{8,24},{10,26},{12,28},{14,30},{16,0},... | collective-permute-start | bytes 147464 | tf_op jit(solution)/shard_map/ppermute | solution.py:44
  30.9 0.5 %planes_terms.1.n_ref = f32[3,16,8,512]{3,2,1,0:T(8,128)S(1)} custom-call(f32[3,16,8,512]{3,2,1,0:T(8,128)S(1)} %copy-done, f32[2,12,8,512]{3,2,1,0:T(8,128)S(1)} %collective-permute-done.1.y_ref, f32[1,12,8,512]{3,2,1,0:T(8,128)S(1)} %collective-permute-done.e_ref.first_ref, ...), custom_call_target="tpu_custom_call", output_to_operand_aliasing={{}: (4, {})} | custom-call | flops 3932160 | bytes 3145728 | tf_op jit(solution)/shard_map/planes_terms/pallas_call | solution.py:423
  31.4 0.9 %sweep.1 = (f32[3,16,8,512]{3,2,1,0:T(8,128)S(1)}, f32[3,16,8,512]{3,2,1,0:T(8,128)}) custom-call(f32[3,16,8,512]{3,2,1,0:T(8,128)S(1)} %copy-done, f32[3,16,8,512]{3,2,1,0:T(8,128)S(1)} %planes_terms.1.n_ref, f32[30,512]{1,0:T(8,128)S(1)} %get-tuple-element.14.power_ref), custom_call_target="tpu_custom_call" | custom-call | flops 1966080 | bytes 2359296 | tf_op jit(solution)/shard_map/sweep/pallas_call | solution.py:508
  32.3 0.9 %collective-permute-done.9.other_ref = f32[2,3,8,256]{3,2,1,0:T(8,128)S(1)} collective-permute-done((f32[2,3,8,256]{3,2,1,0:T(8,128)S(1)}, f32[2,3,8,256]{3,2,1,0:T(8,128)S(1)}, u32[]{:S(2)}, u32[]{:S(2)}) %collective-permute-start.9) | collective-permute-done | bytes 49184 | tf_op jit(solution)/shard_map/ppermute | solution.py:44
  33.4 0.8 %close_own.1.refs_0_ = f32[3,16,8,512]{3,2,1,0:T(8,128)} custom-call(s32[1]{0:T(128)} %bitcast.me_ref, f32[3,16,8,512]{3,2,1,0:T(8,128)S(1)} %get-tuple-element.19.ready_ref.s_ref, f32[30,512]{1,0:T(8,128)S(1)} %get-tuple-element.14.power_ref, f32[2,3,8,256]{3,2,1,0:T(8,128)S(1)} %get-tuple-element.24.entry_ref), custom_call_target="tpu_custom_call" | custom-call | flops 786432 | bytes 1572864 | tf_op jit(solution)/shard_map/close_own/pallas_call | solution.py:628
  34.2 0.4 %collective-permute-done.10.entry_ref = f32[2,3,8,256]{3,2,1,0:T(8,128)S(1)} collective-permute-done((f32[2,3,8,256]{3,2,1,0:T(8,128)S(1)}, f32[2,3,8,256]{3,2,1,0:T(8,128)S(1)}, u32[]{:S(2)}, u32[]{:S(2)}) %collective-permute-start.10) | collective-permute-done | bytes 49184 | tf_op jit(solution)/shard_map/ppermute | solution.py:44
  34.6 0.8 %close_other.1 = f32[3,16,8,512]{3,2,1,0:T(8,128)} custom-call(s32[1]{0:T(128)} %bitcast.me_ref, f32[3,16,8,512]{3,2,1,0:T(8,128)S(1)} %get-tuple-element.19.ready_ref.s_ref, f32[30,512]{1,0:T(8,128)S(1)} %get-tuple-element.14.power_ref, f32[2,3,8,256]{3,2,1,0:T(8,128)S(1)} %collective-permute-done.10.entry_ref, ...), custom_call_target="tpu_custom_call", output_to_operand_aliasing={{}: (4, {})} | custom-call | flops 786432 | bytes 1572864 | tf_op jit(solution)/shard_map/close_other/pallas_call | solution.py:628
  (27 shorter events, 1.3 us)
Async XLA Ops:
  0.6 4.1 %copy-start = (f32[3,16,8,512]{3,2,1,0:T(8,128)S(1)}, f32[3,16,8,512]{3,2,1,0:T(8,128)}, u32[]{:S(2)}) copy-start(f32[3,16,8,512]{3,2,1,0:T(8,128)} %v_ref.27) | copy-start | bytes 2359300
  1.7 8.3 %collective-permute-start = (f32[1,12,8,512]{3,2,1,0:T(8,128)S(1)}, f32[1,12,8,512]{3,2,1,0:T(8,128)S(1)}, u32[]{:S(2)}, u32[]{:S(2)}) collective-permute-start(f32[1,12,8,512]{3,2,1,0:T(8,128)S(1)} %load_axial.1.first_ref), channel_id=1, source_target_pairs={{0,1},{1,0},{2,3},{3,2},{4,5},{5,4},{6,7},{7,6},{8,9},{9,8},{10,11... | collective-permute-start | bytes 589832 | tf_op jit(solution)/shard_map/ppermute | solution.py:44
  4.7 4.6 %copy-start.2 = (f32[21]{0:T(128)S(1)}, f32[21]{0:T(128)}, u32[]{:S(2)}) copy-start(f32[21]{0:T(128)} %stencil_ref.1) | copy-start | bytes 256
  4.8 12.1 %collective-permute-start.3 = (f32[3,10,8,512]{3,2,1,0:T(8,128)S(1)}, f32[3,10,8,512]{3,2,1,0:T(8,128)S(1)}, u32[]{:S(2)}, u32[]{:S(2)}) collective-permute-start(f32[3,10,8,512]{3,2,1,0:T(8,128)S(1)} %pack_chip.1.first_ref), channel_id=1, source_target_pairs={{2,4},{4,2},{6,8},{8,6},{10,12},{12,10},{14,16},{16,14},{18,20},{2... | collective-permute-start | bytes 1474568 | tf_op jit(solution)/shard_map/ppermute | solution.py:52
  8.7 7.7 %collective-permute-start.4 = (f32[3,4,8,128]{3,2,1,0:T(8,128)S(1)}, f32[3,4,8,128]{3,2,1,0:T(8,128)S(1)}, u32[]{:S(2)}, u32[]{:S(2)}) collective-permute-start(f32[3,4,8,128]{3,2,1,0:T(8,128)S(1)} %pack_mirror.1), channel_id=1, source_target_pairs={{0,16},{2,18},{4,20},{6,22},{8,24},{10,26},{12,28},{14,30},{16,0},... | collective-permute-start | bytes 147464 | tf_op jit(solution)/shard_map/ppermute | solution.py:44
  10.6 2.4 %copy-start.1 = (f32[512,544]{0,1:T(8,128)S(1)}, f32[512,544]{0,1:T(8,128)}, u32[]{:S(2)}) copy-start(f32[512,544]{0,1:T(8,128)} %param.5) | copy-start | bytes 3342340
  10.7 6.2 %collective-permute-start.2 = (f32[2,3,8,512]{3,2,1,0:T(8,128)S(1)}, f32[2,3,8,512]{3,2,1,0:T(8,128)S(1)}, u32[]{:S(2)}, u32[]{:S(2)}) collective-permute-start(f32[2,3,8,512]{3,2,1,0:T(8,128)S(1)} %share_terms.1.first_ref), channel_id=1, source_target_pairs={{0,1},{1,0},{2,3},{3,2},{4,5},{5,4},{6,7},{7,6},{8,9},{9,8},{10,11... | collective-permute-start | bytes 294920 | tf_op jit(solution)/shard_map/ppermute | solution.py:44
  12.2 3.0 %collective-permute-start.5 = (f32[3,10,8,512]{3,2,1,0:T(8,128)S(1)}, f32[3,10,8,512]{3,2,1,0:T(8,128)S(1)}, u32[]{:S(2)}, u32[]{:S(2)}) collective-permute-start(f32[3,10,8,512]{3,2,1,0:T(8,128)S(1)} %pack_core.1), channel_id=1, source_target_pairs={{0,2},{2,0},{4,6},{6,4},{8,10},{10,8},{12,14},{14,12},{16,18},{18,... | collective-permute-start | bytes 1474568 | tf_op jit(solution)/shard_map/ppermute | solution.py:44
  12.3 18.6 %collective-permute-start.1 = (f32[2,12,8,512]{3,2,1,0:T(8,128)S(1)}, f32[2,12,8,512]{3,2,1,0:T(8,128)S(1)}, u32[]{:S(2)}, u32[]{:S(2)}) collective-permute-start(f32[2,12,8,512]{3,2,1,0:T(8,128)S(1)} %pack_planes.1), channel_id=1, source_target_pairs={{0,1},{1,0},{2,3},{3,2},{4,5},{5,4},{6,7},{7,6},{8,9},{9,8},{10,11... | collective-permute-start | bytes 1179656 | tf_op jit(solution)/shard_map/ppermute | solution.py:44
  17.3 2.6 %collective-permute-start.6 = (f32[2,3,8,256]{3,2,1,0:T(8,128)S(1)}, f32[2,3,8,256]{3,2,1,0:T(8,128)S(1)}, u32[]{:S(2)}, u32[]{:S(2)}) collective-permute-start(f32[2,3,8,256]{3,2,1,0:T(8,128)S(1)} %ends_other.1.ready_ref), channel_id=1, source_target_pairs={{0,2},{2,0},{4,6},{6,4},{8,10},{10,8},{12,14},{14,12},{16,18},{18,... | collective-permute-start | bytes 147464 | tf_op jit(solution)/shard_map/ppermute | solution.py:44
  19.9 4.2 %collective-permute-start.7 = (f32[2,3,8,256]{3,2,1,0:T(8,128)S(1)}, f32[2,3,8,256]{3,2,1,0:T(8,128)S(1)}, u32[]{:S(2)}, u32[]{:S(2)}) collective-permute-start(f32[2,3,8,256]{3,2,1,0:T(8,128)S(1)} %pair.1.block_ref), channel_id=1, source_target_pairs={{0,4},{2,6},{4,0},{6,2},{8,12},{10,14},{12,8},{14,10},{16,20},{18,... | collective-permute-start | bytes 147464 | tf_op jit(solution)/shard_map/ppermute | solution.py:44
  24.0 4.2 %collective-permute-start.8 = (f32[2,3,8,256]{3,2,1,0:T(8,128)S(1)}, f32[2,3,8,256]{3,2,1,0:T(8,128)S(1)}, u32[]{:S(2)}, u32[]{:S(2)}) collective-permute-start(f32[2,3,8,256]{3,2,1,0:T(8,128)S(1)} %get-tuple-element.16.block_ref), channel_id=1, source_target_pairs={{0,8},{2,10},{4,12},{6,14},{8,0},{10,2},{12,4},{14,6},{16,24},{18,... | collective-permute-start | bytes 147464 | tf_op jit(solution)/shard_map/ppermute | solution.py:44
  28.2 5.1 %collective-permute-start.9 = (f32[2,3,8,256]{3,2,1,0:T(8,128)S(1)}, f32[2,3,8,256]{3,2,1,0:T(8,128)S(1)}, u32[]{:S(2)}, u32[]{:S(2)}) collective-permute-start(f32[2,3,8,256]{3,2,1,0:T(8,128)S(1)} %get-tuple-element.18.ready_ref.block_ref), channel_id=1, source_target_pairs={{0,16},{2,18},{4,20},{6,22},{8,24},{10,26},{12,28},{14,30},{16,0},... | collective-permute-start | bytes 147464 | tf_op jit(solution)/shard_map/ppermute | solution.py:44
  33.3 1.3 %collective-permute-start.10 = (f32[2,3,8,256]{3,2,1,0:T(8,128)S(1)}, f32[2,3,8,256]{3,2,1,0:T(8,128)S(1)}, u32[]{:S(2)}, u32[]{:S(2)}) collective-permute-start(f32[2,3,8,256]{3,2,1,0:T(8,128)S(1)} %get-tuple-element.23), channel_id=1, source_target_pairs={{0,2},{2,0},{4,6},{6,4},{8,10},{10,8},{12,14},{14,12},{16,18},{18,... | collective-permute-start | bytes 147464 | tf_op jit(solution)/shard_map/ppermute | solution.py:44

commit v20 on v15

--- a/solution.py
+++ b/solution.py
@@ -330,13 +330,12 @@
     pl.when(jnp.logical_not(even))(lambda: add(before=True))
 
 
-def late_kernel(me_ref, tap_ref, v_ref, chip_ref, n_in_ref, ready_ref, n_ref, *, own):
-    core = me_ref[0] % 2
-    count = v_ref.shape[3] // (2 * LANES)
-    columns = ((core if own else 1 - core) * count, count)
+def late_kernel(me_ref, tap_ref, v_ref, chip_ref, n_in_ref, ready_ref, n_ref):
+    even = me_ref[0] % 2 == 0
+    columns = (0, v_ref.shape[3] // LANES)
     add = functools.partial(add_side, tap_ref, v_ref, chip_ref, n_in_ref, n_ref, columns=columns)
-    pl.when(core == 0)(lambda: add(before=True))
-    pl.when(core == 1)(lambda: add(before=False))
+    pl.when(even)(lambda: add(before=True))
+    pl.when(jnp.logical_not(even))(lambda: add(before=False))
 
 
 def side_terms(kernel, name, me, taps, v, side, n, ready=()):
@@ -406,6 +405,55 @@
         compiler_params=params(v.size * 4, 4),
         cost_estimate=pl.CostEstimate(flops=20 * v.size, bytes_accessed=8 * v.size, transcendentals=0),
     )(me, v, share, power, n)
+
+
+def chip_ends_kernel(me_ref, tap_ref, v_ref, chip_ref, power_ref, inner_ref, ready_ref, ends_ref, *, own):
+    comps, points, _, radial = v_ref.shape
+    reach = chip_ref.shape[1]
+    core = me_ref[0] % 2
+    count = radial // (2 * LANES)
+    start = (core if own else 1 - core) * count
+
+    def add(before):
+        first = 0 if before else reach + 1
+
+        @pl.loop(0, count)
+        def column(i):
+            k = start + i
+            lanes = pl.ds(pl.multiple_of(k * LANES, LANES), LANES)
+            here = pl.ds(pl.multiple_of(i * LANES, LANES), LANES)
+            inv_r = STEP_WEIGHT * inverse_radius(LANES, k * LANES)
+            weights = [tap_ref[first + j] for j in range(reach)]
+            for c in range(comps):
+                side = [chip_ref[c, h, :, lanes] for h in range(reach)]
+                low, high = inner_ref[0, c, :, here], inner_ref[1, c, :, here]
+                for u in range(reach):
+                    t = u if before else points - reach + u
+                    taps = [(h, h - u) for h in range(u, reach)] if before else [(h, reach - 1 + h - u) for h in range(u + 1)]
+                    around = None
+                    for h, w in taps:
+                        term = weights[w] * side[h]
+                        around = term if around is None else around + term
+                    x = v_ref[1, t, :, lanes] * inv_r * around
+                    low = low - power_ref[points - 1 - t : points - t, lanes] * x
+                    high = high - power_ref[t : t + 1, lanes] * x
+                ends_ref[0, c, :, here] = low
+                ends_ref[1, c, :, here] = high
+
+    pl.when(core == 0)(lambda: add(True))
+    pl.when(core == 1)(lambda: add(False))
+
+
+def chip_ends(me, taps, v, chip, power, inner, ready, own):
+    return pl.pallas_call(
+        functools.partial(chip_ends_kernel, own=own),
+        name="chip_own" if own else "chip_other",
+        out_shape=held(*inner.shape),
+        in_specs=[SMEM] + [VMEM] * 5 + [ANY],
+        out_specs=VMEM,
+        compiler_params=params(v.size * 4, 4),
+        cost_estimate=pl.CostEstimate(flops=SIDE, bytes_accessed=8 * v.size, transcendentals=0),
+    )(me, taps, v, chip, power, inner, ready)
 
 
 def planes_kernel(v_ref, y_ref, e_ref, ready_ref, n_in_ref, n_ref, y_tile_ref, e_tile_ref):
@@ -668,13 +716,12 @@
     planes_in = swap(pack_planes(velocity, share_out), "gz", 1)
     n = side_terms(core_kernel, "core_terms", me, taps, velocity, core_in, n)
     n = mirror_terms(velocity, op, mirror_in, n)
-    late = functools.partial(late_kernel, own=False)
-    n = side_terms(late, "late_other", me, taps, velocity, chip_in, n, (share_in,))
-    send = ends_terms(me, velocity, share_in, power, n, False)
+    inner_other = ends_terms(me, velocity, share_in, power, n, False)
+    inner_own = ends_terms(me, velocity, share_in, power, n, True)
+    send = chip_ends(me, taps, velocity, chip_in, power, inner_other, inner_own, False)
     other = swap(send, "theta", 1)
-    late = functools.partial(late_kernel, own=True)
-    n = side_terms(late, "late_own", me, taps, velocity, chip_in, n, (send,))
-    own = ends_terms(me, velocity, share_in, power, n, True)
+    own = chip_ends(me, taps, velocity, chip_in, power, inner_own, send, True)
+    n = side_terms(late_kernel, "late_terms", me, taps, velocity, chip_in, n, (own,))
     block = pair(me, power, own, other, points)
     entries = ()
     last = sectors.bit_length() - 2

time: 35.7 us -> 35.4 us (level)
    pallas_call x3 -> x2, Pallas kernels: 1.03 us -> 1.01 us  [side_terms(): pl.pallas_call(kernel, name=name, out_shape=held(*v.shape), in_specs=[SME...]
  transfers between devices with their start and end apart: 11 -> 11, of which waited for: 6 -> 6; matrix products, arithmetic and copies ran while one was open for 0% -> 0% of each run, Pallas kernels for 22% -> 23%
where the time goes in v20:
time: 35.4 us; the launch traced here: 35.3 us
  starting transfers between devices  16.7 us (47%)
  Pallas kernels  10 us (28%)
  waiting for transfers between devices  7.11 us (20%)
  between operations  1.5 us (4%)
    ppermute x10, starting transfers between devices, swap(): return lax.ppermute(block, axis, [(i, i ^ bit) for i in range(size)])  12.9 us
    ppermute x10, waiting for transfers between devices, swap(): return lax.ppermute(block, axis, [(i, i ^ bit) for i in range(size)])  7.1 us
    ppermute x1, starting transfers between devices, swap_across(): return lax.ppermute(block, axis, route)  3.76 us
    pallas_call x1, Pallas kernels, inner_terms(): pl.pallas_call(inner_kernel, name='inner_terms', out_shape=held(*v.shape)...  2.2 us
    pallas_call x2, Pallas kernels, close(): pl.pallas_call(functools.partial(close_kernel, own=own), name='close_own'...  1.59 us
    pallas_call x1, Pallas kernels, load(): pl.pallas_call(load_kernel, name='load', out_shape=(held(*v.shape), held(...  1.14 us
    pallas_call x2, Pallas kernels, side_terms(): pl.pallas_call(kernel, name=name, out_shape=held(*v.shape), in_specs=[SME...  1.01 us
    pallas_call x1, Pallas kernels, sweep(): pl.pallas_call(sweep_kernel, name='sweep', out_shape=(held(*v.shape), jax...  0.89 us
  transfers between devices with their start and end apart: 11, of which 6 were waited for; matrix products, arithmetic and copies ran while one was open for 0% of the time, Pallas kernels for 23%

profile of v20, /device:TPU:0, one launch (start us, length us, event | category | flops | bytes accessed | tf_op | source)
XLA Modules:
  0.0 35.3 jit_solution(11573739143507259562)
XLA Ops:
  0.6 1.1 %load.1 = (f32[3,16,8,512]{3,2,1,0:T(8,128)S(1)}, f32[1,12,8,512]{3,2,1,0:T(8,128)S(1)}) custom-call(f32[3,16,8,512]{3,2,1,0:T(8,128)} %hbm_ref.1), custom_call_target="tpu_custom_call" | custom-call | tf_op jit(solution)/shard_map/load/pallas_call | solution.py:111
  1.8 3.0 %collective-permute-start = (f32[1,12,8,512]{3,2,1,0:T(8,128)S(1)}, f32[1,12,8,512]{3,2,1,0:T(8,128)S(1)}, u32[]{:S(2)}, u32[]{:S(2)}) collective-permute-start(f32[1,12,8,512]{3,2,1,0:T(8,128)S(1)} %get-tuple-element.17.first_ref), channel_id=1, source_target_pairs={{0,1},{1,0},{2,3},{3,2},{4,5},{5,4},{6,7},{7,6},{8,9},{9,8},{10,11... | collective-permute-start | bytes 589832 | tf_op jit(solution)/shard_map/ppermute | solution.py:44
  4.8 3.8 %collective-permute-start.2 = (f32[3,10,8,512]{3,2,1,0:T(8,128)S(1)}, f32[3,10,8,512]{3,2,1,0:T(8,128)S(1)}, u32[]{:S(2)}, u32[]{:S(2)}) collective-permute-start(f32[3,10,8,512]{3,2,1,0:T(8,128)S(1)} %pack_chip.1.first_ref), channel_id=1, source_target_pairs={{2,4},{4,2},{6,8},{8,6},{10,12},{12,10},{14,16},{16,14},{18,20},{2... | collective-permute-start | bytes 1474568 | tf_op jit(solution)/shard_map/ppermute | solution.py:52
  9.4 0.6 %table.1 = (f32[30,512]{1,0:T(8,128)S(1)}, f32[21,8,128]{2,1,0:T(8,128)S(1)}) custom-call(s32[1]{0:T(128)} %bitcast.me_ref, f32[1]{0:T(128)S(6)} %copy.16.factor_ref, f32[21]{0:T(128)S(1)} %copy-done.1), custom_call_target="tpu_custom_call" | custom-call | flops 512000 | bytes 204800 | tf_op jit(solution)/shard_map/table/pallas_call | solution.py:520
  10.1 0.6 %share_terms.1.first_ref = f32[2,3,8,512]{3,2,1,0:T(8,128)S(1)} custom-call(f32[3,16,8,512]{3,2,1,0:T(8,128)S(1)} %get-tuple-element.16.v_ref, f32[1,12,8,512]{3,2,1,0:T(8,128)S(1)} %collective-permute-done.e_ref.first_ref, f32[30,512]{1,0:T(8,128)S(1)} %get-tuple-element.18.power_ref), custom_call_target="tpu_custom_call" | custom-call | flops 3932160 | bytes 1572864 | tf_op jit(solution)/shard_map/share_terms/pallas_call | solution.py:371
  10.7 1.4 %collective-permute-start.3 = (f32[2,3,8,512]{3,2,1,0:T(8,128)S(1)}, f32[2,3,8,512]{3,2,1,0:T(8,128)S(1)}, u32[]{:S(2)}, u32[]{:S(2)}) collective-permute-start(f32[2,3,8,512]{3,2,1,0:T(8,128)S(1)} %share_terms.1.first_ref), channel_id=1, source_target_pairs={{0,1},{1,0},{2,3},{3,2},{4,5},{5,4},{6,7},{7,6},{8,9},{9,8},{10,11... | collective-permute-start | bytes 294920 | tf_op jit(solution)/shard_map/ppermute | solution.py:44
  12.3 0.7 %collective-permute-start.1 = (f32[2,12,8,512]{3,2,1,0:T(8,128)S(1)}, f32[2,12,8,512]{3,2,1,0:T(8,128)S(1)}, u32[]{:S(2)}, u32[]{:S(2)}) collective-permute-start(f32[2,12,8,512]{3,2,1,0:T(8,128)S(1)} %pack_planes.1), channel_id=1, source_target_pairs={{0,1},{1,0},{2,3},{3,2},{4,5},{5,4},{6,7},{7,6},{8,9},{9,8},{10,11... | collective-permute-start | bytes 1179656 | tf_op jit(solution)/shard_map/ppermute | solution.py:44
  13.1 2.2 %inner_terms.1.n_in_ref = f32[3,16,8,512]{3,2,1,0:T(8,128)S(1)} custom-call(f32[21,8,128]{2,1,0:T(8,128)S(1)} %get-tuple-element.19.tap_ref, f32[3,16,8,512]{3,2,1,0:T(8,128)S(1)} %get-tuple-element.16.v_ref, f32[544,512]{1,0:T(8,128)S(1)} %bitcast.2), custom_call_target="tpu_custom_call" | custom-call | flops 5368709120 | bytes 3145728 | tf_op jit(solution)/shard_map/inner_terms/pallas_call | solution.py:288
  15.3 0.5 %core_terms.1.n_in_ref = f32[3,16,8,512]{3,2,1,0:T(8,128)S(1)} custom-call(s32[1]{0:T(128)} %bitcast.me_ref, f32[21,8,128]{2,1,0:T(8,128)S(1)} %get-tuple-element.19.tap_ref, f32[3,16,8,512]{3,2,1,0:T(8,128)S(1)} %get-tuple-element.16.v_ref, f32[3,10,8,512]{3,2,1,0:T(8,128)S(1)} %collective-permute-done.5.core_ref, ...), custom_call_target="tpu_custom_call", output_to_operand_aliasing={{}: (4, {})} | custom-call | flops 67108864 | bytes 2359296 | tf_op jit(solution)/shard_map/core_terms/pallas_call | solution.py:342
  15.8 0.6 %collective-permute-done.4.mirror_ref = f32[3,4,8,128]{3,2,1,0:T(8,128)S(1)} collective-permute-done((f32[3,4,8,128]{3,2,1,0:T(8,128)S(1)}, f32[3,4,8,128]{3,2,1,0:T(8,128)S(1)}, u32[]{:S(2)}, u32[]{:S(2)}) %collective-permute-start.4) | collective-permute-done | bytes 49184 | tf_op jit(solution)/shard_map/ppermute | solution.py:44
  16.4 0.5 %mirror_terms.1.n_ref.n_in_ref = f32[3,16,8,512]{3,2,1,0:T(8,128)S(1)} custom-call(f32[3,16,8,512]{3,2,1,0:T(8,128)S(1)} %get-tuple-element.16.v_ref, f32[544,512]{1,0:T(8,128)S(1)} %bitcast.3, f32[3,4,8,128]{3,2,1,0:T(8,128)S(1)} %collective-permute-done.4.mirror_ref, f32[3,16,8,512]{3,2,1,0:T(8,128)S(1)} %core_terms.1.n_in_ref), custom_call_target="tpu_custom_call", output_to_operand_aliasing={{}: (3, {})} | custom-call | flops 67108864 | bytes 3145728 | tf_op jit(solution)/shard_map/mirror_terms/pallas_call | solution.py:243
  17.4 1.4 %collective-permute-start.6 = (f32[2,3,8,256]{3,2,1,0:T(8,128)S(1)}, f32[2,3,8,256]{3,2,1,0:T(8,128)S(1)}, u32[]{:S(2)}, u32[]{:S(2)}) collective-permute-start(f32[2,3,8,256]{3,2,1,0:T(8,128)S(1)} %chip_other.1.ready_ref), channel_id=1, source_target_pairs={{0,2},{2,0},{4,6},{6,4},{8,10},{10,8},{12,14},{14,12},{16,18},{18,... | collective-permute-start | bytes 147464 | tf_op jit(solution)/shard_map/ppermute | solution.py:44
  19.0 0.7 %collective-permute-done.6.other_ref = f32[2,3,8,256]{3,2,1,0:T(8,128)S(1)} collective-permute-done((f32[2,3,8,256]{3,2,1,0:T(8,128)S(1)}, f32[2,3,8,256]{3,2,1,0:T(8,128)S(1)}, u32[]{:S(2)}, u32[]{:S(2)}) %collective-permute-start.6) | collective-permute-done | bytes 49184 | tf_op jit(solution)/shard_map/ppermute | solution.py:44
  19.7 1.8 %collective-permute-start.7 = (f32[2,3,8,256]{3,2,1,0:T(8,128)S(1)}, f32[2,3,8,256]{3,2,1,0:T(8,128)S(1)}, u32[]{:S(2)}, u32[]{:S(2)}) collective-permute-start(f32[2,3,8,256]{3,2,1,0:T(8,128)S(1)} %pair.1.block_ref), channel_id=1, source_target_pairs={{0,4},{2,6},{4,0},{6,2},{8,12},{10,14},{12,8},{14,10},{16,20},{18,... | collective-permute-start | bytes 147464 | tf_op jit(solution)/shard_map/ppermute | solution.py:44
  21.5 2.4 %collective-permute-done.7.other_ref = f32[2,3,8,256]{3,2,1,0:T(8,128)S(1)} collective-permute-done((f32[2,3,8,256]{3,2,1,0:T(8,128)S(1)}, f32[2,3,8,256]{3,2,1,0:T(8,128)S(1)}, u32[]{:S(2)}, u32[]{:S(2)}) %collective-permute-start.7) | collective-permute-done | bytes 49184 | tf_op jit(solution)/shard_map/ppermute | solution.py:44
  23.9 1.6 %collective-permute-start.8 = (f32[2,3,8,256]{3,2,1,0:T(8,128)S(1)}, f32[2,3,8,256]{3,2,1,0:T(8,128)S(1)}, u32[]{:S(2)}, u32[]{:S(2)}) collective-permute-start(f32[2,3,8,256]{3,2,1,0:T(8,128)S(1)} %get-tuple-element.20.block_ref), channel_id=1, source_target_pairs={{0,8},{2,10},{4,12},{6,14},{8,0},{10,2},{12,4},{14,6},{16,24},{18,... | collective-permute-start | bytes 147464 | tf_op jit(solution)/shard_map/ppermute | solution.py:44
  25.5 2.5 %collective-permute-done.8.other_ref = f32[2,3,8,256]{3,2,1,0:T(8,128)S(1)} collective-permute-done((f32[2,3,8,256]{3,2,1,0:T(8,128)S(1)}, f32[2,3,8,256]{3,2,1,0:T(8,128)S(1)}, u32[]{:S(2)}, u32[]{:S(2)}) %collective-permute-start.8) | collective-permute-done | bytes 49184 | tf_op jit(solution)/shard_map/ppermute | solution.py:44
  28.1 2.7 %collective-permute-start.9 = (f32[2,3,8,256]{3,2,1,0:T(8,128)S(1)}, f32[2,3,8,256]{3,2,1,0:T(8,128)S(1)}, u32[]{:S(2)}, u32[]{:S(2)}) collective-permute-start(f32[2,3,8,256]{3,2,1,0:T(8,128)S(1)} %get-tuple-element.22.ready_ref.block_ref), channel_id=1, source_target_pairs={{0,16},{2,18},{4,20},{6,22},{8,24},{10,26},{12,28},{14,30},{16,0},... | collective-permute-start | bytes 147464 | tf_op jit(solution)/shard_map/ppermute | solution.py:44
  30.7 0.5 %late_terms.1.n_in_ref = f32[3,16,8,512]{3,2,1,0:T(8,128)S(1)} custom-call(s32[1]{0:T(128)} %bitcast.me_ref, f32[21,8,128]{2,1,0:T(8,128)S(1)} %get-tuple-element.19.tap_ref, f32[3,16,8,512]{3,2,1,0:T(8,128)S(1)} %get-tuple-element.16.v_ref, f32[3,10,8,512]{3,2,1,0:T(8,128)S(1)} %collective-permute-done.2.chip_ref, ...), custom_call_target="tpu_custom_call", output_to_operand_aliasing={{}: (4, {})} | custom-call | flops 67108864 | bytes 2359296 | tf_op jit(solution)/shard_map/late_terms/pallas_call | solution.py:342
  31.2 0.6 %planes_terms.1.n_ref = f32[3,16,8,512]{3,2,1,0:T(8,128)S(1)} custom-call(f32[3,16,8,512]{3,2,1,0:T(8,128)S(1)} %get-tuple-element.16.v_ref, f32[2,12,8,512]{3,2,1,0:T(8,128)S(1)} %collective-permute-done.1.y_ref, f32[1,12,8,512]{3,2,1,0:T(8,128)S(1)} %collective-permute-done.e_ref.first_ref, ...), custom_call_target="tpu_custom_call", output_to_operand_aliasing={{}: (4, {})} | custom-call | flops 3932160 | bytes 3145728 | tf_op jit(solution)/shard_map/planes_terms/pallas_call | solution.py:475
  31.8 0.9 %sweep.1 = (f32[3,16,8,512]{3,2,1,0:T(8,128)S(1)}, f32[3,16,8,512]{3,2,1,0:T(8,128)}) custom-call(f32[3,16,8,512]{3,2,1,0:T(8,128)S(1)} %get-tuple-element.16.v_ref, f32[3,16,8,512]{3,2,1,0:T(8,128)S(1)} %planes_terms.1.n_ref, f32[30,512]{1,0:T(8,128)S(1)} %get-tuple-element.18.power_ref), custom_call_target="tpu_custom_call" | custom-call | flops 1966080 | bytes 2359296 | tf_op jit(solution)/shard_map/sweep/pallas_call | solution.py:560
  32.7 0.4 %collective-permute-done.9.other_ref = f32[2,3,8,256]{3,2,1,0:T(8,128)S(1)} collective-permute-done((f32[2,3,8,256]{3,2,1,0:T(8,128)S(1)}, f32[2,3,8,256]{3,2,1,0:T(8,128)S(1)}, u32[]{:S(2)}, u32[]{:S(2)}) %collective-permute-start.9) | collective-permute-done | bytes 49184 | tf_op jit(solution)/shard_map/ppermute | solution.py:44
  33.3 0.8 %close_own.1.refs_0_ = f32[3,16,8,512]{3,2,1,0:T(8,128)} custom-call(s32[1]{0:T(128)} %bitcast.me_ref, f32[3,16,8,512]{3,2,1,0:T(8,128)S(1)} %get-tuple-element.23.ready_ref.s_ref, f32[30,512]{1,0:T(8,128)S(1)} %get-tuple-element.18.power_ref, f32[2,3,8,256]{3,2,1,0:T(8,128)S(1)} %get-tuple-element.28.entry_ref), custom_call_target="tpu_custom_call" | custom-call | flops 786432 | bytes 1572864 | tf_op jit(solution)/shard_map/close_own/pallas_call | solution.py:680
  34.5 0.8 %close_other.1 = f32[3,16,8,512]{3,2,1,0:T(8,128)} custom-call(s32[1]{0:T(128)} %bitcast.me_ref, f32[3,16,8,512]{3,2,1,0:T(8,128)S(1)} %get-tuple-element.23.ready_ref.s_ref, f32[30,512]{1,0:T(8,128)S(1)} %get-tuple-element.18.power_ref, f32[2,3,8,256]{3,2,1,0:T(8,128)S(1)} %collective-permute-done.10.entry_ref, ...), custom_call_target="tpu_custom_call", output_to_operand_aliasing={{}: (4, {})} | custom-call | flops 786432 | bytes 1572864 | tf_op jit(solution)/shard_map/close_other/pallas_call | solution.py:680
  (26 shorter events, 1.5 us)
Async XLA Ops:
  1.8 8.3 %collective-permute-start = (f32[1,12,8,512]{3,2,1,0:T(8,128)S(1)}, f32[1,12,8,512]{3,2,1,0:T(8,128)S(1)}, u32[]{:S(2)}, u32[]{:S(2)}) collective-permute-start(f32[1,12,8,512]{3,2,1,0:T(8,128)S(1)} %get-tuple-element.17.first_ref), channel_id=1, source_target_pairs={{0,1},{1,0},{2,3},{3,2},{4,5},{5,4},{6,7},{7,6},{8,9},{9,8},{10,11... | collective-permute-start | bytes 589832 | tf_op jit(solution)/shard_map/ppermute | solution.py:44
  4.8 4.6 %copy-start.1 = (f32[21]{0:T(128)S(1)}, f32[21]{0:T(128)}, u32[]{:S(2)}) copy-start(f32[21]{0:T(128)} %stencil_ref.1) | copy-start | bytes 256
  4.8 12.3 %collective-permute-start.2 = (f32[3,10,8,512]{3,2,1,0:T(8,128)S(1)}, f32[3,10,8,512]{3,2,1,0:T(8,128)S(1)}, u32[]{:S(2)}, u32[]{:S(2)}) collective-permute-start(f32[3,10,8,512]{3,2,1,0:T(8,128)S(1)} %pack_chip.1.first_ref), channel_id=1, source_target_pairs={{2,4},{4,2},{6,8},{8,6},{10,12},{12,10},{14,16},{16,14},{18,20},{2... | collective-permute-start | bytes 1474568 | tf_op jit(solution)/shard_map/ppermute | solution.py:52
  8.7 7.7 %collective-permute-start.4 = (f32[3,4,8,128]{3,2,1,0:T(8,128)S(1)}, f32[3,4,8,128]{3,2,1,0:T(8,128)S(1)}, u32[]{:S(2)}, u32[]{:S(2)}) collective-permute-start(f32[3,4,8,128]{3,2,1,0:T(8,128)S(1)} %pack_mirror.1), channel_id=1, source_target_pairs={{0,16},{2,18},{4,20},{6,22},{8,24},{10,26},{12,28},{14,30},{16,0},... | collective-permute-start | bytes 147464 | tf_op jit(solution)/shard_map/ppermute | solution.py:44
  10.7 2.4 %copy-start = (f32[512,544]{0,1:T(8,128)S(1)}, f32[512,544]{0,1:T(8,128)}, u32[]{:S(2)}) copy-start(f32[512,544]{0,1:T(8,128)} %param.5) | copy-start | bytes 3342340
  10.7 6.2 %collective-permute-start.3 = (f32[2,3,8,512]{3,2,1,0:T(8,128)S(1)}, f32[2,3,8,512]{3,2,1,0:T(8,128)S(1)}, u32[]{:S(2)}, u32[]{:S(2)}) collective-permute-start(f32[2,3,8,512]{3,2,1,0:T(8,128)S(1)} %share_terms.1.first_ref), channel_id=1, source_target_pairs={{0,1},{1,0},{2,3},{3,2},{4,5},{5,4},{6,7},{7,6},{8,9},{9,8},{10,11... | collective-permute-start | bytes 294920 | tf_op jit(solution)/shard_map/ppermute | solution.py:44
  12.3 3.0 %collective-permute-start.5 = (f32[3,10,8,512]{3,2,1,0:T(8,128)S(1)}, f32[3,10,8,512]{3,2,1,0:T(8,128)S(1)}, u32[]{:S(2)}, u32[]{:S(2)}) collective-permute-start(f32[3,10,8,512]{3,2,1,0:T(8,128)S(1)} %pack_core.1), channel_id=1, source_target_pairs={{0,2},{2,0},{4,6},{6,4},{8,10},{10,8},{12,14},{14,12},{16,18},{18,... | collective-permute-start | bytes 1474568 | tf_op jit(solution)/shard_map/ppermute | solution.py:44
  12.3 18.9 %collective-permute-start.1 = (f32[2,12,8,512]{3,2,1,0:T(8,128)S(1)}, f32[2,12,8,512]{3,2,1,0:T(8,128)S(1)}, u32[]{:S(2)}, u32[]{:S(2)}) collective-permute-start(f32[2,12,8,512]{3,2,1,0:T(8,128)S(1)} %pack_planes.1), channel_id=1, source_target_pairs={{0,1},{1,0},{2,3},{3,2},{4,5},{5,4},{6,7},{7,6},{8,9},{9,8},{10,11... | collective-permute-start | bytes 1179656 | tf_op jit(solution)/shard_map/ppermute | solution.py:44
  17.4 2.3 %collective-permute-start.6 = (f32[2,3,8,256]{3,2,1,0:T(8,128)S(1)}, f32[2,3,8,256]{3,2,1,0:T(8,128)S(1)}, u32[]{:S(2)}, u32[]{:S(2)}) collective-permute-start(f32[2,3,8,256]{3,2,1,0:T(8,128)S(1)} %chip_other.1.ready_ref), channel_id=1, source_target_pairs={{0,2},{2,0},{4,6},{6,4},{8,10},{10,8},{12,14},{14,12},{16,18},{18,... | collective-permute-start | bytes 147464 | tf_op jit(solution)/shard_map/ppermute | solution.py:44
  19.7 4.2 %collective-permute-start.7 = (f32[2,3,8,256]{3,2,1,0:T(8,128)S(1)}, f32[2,3,8,256]{3,2,1,0:T(8,128)S(1)}, u32[]{:S(2)}, u32[]{:S(2)}) collective-permute-start(f32[2,3,8,256]{3,2,1,0:T(8,128)S(1)} %pair.1.block_ref), channel_id=1, source_target_pairs={{0,4},{2,6},{4,0},{6,2},{8,12},{10,14},{12,8},{14,10},{16,20},{18,... | collective-permute-start | bytes 147464 | tf_op jit(solution)/shard_map/ppermute | solution.py:44
  23.9 4.2 %collective-permute-start.8 = (f32[2,3,8,256]{3,2,1,0:T(8,128)S(1)}, f32[2,3,8,256]{3,2,1,0:T(8,128)S(1)}, u32[]{:S(2)}, u32[]{:S(2)}) collective-permute-start(f32[2,3,8,256]{3,2,1,0:T(8,128)S(1)} %get-tuple-element.20.block_ref), channel_id=1, source_target_pairs={{0,8},{2,10},{4,12},{6,14},{8,0},{10,2},{12,4},{14,6},{16,24},{18,... | collective-permute-start | bytes 147464 | tf_op jit(solution)/shard_map/ppermute | solution.py:44
  28.1 5.1 %collective-permute-start.9 = (f32[2,3,8,256]{3,2,1,0:T(8,128)S(1)}, f32[2,3,8,256]{3,2,1,0:T(8,128)S(1)}, u32[]{:S(2)}, u32[]{:S(2)}) collective-permute-start(f32[2,3,8,256]{3,2,1,0:T(8,128)S(1)} %get-tuple-element.22.ready_ref.block_ref), channel_id=1, source_target_pairs={{0,16},{2,18},{4,20},{6,22},{8,24},{10,26},{12,28},{14,30},{16,0},... | collective-permute-start | bytes 147464 | tf_op jit(solution)/shard_map/ppermute | solution.py:44
  33.2 1.3 %collective-permute-start.10 = (f32[2,3,8,256]{3,2,1,0:T(8,128)S(1)}, f32[2,3,8,256]{3,2,1,0:T(8,128)S(1)}, u32[]{:S(2)}, u32[]{:S(2)}) collective-permute-start(f32[2,3,8,256]{3,2,1,0:T(8,128)S(1)} %get-tuple-element.27), channel_id=1, source_target_pairs={{0,2},{2,0},{4,6},{6,4},{8,10},{10,8},{12,14},{14,12},{16,18},{18,... | collective-permute-start | bytes 147464 | tf_op jit(solution)/shard_map/ppermute | solution.py:44

commit v21 on v20

--- a/solution.py
+++ b/solution.py
@@ -659,18 +659,18 @@
 def close_kernel(me_ref, s_ref, power_ref, entry_ref, *refs, own):
     out_ref, x_ref, sems = refs[-3:]
     comps, points, _, _ = s_ref.shape
+    chunk = points // sems.shape[1]
     lanes = half_lanes(me_ref, entry_ref.shape[3], own)
     leaves = []
     for c in range(comps):
         before, after = entry_ref[0, c], entry_ref[1, c]
-
-        def point(t):
-            decayed = power_ref[pl.ds(t + 1, 1), lanes] * before + power_ref[pl.ds(points - t, 1), lanes] * after
-            x_ref[c, t] = s_ref[c, t, :, lanes] + decayed
-
-        each(points, point)
-        leaves.append(pltpu.make_async_copy(x_ref.at[c], out_ref.at[c, :, :, lanes], sems.at[c]))
-        leaves[c].start()
+        for k in range(sems.shape[1]):
+            for t in range(k * chunk, (k + 1) * chunk):
+                decayed = power_ref[t + 1 : t + 2, lanes] * before + power_ref[points - t : points - t + 1, lanes] * after
+                x_ref[c, t] = s_ref[c, t, :, lanes] + decayed
+            some = pl.ds(k * chunk, chunk)
+            leaves.append(pltpu.make_async_copy(x_ref.at[c, some], out_ref.at[c, some, :, lanes], sems.at[c, k]))
+            leaves[-1].start()
     for leave in leaves:
         leave.wait()
 
@@ -685,7 +685,7 @@
         out_specs=ANY,
         scratch_shapes=[
             pltpu.VMEM((comps, points, planes, radial // 2), jnp.float32),
-            pltpu.SemaphoreType.DMA((comps,)),
+            pltpu.SemaphoreType.DMA((comps, 4 if points % 4 == 0 else 1)),
         ],
         input_output_aliases={4: 0} if out else {},
         compiler_params=params(s.size * 4, 5),

time: 35.4 us -> 35.5 us (level)
  no operation moved by 1% of the time
where the time goes in v21:
time: 35.5 us; the launch traced here: 35.3 us
  starting transfers between devices  16.7 us (47%)
  Pallas kernels  10.1 us (28%)
  waiting for transfers between devices  7.05 us (20%)
  between operations  1.5 us (4%)
    ppermute x10, starting transfers between devices, swap(): return lax.ppermute(block, axis, [(i, i ^ bit) for i in range(size)])  12.9 us
    ppermute x10, waiting for transfers between devices, swap(): return lax.ppermute(block, axis, [(i, i ^ bit) for i in range(size)])  7.05 us
    ppermute x1, starting transfers between devices, swap_across(): return lax.ppermute(block, axis, route)  3.76 us
    pallas_call x1, Pallas kernels, inner_terms(): pl.pallas_call(inner_kernel, name='inner_terms', out_shape=held(*v.shape)...  2.2 us
    pallas_call x2, Pallas kernels, close(): pl.pallas_call(functools.partial(close_kernel, own=own), name='close_own'...  1.71 us
    pallas_call x1, Pallas kernels, load(): pl.pallas_call(load_kernel, name='load', out_shape=(held(*v.shape), held(...  1.14 us
    pallas_call x2, Pallas kernels, side_terms(): pl.pallas_call(kernel, name=name, out_shape=held(*v.shape), in_specs=[SME...  1.01 us
    pallas_call x1, Pallas kernels, sweep(): pl.pallas_call(sweep_kernel, name='sweep', out_shape=(held(*v.shape), jax...  0.89 us
  transfers between devices with their start and end apart: 11, of which 6 were waited for; matrix products, arithmetic and copies ran while one was open for 0% of the time, Pallas kernels for 23%

profile of v21, /device:TPU:0, one launch (start us, length us, event | category | flops | bytes accessed | tf_op | source)
XLA Modules:
  0.0 35.3 jit_solution(4254192370185845546)
XLA Ops:
  0.6 1.1 %load.1 = (f32[3,16,8,512]{3,2,1,0:T(8,128)S(1)}, f32[1,12,8,512]{3,2,1,0:T(8,128)S(1)}) custom-call(f32[3,16,8,512]{3,2,1,0:T(8,128)} %hbm_ref.1), custom_call_target="tpu_custom_call" | custom-call | tf_op jit(solution)/shard_map/load/pallas_call | solution.py:111
  1.8 3.0 %collective-permute-start = (f32[1,12,8,512]{3,2,1,0:T(8,128)S(1)}, f32[1,12,8,512]{3,2,1,0:T(8,128)S(1)}, u32[]{:S(2)}, u32[]{:S(2)}) collective-permute-start(f32[1,12,8,512]{3,2,1,0:T(8,128)S(1)} %get-tuple-element.17.first_ref), channel_id=1, source_target_pairs={{0,1},{1,0},{2,3},{3,2},{4,5},{5,4},{6,7},{7,6},{8,9},{9,8},{10,11... | collective-permute-start | bytes 589832 | tf_op jit(solution)/shard_map/ppermute | solution.py:44
  4.8 3.8 %collective-permute-start.2 = (f32[3,10,8,512]{3,2,1,0:T(8,128)S(1)}, f32[3,10,8,512]{3,2,1,0:T(8,128)S(1)}, u32[]{:S(2)}, u32[]{:S(2)}) collective-permute-start(f32[3,10,8,512]{3,2,1,0:T(8,128)S(1)} %pack_chip.1.first_ref), channel_id=1, source_target_pairs={{2,4},{4,2},{6,8},{8,6},{10,12},{12,10},{14,16},{16,14},{18,20},{2... | collective-permute-start | bytes 1474568 | tf_op jit(solution)/shard_map/ppermute | solution.py:52
  9.4 0.6 %table.1 = (f32[30,512]{1,0:T(8,128)S(1)}, f32[21,8,128]{2,1,0:T(8,128)S(1)}) custom-call(s32[1]{0:T(128)} %bitcast.me_ref, f32[1]{0:T(128)S(6)} %copy.16.factor_ref, f32[21]{0:T(128)S(1)} %copy-done.1), custom_call_target="tpu_custom_call" | custom-call | flops 512000 | bytes 204800 | tf_op jit(solution)/shard_map/table/pallas_call | solution.py:520
  10.1 0.6 %share_terms.1.first_ref = f32[2,3,8,512]{3,2,1,0:T(8,128)S(1)} custom-call(f32[3,16,8,512]{3,2,1,0:T(8,128)S(1)} %get-tuple-element.16.v_ref, f32[1,12,8,512]{3,2,1,0:T(8,128)S(1)} %collective-permute-done.e_ref.first_ref, f32[30,512]{1,0:T(8,128)S(1)} %get-tuple-element.18.power_ref), custom_call_target="tpu_custom_call" | custom-call | flops 3932160 | bytes 1572864 | tf_op jit(solution)/shard_map/share_terms/pallas_call | solution.py:371
  10.7 1.4 %collective-permute-start.3 = (f32[2,3,8,512]{3,2,1,0:T(8,128)S(1)}, f32[2,3,8,512]{3,2,1,0:T(8,128)S(1)}, u32[]{:S(2)}, u32[]{:S(2)}) collective-permute-start(f32[2,3,8,512]{3,2,1,0:T(8,128)S(1)} %share_terms.1.first_ref), channel_id=1, source_target_pairs={{0,1},{1,0},{2,3},{3,2},{4,5},{5,4},{6,7},{7,6},{8,9},{9,8},{10,11... | collective-permute-start | bytes 294920 | tf_op jit(solution)/shard_map/ppermute | solution.py:44
  12.3 0.7 %collective-permute-start.1 = (f32[2,12,8,512]{3,2,1,0:T(8,128)S(1)}, f32[2,12,8,512]{3,2,1,0:T(8,128)S(1)}, u32[]{:S(2)}, u32[]{:S(2)}) collective-permute-start(f32[2,12,8,512]{3,2,1,0:T(8,128)S(1)} %pack_planes.1), channel_id=1, source_target_pairs={{0,1},{1,0},{2,3},{3,2},{4,5},{5,4},{6,7},{7,6},{8,9},{9,8},{10,11... | collective-permute-start | bytes 1179656 | tf_op jit(solution)/shard_map/ppermute | solution.py:44
  13.1 2.2 %inner_terms.1.n_in_ref = f32[3,16,8,512]{3,2,1,0:T(8,128)S(1)} custom-call(f32[21,8,128]{2,1,0:T(8,128)S(1)} %get-tuple-element.19.tap_ref, f32[3,16,8,512]{3,2,1,0:T(8,128)S(1)} %get-tuple-element.16.v_ref, f32[544,512]{1,0:T(8,128)S(1)} %bitcast.2), custom_call_target="tpu_custom_call" | custom-call | flops 5368709120 | bytes 3145728 | tf_op jit(solution)/shard_map/inner_terms/pallas_call | solution.py:288
  15.3 0.5 %core_terms.1.n_in_ref = f32[3,16,8,512]{3,2,1,0:T(8,128)S(1)} custom-call(s32[1]{0:T(128)} %bitcast.me_ref, f32[21,8,128]{2,1,0:T(8,128)S(1)} %get-tuple-element.19.tap_ref, f32[3,16,8,512]{3,2,1,0:T(8,128)S(1)} %get-tuple-element.16.v_ref, f32[3,10,8,512]{3,2,1,0:T(8,128)S(1)} %collective-permute-done.5.core_ref, ...), custom_call_target="tpu_custom_call", output_to_operand_aliasing={{}: (4, {})} | custom-call | flops 67108864 | bytes 2359296 | tf_op jit(solution)/shard_map/core_terms/pallas_call | solution.py:342
  15.8 0.6 %collective-permute-done.4.mirror_ref = f32[3,4,8,128]{3,2,1,0:T(8,128)S(1)} collective-permute-done((f32[3,4,8,128]{3,2,1,0:T(8,128)S(1)}, f32[3,4,8,128]{3,2,1,0:T(8,128)S(1)}, u32[]{:S(2)}, u32[]{:S(2)}) %collective-permute-start.4) | collective-permute-done | bytes 49184 | tf_op jit(solution)/shard_map/ppermute | solution.py:44
  16.4 0.5 %mirror_terms.1.n_ref.n_in_ref = f32[3,16,8,512]{3,2,1,0:T(8,128)S(1)} custom-call(f32[3,16,8,512]{3,2,1,0:T(8,128)S(1)} %get-tuple-element.16.v_ref, f32[544,512]{1,0:T(8,128)S(1)} %bitcast.3, f32[3,4,8,128]{3,2,1,0:T(8,128)S(1)} %collective-permute-done.4.mirror_ref, f32[3,16,8,512]{3,2,1,0:T(8,128)S(1)} %core_terms.1.n_in_ref), custom_call_target="tpu_custom_call", output_to_operand_aliasing={{}: (3, {})} | custom-call | flops 67108864 | bytes 3145728 | tf_op jit(solution)/shard_map/mirror_terms/pallas_call | solution.py:243
  17.4 1.4 %collective-permute-start.6 = (f32[2,3,8,256]{3,2,1,0:T(8,128)S(1)}, f32[2,3,8,256]{3,2,1,0:T(8,128)S(1)}, u32[]{:S(2)}, u32[]{:S(2)}) collective-permute-start(f32[2,3,8,256]{3,2,1,0:T(8,128)S(1)} %chip_other.1.ready_ref), channel_id=1, source_target_pairs={{0,2},{2,0},{4,6},{6,4},{8,10},{10,8},{12,14},{14,12},{16,18},{18,... | collective-permute-start | bytes 147464 | tf_op jit(solution)/shard_map/ppermute | solution.py:44
  19.0 0.7 %collective-permute-done.6.other_ref = f32[2,3,8,256]{3,2,1,0:T(8,128)S(1)} collective-permute-done((f32[2,3,8,256]{3,2,1,0:T(8,128)S(1)}, f32[2,3,8,256]{3,2,1,0:T(8,128)S(1)}, u32[]{:S(2)}, u32[]{:S(2)}) %collective-permute-start.6) | collective-permute-done | bytes 49184 | tf_op jit(solution)/shard_map/ppermute | solution.py:44
  19.7 1.8 %collective-permute-start.7 = (f32[2,3,8,256]{3,2,1,0:T(8,128)S(1)}, f32[2,3,8,256]{3,2,1,0:T(8,128)S(1)}, u32[]{:S(2)}, u32[]{:S(2)}) collective-permute-start(f32[2,3,8,256]{3,2,1,0:T(8,128)S(1)} %pair.1.block_ref), channel_id=1, source_target_pairs={{0,4},{2,6},{4,0},{6,2},{8,12},{10,14},{12,8},{14,10},{16,20},{18,... | collective-permute-start | bytes 147464 | tf_op jit(solution)/shard_map/ppermute | solution.py:44
  21.5 2.4 %collective-permute-done.7.other_ref = f32[2,3,8,256]{3,2,1,0:T(8,128)S(1)} collective-permute-done((f32[2,3,8,256]{3,2,1,0:T(8,128)S(1)}, f32[2,3,8,256]{3,2,1,0:T(8,128)S(1)}, u32[]{:S(2)}, u32[]{:S(2)}) %collective-permute-start.7) | collective-permute-done | bytes 49184 | tf_op jit(solution)/shard_map/ppermute | solution.py:44
  23.9 1.6 %collective-permute-start.8 = (f32[2,3,8,256]{3,2,1,0:T(8,128)S(1)}, f32[2,3,8,256]{3,2,1,0:T(8,128)S(1)}, u32[]{:S(2)}, u32[]{:S(2)}) collective-permute-start(f32[2,3,8,256]{3,2,1,0:T(8,128)S(1)} %get-tuple-element.20.block_ref), channel_id=1, source_target_pairs={{0,8},{2,10},{4,12},{6,14},{8,0},{10,2},{12,4},{14,6},{16,24},{18,... | collective-permute-start | bytes 147464 | tf_op jit(solution)/shard_map/ppermute | solution.py:44
  25.5 2.5 %collective-permute-done.8.other_ref = f32[2,3,8,256]{3,2,1,0:T(8,128)S(1)} collective-permute-done((f32[2,3,8,256]{3,2,1,0:T(8,128)S(1)}, f32[2,3,8,256]{3,2,1,0:T(8,128)S(1)}, u32[]{:S(2)}, u32[]{:S(2)}) %collective-permute-start.8) | collective-permute-done | bytes 49184 | tf_op jit(solution)/shard_map/ppermute | solution.py:44
  28.1 2.7 %collective-permute-start.9 = (f32[2,3,8,256]{3,2,1,0:T(8,128)S(1)}, f32[2,3,8,256]{3,2,1,0:T(8,128)S(1)}, u32[]{:S(2)}, u32[]{:S(2)}) collective-permute-start(f32[2,3,8,256]{3,2,1,0:T(8,128)S(1)} %get-tuple-element.22.ready_ref.block_ref), channel_id=1, source_target_pairs={{0,16},{2,18},{4,20},{6,22},{8,24},{10,26},{12,28},{14,30},{16,0},... | collective-permute-start | bytes 147464 | tf_op jit(solution)/shard_map/ppermute | solution.py:44
  30.7 0.5 %late_terms.1.n_in_ref = f32[3,16,8,512]{3,2,1,0:T(8,128)S(1)} custom-call(s32[1]{0:T(128)} %bitcast.me_ref, f32[21,8,128]{2,1,0:T(8,128)S(1)} %get-tuple-element.19.tap_ref, f32[3,16,8,512]{3,2,1,0:T(8,128)S(1)} %get-tuple-element.16.v_ref, f32[3,10,8,512]{3,2,1,0:T(8,128)S(1)} %collective-permute-done.2.chip_ref, ...), custom_call_target="tpu_custom_call", output_to_operand_aliasing={{}: (4, {})} | custom-call | flops 67108864 | bytes 2359296 | tf_op jit(solution)/shard_map/late_terms/pallas_call | solution.py:342
  31.2 0.6 %planes_terms.1.n_ref = f32[3,16,8,512]{3,2,1,0:T(8,128)S(1)} custom-call(f32[3,16,8,512]{3,2,1,0:T(8,128)S(1)} %get-tuple-element.16.v_ref, f32[2,12,8,512]{3,2,1,0:T(8,128)S(1)} %collective-permute-done.1.y_ref, f32[1,12,8,512]{3,2,1,0:T(8,128)S(1)} %collective-permute-done.e_ref.first_ref, ...), custom_call_target="tpu_custom_call", output_to_operand_aliasing={{}: (4, {})} | custom-call | flops 3932160 | bytes 3145728 | tf_op jit(solution)/shard_map/planes_terms/pallas_call | solution.py:475
  31.8 0.9 %sweep.1 = (f32[3,16,8,512]{3,2,1,0:T(8,128)S(1)}, f32[3,16,8,512]{3,2,1,0:T(8,128)}) custom-call(f32[3,16,8,512]{3,2,1,0:T(8,128)S(1)} %get-tuple-element.16.v_ref, f32[3,16,8,512]{3,2,1,0:T(8,128)S(1)} %planes_terms.1.n_ref, f32[30,512]{1,0:T(8,128)S(1)} %get-tuple-element.18.power_ref), custom_call_target="tpu_custom_call" | custom-call | flops 1966080 | bytes 2359296 | tf_op jit(solution)/shard_map/sweep/pallas_call | solution.py:560
  32.7 0.4 %collective-permute-done.9.other_ref = f32[2,3,8,256]{3,2,1,0:T(8,128)S(1)} collective-permute-done((f32[2,3,8,256]{3,2,1,0:T(8,128)S(1)}, f32[2,3,8,256]{3,2,1,0:T(8,128)S(1)}, u32[]{:S(2)}, u32[]{:S(2)}) %collective-permute-start.9) | collective-permute-done | bytes 49184 | tf_op jit(solution)/shard_map/ppermute | solution.py:44
  33.3 0.9 %close_own.1.refs_0_ = f32[3,16,8,512]{3,2,1,0:T(8,128)} custom-call(s32[1]{0:T(128)} %bitcast.me_ref, f32[3,16,8,512]{3,2,1,0:T(8,128)S(1)} %get-tuple-element.23.ready_ref.s_ref, f32[30,512]{1,0:T(8,128)S(1)} %get-tuple-element.18.power_ref, f32[2,3,8,256]{3,2,1,0:T(8,128)S(1)} %get-tuple-element.28.entry_ref), custom_call_target="tpu_custom_call" | custom-call | flops 786432 | bytes 1572864 | tf_op jit(solution)/shard_map/close_own/pallas_call | solution.py:680
  34.5 0.8 %close_other.1 = f32[3,16,8,512]{3,2,1,0:T(8,128)} custom-call(s32[1]{0:T(128)} %bitcast.me_ref, f32[3,16,8,512]{3,2,1,0:T(8,128)S(1)} %get-tuple-element.23.ready_ref.s_ref, f32[30,512]{1,0:T(8,128)S(1)} %get-tuple-element.18.power_ref, f32[2,3,8,256]{3,2,1,0:T(8,128)S(1)} %collective-permute-done.10.entry_ref, ...), custom_call_target="tpu_custom_call", output_to_operand_aliasing={{}: (4, {})} | custom-call | flops 786432 | bytes 1572864 | tf_op jit(solution)/shard_map/close_other/pallas_call | solution.py:680
  (26 shorter events, 1.5 us)
Async XLA Ops:
  1.8 8.3 %collective-permute-start = (f32[1,12,8,512]{3,2,1,0:T(8,128)S(1)}, f32[1,12,8,512]{3,2,1,0:T(8,128)S(1)}, u32[]{:S(2)}, u32[]{:S(2)}) collective-permute-start(f32[1,12,8,512]{3,2,1,0:T(8,128)S(1)} %get-tuple-element.17.first_ref), channel_id=1, source_target_pairs={{0,1},{1,0},{2,3},{3,2},{4,5},{5,4},{6,7},{7,6},{8,9},{9,8},{10,11... | collective-permute-start | bytes 589832 | tf_op jit(solution)/shard_map/ppermute | solution.py:44
  4.8 4.6 %copy-start.1 = (f32[21]{0:T(128)S(1)}, f32[21]{0:T(128)}, u32[]{:S(2)}) copy-start(f32[21]{0:T(128)} %stencil_ref.1) | copy-start | bytes 256
  4.8 12.3 %collective-permute-start.2 = (f32[3,10,8,512]{3,2,1,0:T(8,128)S(1)}, f32[3,10,8,512]{3,2,1,0:T(8,128)S(1)}, u32[]{:S(2)}, u32[]{:S(2)}) collective-permute-start(f32[3,10,8,512]{3,2,1,0:T(8,128)S(1)} %pack_chip.1.first_ref), channel_id=1, source_target_pairs={{2,4},{4,2},{6,8},{8,6},{10,12},{12,10},{14,16},{16,14},{18,20},{2... | collective-permute-start | bytes 1474568 | tf_op jit(solution)/shard_map/ppermute | solution.py:52
  8.7 7.7 %collective-permute-start.4 = (f32[3,4,8,128]{3,2,1,0:T(8,128)S(1)}, f32[3,4,8,128]{3,2,1,0:T(8,128)S(1)}, u32[]{:S(2)}, u32[]{:S(2)}) collective-permute-start(f32[3,4,8,128]{3,2,1,0:T(8,128)S(1)} %pack_mirror.1), channel_id=1, source_target_pairs={{0,16},{2,18},{4,20},{6,22},{8,24},{10,26},{12,28},{14,30},{16,0},... | collective-permute-start | bytes 147464 | tf_op jit(solution)/shard_map/ppermute | solution.py:44
  10.7 2.4 %copy-start = (f32[512,544]{0,1:T(8,128)S(1)}, f32[512,544]{0,1:T(8,128)}, u32[]{:S(2)}) copy-start(f32[512,544]{0,1:T(8,128)} %param.5) | copy-start | bytes 3342340
  10.7 6.2 %collective-permute-start.3 = (f32[2,3,8,512]{3,2,1,0:T(8,128)S(1)}, f32[2,3,8,512]{3,2,1,0:T(8,128)S(1)}, u32[]{:S(2)}, u32[]{:S(2)}) collective-permute-start(f32[2,3,8,512]{3,2,1,0:T(8,128)S(1)} %share_terms.1.first_ref), channel_id=1, source_target_pairs={{0,1},{1,0},{2,3},{3,2},{4,5},{5,4},{6,7},{7,6},{8,9},{9,8},{10,11... | collective-permute-start | bytes 294920 | tf_op jit(solution)/shard_map/ppermute | solution.py:44
  12.3 3.0 %collective-permute-start.5 = (f32[3,10,8,512]{3,2,1,0:T(8,128)S(1)}, f32[3,10,8,512]{3,2,1,0:T(8,128)S(1)}, u32[]{:S(2)}, u32[]{:S(2)}) collective-permute-start(f32[3,10,8,512]{3,2,1,0:T(8,128)S(1)} %pack_core.1), channel_id=1, source_target_pairs={{0,2},{2,0},{4,6},{6,4},{8,10},{10,8},{12,14},{14,12},{16,18},{18,... | collective-permute-start | bytes 1474568 | tf_op jit(solution)/shard_map/ppermute | solution.py:44
  12.3 18.9 %collective-permute-start.1 = (f32[2,12,8,512]{3,2,1,0:T(8,128)S(1)}, f32[2,12,8,512]{3,2,1,0:T(8,128)S(1)}, u32[]{:S(2)}, u32[]{:S(2)}) collective-permute-start(f32[2,12,8,512]{3,2,1,0:T(8,128)S(1)} %pack_planes.1), channel_id=1, source_target_pairs={{0,1},{1,0},{2,3},{3,2},{4,5},{5,4},{6,7},{7,6},{8,9},{9,8},{10,11... | collective-permute-start | bytes 1179656 | tf_op jit(solution)/shard_map/ppermute | solution.py:44
  17.4 2.3 %collective-permute-start.6 = (f32[2,3,8,256]{3,2,1,0:T(8,128)S(1)}, f32[2,3,8,256]{3,2,1,0:T(8,128)S(1)}, u32[]{:S(2)}, u32[]{:S(2)}) collective-permute-start(f32[2,3,8,256]{3,2,1,0:T(8,128)S(1)} %chip_other.1.ready_ref), channel_id=1, source_target_pairs={{0,2},{2,0},{4,6},{6,4},{8,10},{10,8},{12,14},{14,12},{16,18},{18,... | collective-permute-start | bytes 147464 | tf_op jit(solution)/shard_map/ppermute | solution.py:44
  19.7 4.2 %collective-permute-start.7 = (f32[2,3,8,256]{3,2,1,0:T(8,128)S(1)}, f32[2,3,8,256]{3,2,1,0:T(8,128)S(1)}, u32[]{:S(2)}, u32[]{:S(2)}) collective-permute-start(f32[2,3,8,256]{3,2,1,0:T(8,128)S(1)} %pair.1.block_ref), channel_id=1, source_target_pairs={{0,4},{2,6},{4,0},{6,2},{8,12},{10,14},{12,8},{14,10},{16,20},{18,... | collective-permute-start | bytes 147464 | tf_op jit(solution)/shard_map/ppermute | solution.py:44
  23.9 4.2 %collective-permute-start.8 = (f32[2,3,8,256]{3,2,1,0:T(8,128)S(1)}, f32[2,3,8,256]{3,2,1,0:T(8,128)S(1)}, u32[]{:S(2)}, u32[]{:S(2)}) collective-permute-start(f32[2,3,8,256]{3,2,1,0:T(8,128)S(1)} %get-tuple-element.20.block_ref), channel_id=1, source_target_pairs={{0,8},{2,10},{4,12},{6,14},{8,0},{10,2},{12,4},{14,6},{16,24},{18,... | collective-permute-start | bytes 147464 | tf_op jit(solution)/shard_map/ppermute | solution.py:44
  28.1 5.1 %collective-permute-start.9 = (f32[2,3,8,256]{3,2,1,0:T(8,128)S(1)}, f32[2,3,8,256]{3,2,1,0:T(8,128)S(1)}, u32[]{:S(2)}, u32[]{:S(2)}) collective-permute-start(f32[2,3,8,256]{3,2,1,0:T(8,128)S(1)} %get-tuple-element.22.ready_ref.block_ref), channel_id=1, source_target_pairs={{0,16},{2,18},{4,20},{6,22},{8,24},{10,26},{12,28},{14,30},{16,0},... | collective-permute-start | bytes 147464 | tf_op jit(solution)/shard_map/ppermute | solution.py:44
  33.2 1.3 %collective-permute-start.10 = (f32[2,3,8,256]{3,2,1,0:T(8,128)S(1)}, f32[2,3,8,256]{3,2,1,0:T(8,128)S(1)}, u32[]{:S(2)}, u32[]{:S(2)}) collective-permute-start(f32[2,3,8,256]{3,2,1,0:T(8,128)S(1)} %get-tuple-element.27), channel_id=1, source_target_pairs={{0,2},{2,0},{4,6},{6,4},{8,10},{10,8},{12,14},{14,12},{16,18},{18,... | collective-permute-start | bytes 147464 | tf_op jit(solution)/shard_map/ppermute | solution.py:44

commit v22 on v20

--- a/solution.py
+++ b/solution.py
@@ -95,26 +95,22 @@
             tile_ref[c, j, hi + 1 :] = y_ref[c, 3 * j + 2, lo:hi]
 
 
-def load_kernel(hbm_ref, v_ref, y_ref, sems):
-    order = list(range(v_ref.shape[0]))
-    loads = [pltpu.make_async_copy(hbm_ref.at[c], v_ref.at[c], sems.at[c]) for c in order]
-    for c in reversed(order):
-        loads[c].start()
-    loads[-1].wait()
-    pack_tiles(v_ref, y_ref, order[-1:])
-    for c in order[:-1]:
-        loads[c].wait()
-
-
-def load(v):
+def load_axial_kernel(hbm_ref, y_ref, e_ref, sem):
+    load = pltpu.make_async_copy(hbm_ref.at[pl.ds(hbm_ref.shape[0] - 1, 1)], e_ref, sem)
+    load.start()
+    load.wait()
+    pack_tiles(e_ref, y_ref, (0,))
+
+
+def load_axial(v):
     comps, points, planes, radial = v.shape
     return pl.pallas_call(
-        load_kernel,
-        name="load",
-        out_shape=(held(*v.shape), held(1, points - points // 4, planes, radial)),
+        load_axial_kernel,
+        name="load_axial",
+        out_shape=held(1, points - points // 4, planes, radial),
         in_specs=[HBM],
-        out_specs=(VMEM, VMEM),
-        scratch_shapes=[pltpu.SemaphoreType.DMA((comps,))],
+        out_specs=VMEM,
+        scratch_shapes=[pltpu.VMEM((1, points, planes, radial), jnp.float32), pltpu.SemaphoreType.DMA],
         compiler_params=params(v.size * 4, 2),
     )(v)
 
@@ -701,7 +697,7 @@
     me = lax.axis_index("theta").astype(jnp.int32).reshape(1)
     op = radial_op.T
 
-    velocity, axial_out = load(pltpu.with_memory_space_constraint(velocity, pltpu.HBM))
+    axial_out = load_axial(pltpu.with_memory_space_constraint(velocity, pltpu.HBM))
     axial_in = swap(axial_out, "gz", 1)
     chip_out = pack_side(me, velocity, axial_out, reach, False)
     chip_in = swap_across(chip_out, "theta")

time: 35.4 us -> 35.4 us (level)
  no operation moved by 1% of the time
where the time goes in v22:
time: 35.4 us; the launch traced here: 35.2 us
  starting transfers between devices  16.7 us (47%)
  Pallas kernels  9.92 us (28%)
  waiting for transfers between devices  7.11 us (20%)
  between operations  1.51 us (4%)
    ppermute x10, starting transfers between devices, swap(): return lax.ppermute(block, axis, [(i, i ^ bit) for i in range(size)])  12.9 us
    ppermute x10, waiting for transfers between devices, swap(): return lax.ppermute(block, axis, [(i, i ^ bit) for i in range(size)])  7.1 us
    ppermute x1, starting transfers between devices, swap_across(): return lax.ppermute(block, axis, route)  3.76 us
    pallas_call x1, Pallas kernels, inner_terms(): pl.pallas_call(inner_kernel, name='inner_terms', out_shape=held(*v.shape)...  2.2 us
    pallas_call x2, Pallas kernels, close(): pl.pallas_call(functools.partial(close_kernel, own=own), name='close_own'...  1.59 us
    pallas_call x1, Pallas kernels, load_axial(): pl.pallas_call(load_axial_kernel, name='load_axial', out_shape=held(1, po...  1.06 us
    pallas_call x2, Pallas kernels, side_terms(): pl.pallas_call(kernel, name=name, out_shape=held(*v.shape), in_specs=[SME...  1.01 us
    pallas_call x1, Pallas kernels, sweep(): pl.pallas_call(sweep_kernel, name='sweep', out_shape=(held(*v.shape), jax...  0.89 us
  transfers between devices with their start and end apart: 11, of which 6 were waited for; matrix products, arithmetic and copies ran while one was open for 0% of the time, Pallas kernels for 23%

profile of v22, /device:TPU:0, one launch (start us, length us, event | category | flops | bytes accessed | tf_op | source)
XLA Modules:
  0.0 35.2 jit_solution(7089733848818103761)
XLA Ops:
  0.6 1.1 %load_axial.1.first_ref = f32[1,12,8,512]{3,2,1,0:T(8,128)S(1)} custom-call(f32[3,16,8,512]{3,2,1,0:T(8,128)} %v_ref.29), custom_call_target="tpu_custom_call" | custom-call | tf_op jit(solution)/shard_map/load_axial/pallas_call | solution.py:107
  1.7 3.0 %collective-permute-start = (f32[1,12,8,512]{3,2,1,0:T(8,128)S(1)}, f32[1,12,8,512]{3,2,1,0:T(8,128)S(1)}, u32[]{:S(2)}, u32[]{:S(2)}) collective-permute-start(f32[1,12,8,512]{3,2,1,0:T(8,128)S(1)} %load_axial.1.first_ref), channel_id=1, source_target_pairs={{0,1},{1,0},{2,3},{3,2},{4,5},{5,4},{6,7},{7,6},{8,9},{9,8},{10,11... | collective-permute-start | bytes 589832 | tf_op jit(solution)/shard_map/ppermute | solution.py:44
  4.8 3.8 %collective-permute-start.2 = (f32[3,10,8,512]{3,2,1,0:T(8,128)S(1)}, f32[3,10,8,512]{3,2,1,0:T(8,128)S(1)}, u32[]{:S(2)}, u32[]{:S(2)}) collective-permute-start(f32[3,10,8,512]{3,2,1,0:T(8,128)S(1)} %pack_chip.1.first_ref), channel_id=1, source_target_pairs={{2,4},{4,2},{6,8},{8,6},{10,12},{12,10},{14,16},{16,14},{18,20},{2... | collective-permute-start | bytes 1474568 | tf_op jit(solution)/shard_map/ppermute | solution.py:52
  9.4 0.6 %table.1 = (f32[30,512]{1,0:T(8,128)S(1)}, f32[21,8,128]{2,1,0:T(8,128)S(1)}) custom-call(s32[1]{0:T(128)} %bitcast.me_ref, f32[1]{0:T(128)S(6)} %copy.16.factor_ref, f32[21]{0:T(128)S(1)} %copy-done.2), custom_call_target="tpu_custom_call" | custom-call | flops 512000 | bytes 204800 | tf_op jit(solution)/shard_map/table/pallas_call | solution.py:516
  10.0 0.6 %share_terms.1.first_ref = f32[2,3,8,512]{3,2,1,0:T(8,128)S(1)} custom-call(f32[3,16,8,512]{3,2,1,0:T(8,128)S(1)} %copy-done, f32[1,12,8,512]{3,2,1,0:T(8,128)S(1)} %collective-permute-done.e_ref.first_ref, f32[30,512]{1,0:T(8,128)S(1)} %get-tuple-element.14.power_ref), custom_call_target="tpu_custom_call" | custom-call | flops 3932160 | bytes 1572864 | tf_op jit(solution)/shard_map/share_terms/pallas_call | solution.py:367
  10.7 1.4 %collective-permute-start.3 = (f32[2,3,8,512]{3,2,1,0:T(8,128)S(1)}, f32[2,3,8,512]{3,2,1,0:T(8,128)S(1)}, u32[]{:S(2)}, u32[]{:S(2)}) collective-permute-start(f32[2,3,8,512]{3,2,1,0:T(8,128)S(1)} %share_terms.1.first_ref), channel_id=1, source_target_pairs={{0,1},{1,0},{2,3},{3,2},{4,5},{5,4},{6,7},{7,6},{8,9},{9,8},{10,11... | collective-permute-start | bytes 294920 | tf_op jit(solution)/shard_map/ppermute | solution.py:44
  12.3 0.7 %collective-permute-start.1 = (f32[2,12,8,512]{3,2,1,0:T(8,128)S(1)}, f32[2,12,8,512]{3,2,1,0:T(8,128)S(1)}, u32[]{:S(2)}, u32[]{:S(2)}) collective-permute-start(f32[2,12,8,512]{3,2,1,0:T(8,128)S(1)} %pack_planes.1), channel_id=1, source_target_pairs={{0,1},{1,0},{2,3},{3,2},{4,5},{5,4},{6,7},{7,6},{8,9},{9,8},{10,11... | collective-permute-start | bytes 1179656 | tf_op jit(solution)/shard_map/ppermute | solution.py:44
  13.0 2.2 %inner_terms.1.n_in_ref = f32[3,16,8,512]{3,2,1,0:T(8,128)S(1)} custom-call(f32[21,8,128]{2,1,0:T(8,128)S(1)} %get-tuple-element.15.tap_ref, f32[3,16,8,512]{3,2,1,0:T(8,128)S(1)} %copy-done, f32[544,512]{1,0:T(8,128)S(1)} %bitcast.2), custom_call_target="tpu_custom_call" | custom-call | flops 5368709120 | bytes 3145728 | tf_op jit(solution)/shard_map/inner_terms/pallas_call | solution.py:284
  15.2 0.5 %core_terms.1.n_in_ref = f32[3,16,8,512]{3,2,1,0:T(8,128)S(1)} custom-call(s32[1]{0:T(128)} %bitcast.me_ref, f32[21,8,128]{2,1,0:T(8,128)S(1)} %get-tuple-element.15.tap_ref, f32[3,16,8,512]{3,2,1,0:T(8,128)S(1)} %copy-done, f32[3,10,8,512]{3,2,1,0:T(8,128)S(1)} %collective-permute-done.5.core_ref, ...), custom_call_target="tpu_custom_call", output_to_operand_aliasing={{}: (4, {})} | custom-call | flops 67108864 | bytes 2359296 | tf_op jit(solution)/shard_map/core_terms/pallas_call | solution.py:338
  15.8 0.6 %collective-permute-done.4.mirror_ref = f32[3,4,8,128]{3,2,1,0:T(8,128)S(1)} collective-permute-done((f32[3,4,8,128]{3,2,1,0:T(8,128)S(1)}, f32[3,4,8,128]{3,2,1,0:T(8,128)S(1)}, u32[]{:S(2)}, u32[]{:S(2)}) %collective-permute-start.4) | collective-permute-done | bytes 49184 | tf_op jit(solution)/shard_map/ppermute | solution.py:44
  16.4 0.5 %mirror_terms.1.n_ref.n_in_ref = f32[3,16,8,512]{3,2,1,0:T(8,128)S(1)} custom-call(f32[3,16,8,512]{3,2,1,0:T(8,128)S(1)} %copy-done, f32[544,512]{1,0:T(8,128)S(1)} %bitcast.3, f32[3,4,8,128]{3,2,1,0:T(8,128)S(1)} %collective-permute-done.4.mirror_ref, f32[3,16,8,512]{3,2,1,0:T(8,128)S(1)} %core_terms.1.n_in_ref), custom_call_target="tpu_custom_call", output_to_operand_aliasing={{}: (3, {})} | custom-call | flops 67108864 | bytes 3145728 | tf_op jit(solution)/shard_map/mirror_terms/pallas_call | solution.py:239
  17.3 1.4 %collective-permute-start.6 = (f32[2,3,8,256]{3,2,1,0:T(8,128)S(1)}, f32[2,3,8,256]{3,2,1,0:T(8,128)S(1)}, u32[]{:S(2)}, u32[]{:S(2)}) collective-permute-start(f32[2,3,8,256]{3,2,1,0:T(8,128)S(1)} %chip_other.1.ready_ref), channel_id=1, source_target_pairs={{0,2},{2,0},{4,6},{6,4},{8,10},{10,8},{12,14},{14,12},{16,18},{18,... | collective-permute-start | bytes 147464 | tf_op jit(solution)/shard_map/ppermute | solution.py:44
  18.9 0.7 %collective-permute-done.6.other_ref = f32[2,3,8,256]{3,2,1,0:T(8,128)S(1)} collective-permute-done((f32[2,3,8,256]{3,2,1,0:T(8,128)S(1)}, f32[2,3,8,256]{3,2,1,0:T(8,128)S(1)}, u32[]{:S(2)}, u32[]{:S(2)}) %collective-permute-start.6) | collective-permute-done | bytes 49184 | tf_op jit(solution)/shard_map/ppermute | solution.py:44
  19.6 1.8 %collective-permute-start.7 = (f32[2,3,8,256]{3,2,1,0:T(8,128)S(1)}, f32[2,3,8,256]{3,2,1,0:T(8,128)S(1)}, u32[]{:S(2)}, u32[]{:S(2)}) collective-permute-start(f32[2,3,8,256]{3,2,1,0:T(8,128)S(1)} %pair.1.block_ref), channel_id=1, source_target_pairs={{0,4},{2,6},{4,0},{6,2},{8,12},{10,14},{12,8},{14,10},{16,20},{18,... | collective-permute-start | bytes 147464 | tf_op jit(solution)/shard_map/ppermute | solution.py:44
  21.4 2.4 %collective-permute-done.7.other_ref = f32[2,3,8,256]{3,2,1,0:T(8,128)S(1)} collective-permute-done((f32[2,3,8,256]{3,2,1,0:T(8,128)S(1)}, f32[2,3,8,256]{3,2,1,0:T(8,128)S(1)}, u32[]{:S(2)}, u32[]{:S(2)}) %collective-permute-start.7) | collective-permute-done | bytes 49184 | tf_op jit(solution)/shard_map/ppermute | solution.py:44
  23.8 1.6 %collective-permute-start.8 = (f32[2,3,8,256]{3,2,1,0:T(8,128)S(1)}, f32[2,3,8,256]{3,2,1,0:T(8,128)S(1)}, u32[]{:S(2)}, u32[]{:S(2)}) collective-permute-start(f32[2,3,8,256]{3,2,1,0:T(8,128)S(1)} %get-tuple-element.16.block_ref), channel_id=1, source_target_pairs={{0,8},{2,10},{4,12},{6,14},{8,0},{10,2},{12,4},{14,6},{16,24},{18,... | collective-permute-start | bytes 147464 | tf_op jit(solution)/shard_map/ppermute | solution.py:44
  25.5 2.5 %collective-permute-done.8.other_ref = f32[2,3,8,256]{3,2,1,0:T(8,128)S(1)} collective-permute-done((f32[2,3,8,256]{3,2,1,0:T(8,128)S(1)}, f32[2,3,8,256]{3,2,1,0:T(8,128)S(1)}, u32[]{:S(2)}, u32[]{:S(2)}) %collective-permute-start.8) | collective-permute-done | bytes 49184 | tf_op jit(solution)/shard_map/ppermute | solution.py:44
  28.0 2.7 %collective-permute-start.9 = (f32[2,3,8,256]{3,2,1,0:T(8,128)S(1)}, f32[2,3,8,256]{3,2,1,0:T(8,128)S(1)}, u32[]{:S(2)}, u32[]{:S(2)}) collective-permute-start(f32[2,3,8,256]{3,2,1,0:T(8,128)S(1)} %get-tuple-element.18.ready_ref.block_ref), channel_id=1, source_target_pairs={{0,16},{2,18},{4,20},{6,22},{8,24},{10,26},{12,28},{14,30},{16,0},... | collective-permute-start | bytes 147464 | tf_op jit(solution)/shard_map/ppermute | solution.py:44
  30.7 0.5 %late_terms.1.n_in_ref = f32[3,16,8,512]{3,2,1,0:T(8,128)S(1)} custom-call(s32[1]{0:T(128)} %bitcast.me_ref, f32[21,8,128]{2,1,0:T(8,128)S(1)} %get-tuple-element.15.tap_ref, f32[3,16,8,512]{3,2,1,0:T(8,128)S(1)} %copy-done, f32[3,10,8,512]{3,2,1,0:T(8,128)S(1)} %collective-permute-done.2.chip_ref, ...), custom_call_target="tpu_custom_call", output_to_operand_aliasing={{}: (4, {})} | custom-call | flops 67108864 | bytes 2359296 | tf_op jit(solution)/shard_map/late_terms/pallas_call | solution.py:338
  31.2 0.6 %planes_terms.1.n_ref = f32[3,16,8,512]{3,2,1,0:T(8,128)S(1)} custom-call(f32[3,16,8,512]{3,2,1,0:T(8,128)S(1)} %copy-done, f32[2,12,8,512]{3,2,1,0:T(8,128)S(1)} %collective-permute-done.1.y_ref, f32[1,12,8,512]{3,2,1,0:T(8,128)S(1)} %collective-permute-done.e_ref.first_ref, ...), custom_call_target="tpu_custom_call", output_to_operand_aliasing={{}: (4, {})} | custom-call | flops 3932160 | bytes 3145728 | tf_op jit(solution)/shard_map/planes_terms/pallas_call | solution.py:471
  31.7 0.9 %sweep.1 = (f32[3,16,8,512]{3,2,1,0:T(8,128)S(1)}, f32[3,16,8,512]{3,2,1,0:T(8,128)}) custom-call(f32[3,16,8,512]{3,2,1,0:T(8,128)S(1)} %copy-done, f32[3,16,8,512]{3,2,1,0:T(8,128)S(1)} %planes_terms.1.n_ref, f32[30,512]{1,0:T(8,128)S(1)} %get-tuple-element.14.power_ref), custom_call_target="tpu_custom_call" | custom-call | flops 1966080 | bytes 2359296 | tf_op jit(solution)/shard_map/sweep/pallas_call | solution.py:556
  32.6 0.4 %collective-permute-done.9.other_ref = f32[2,3,8,256]{3,2,1,0:T(8,128)S(1)} collective-permute-done((f32[2,3,8,256]{3,2,1,0:T(8,128)S(1)}, f32[2,3,8,256]{3,2,1,0:T(8,128)S(1)}, u32[]{:S(2)}, u32[]{:S(2)}) %collective-permute-start.9) | collective-permute-done | bytes 49184 | tf_op jit(solution)/shard_map/ppermute | solution.py:44
  33.2 0.8 %close_own.1.refs_0_ = f32[3,16,8,512]{3,2,1,0:T(8,128)} custom-call(s32[1]{0:T(128)} %bitcast.me_ref, f32[3,16,8,512]{3,2,1,0:T(8,128)S(1)} %get-tuple-element.19.ready_ref.s_ref, f32[30,512]{1,0:T(8,128)S(1)} %get-tuple-element.14.power_ref, f32[2,3,8,256]{3,2,1,0:T(8,128)S(1)} %get-tuple-element.24.entry_ref), custom_call_target="tpu_custom_call" | custom-call | flops 786432 | bytes 1572864 | tf_op jit(solution)/shard_map/close_own/pallas_call | solution.py:676
  34.4 0.8 %close_other.1 = f32[3,16,8,512]{3,2,1,0:T(8,128)} custom-call(s32[1]{0:T(128)} %bitcast.me_ref, f32[3,16,8,512]{3,2,1,0:T(8,128)S(1)} %get-tuple-element.19.ready_ref.s_ref, f32[30,512]{1,0:T(8,128)S(1)} %get-tuple-element.14.power_ref, f32[2,3,8,256]{3,2,1,0:T(8,128)S(1)} %collective-permute-done.10.entry_ref, ...), custom_call_target="tpu_custom_call", output_to_operand_aliasing={{}: (4, {})} | custom-call | flops 786432 | bytes 1572864 | tf_op jit(solution)/shard_map/close_other/pallas_call | solution.py:676
  (28 shorter events, 1.5 us)
Async XLA Ops:
  0.6 4.1 %copy-start = (f32[3,16,8,512]{3,2,1,0:T(8,128)S(1)}, f32[3,16,8,512]{3,2,1,0:T(8,128)}, u32[]{:S(2)}) copy-start(f32[3,16,8,512]{3,2,1,0:T(8,128)} %v_ref.29) | copy-start | bytes 2359300
  1.7 8.3 %collective-permute-start = (f32[1,12,8,512]{3,2,1,0:T(8,128)S(1)}, f32[1,12,8,512]{3,2,1,0:T(8,128)S(1)}, u32[]{:S(2)}, u32[]{:S(2)}) collective-permute-start(f32[1,12,8,512]{3,2,1,0:T(8,128)S(1)} %load_axial.1.first_ref), channel_id=1, source_target_pairs={{0,1},{1,0},{2,3},{3,2},{4,5},{5,4},{6,7},{7,6},{8,9},{9,8},{10,11... | collective-permute-start | bytes 589832 | tf_op jit(solution)/shard_map/ppermute | solution.py:44
  4.7 4.6 %copy-start.2 = (f32[21]{0:T(128)S(1)}, f32[21]{0:T(128)}, u32[]{:S(2)}) copy-start(f32[21]{0:T(128)} %stencil_ref.1) | copy-start | bytes 256
  4.8 12.3 %collective-permute-start.2 = (f32[3,10,8,512]{3,2,1,0:T(8,128)S(1)}, f32[3,10,8,512]{3,2,1,0:T(8,128)S(1)}, u32[]{:S(2)}, u32[]{:S(2)}) collective-permute-start(f32[3,10,8,512]{3,2,1,0:T(8,128)S(1)} %pack_chip.1.first_ref), channel_id=1, source_target_pairs={{2,4},{4,2},{6,8},{8,6},{10,12},{12,10},{14,16},{16,14},{18,20},{2... | collective-permute-start | bytes 1474568 | tf_op jit(solution)/shard_map/ppermute | solution.py:52
  8.7 7.7 %collective-permute-start.4 = (f32[3,4,8,128]{3,2,1,0:T(8,128)S(1)}, f32[3,4,8,128]{3,2,1,0:T(8,128)S(1)}, u32[]{:S(2)}, u32[]{:S(2)}) collective-permute-start(f32[3,4,8,128]{3,2,1,0:T(8,128)S(1)} %pack_mirror.1), channel_id=1, source_target_pairs={{0,16},{2,18},{4,20},{6,22},{8,24},{10,26},{12,28},{14,30},{16,0},... | collective-permute-start | bytes 147464 | tf_op jit(solution)/shard_map/ppermute | solution.py:44
  10.6 2.4 %copy-start.1 = (f32[512,544]{0,1:T(8,128)S(1)}, f32[512,544]{0,1:T(8,128)}, u32[]{:S(2)}) copy-start(f32[512,544]{0,1:T(8,128)} %param.5) | copy-start | bytes 3342340
  10.7 6.2 %collective-permute-start.3 = (f32[2,3,8,512]{3,2,1,0:T(8,128)S(1)}, f32[2,3,8,512]{3,2,1,0:T(8,128)S(1)}, u32[]{:S(2)}, u32[]{:S(2)}) collective-permute-start(f32[2,3,8,512]{3,2,1,0:T(8,128)S(1)} %share_terms.1.first_ref), channel_id=1, source_target_pairs={{0,1},{1,0},{2,3},{3,2},{4,5},{5,4},{6,7},{7,6},{8,9},{9,8},{10,11... | collective-permute-start | bytes 294920 | tf_op jit(solution)/shard_map/ppermute | solution.py:44
  12.2 3.0 %collective-permute-start.5 = (f32[3,10,8,512]{3,2,1,0:T(8,128)S(1)}, f32[3,10,8,512]{3,2,1,0:T(8,128)S(1)}, u32[]{:S(2)}, u32[]{:S(2)}) collective-permute-start(f32[3,10,8,512]{3,2,1,0:T(8,128)S(1)} %pack_core.1), channel_id=1, source_target_pairs={{0,2},{2,0},{4,6},{6,4},{8,10},{10,8},{12,14},{14,12},{16,18},{18,... | collective-permute-start | bytes 1474568 | tf_op jit(solution)/shard_map/ppermute | solution.py:44
  12.3 18.9 %collective-permute-start.1 = (f32[2,12,8,512]{3,2,1,0:T(8,128)S(1)}, f32[2,12,8,512]{3,2,1,0:T(8,128)S(1)}, u32[]{:S(2)}, u32[]{:S(2)}) collective-permute-start(f32[2,12,8,512]{3,2,1,0:T(8,128)S(1)} %pack_planes.1), channel_id=1, source_target_pairs={{0,1},{1,0},{2,3},{3,2},{4,5},{5,4},{6,7},{7,6},{8,9},{9,8},{10,11... | collective-permute-start | bytes 1179656 | tf_op jit(solution)/shard_map/ppermute | solution.py:44
  17.3 2.3 %collective-permute-start.6 = (f32[2,3,8,256]{3,2,1,0:T(8,128)S(1)}, f32[2,3,8,256]{3,2,1,0:T(8,128)S(1)}, u32[]{:S(2)}, u32[]{:S(2)}) collective-permute-start(f32[2,3,8,256]{3,2,1,0:T(8,128)S(1)} %chip_other.1.ready_ref), channel_id=1, source_target_pairs={{0,2},{2,0},{4,6},{6,4},{8,10},{10,8},{12,14},{14,12},{16,18},{18,... | collective-permute-start | bytes 147464 | tf_op jit(solution)/shard_map/ppermute | solution.py:44
  19.6 4.2 %collective-permute-start.7 = (f32[2,3,8,256]{3,2,1,0:T(8,128)S(1)}, f32[2,3,8,256]{3,2,1,0:T(8,128)S(1)}, u32[]{:S(2)}, u32[]{:S(2)}) collective-permute-start(f32[2,3,8,256]{3,2,1,0:T(8,128)S(1)} %pair.1.block_ref), channel_id=1, source_target_pairs={{0,4},{2,6},{4,0},{6,2},{8,12},{10,14},{12,8},{14,10},{16,20},{18,... | collective-permute-start | bytes 147464 | tf_op jit(solution)/shard_map/ppermute | solution.py:44
  23.8 4.2 %collective-permute-start.8 = (f32[2,3,8,256]{3,2,1,0:T(8,128)S(1)}, f32[2,3,8,256]{3,2,1,0:T(8,128)S(1)}, u32[]{:S(2)}, u32[]{:S(2)}) collective-permute-start(f32[2,3,8,256]{3,2,1,0:T(8,128)S(1)} %get-tuple-element.16.block_ref), channel_id=1, source_target_pairs={{0,8},{2,10},{4,12},{6,14},{8,0},{10,2},{12,4},{14,6},{16,24},{18,... | collective-permute-start | bytes 147464 | tf_op jit(solution)/shard_map/ppermute | solution.py:44
  28.0 5.1 %collective-permute-start.9 = (f32[2,3,8,256]{3,2,1,0:T(8,128)S(1)}, f32[2,3,8,256]{3,2,1,0:T(8,128)S(1)}, u32[]{:S(2)}, u32[]{:S(2)}) collective-permute-start(f32[2,3,8,256]{3,2,1,0:T(8,128)S(1)} %get-tuple-element.18.ready_ref.block_ref), channel_id=1, source_target_pairs={{0,16},{2,18},{4,20},{6,22},{8,24},{10,26},{12,28},{14,30},{16,0},... | collective-permute-start | bytes 147464 | tf_op jit(solution)/shard_map/ppermute | solution.py:44
  33.1 1.3 %collective-permute-start.10 = (f32[2,3,8,256]{3,2,1,0:T(8,128)S(1)}, f32[2,3,8,256]{3,2,1,0:T(8,128)S(1)}, u32[]{:S(2)}, u32[]{:S(2)}) collective-permute-start(f32[2,3,8,256]{3,2,1,0:T(8,128)S(1)} %get-tuple-element.23), channel_id=1, source_target_pairs={{0,2},{2,0},{4,6},{6,4},{8,10},{10,8},{12,14},{14,12},{16,18},{18,... | collective-permute-start | bytes 147464 | tf_op jit(solution)/shard_map/ppermute | solution.py:44

commit v23 on v22

--- a/solution.py
+++ b/solution.py
@@ -95,10 +95,16 @@
             tile_ref[c, j, hi + 1 :] = y_ref[c, 3 * j + 2, lo:hi]
 
 
-def load_axial_kernel(hbm_ref, y_ref, e_ref, sem):
-    load = pltpu.make_async_copy(hbm_ref.at[pl.ds(hbm_ref.shape[0] - 1, 1)], e_ref, sem)
-    load.start()
-    load.wait()
+def load_axial_kernel(hbm_ref, y_ref, e_ref, sems):
+    count = sems.shape[0]
+    part = e_ref.shape[1] // count
+    loads = []
+    for k in range(count):
+        some = pl.ds(k * part, part)
+        loads.append(pltpu.make_async_copy(hbm_ref.at[hbm_ref.shape[0] - 1, some], e_ref.at[0, some], sems.at[k]))
+        loads[k].start()
+    for load in loads:
+        load.wait()
     pack_tiles(e_ref, y_ref, (0,))
 
 
@@ -110,7 +116,10 @@
         out_shape=held(1, points - points // 4, planes, radial),
         in_specs=[HBM],
         out_specs=VMEM,
-        scratch_shapes=[pltpu.VMEM((1, points, planes, radial), jnp.float32), pltpu.SemaphoreType.DMA],
+        scratch_shapes=[
+            pltpu.VMEM((1, points, planes, radial), jnp.float32),
+            pltpu.SemaphoreType.DMA((4 if points % 4 == 0 else 1,)),
+        ],
         compiler_params=params(v.size * 4, 2),
     )(v)
 

time: 35.4 us -> 35.4 us (level)
  no operation moved by 1% of the time
where the time goes in v23:
time: 35.4 us; the launch traced here: 35.2 us
  starting transfers between devices  16.7 us (47%)
  Pallas kernels  9.93 us (28%)
  waiting for transfers between devices  7.11 us (20%)
  between operations  1.51 us (4%)
    ppermute x10, starting transfers between devices, swap(): return lax.ppermute(block, axis, [(i, i ^ bit) for i in range(size)])  12.9 us
    ppermute x10, waiting for transfers between devices, swap(): return lax.ppermute(block, axis, [(i, i ^ bit) for i in range(size)])  7.1 us
    ppermute x1, starting transfers between devices, swap_across(): return lax.ppermute(block, axis, route)  3.76 us
    pallas_call x1, Pallas kernels, inner_terms(): pl.pallas_call(inner_kernel, name='inner_terms', out_shape=held(*v.shape)...  2.2 us
    pallas_call x2, Pallas kernels, close(): pl.pallas_call(functools.partial(close_kernel, own=own), name='close_own'...  1.59 us
    pallas_call x1, Pallas kernels, load_axial(): pl.pallas_call(load_axial_kernel, name='load_axial', out_shape=held(1, po...  1.07 us
    pallas_call x2, Pallas kernels, side_terms(): pl.pallas_call(kernel, name=name, out_shape=held(*v.shape), in_specs=[SME...  1.01 us
    pallas_call x1, Pallas kernels, sweep(): pl.pallas_call(sweep_kernel, name='sweep', out_shape=(held(*v.shape), jax...  0.89 us
  transfers between devices with their start and end apart: 11, of which 6 were waited for; matrix products, arithmetic and copies ran while one was open for 0% of the time, Pallas kernels for 23%

profile of v23, /device:TPU:0, one launch (start us, length us, event | category | flops | bytes accessed | tf_op | source)
XLA Modules:
  0.0 35.2 jit_solution(1932532410731442786)
XLA Ops:
  0.6 1.1 %load_axial.1.first_ref = f32[1,12,8,512]{3,2,1,0:T(8,128)S(1)} custom-call(f32[3,16,8,512]{3,2,1,0:T(8,128)} %v_ref.29), custom_call_target="tpu_custom_call" | custom-call | tf_op jit(solution)/shard_map/load_axial/pallas_call | solution.py:113
  1.7 3.0 %collective-permute-start = (f32[1,12,8,512]{3,2,1,0:T(8,128)S(1)}, f32[1,12,8,512]{3,2,1,0:T(8,128)S(1)}, u32[]{:S(2)}, u32[]{:S(2)}) collective-permute-start(f32[1,12,8,512]{3,2,1,0:T(8,128)S(1)} %load_axial.1.first_ref), channel_id=1, source_target_pairs={{0,1},{1,0},{2,3},{3,2},{4,5},{5,4},{6,7},{7,6},{8,9},{9,8},{10,11... | collective-permute-start | bytes 589832 | tf_op jit(solution)/shard_map/ppermute | solution.py:44
  4.8 3.8 %collective-permute-start.2 = (f32[3,10,8,512]{3,2,1,0:T(8,128)S(1)}, f32[3,10,8,512]{3,2,1,0:T(8,128)S(1)}, u32[]{:S(2)}, u32[]{:S(2)}) collective-permute-start(f32[3,10,8,512]{3,2,1,0:T(8,128)S(1)} %pack_chip.1.first_ref), channel_id=1, source_target_pairs={{2,4},{4,2},{6,8},{8,6},{10,12},{12,10},{14,16},{16,14},{18,20},{2... | collective-permute-start | bytes 1474568 | tf_op jit(solution)/shard_map/ppermute | solution.py:52
  9.4 0.6 %table.1 = (f32[30,512]{1,0:T(8,128)S(1)}, f32[21,8,128]{2,1,0:T(8,128)S(1)}) custom-call(s32[1]{0:T(128)} %bitcast.me_ref, f32[1]{0:T(128)S(6)} %copy.16.factor_ref, f32[21]{0:T(128)S(1)} %copy-done.2), custom_call_target="tpu_custom_call" | custom-call | flops 512000 | bytes 204800 | tf_op jit(solution)/shard_map/table/pallas_call | solution.py:525
  10.0 0.6 %share_terms.1.first_ref = f32[2,3,8,512]{3,2,1,0:T(8,128)S(1)} custom-call(f32[3,16,8,512]{3,2,1,0:T(8,128)S(1)} %copy-done, f32[1,12,8,512]{3,2,1,0:T(8,128)S(1)} %collective-permute-done.e_ref.first_ref, f32[30,512]{1,0:T(8,128)S(1)} %get-tuple-element.14.power_ref), custom_call_target="tpu_custom_call" | custom-call | flops 3932160 | bytes 1572864 | tf_op jit(solution)/shard_map/share_terms/pallas_call | solution.py:376
  10.7 1.4 %collective-permute-start.3 = (f32[2,3,8,512]{3,2,1,0:T(8,128)S(1)}, f32[2,3,8,512]{3,2,1,0:T(8,128)S(1)}, u32[]{:S(2)}, u32[]{:S(2)}) collective-permute-start(f32[2,3,8,512]{3,2,1,0:T(8,128)S(1)} %share_terms.1.first_ref), channel_id=1, source_target_pairs={{0,1},{1,0},{2,3},{3,2},{4,5},{5,4},{6,7},{7,6},{8,9},{9,8},{10,11... | collective-permute-start | bytes 294920 | tf_op jit(solution)/shard_map/ppermute | solution.py:44
  12.3 0.7 %collective-permute-start.1 = (f32[2,12,8,512]{3,2,1,0:T(8,128)S(1)}, f32[2,12,8,512]{3,2,1,0:T(8,128)S(1)}, u32[]{:S(2)}, u32[]{:S(2)}) collective-permute-start(f32[2,12,8,512]{3,2,1,0:T(8,128)S(1)} %pack_planes.1), channel_id=1, source_target_pairs={{0,1},{1,0},{2,3},{3,2},{4,5},{5,4},{6,7},{7,6},{8,9},{9,8},{10,11... | collective-permute-start | bytes 1179656 | tf_op jit(solution)/shard_map/ppermute | solution.py:44
  13.0 2.2 %inner_terms.1.n_in_ref = f32[3,16,8,512]{3,2,1,0:T(8,128)S(1)} custom-call(f32[21,8,128]{2,1,0:T(8,128)S(1)} %get-tuple-element.15.tap_ref, f32[3,16,8,512]{3,2,1,0:T(8,128)S(1)} %copy-done, f32[544,512]{1,0:T(8,128)S(1)} %bitcast.2), custom_call_target="tpu_custom_call" | custom-call | flops 5368709120 | bytes 3145728 | tf_op jit(solution)/shard_map/inner_terms/pallas_call | solution.py:293
  15.2 0.5 %core_terms.1.n_in_ref = f32[3,16,8,512]{3,2,1,0:T(8,128)S(1)} custom-call(s32[1]{0:T(128)} %bitcast.me_ref, f32[21,8,128]{2,1,0:T(8,128)S(1)} %get-tuple-element.15.tap_ref, f32[3,16,8,512]{3,2,1,0:T(8,128)S(1)} %copy-done, f32[3,10,8,512]{3,2,1,0:T(8,128)S(1)} %collective-permute-done.5.core_ref, ...), custom_call_target="tpu_custom_call", output_to_operand_aliasing={{}: (4, {})} | custom-call | flops 67108864 | bytes 2359296 | tf_op jit(solution)/shard_map/core_terms/pallas_call | solution.py:347
  15.8 0.6 %collective-permute-done.4.mirror_ref = f32[3,4,8,128]{3,2,1,0:T(8,128)S(1)} collective-permute-done((f32[3,4,8,128]{3,2,1,0:T(8,128)S(1)}, f32[3,4,8,128]{3,2,1,0:T(8,128)S(1)}, u32[]{:S(2)}, u32[]{:S(2)}) %collective-permute-start.4) | collective-permute-done | bytes 49184 | tf_op jit(solution)/shard_map/ppermute | solution.py:44
  16.4 0.5 %mirror_terms.1.n_ref.n_in_ref = f32[3,16,8,512]{3,2,1,0:T(8,128)S(1)} custom-call(f32[3,16,8,512]{3,2,1,0:T(8,128)S(1)} %copy-done, f32[544,512]{1,0:T(8,128)S(1)} %bitcast.3, f32[3,4,8,128]{3,2,1,0:T(8,128)S(1)} %collective-permute-done.4.mirror_ref, f32[3,16,8,512]{3,2,1,0:T(8,128)S(1)} %core_terms.1.n_in_ref), custom_call_target="tpu_custom_call", output_to_operand_aliasing={{}: (3, {})} | custom-call | flops 67108864 | bytes 3145728 | tf_op jit(solution)/shard_map/mirror_terms/pallas_call | solution.py:248
  17.3 1.4 %collective-permute-start.6 = (f32[2,3,8,256]{3,2,1,0:T(8,128)S(1)}, f32[2,3,8,256]{3,2,1,0:T(8,128)S(1)}, u32[]{:S(2)}, u32[]{:S(2)}) collective-permute-start(f32[2,3,8,256]{3,2,1,0:T(8,128)S(1)} %chip_other.1.ready_ref), channel_id=1, source_target_pairs={{0,2},{2,0},{4,6},{6,4},{8,10},{10,8},{12,14},{14,12},{16,18},{18,... | collective-permute-start | bytes 147464 | tf_op jit(solution)/shard_map/ppermute | solution.py:44
  18.9 0.7 %collective-permute-done.6.other_ref = f32[2,3,8,256]{3,2,1,0:T(8,128)S(1)} collective-permute-done((f32[2,3,8,256]{3,2,1,0:T(8,128)S(1)}, f32[2,3,8,256]{3,2,1,0:T(8,128)S(1)}, u32[]{:S(2)}, u32[]{:S(2)}) %collective-permute-start.6) | collective-permute-done | bytes 49184 | tf_op jit(solution)/shard_map/ppermute | solution.py:44
  19.7 1.8 %collective-permute-start.7 = (f32[2,3,8,256]{3,2,1,0:T(8,128)S(1)}, f32[2,3,8,256]{3,2,1,0:T(8,128)S(1)}, u32[]{:S(2)}, u32[]{:S(2)}) collective-permute-start(f32[2,3,8,256]{3,2,1,0:T(8,128)S(1)} %pair.1.block_ref), channel_id=1, source_target_pairs={{0,4},{2,6},{4,0},{6,2},{8,12},{10,14},{12,8},{14,10},{16,20},{18,... | collective-permute-start | bytes 147464 | tf_op jit(solution)/shard_map/ppermute | solution.py:44
  21.4 2.4 %collective-permute-done.7.other_ref = f32[2,3,8,256]{3,2,1,0:T(8,128)S(1)} collective-permute-done((f32[2,3,8,256]{3,2,1,0:T(8,128)S(1)}, f32[2,3,8,256]{3,2,1,0:T(8,128)S(1)}, u32[]{:S(2)}, u32[]{:S(2)}) %collective-permute-start.7) | collective-permute-done | bytes 49184 | tf_op jit(solution)/shard_map/ppermute | solution.py:44
  23.8 1.6 %collective-permute-start.8 = (f32[2,3,8,256]{3,2,1,0:T(8,128)S(1)}, f32[2,3,8,256]{3,2,1,0:T(8,128)S(1)}, u32[]{:S(2)}, u32[]{:S(2)}) collective-permute-start(f32[2,3,8,256]{3,2,1,0:T(8,128)S(1)} %get-tuple-element.16.block_ref), channel_id=1, source_target_pairs={{0,8},{2,10},{4,12},{6,14},{8,0},{10,2},{12,4},{14,6},{16,24},{18,... | collective-permute-start | bytes 147464 | tf_op jit(solution)/shard_map/ppermute | solution.py:44
  25.5 2.5 %collective-permute-done.8.other_ref = f32[2,3,8,256]{3,2,1,0:T(8,128)S(1)} collective-permute-done((f32[2,3,8,256]{3,2,1,0:T(8,128)S(1)}, f32[2,3,8,256]{3,2,1,0:T(8,128)S(1)}, u32[]{:S(2)}, u32[]{:S(2)}) %collective-permute-start.8) | collective-permute-done | bytes 49184 | tf_op jit(solution)/shard_map/ppermute | solution.py:44
  28.0 2.7 %collective-permute-start.9 = (f32[2,3,8,256]{3,2,1,0:T(8,128)S(1)}, f32[2,3,8,256]{3,2,1,0:T(8,128)S(1)}, u32[]{:S(2)}, u32[]{:S(2)}) collective-permute-start(f32[2,3,8,256]{3,2,1,0:T(8,128)S(1)} %get-tuple-element.18.ready_ref.block_ref), channel_id=1, source_target_pairs={{0,16},{2,18},{4,20},{6,22},{8,24},{10,26},{12,28},{14,30},{16,0},... | collective-permute-start | bytes 147464 | tf_op jit(solution)/shard_map/ppermute | solution.py:44
  30.7 0.5 %late_terms.1.n_in_ref = f32[3,16,8,512]{3,2,1,0:T(8,128)S(1)} custom-call(s32[1]{0:T(128)} %bitcast.me_ref, f32[21,8,128]{2,1,0:T(8,128)S(1)} %get-tuple-element.15.tap_ref, f32[3,16,8,512]{3,2,1,0:T(8,128)S(1)} %copy-done, f32[3,10,8,512]{3,2,1,0:T(8,128)S(1)} %collective-permute-done.2.chip_ref, ...), custom_call_target="tpu_custom_call", output_to_operand_aliasing={{}: (4, {})} | custom-call | flops 67108864 | bytes 2359296 | tf_op jit(solution)/shard_map/late_terms/pallas_call | solution.py:347
  31.2 0.6 %planes_terms.1.n_ref = f32[3,16,8,512]{3,2,1,0:T(8,128)S(1)} custom-call(f32[3,16,8,512]{3,2,1,0:T(8,128)S(1)} %copy-done, f32[2,12,8,512]{3,2,1,0:T(8,128)S(1)} %collective-permute-done.1.y_ref, f32[1,12,8,512]{3,2,1,0:T(8,128)S(1)} %collective-permute-done.e_ref.first_ref, ...), custom_call_target="tpu_custom_call", output_to_operand_aliasing={{}: (4, {})} | custom-call | flops 3932160 | bytes 3145728 | tf_op jit(solution)/shard_map/planes_terms/pallas_call | solution.py:480
  31.7 0.9 %sweep.1 = (f32[3,16,8,512]{3,2,1,0:T(8,128)S(1)}, f32[3,16,8,512]{3,2,1,0:T(8,128)}) custom-call(f32[3,16,8,512]{3,2,1,0:T(8,128)S(1)} %copy-done, f32[3,16,8,512]{3,2,1,0:T(8,128)S(1)} %planes_terms.1.n_ref, f32[30,512]{1,0:T(8,128)S(1)} %get-tuple-element.14.power_ref), custom_call_target="tpu_custom_call" | custom-call | flops 1966080 | bytes 2359296 | tf_op jit(solution)/shard_map/sweep/pallas_call | solution.py:565
  32.6 0.4 %collective-permute-done.9.other_ref = f32[2,3,8,256]{3,2,1,0:T(8,128)S(1)} collective-permute-done((f32[2,3,8,256]{3,2,1,0:T(8,128)S(1)}, f32[2,3,8,256]{3,2,1,0:T(8,128)S(1)}, u32[]{:S(2)}, u32[]{:S(2)}) %collective-permute-start.9) | collective-permute-done | bytes 49184 | tf_op jit(solution)/shard_map/ppermute | solution.py:44
  33.2 0.8 %close_own.1.refs_0_ = f32[3,16,8,512]{3,2,1,0:T(8,128)} custom-call(s32[1]{0:T(128)} %bitcast.me_ref, f32[3,16,8,512]{3,2,1,0:T(8,128)S(1)} %get-tuple-element.19.ready_ref.s_ref, f32[30,512]{1,0:T(8,128)S(1)} %get-tuple-element.14.power_ref, f32[2,3,8,256]{3,2,1,0:T(8,128)S(1)} %get-tuple-element.24.entry_ref), custom_call_target="tpu_custom_call" | custom-call | flops 786432 | bytes 1572864 | tf_op jit(solution)/shard_map/close_own/pallas_call | solution.py:685
  34.4 0.8 %close_other.1 = f32[3,16,8,512]{3,2,1,0:T(8,128)} custom-call(s32[1]{0:T(128)} %bitcast.me_ref, f32[3,16,8,512]{3,2,1,0:T(8,128)S(1)} %get-tuple-element.19.ready_ref.s_ref, f32[30,512]{1,0:T(8,128)S(1)} %get-tuple-element.14.power_ref, f32[2,3,8,256]{3,2,1,0:T(8,128)S(1)} %collective-permute-done.10.entry_ref, ...), custom_call_target="tpu_custom_call", output_to_operand_aliasing={{}: (4, {})} | custom-call | flops 786432 | bytes 1572864 | tf_op jit(solution)/shard_map/close_other/pallas_call | solution.py:685
  (28 shorter events, 1.5 us)
Async XLA Ops:
  0.6 4.1 %copy-start = (f32[3,16,8,512]{3,2,1,0:T(8,128)S(1)}, f32[3,16,8,512]{3,2,1,0:T(8,128)}, u32[]{:S(2)}) copy-start(f32[3,16,8,512]{3,2,1,0:T(8,128)} %v_ref.29) | copy-start | bytes 2359300
  1.7 8.3 %collective-permute-start = (f32[1,12,8,512]{3,2,1,0:T(8,128)S(1)}, f32[1,12,8,512]{3,2,1,0:T(8,128)S(1)}, u32[]{:S(2)}, u32[]{:S(2)}) collective-permute-start(f32[1,12,8,512]{3,2,1,0:T(8,128)S(1)} %load_axial.1.first_ref), channel_id=1, source_target_pairs={{0,1},{1,0},{2,3},{3,2},{4,5},{5,4},{6,7},{7,6},{8,9},{9,8},{10,11... | collective-permute-start | bytes 589832 | tf_op jit(solution)/shard_map/ppermute | solution.py:44
  4.8 4.6 %copy-start.2 = (f32[21]{0:T(128)S(1)}, f32[21]{0:T(128)}, u32[]{:S(2)}) copy-start(f32[21]{0:T(128)} %stencil_ref.1) | copy-start | bytes 256
  4.8 12.3 %collective-permute-start.2 = (f32[3,10,8,512]{3,2,1,0:T(8,128)S(1)}, f32[3,10,8,512]{3,2,1,0:T(8,128)S(1)}, u32[]{:S(2)}, u32[]{:S(2)}) collective-permute-start(f32[3,10,8,512]{3,2,1,0:T(8,128)S(1)} %pack_chip.1.first_ref), channel_id=1, source_target_pairs={{2,4},{4,2},{6,8},{8,6},{10,12},{12,10},{14,16},{16,14},{18,20},{2... | collective-permute-start | bytes 1474568 | tf_op jit(solution)/shard_map/ppermute | solution.py:52
  8.7 7.7 %collective-permute-start.4 = (f32[3,4,8,128]{3,2,1,0:T(8,128)S(1)}, f32[3,4,8,128]{3,2,1,0:T(8,128)S(1)}, u32[]{:S(2)}, u32[]{:S(2)}) collective-permute-start(f32[3,4,8,128]{3,2,1,0:T(8,128)S(1)} %pack_mirror.1), channel_id=1, source_target_pairs={{0,16},{2,18},{4,20},{6,22},{8,24},{10,26},{12,28},{14,30},{16,0},... | collective-permute-start | bytes 147464 | tf_op jit(solution)/shard_map/ppermute | solution.py:44
  10.7 2.4 %copy-start.1 = (f32[512,544]{0,1:T(8,128)S(1)}, f32[512,544]{0,1:T(8,128)}, u32[]{:S(2)}) copy-start(f32[512,544]{0,1:T(8,128)} %param.5) | copy-start | bytes 3342340
  10.7 6.2 %collective-permute-start.3 = (f32[2,3,8,512]{3,2,1,0:T(8,128)S(1)}, f32[2,3,8,512]{3,2,1,0:T(8,128)S(1)}, u32[]{:S(2)}, u32[]{:S(2)}) collective-permute-start(f32[2,3,8,512]{3,2,1,0:T(8,128)S(1)} %share_terms.1.first_ref), channel_id=1, source_target_pairs={{0,1},{1,0},{2,3},{3,2},{4,5},{5,4},{6,7},{7,6},{8,9},{9,8},{10,11... | collective-permute-start | bytes 294920 | tf_op jit(solution)/shard_map/ppermute | solution.py:44
  12.2 3.0 %collective-permute-start.5 = (f32[3,10,8,512]{3,2,1,0:T(8,128)S(1)}, f32[3,10,8,512]{3,2,1,0:T(8,128)S(1)}, u32[]{:S(2)}, u32[]{:S(2)}) collective-permute-start(f32[3,10,8,512]{3,2,1,0:T(8,128)S(1)} %pack_core.1), channel_id=1, source_target_pairs={{0,2},{2,0},{4,6},{6,4},{8,10},{10,8},{12,14},{14,12},{16,18},{18,... | collective-permute-start | bytes 1474568 | tf_op jit(solution)/shard_map/ppermute | solution.py:44
  12.3 18.9 %collective-permute-start.1 = (f32[2,12,8,512]{3,2,1,0:T(8,128)S(1)}, f32[2,12,8,512]{3,2,1,0:T(8,128)S(1)}, u32[]{:S(2)}, u32[]{:S(2)}) collective-permute-start(f32[2,12,8,512]{3,2,1,0:T(8,128)S(1)} %pack_planes.1), channel_id=1, source_target_pairs={{0,1},{1,0},{2,3},{3,2},{4,5},{5,4},{6,7},{7,6},{8,9},{9,8},{10,11... | collective-permute-start | bytes 1179656 | tf_op jit(solution)/shard_map/ppermute | solution.py:44
  17.3 2.3 %collective-permute-start.6 = (f32[2,3,8,256]{3,2,1,0:T(8,128)S(1)}, f32[2,3,8,256]{3,2,1,0:T(8,128)S(1)}, u32[]{:S(2)}, u32[]{:S(2)}) collective-permute-start(f32[2,3,8,256]{3,2,1,0:T(8,128)S(1)} %chip_other.1.ready_ref), channel_id=1, source_target_pairs={{0,2},{2,0},{4,6},{6,4},{8,10},{10,8},{12,14},{14,12},{16,18},{18,... | collective-permute-start | bytes 147464 | tf_op jit(solution)/shard_map/ppermute | solution.py:44
  19.7 4.2 %collective-permute-start.7 = (f32[2,3,8,256]{3,2,1,0:T(8,128)S(1)}, f32[2,3,8,256]{3,2,1,0:T(8,128)S(1)}, u32[]{:S(2)}, u32[]{:S(2)}) collective-permute-start(f32[2,3,8,256]{3,2,1,0:T(8,128)S(1)} %pair.1.block_ref), channel_id=1, source_target_pairs={{0,4},{2,6},{4,0},{6,2},{8,12},{10,14},{12,8},{14,10},{16,20},{18,... | collective-permute-start | bytes 147464 | tf_op jit(solution)/shard_map/ppermute | solution.py:44
  23.8 4.2 %collective-permute-start.8 = (f32[2,3,8,256]{3,2,1,0:T(8,128)S(1)}, f32[2,3,8,256]{3,2,1,0:T(8,128)S(1)}, u32[]{:S(2)}, u32[]{:S(2)}) collective-permute-start(f32[2,3,8,256]{3,2,1,0:T(8,128)S(1)} %get-tuple-element.16.block_ref), channel_id=1, source_target_pairs={{0,8},{2,10},{4,12},{6,14},{8,0},{10,2},{12,4},{14,6},{16,24},{18,... | collective-permute-start | bytes 147464 | tf_op jit(solution)/shard_map/ppermute | solution.py:44
  28.0 5.1 %collective-permute-start.9 = (f32[2,3,8,256]{3,2,1,0:T(8,128)S(1)}, f32[2,3,8,256]{3,2,1,0:T(8,128)S(1)}, u32[]{:S(2)}, u32[]{:S(2)}) collective-permute-start(f32[2,3,8,256]{3,2,1,0:T(8,128)S(1)} %get-tuple-element.18.ready_ref.block_ref), channel_id=1, source_target_pairs={{0,16},{2,18},{4,20},{6,22},{8,24},{10,26},{12,28},{14,30},{16,0},... | collective-permute-start | bytes 147464 | tf_op jit(solution)/shard_map/ppermute | solution.py:44
  33.1 1.3 %collective-permute-start.10 = (f32[2,3,8,256]{3,2,1,0:T(8,128)S(1)}, f32[2,3,8,256]{3,2,1,0:T(8,128)S(1)}, u32[]{:S(2)}, u32[]{:S(2)}) collective-permute-start(f32[2,3,8,256]{3,2,1,0:T(8,128)S(1)} %get-tuple-element.23), channel_id=1, source_target_pairs={{0,2},{2,0},{4,6},{6,4},{8,10},{10,8},{12,14},{14,12},{16,18},{18,... | collective-permute-start | bytes 147464 | tf_op jit(solution)/shard_map/ppermute | solution.py:44
